TPU v7x, 32 devices: a whole 2x2x4 slice. The times are simulated.
32 devices in a mesh: rows: 8 (over z, y), cols: 4 (over x, core).
Axes of the slice: x: 2, y: 2, z: 4, core: 2. Of those that a mesh axis runs over, the one named last changes fastest.
Arguments:
- inputs: bfloat16 [192, 180, 768], P('rows', 'cols'), may hold values from -6 to 6
- valid_mask: int32 [192, 180], P('rows', 'cols'), may hold values from 0 to 1, as said below
- cotangent: bfloat16 [192, 180, 768], P('rows', 'cols'), may hold values from -6 to 6
- first_gain: float32 [768], replicated, may hold values from 0.5 to 1.5
- first_shift: float32 [768], replicated, may hold values from -1.5 to 1.5
- mix_weight_a: bfloat16 [2, 8, 96, 96], replicated, may hold values from -0.4375 to 0.4375
- mix_bias_a: float32 [2, 768], replicated, may hold values from -0.1 to 0.1
- mix_weight_b: bfloat16 [2, 8, 96, 96], replicated, may hold values from -0.4375 to 0.4375
- mix_bias_b: float32 [2, 768], replicated, may hold values from -0.2 to 0.2
- second_gain: float32 [768], replicated, may hold values from 0.5 to 1.5
- second_shift: float32 [768], replicated, may hold values from -1.5 to 1.5
- expand_weight: bfloat16 [768, 3072], replicated, may hold values from -0.21875 to 0.21875
- expand_bias: float32 [3072], replicated, may hold values from -1.5 to 1.5
- reduce_weight: bfloat16 [3072, 768], replicated, may hold values from -0.109375 to 0.109375
- reduce_bias: float32 [768], replicated, may hold values from -1.5 to 1.5
Outputs:
- outputs: float32 [192, 180, 768], P('rows', 'cols')
- grad_inputs: float32 [192, 180, 768], P('rows', 'cols')
- grad_first_gain: float32 [768], replicated
- grad_first_shift: float32 [768], replicated
- grad_mix_weight_a: float32 [2, 8, 96, 96], replicated
- grad_mix_bias_a: float32 [2, 768], replicated
- grad_mix_weight_b: float32 [2, 8, 96, 96], replicated
- grad_mix_bias_b: float32 [2, 768], replicated
- grad_second_gain: float32 [768], replicated
- grad_second_shift: float32 [768], replicated
- grad_expand_weight: float32 [768, 3072], replicated
- grad_expand_bias: float32 [3072], replicated
- grad_reduce_weight: float32 [3072, 768], replicated
- grad_reduce_bias: float32 [768], replicated
Inputs may be any that keep to these rules, and one draw needn't show every extreme that they name: `valid_mask`: 1 marks a patch that holds data; rows whose latitude within a snapshot is 90 or more are 0.
All inputs are finite; a program needn't handle non-finite values.
Results may differ from a plain program's by a relative error of at most 0.022.
Values may be sent and summed in bfloat16 or wider, within the bound.
No kernel may reach another device: no remote copies, remote signals or barrier semaphores. Data moves between devices by JAX's collectives and lax.ppermute only.
A program may use at most 256 MiB of HBM per device.

v0:
```python
import math

import jax
import jax.numpy as jnp
from jax import lax
from jax.sharding import PartitionSpec as P

BLOCKS = 8
LAT = 96


shrink_level = 0.01
shrink_soft = 0.1
norm_eps = 1e-05


def layer_norm(source, gain_in, shift_in):
    average = jnp.mean(source, axis=-1, keepdims=True)
    centred = source - average
    spread = jnp.mean(centred * centred, axis=-1, keepdims=True)
    return centred * lax.rsqrt(spread + norm_eps) * gain_in + shift_in


def shrink(values):
    return values - shrink_level * jnp.tanh(values / shrink_soft)


def shrink_factor(values):
    squash = jnp.tanh(values / shrink_soft)
    return 1.0 - shrink_level / shrink_soft * (1.0 - squash * squash)


def dft_tables(length, modes_count):
    positions = jnp.arange(length, dtype=jnp.int32)[:, None]
    frequency = jnp.arange(modes_count, dtype=jnp.int32)[None, :]
    angles = (positions * frequency % length).astype(jnp.float32) * (2.0 * math.pi / length)
    factor = 1.0 / math.sqrt(length)
    return (jnp.cos(angles) * factor, jnp.sin(angles) * factor)


def split_halves(values):
    upper = values.astype(jnp.bfloat16)
    lower = (values - upper.astype(jnp.float32)).astype(jnp.bfloat16)
    return (upper, lower)


def exact_product(form, left, right):
    left_up, left_down = split_halves(left)
    right_up, right_down = split_halves(right)
    total = jnp.einsum(form, left_up, right_up, preferred_element_type=jnp.float32)
    total = total + jnp.einsum(form, left_up, right_down, preferred_element_type=jnp.float32)
    return total + jnp.einsum(form, left_down, right_up, preferred_element_type=jnp.float32)


def lon_forward(cells, lon_size):
    lon_cos, lon_sin = dft_tables(lon_size, lon_size // 2 + 1)
    return (
        exact_product("slnc,nf->slfc", cells, lon_cos),
        -exact_product("slnc,nf->slfc", cells, lon_sin),
    )


def lat_forward(real_in, imag_in, lat_size):
    lat_cos, lat_sin = dft_tables(lat_size, lat_size)
    real_out = exact_product("lk,slfc->skfc", lat_cos, real_in) + exact_product(
        "lk,slfc->skfc", lat_sin, imag_in
    )
    imag_out = exact_product("lk,slfc->skfc", lat_cos, imag_in) - exact_product(
        "lk,slfc->skfc", lat_sin, real_in
    )
    return (real_out, imag_out)


def lat_inverse(real_in, imag_in, lat_size):
    lat_cos, lat_sin = dft_tables(lat_size, lat_size)
    real_out = exact_product("lk,skfc->slfc", lat_cos, real_in) - exact_product(
        "lk,skfc->slfc", lat_sin, imag_in
    )
    imag_out = exact_product("lk,skfc->slfc", lat_cos, imag_in) + exact_product(
        "lk,skfc->slfc", lat_sin, real_in
    )
    return (real_out, imag_out)


def lon_inverse(real_in, imag_in, lon_size, weights_lon):
    lon_cos, lon_sin = dft_tables(lon_size, lon_size // 2 + 1)
    scale = weights_lon[None, None, :, None]
    return exact_product("slfc,nf->slnc", real_in * scale, lon_cos) - exact_product(
        "slfc,nf->slnc", imag_in * scale, lon_sin
    )


def mode_weights(lon_size):
    lon_modes = lon_size // 2 + 1
    frequency = jnp.arange(lon_modes, dtype=jnp.int32)
    return jnp.where((frequency == 0) | (frequency == lon_modes - 1), 1.0, 2.0).astype(jnp.float32)


def block_apply(weight, source):
    return jnp.einsum("mbi,bio->mbo", source, weight, preferred_element_type=jnp.float32)


def block_back(weight, grad_out):
    return jnp.einsum("mbo,bio->mbi", grad_out, weight, preferred_element_type=jnp.float32)


def block_outer(source, grad_out):
    return jnp.einsum("mbi,mbo->bio", source, grad_out, preferred_element_type=jnp.float32)


def complex_layer(source, weight, bias_row):
    real_part = block_apply(weight[0], source[0]) - block_apply(weight[1], source[1])
    imag_part = block_apply(weight[0], source[1]) + block_apply(weight[1], source[0])
    stacked = jnp.stack([real_part, imag_part])
    return stacked + bias_row.reshape(2, 1, weight.shape[1], weight.shape[3])


def complex_back(grad_out, source, weight):
    grad_real = block_back(weight[0], grad_out[0]) + block_back(weight[1], grad_out[1])
    grad_imag = block_back(weight[0], grad_out[1]) - block_back(weight[1], grad_out[0])
    weight_real = block_outer(source[0], grad_out[0]) + block_outer(source[1], grad_out[1])
    weight_imag = block_outer(source[0], grad_out[1]) - block_outer(source[1], grad_out[0])
    bias_grad = jnp.sum(grad_out.astype(jnp.float32), axis=1).reshape(2, -1)
    return (jnp.stack([grad_real, grad_imag]), jnp.stack([weight_real, weight_imag]), bias_grad)


def inner_rows(left, right):
    return lax.dot_general(
        left, right, (((0,), (0,)), ((), ())), preferred_element_type=jnp.float32
    )


def outer_cols(left, right):
    return lax.dot_general(
        left, right, (((1,), (1,)), ((), ())), preferred_element_type=jnp.float32
    )


def per_device(
    inputs,
    valid_mask,
    cotangent,
    first_gain,
    first_shift,
    mix_weight_a,
    mix_bias_a,
    mix_weight_b,
    mix_bias_b,
    second_gain,
    second_shift,
    expand_weight,
    expand_bias,
    reduce_weight,
    reduce_bias,
):
    row_devs = lax.axis_size("rows")
    col_devs = lax.axis_size("cols")
    rows_here, cols_here, channels = inputs.shape
    lon_size = cols_here * col_devs
    lon_modes = lon_size // 2 + 1
    block_size = channels // BLOCKS
    share = channels // (row_devs * col_devs)
    total_rows = rows_here * row_devs
    snaps = total_rows // LAT
    mode_count = total_rows * lon_modes // (row_devs * col_devs)
    grid_shape = (rows_here, cols_here, col_devs, row_devs, share)
    chan_shape = (total_rows, lon_size, 1, 1, share)
    spec_shape = (2, col_devs, row_devs, mode_count, 1, 1, share)
    mixed_shape = (2, 1, 1, mode_count, col_devs, row_devs, share)
    weights_lon = mode_weights(lon_size)
    ones_lon = jnp.ones((lon_modes,), jnp.float32)
    masked = valid_mask.astype(jnp.float32)[:, :, None]
    fields = inputs.astype(jnp.float32)

    def first_branch(source, gain_in, shift_in):
        return masked * layer_norm(source, gain_in, shift_in)

    def modes_of(cells_low):
        cells = cells_low.astype(jnp.float32).reshape(snaps, LAT, lon_size, share)
        half_real, half_imag = lon_forward(cells, lon_size)
        full_real, full_imag = lat_forward(half_real, half_imag, LAT)
        return jnp.stack([full_real, full_imag]).astype(jnp.bfloat16).reshape(spec_shape)

    def spectral_mix(modes_in):
        blocked = modes_in.reshape(2, mode_count, BLOCKS, block_size)
        pre_first = complex_layer(blocked, mix_weight_a, mix_bias_a)
        hidden_low = jax.nn.gelu(pre_first).astype(jnp.bfloat16)
        pre_second = complex_layer(hidden_low, mix_weight_b, mix_bias_b)
        return (blocked, pre_first, hidden_low, pre_second)

    normed, first_pull = jax.vjp(first_branch, fields, first_gain, first_shift)
    normed_low = normed.astype(jnp.bfloat16)
    chan_cells = lax.all_to_all(
        lax.all_to_all(
            normed_low.reshape(grid_shape), "rows", split_axis=3, concat_axis=0, tiled=True
        ),
        "cols",
        split_axis=2,
        concat_axis=1,
        tiled=True,
    )
    chan_modes = modes_of(chan_cells)
    modes_low = lax.all_to_all(
        lax.all_to_all(chan_modes, "rows", split_axis=2, concat_axis=5, tiled=True),
        "cols",
        split_axis=1,
        concat_axis=4,
        tiled=True,
    )
    blocked, pre_first, hidden_low, pre_second = spectral_mix(modes_low)
    shrunk_low = shrink(pre_second).astype(jnp.bfloat16).reshape(mixed_shape)
    arrived = lax.all_to_all(
        lax.all_to_all(shrunk_low, "rows", split_axis=5, concat_axis=2, tiled=True),
        "cols",
        split_axis=4,
        concat_axis=1,
        tiled=True,
    )
    chan_shrunk = arrived.astype(jnp.float32).reshape(2, snaps, LAT, lon_modes, share)
    back_real, back_imag = lat_inverse(chan_shrunk[0], chan_shrunk[1], LAT)
    chan_spatial = lon_inverse(back_real, back_imag, lon_size, weights_lon).astype(jnp.bfloat16)
    grid_spatial = lax.all_to_all(
        lax.all_to_all(
            chan_spatial.reshape(chan_shape), "rows", split_axis=0, concat_axis=3, tiled=True
        ),
        "cols",
        split_axis=1,
        concat_axis=2,
        tiled=True,
    )
    spectral = grid_spatial.reshape(rows_here, cols_here, channels).astype(jnp.float32)
    residual = fields + normed_low.astype(jnp.float32) + masked * spectral
    second_norm, second_pull = jax.vjp(layer_norm, residual, second_gain, second_shift)
    tokens_low = second_norm.astype(jnp.bfloat16).reshape(-1, channels)
    pre_up = jnp.dot(tokens_low, expand_weight, preferred_element_type=jnp.float32) + expand_bias
    active_low = jax.nn.gelu(pre_up).astype(jnp.bfloat16)
    branch_out = (
        jnp.dot(active_low, reduce_weight, preferred_element_type=jnp.float32) + reduce_bias
    )
    outputs = residual + branch_out.reshape(rows_here, cols_here, channels)
    grad_rows_out = cotangent.reshape(-1, channels)
    grad_reduce = inner_rows(active_low, grad_rows_out)
    grad_reduce_bias = jnp.sum(grad_rows_out.astype(jnp.float32), axis=0)
    grad_active = outer_cols(grad_rows_out, reduce_weight)
    _, up_pull = jax.vjp(jax.nn.gelu, pre_up)
    grad_pre_up = up_pull(grad_active)[0].astype(jnp.bfloat16)
    grad_expand = inner_rows(tokens_low, grad_pre_up)
    grad_expand_bias = jnp.sum(grad_pre_up.astype(jnp.float32), axis=0)
    grad_tokens = outer_cols(grad_pre_up, expand_weight).reshape(rows_here, cols_here, channels)
    grad_resid_part, grad_second_gain, grad_second_shift = second_pull(grad_tokens)
    grad_residual = cotangent.astype(jnp.float32) + grad_resid_part
    grad_spatial = (masked * grad_residual).astype(jnp.bfloat16)
    chan_grad = lax.all_to_all(
        lax.all_to_all(
            grad_spatial.reshape(grid_shape), "rows", split_axis=3, concat_axis=0, tiled=True
        ),
        "cols",
        split_axis=2,
        concat_axis=1,
        tiled=True,
    )
    chan_grad_cells = chan_grad.astype(jnp.float32).reshape(snaps, LAT, lon_size, share)
    grad_half_real, grad_half_imag = lon_forward(chan_grad_cells, lon_size)
    scale = weights_lon[None, None, :, None]
    grad_full_real, grad_full_imag = lat_forward(
        grad_half_real * scale, grad_half_imag * scale, LAT
    )
    grad_chan_shrunk = (
        jnp.stack([grad_full_real, grad_full_imag]).astype(jnp.bfloat16).reshape(spec_shape)
    )
    again_modes = modes_of(chan_cells)
    grad_modes_in, modes_again = (
        lax.all_to_all(
            lax.all_to_all(grad_chan_shrunk, "rows", split_axis=2, concat_axis=5, tiled=True),
            "cols",
            split_axis=1,
            concat_axis=4,
            tiled=True,
        ),
        lax.all_to_all(
            lax.all_to_all(again_modes, "rows", split_axis=2, concat_axis=5, tiled=True),
            "cols",
            split_axis=1,
            concat_axis=4,
            tiled=True,
        ),
    )
    blocked_use, pre_first_use, hidden_use, pre_second_use = spectral_mix(modes_again)
    grad_second = grad_modes_in.astype(jnp.float32).reshape(2, mode_count, BLOCKS, block_size)
    grad_pre_second = (shrink_factor(pre_second_use) * grad_second).astype(jnp.bfloat16)
    grad_hidden, grad_weight_b, grad_bias_b = complex_back(
        grad_pre_second, hidden_use, mix_weight_b
    )
    _, first_gelu_pull = jax.vjp(jax.nn.gelu, pre_first_use)
    grad_pre_first = first_gelu_pull(grad_hidden)[0].astype(jnp.bfloat16)
    grad_blocked, grad_weight_a, grad_bias_a = complex_back(
        grad_pre_first, blocked_use, mix_weight_a
    )
    grad_modes_low = grad_blocked.astype(jnp.bfloat16).reshape(mixed_shape)
    grad_arrived = lax.all_to_all(
        lax.all_to_all(grad_modes_low, "rows", split_axis=5, concat_axis=2, tiled=True),
        "cols",
        split_axis=4,
        concat_axis=1,
        tiled=True,
    )
    grad_chan_modes = grad_arrived.astype(jnp.float32).reshape(2, snaps, LAT, lon_modes, share)
    grad_lat_real, grad_lat_imag = lat_inverse(grad_chan_modes[0], grad_chan_modes[1], LAT)
    grad_chan_cells = lon_inverse(grad_lat_real, grad_lat_imag, lon_size, ones_lon).astype(
        jnp.bfloat16
    )
    grad_grid = lax.all_to_all(
        lax.all_to_all(
            grad_chan_cells.reshape(chan_shape), "rows", split_axis=0, concat_axis=3, tiled=True
        ),
        "cols",
        split_axis=1,
        concat_axis=2,
        tiled=True,
    )
    grad_normed = grad_residual + grad_grid.reshape(rows_here, cols_here, channels).astype(
        jnp.float32
    )
    grad_fields, grad_first_gain, grad_first_shift = first_pull(grad_normed)
    grad_inputs = grad_residual + grad_fields
    summed = lax.psum(
        (
            grad_first_gain,
            grad_first_shift,
            grad_weight_a,
            grad_bias_a,
            grad_weight_b,
            grad_bias_b,
            grad_second_gain,
            grad_second_shift,
            grad_expand,
            grad_expand_bias,
            grad_reduce,
            grad_reduce_bias,
        ),
        ("rows", "cols"),
    )
    return (outputs, grad_inputs) + tuple(summed)


def solution(mesh):
    placed = (
        P("rows", "cols", None),
        P("rows", "cols"),
        P("rows", "cols", None),
        P(),
        P(),
        P(),
        P(),
        P(),
        P(),
        P(),
        P(),
        P(),
        P(),
        P(),
        P(),
    )
    return jax.shard_map(
        per_device,
        mesh=mesh,
        in_specs=placed,
        out_specs=(
            P("rows", "cols", None),
            P("rows", "cols", None),
            P(),
            P(),
            P(),
            P(),
            P(),
            P(),
            P(),
            P(),
            P(),
            P(),
            P(),
            P(),
        ),
        check_vma=False,
    )
```

profile of v0, /device:TPU:0, one launch (start us, length us, event | category | flops | bytes accessed | tf_op | source)
XLA Modules:
  0.0 1403.4 jit_solution(12976493317467141853)
XLA Ops:
  7.2 6.1 copy.438
  25.6 10.2 reshape.464
  35.7 46.5 %all_to_all.250 = bf16[8,2,51840]{2,1,0:T(2,128)(2,1)S(1)} all-to-all(bf16[8,2,51840]{2,1,0:T(2,128)(2,1)S(1)} %reshape.464), channel_id=1, replica_groups=mesh['rows'=8,'cols'=4] {'rows'}, dimensions={0} | all-to-all | bytes 3317760 | tf_op jit(solution)/shard_map/all_to_all | solution.py:194
  82.2 13.8 reshape.465
  96.0 7.2 copy.440
  103.3 29.5 %all_to_all.251 = bf16[192,45,4,1,24]{0,4,3,1,2:T(8,128)(2,1)S(1)} all-to-all(bf16[192,45,4,1,24]{0,4,3,1,2:T(8,128)(2,1)S(1)} %copy.440), channel_id=1, replica_groups=mesh['rows'=8,'cols'=4] {'cols'}, dimensions={2} | all-to-all | bytes 3317760 | tf_op jit(solution)/shard_map/all_to_all | solution.py:193
  134.6 5.5 all_to_all.193
  167.5 5.5 fusion.93
  175.7 48.3 %all_to_all.252 = bf16[2,4,8,546,1,1,24]{3,1,6,5,4,0,2:T(4,128)(2,1)S(1)} all-to-all(bf16[2,4,8,546,1,1,24]{3,1,6,5,4,0,2:T(4,128)(2,1)S(1)} %copy.452), channel_id=1, replica_groups=mesh['rows'=8,'cols'=4] {'rows'}, dimensions={2} | all-to-all | bytes 3354624 | tf_op jit(solution)/shard_map/all_to_all | solution.py:204
  230.5 23.9 %all-to-all-done.3 = bf16[2,4,1,546,1,8,24]{3,5,6,0,4,2,1:T(8,128)(2,1)S(1)} async-done(((bf16[2,4,1,546,1,8,24]{3,5,6,0,4,2,1:T(8,128)(2,1)}), bf16[2,4,1,546,1,8,24]{3,5,6,0,4,2,1:T(8,128)(2,1)S(1)}, u32[]{:S(2)}, u32[]{:S(2)}) %all-to-all-start.3) | async-done | bytes 1677344 | tf_op jit(solution)/shard_map/all_to_all | solution.py:203
  266.4 48.6 %all_to_all.253 = bf16[2,1,1,546,4,8,24]{3,4,6,0,2,1,5:T(4,128)(2,1)S(1)} all-to-all(bf16[2,1,1,546,4,8,24]{3,4,6,0,2,1,5:T(4,128)(2,1)S(1)} %subtract_convert_fusion.4), channel_id=1, replica_groups=mesh['rows'=8,'cols'=4] {'rows'}, dimensions={5} | all-to-all | bytes 3354624 | tf_op jit(solution)/shard_map/all_to_all | solution.py:213
  321.4 24.2 %all-to-all-done.5 = bf16[2,1,8,546,4,1,24]{3,2,6,0,5,1,4:T(8,128)(2,1)S(1)} async-done(((bf16[2,1,8,546,4,1,24]{3,2,6,0,5,1,4:T(8,128)(2,1)}), bf16[2,1,8,546,4,1,24]{3,2,6,0,5,1,4:T(8,128)(2,1)S(1)}, u32[]{:S(2)}, u32[]{:S(2)}) %all-to-all-start.5) | async-done | bytes 1677344 | tf_op jit(solution)/shard_map/all_to_all | solution.py:212
  381.2 26.7 %fusion.58 = (f32[2,91,24,96]{3,2,1,0:T(8,128)S(1)}, f32[2,91,24,96]{3,2,1,0:T(8,128)S(1)}) fusion(f32[2,91,24,96]{3,1,2,0:T(8,128)} %fusion.320, f32[2,91,24,96]{3,1,2,0:T(8,128)S(1)} %fusion.236, f32[2,91,24,96]{3,1,2,0:T(8,128)S(1)} %fusion.238, f32[2,91,24,96]{3,1,2,0:T(8,128)} %fusion.334, f32[2,91,24,96]{3,1,2,0:T(8,128)S(1)} %fusion.268, ...), kind=kLoop, calls=%fused_computation.137 | loop fusion | flops 5031936 | bytes 23482732 | tf_op jit(solution)/shard_map/mul | solution.py:88
  431.5 57.1 %all_to_all.254 = bf16[192,180,1,1,24]{1,4,3,2,0:T(8,128)(2,1)} all-to-all(bf16[192,180,1,1,24]{1,4,3,2,0:T(8,128)(2,1)S(1)} %bitcast.744), channel_id=1, replica_groups=mesh['rows'=8,'cols'=4] {'rows'}, dimensions={0} | all-to-all | bytes 3317760 | tf_op jit(solution)/shard_map/all_to_all | solution.py:223
  488.6 8.9 copy.490
  497.6 14.9 %reshape.466 = bf16[4,2,103680]{2,1,0:T(2,128)(2,1)} reshape(bf16[180,1,8,24,24]{4,3,2,1,0:T(8,128)(2,1)} %bitcast.709) | data formatting | bytes 3317760
  518.0 6.1 copy.495
  526.0 11.2 all-to-all-done.7
  537.1 16.3 %reshape.467 = bf16[180,1,8,24,24]{4,3,2,1,0:T(8,128)(2,1)} reshape(bf16[4,2,103680]{2,1,0:T(2,128)(2,1)S(1)} %all-to-all-done.7) | data formatting | bytes 3317760
  553.5 8.2 copy.491
  561.7 7.7 reshape.453
  569.4 9.0 copy.492
  578.4 7.2 fusion.682
  594.0 5.1 copy.493
  599.8 11.2 convolution_add_fusion
  611.0 17.3 %convert_reduce_fusion.1 = (f32[3072]{0:T(1024)}, bf16[1080,3072]{1,0:T(8,128)(2,1)S(1)}) fusion(f32[1080,3072]{1,0:T(8,128)} %convolution_add_fusion, bf16[1080,768]{1,0:T(8,128)(2,1)S(1)} %copy-done.42, bf16[3072,768]{1,0:T(8,128)(2,1)} %param.28), kind=kOutput, calls=%fused_computation.19 | convolution fusion | flops 5169067008 | bytes 26296320 | tf_op jit(solution)/shard_map/dot_general | solution.py:134
  628.3 7.8 fusion.687
  638.9 5.8 copy.497
  644.8 9.2 multiply_reduce_fusion
  654.6 13.3 convolution_add_fusion.1
  670.7 5.8 copy.494
  676.6 14.8 %fusion.681 = (f32[24,45]{1,0:T(8,128)S(1)}, f32[24,45,768]{1,2,0:T(8,128)S(1)}, f32[24,45,768]{1,2,0:T(8,128)}) fusion(f32[24,45]{1,0:T(8,128)} %multiply_multiply_fusion.5, f32[24,45,768]{1,2,0:T(8,128)} %copy-done.1, f32[24,45]{1,0:T(8,128)S(1)} %broadcast_multiply_fusion, f32[24,45]{1,0:T(8,128)} %copy-done.59, f32[24,45,768]{1,2,0:T(8,128)} %copy.497, ...), kind=kLoop, calls=%fused_computation.704 | loop fusion | flops 6634440 | bytes 16609152 | tf_op jit(solution)/shard_map/transpose(jvp())/reduce_sum | solution.py:19
  691.4 10.0 multiply_convert_fusion.1
  701.4 5.4 copy.696
  706.8 10.2 reshape.468
  716.9 42.6 %all_to_all.255 = bf16[8,2,51840]{2,1,0:T(2,128)(2,1)S(1)} all-to-all(bf16[8,2,51840]{2,1,0:T(2,128)(2,1)S(1)} %reshape.468), channel_id=1, replica_groups=mesh['rows'=8,'cols'=4] {'rows'}, dimensions={0} | all-to-all | bytes 3317760 | tf_op jit(solution)/shard_map/all_to_all | solution.py:254
  759.5 13.8 reshape.469
  773.3 7.2 copy.499
  780.6 29.4 %all_to_all.256 = bf16[192,45,4,1,24]{0,4,3,1,2:T(8,128)(2,1)S(1)} all-to-all(bf16[192,45,4,1,24]{0,4,3,1,2:T(8,128)(2,1)S(1)} %copy.499), channel_id=1, replica_groups=mesh['rows'=8,'cols'=4] {'cols'}, dimensions={2} | all-to-all | bytes 3317760 | tf_op jit(solution)/shard_map/all_to_all | solution.py:253
  811.8 5.3 all_to_all.218
  844.8 5.5 fusion.95
  852.9 48.3 %all_to_all.257 = bf16[2,4,8,546,1,1,24]{3,1,6,5,4,0,2:T(4,128)(2,1)S(1)} all-to-all(bf16[2,4,8,546,1,1,24]{3,1,6,5,4,0,2:T(4,128)(2,1)S(1)} %copy.511), channel_id=1, replica_groups=mesh['rows'=8,'cols'=4] {'rows'}, dimensions={2} | all-to-all | bytes 3354624 | tf_op jit(solution)/shard_map/all_to_all | solution.py:274
  907.9 24.2 %all-to-all-done.11 = bf16[2,4,1,546,1,8,24]{3,5,6,0,4,2,1:T(8,128)(2,1)S(1)} async-done(((bf16[2,4,1,546,1,8,24]{3,5,6,0,4,2,1:T(8,128)(2,1)}), bf16[2,4,1,546,1,8,24]{3,5,6,0,4,2,1:T(8,128)(2,1)S(1)}, u32[]{:S(2)}, u32[]{:S(2)}) %all-to-all-start.11) | async-done | bytes 1677344 | tf_op jit(solution)/shard_map/all_to_all | solution.py:273
  954.4 13.9 fusion.662
  968.3 11.9 fusion.720
  982.9 17.0 %all-to-all-done.12 = bf16[2,1,1,546,4,8,24]{3,4,6,0,2,1,5:T(4,128)(2,1)} async-done(((bf16[2,1,1,546,4,8,24]{3,4,6,0,2,1,5:T(4,128)(2,1)}), bf16[2,1,1,546,4,8,24]{3,4,6,0,2,1,5:T(4,128)(2,1)}, u32[]{:S(2)}, u32[]{:S(2)}) %all-to-all-start.12) | async-done | bytes 1677344 | tf_op jit(solution)/shard_map/all_to_all | solution.py:301
  1013.4 29.0 %all-to-all-done.13 = bf16[2,1,8,546,4,1,24]{3,2,6,0,5,1,4:T(8,128)(2,1)} async-done(((bf16[2,1,8,546,4,1,24]{3,2,6,0,5,1,4:T(8,128)(2,1)}), bf16[2,1,8,546,4,1,24]{3,2,6,0,5,1,4:T(8,128)(2,1)}, u32[]{:S(2)}, u32[]{:S(2)}) %all-to-all-start.13) | async-done | bytes 1677344 | tf_op jit(solution)/shard_map/all_to_all | solution.py:300
  1071.4 10.6 fusion.50
  1094.9 9.1 fusion.49
  1116.3 82.9 %all_to_all.258 = bf16[192,180,1,1,24]{1,4,3,2,0:T(8,128)(2,1)} all-to-all(bf16[192,180,1,1,24]{1,4,3,2,0:T(8,128)(2,1)S(1)} %bitcast.745), channel_id=1, replica_groups=mesh['rows'=8,'cols'=4] {'rows'}, dimensions={0} | all-to-all | bytes 3317760 | tf_op jit(solution)/shard_map/all_to_all | solution.py:313
  1199.2 9.0 copy.551
  1208.2 14.9 %reshape.470 = bf16[4,2,103680]{2,1,0:T(2,128)(2,1)} reshape(bf16[180,1,8,24,24]{4,3,2,1,0:T(8,128)(2,1)} %bitcast.711) | data formatting | bytes 3317760
  1231.9 8.3 copy.560
  1243.8 13.7 all-to-all-done.15
  1257.5 16.6 %reshape.471 = bf16[180,1,8,24,24]{4,3,2,1,0:T(8,128)(2,1)} reshape(bf16[4,2,103680]{2,1,0:T(2,128)(2,1)} %all-to-all-done.15) | data formatting | bytes 3317760
  1274.1 8.7 copy.552
  1282.9 7.7 reshape.455
  1290.5 9.1 copy.553
  1299.7 12.8 fusion.663
  1312.5 5.9 fusion.16
  1318.5 9.6 add_add_fusion.2
  1328.0 8.3 copy.561
  1336.4 39.1 %all-reduce = (f32[768]{0:T(1024)}, f32[768]{0:T(1024)}, f32[2,768]{1,0:T(2,128)}, f32[2,768]{1,0:T(2,128)}, f32[768]{0:T(1024)}, /*index=5*/f32[768]{0:T(1024)}, f32[3072]{0:T(1024)}, f32[768]{0:T(1024)}) all-reduce(f32[768]{0:T(1024)S(1)} %get-tuple-element.86, ...), channel_id=1, replica_groups=mesh['rows'=8,'cols'=4] {'rows','cols'}, use_global_device_ids=true, to_apply=%region_9.10 | all-reduce | flops 9984 | bytes 79872 | tf_op jit(solution)/shard_map/psum | solution.py:326
  1383.9 8.8 copy.704
  (419 shorter events, 305.9 us)
Async XLA Ops:
  13.3 3.8 copy-start
  226.4 3.7 copy-start.77
  226.4 3.8 copy-start.70
  226.4 28.0 %all-to-all-start.3 = ((bf16[2,4,1,546,1,8,24]{3,5,6,0,4,2,1:T(8,128)(2,1)}), bf16[2,4,1,546,1,8,24]{3,5,6,0,4,2,1:T(8,128)(2,1)S(1)}, u32[]{:S(2)}, u32[]{:S(2)}) async-start(bf16[2,4,1,546,1,8,24]{3,5,6,0,4,2,1:T(8,128)(2,1)} %copy.453), calls=%async_computation.3 | async-start | bytes 3932160 | tf_op jit(solution)/shard_map/all_to_all | solution.py:203
  230.2 27.3 %copy-start.67 = (f32[2,8,96]{2,1,0:T(8,128)}, f32[2,8,96]{2,1,0:T(8,128)S(1)}, u32[]{:S(2)}) copy-start(f32[2,8,96]{2,1,0:T(8,128)S(1)} %add.618) | copy-start | bytes 18436
  230.3 24.4 %copy-start.55 = (f32[2,4,8,24]{3,2,1,0:T(8,128)}, f32[2,4,8,24]{3,2,1,0:T(8,128)S(1)}, u32[]{:S(2)}) copy-start(f32[2,4,8,24]{3,2,1,0:T(8,128)S(1)} %add.625) | copy-start | bytes 18436
  317.4 28.3 %all-to-all-start.5 = ((bf16[2,1,8,546,4,1,24]{3,2,6,0,5,1,4:T(8,128)(2,1)}), bf16[2,1,8,546,4,1,24]{3,2,6,0,5,1,4:T(8,128)(2,1)S(1)}, u32[]{:S(2)}, u32[]{:S(2)}) async-start(bf16[2,1,8,546,4,1,24]{3,2,6,0,5,1,4:T(8,128)(2,1)} %copy.463), calls=%async_computation.5 | async-start | bytes 3932160 | tf_op jit(solution)/shard_map/all_to_all | solution.py:212
  321.4 58.7 %copy-start.78 = (f32[91]{0:T(128)}, f32[91]{0:T(128)S(1)}, u32[]{:S(2)}) copy-start(f32[91]{0:T(128)S(1)} %or_select_fusion) | copy-start | bytes 1096
  420.0 4.3 slice-start.11
  420.0 4.3 slice-start.13
  512.4 24.7 %all-to-all-start.7 = ((bf16[4,2,103680]{2,1,0:T(2,128)(2,1)}), bf16[4,2,103680]{2,1,0:T(2,128)(2,1)S(1)}, u32[]{:S(2)}, u32[]{:S(2)}) async-start(bf16[4,2,103680]{2,1,0:T(2,128)(2,1)} %reshape.466), calls=%async_computation.7 | async-start | bytes 3317760 | tf_op jit(solution)/shard_map/all_to_all | solution.py:222
  561.7 16.7 %slice-start = ((s8[4718592]{0:T(1024)(128)(4,1)}), s8[524288]{0:T(1024)(128)(4,1)S(1)}, s32[]{:S(2)}) async-start(s8[4718592]{0:T(1024)(128)(4,1)} %bitcast.699), calls=%async_computation.17 | async-start | bytes 1048576
  569.3 9.0 slice-start.1
  569.3 9.0 copy-start.46
  569.3 9.0 copy-start.49
  569.3 9.0 copy-start.52
  569.3 9.1 copy-start.65
  569.4 9.1 copy-start.73
  585.6 3.7 copy-start.1
  585.6 4.3 copy-start.69
  585.6 4.3 copy-start.80
  599.8 11.2 copy-start.43
  599.8 11.2 copy-start.42
  599.8 28.5 %slice-start.18 = ((s8[4718592]{0:T(1024)(128)(4,1)}), s8[4194304]{0:T(1024)(128)(4,1)S(1)}, s32[]{:S(2)}) async-start(s8[4718592]{0:T(1024)(128)(4,1)} %bitcast.756), calls=%async_computation.35 | async-start | bytes 8388608
  611.0 17.3 %slice-start.19 = ((s8[4718592]{0:T(1024)(128)(4,1)}), s8[524288]{0:T(1024)(128)(4,1)S(1)}, s32[]{:S(2)}) async-start(s8[4718592]{0:T(1024)(128)(4,1)} %bitcast.756), calls=%async_computation.36 | async-start | bytes 1048576
  628.3 7.8 copy-start.84
  644.8 9.2 copy-start.63
  644.8 9.8 copy-start.83
  676.6 14.8 %copy-start.53 = (f32[24,45]{1,0:T(8,128)S(1)}, f32[24,45]{1,0:T(8,128)}, u32[]{:S(2)}) copy-start(f32[24,45]{1,0:T(8,128)} %copy-done.51) | copy-start | bytes 12964
  691.3 10.0 copy-start.5
  691.3 10.0 copy-start.57
  903.6 4.2 copy-start.71
  903.6 28.4 %all-to-all-start.11 = ((bf16[2,4,1,546,1,8,24]{3,5,6,0,4,2,1:T(8,128)(2,1)}), bf16[2,4,1,546,1,8,24]{3,5,6,0,4,2,1:T(8,128)(2,1)S(1)}, u32[]{:S(2)}, u32[]{:S(2)}) async-start(bf16[2,4,1,546,1,8,24]{3,5,6,0,4,2,1:T(8,128)(2,1)} %copy.512), calls=%async_computation.11 | async-start | bytes 3932160 | tf_op jit(solution)/shard_map/all_to_all | solution.py:273
  940.2 3.7 copy-start.35
  949.8 50.0 %all-to-all-start.12 = ((bf16[2,1,1,546,4,8,24]{3,4,6,0,2,1,5:T(4,128)(2,1)}), bf16[2,1,1,546,4,8,24]{3,4,6,0,2,1,5:T(4,128)(2,1)}, u32[]{:S(2)}, u32[]{:S(2)}) async-start(bf16[2,1,1,546,4,8,24]{3,4,6,0,2,1,5:T(4,128)(2,1)} %pad_maximum_fusion.3), calls=%async_computation.12 | async-start | bytes 3932160 | tf_op jit(solution)/shard_map/all_to_all | solution.py:301
  954.3 13.9 copy-start.44
  968.3 11.9 copy-start.7
  968.3 11.9 copy-start.9
  1003.8 6.7 copy-start.17
  1003.8 38.7 %all-to-all-start.13 = ((bf16[2,1,8,546,4,1,24]{3,2,6,0,5,1,4:T(8,128)(2,1)}), bf16[2,1,8,546,4,1,24]{3,2,6,0,5,1,4:T(8,128)(2,1)}, u32[]{:S(2)}, u32[]{:S(2)}) async-start(bf16[2,1,8,546,4,1,24]{3,2,6,0,5,1,4:T(8,128)(2,1)} %copy.524), calls=%async_computation.13 | async-start | bytes 3932160 | tf_op jit(solution)/shard_map/all_to_all | solution.py:300
  1008.4 371.2 %all-reduce.4.cloned.1.call-start = ((), (), s32[]{:S(2)}) async-start(), calls=%async_computation.16 | async-start | bytes 40894464 | tf_op jit(solution)/shard_map/psum | solution.py:326
  1105.0 4.4 slice-start.7
  1105.0 4.4 slice-start.9
  1223.1 4.9 copy-start.56
  1223.1 5.0 copy-start.12
  1223.1 34.4 %all-to-all-start.15 = ((bf16[4,2,103680]{2,1,0:T(2,128)(2,1)}), bf16[4,2,103680]{2,1,0:T(2,128)(2,1)}, u32[]{:S(2)}, u32[]{:S(2)}) async-start(bf16[4,2,103680]{2,1,0:T(2,128)(2,1)} %reshape.470), calls=%async_computation.15 | async-start | bytes 3317760 | tf_op jit(solution)/shard_map/all_to_all | solution.py:312
  1231.8 8.3 copy-start.25
  1282.8 16.8 %slice-start.2 = ((s8[4718592]{0:T(1024)(128)(4,1)}), s8[524288]{0:T(1024)(128)(4,1)S(1)}, s32[]{:S(2)}) async-start(s8[4718592]{0:T(1024)(128)(4,1)} %bitcast.701), calls=%async_computation.19 | async-start | bytes 1048576
  1290.5 9.1 slice-start.3
  1290.5 9.1 copy-start.47
  1290.5 9.1 copy-start.54
  1290.5 9.1 copy-start.58
  1290.5 9.2 copy-start.66
  1290.5 27.9 %slice-start.4 = ((s8[9437184]{0:T(1024)(128)(4,1)}), s8[1048576]{0:T(1024)(128)(4,1)S(1)}, s32[]{:S(2)}) async-start(s8[9437184]{0:T(1024)(128)(4,1)} %bitcast.703), calls=%async_computation.21 | async-start | bytes 2097152
  1299.7 12.8 copy-start.61
  1299.7 12.8 copy-start.50
  1299.7 18.7 %slice-start.5 = ((s8[9437184]{0:T(1024)(128)(4,1)}), s8[4194304]{0:T(1024)(128)(4,1)S(1)}, s32[]{:S(2)}) async-start(s8[9437184]{0:T(1024)(128)(4,1)} %bitcast.703), calls=%async_computation.22 | async-start | bytes 8388608
  1299.7 18.7 %slice-start.6 = ((s8[9437184]{0:T(1024)(128)(4,1)}), s8[4194304]{0:T(1024)(128)(4,1)S(1)}, s32[]{:S(2)}) async-start(s8[9437184]{0:T(1024)(128)(4,1)} %bitcast.703), calls=%async_computation.23 | async-start | bytes 8388608
  1328.0 8.4 copy-start.74
  1328.0 8.4 copy-start.76
  1328.0 8.4 copy-start.81
  1381.7 11.0 slice-start.15
  1383.9 8.8 slice-start.16
  1383.9 8.8 slice-start.17
  (49 other events, 103.0 us)
Sparse Core Ops, SparseCore 0:
  1016.2 363.3 all-reduce.3
where the time goes:
time: 1410 us; the launch traced here: 1400 us
  blocking collectives  472 us (33%)
  local copies, waits for them, and re-layouts  379 us (27%)
  matrix products  205 us (15%)
  other arithmetic  154 us (11%)
  waiting for transfers between devices  147 us (10%)
  starting transfers between devices  29.7 us (2%)
  between operations  16.1 us (1%)
    unnamed x227, local copies, waits for them, and re-layouts  173 us
    all_to_all x1, blocking collectives, per_device(): lax.all_to_all(grad_chan_cells.reshape(chan_shape), 'rows', split_axis=0,...  82.9 us
    all_to_all x1, blocking collectives, per_device(): lax.all_to_all(chan_spatial.reshape(chan_shape), 'rows', split_axis=0, co...  57.1 us
    all_to_all x1, blocking collectives, per_device(): lax.all_to_all(shrunk_low, 'rows', split_axis=5, concat_axis=2, tiled=True)  48.6 us
    all_to_all x1, blocking collectives, per_device(): lax.all_to_all(chan_modes, 'rows', split_axis=2, concat_axis=5, tiled=True)  48.3 us
    all_to_all x1, blocking collectives, per_device(): lax.all_to_all(grad_chan_shrunk, 'rows', split_axis=2, concat_axis=5, til...  48.3 us
    all_to_all x1, blocking collectives, per_device(): lax.all_to_all(normed_low.reshape(grid_shape), 'rows', split_axis=3, conc...  46.5 us
    dot_general x24, matrix products, exact_product(): jnp.einsum(form, left_down, right_up, preferred_element_type=jnp.float32)  45 us
  transfers between devices with their start and end apart: 8, of which 8 were waited for; matrix products, arithmetic and copies ran while one was open for 17% of the time, Pallas kernels for 0%

commit v1 on v0

v1 whole, which is shorter than its diff:
```python
import math

import jax
import jax.numpy as jnp
import numpy as np
from jax import lax
from jax.experimental import pallas as pl
from jax.experimental.pallas import tpu as pltpu
from jax.sharding import PartitionSpec as P

BLOCKS = 8
LAT = 96
CORES = 2
PACK = 4
LANES = 128

shrink_level = 0.01
shrink_soft = 0.1
norm_eps = 1e-05
gelu_root = math.sqrt(2.0 / math.pi)
gelu_cube = 0.044715

BF = jnp.bfloat16
F32 = jnp.float32
AXES = ("rows", "cols")


def up_to(value, step):
    return (value + step - 1) // step * step


def params(limit=56):
    return pltpu.CompilerParams(vmem_limit_bytes=limit * 1024 * 1024)


def lon_table(lon_size, col_devs, cols_here, cols_pad, slots, slots_pad):
    modes = lon_size // 2 + 1
    table = np.zeros((CORES, 2, slots_pad, col_devs, cols_pad), np.float64)
    weights = np.zeros((CORES, slots_pad), np.float64)
    place = np.arange(lon_size).reshape(col_devs, cols_here)
    for half in range(CORES):
        for slot in range(slots):
            mode = half * slots + slot
            if mode >= modes:
                continue
            angle = (place * mode % lon_size) * (2.0 * math.pi / lon_size)
            table[half, 0, slot, :, :cols_here] = np.cos(angle) / math.sqrt(lon_size)
            edge = mode == 0 or 2 * mode == lon_size
            if not edge:
                table[half, 1, slot, :, :cols_here] = np.sin(angle) / math.sqrt(lon_size)
            weights[half, slot] = 1.0 if edge else 2.0
    weighted = table * weights[:, None, :, None, None]
    rows = 2 * slots_pad
    flat = [a.reshape(CORES, rows, col_devs * cols_pad) for a in (table, weighted)]
    return [
        np.stack([np.concatenate([a[h], a[1 - h]], 0) for h in range(CORES)]) for a in flat
    ]


def lat_table(rows_here, row_group):
    share = rows_here // CORES
    out = []
    for h in range(CORES):
        own = [
            rows_here * r + share * h + i for r in range(row_group) for i in range(share)
        ]
        other = [
            rows_here * r + share * (1 - h) + i for r in range(row_group) for i in range(share)
        ]
        angle = np.outer(np.arange(LAT), np.array(own + other)) % LAT * (2.0 * math.pi / LAT)
        cos, sin = np.cos(angle) / math.sqrt(LAT), np.sin(angle) / math.sqrt(LAT)
        out.append(np.block([[cos, -sin], [-sin, -cos]]))
    return np.stack(out)


def pack_lanes(tiles):
    a, b, c, d = tiles
    lane = lax.broadcasted_iota(jnp.int32, a.shape, a.ndim - 1)
    axis = a.ndim - 1
    b, c, d = pltpu.roll(b, 96, axis), pltpu.roll(c, 64, axis), pltpu.roll(d, 32, axis)
    return [
        jnp.where(lane < 96, a, b),
        jnp.where(lane < 64, b, c),
        jnp.where(lane < 32, c, d),
    ]


def unpack_lanes(tiles):
    a, b, c = tiles
    lane = lax.broadcasted_iota(jnp.int32, a.shape, a.ndim - 1)
    axis = a.ndim - 1
    return [
        a,
        pltpu.roll(jnp.where(lane >= 96, a, b), 32, axis),
        pltpu.roll(jnp.where(lane >= 64, b, c), 64, axis),
        pltpu.roll(c, 96, axis),
    ]


def tiles_of(value):
    return [value[:, LANES * i : LANES * (i + 1)] for i in range(value.shape[1] // LANES)]


def split_blocks(value):
    tiles = tiles_of(value)
    out = []
    for i in range(0, len(tiles), 3):
        out += unpack_lanes(tiles[i : i + 3])
    return out


def join_blocks(tiles):
    out = []
    for i in range(0, len(tiles), 4):
        out += pack_lanes(tiles[i : i + 4])
    return jnp.concatenate(out, axis=1)


def pad_rows(value, rows):
    return jnp.concatenate(
        [value, jnp.zeros((rows - value.shape[0], value.shape[1]), value.dtype)], axis=0
    )


def store_packed(ref, half, per_lat):
    split = [split_blocks(v) for v in per_lat]
    for q in range(BLOCKS):
        packed = pack_lanes([split[j][q] for j in range(PACK)])
        ref[q, half, 0] = jnp.concatenate(packed, axis=1).astype(ref.dtype)


def load_packed(ref, half):
    by_lat = [[] for _ in range(PACK)]
    for q in range(BLOCKS):
        parts = unpack_lanes(tiles_of(ref[q, half, 0].astype(F32)))
        for j in range(PACK):
            by_lat[j].append(parts[j])
    return [join_blocks(tiles) for tiles in by_lat]


def stats(x):
    average = jnp.mean(x, axis=-1, keepdims=True)
    centred = x - average
    spread = jnp.mean(centred * centred, axis=-1, keepdims=True)
    inv = lax.rsqrt(spread + norm_eps)
    return centred * inv, inv


def norm_back(grad, xhat, inv, gain):
    scaled = grad * gain
    m1 = jnp.mean(scaled, axis=-1, keepdims=True)
    m2 = jnp.mean(scaled * xhat, axis=-1, keepdims=True)
    return inv * (scaled - m1 - xhat * m2)


def first_kernel(x_ref, mask_ref, gain_ref, shift_ref, normed_ref, out_ref):
    rows = normed_ref.shape[3]
    for half in range(CORES):
        lats = []
        for j in range(PACK):
            x = pad_rows(x_ref[half, 0, j].astype(F32), rows)
            xhat, _ = stats(x)
            y = mask_ref[half, 0, j] * (xhat * gain_ref[...] + shift_ref[...])
            normed_ref[half, 0, j] = y.astype(BF)
            lats.append(y)
        store_packed(out_ref, half, lats)


def second_kernel(
    x_ref, normed_ref, mask_ref, cot_ref, got_ref, gain_ref, shift_ref, resid_ref, tok_ref, cot_out
):
    rows = normed_ref.shape[3]
    for half in range(CORES):
        spatial = load_packed(got_ref, half)
        for j in range(PACK):
            x = pad_rows(x_ref[half, 0, j].astype(F32), rows)
            resid = x + normed_ref[half, 0, j].astype(F32) + mask_ref[half, 0, j] * spatial[j]
            resid_ref[half, 0, j] = resid
            xhat, _ = stats(resid)
            tok_ref[half, 0, j] = (xhat * gain_ref[...] + shift_ref[...]).astype(BF)
            cot_out[half, 0, j] = pad_rows(cot_ref[half, 0, j].astype(F32), rows).astype(BF)


def third_kernel(
    resid_ref, branch_ref, gtok_ref, cot_ref, mask_ref, gain_ref, bias_ref,
    out_ref, gresid_ref, send_ref, ggain_ref, gshift_ref, gbias_ref,
):
    @pl.when(pl.program_id(0) == 0)
    def _():
        ggain_ref[...] = jnp.zeros_like(ggain_ref)
        gshift_ref[...] = jnp.zeros_like(gshift_ref)
        gbias_ref[...] = jnp.zeros_like(gbias_ref)

    here = out_ref.shape[3]
    for half in range(CORES):
        lats = []
        for j in range(PACK):
            resid = resid_ref[half, 0, j]
            out_ref[half, 0, j] = (resid + branch_ref[half, 0, j] + bias_ref[...])[:here]
            xhat, inv = stats(resid)
            gtok = gtok_ref[half, 0, j]
            cot = cot_ref[half, 0, j].astype(F32)
            ggain_ref[...] += jnp.sum(gtok * xhat, axis=0, keepdims=True)
            gshift_ref[...] += jnp.sum(gtok, axis=0, keepdims=True)
            gbias_ref[...] += jnp.sum(cot, axis=0, keepdims=True)
            gres = cot + norm_back(gtok, xhat, inv, gain_ref[...])
            gresid_ref[half, 0, j] = gres
            lats.append(mask_ref[half, 0, j] * gres)
        store_packed(send_ref, half, lats)


def last_kernel(
    x_ref, gresid_ref, mask_ref, got_ref, gain_ref, out_ref, ggain_ref, gshift_ref
):
    @pl.when(pl.program_id(0) == 0)
    def _():
        ggain_ref[...] = jnp.zeros_like(ggain_ref)
        gshift_ref[...] = jnp.zeros_like(gshift_ref)

    here = out_ref.shape[3]
    rows = gresid_ref.shape[3]
    for half in range(CORES):
        got = load_packed(got_ref, half)
        for j in range(PACK):
            x = pad_rows(x_ref[half, 0, j].astype(F32), rows)
            xhat, inv = stats(x)
            gres = gresid_ref[half, 0, j]
            grad = mask_ref[half, 0, j] * (gres + got[j])
            ggain_ref[...] += jnp.sum(grad * xhat, axis=0, keepdims=True)
            gshift_ref[...] += jnp.sum(grad, axis=0, keepdims=True)
            out_ref[half, 0, j] = (gres + norm_back(grad, xhat, inv, gain_ref[...]))[:here]


def lon_kernel(col_devs, row_group, x_ref, table_ref, own_ref, other_ref, turn_ref):
    groups = x_ref.shape[1]
    rows = table_ref.shape[0]
    lats = own_ref.shape[1]
    slots = own_ref.shape[0]
    for r in range(row_group):
        for g in range(groups):
            cells = jnp.concatenate(
                [x_ref[r * col_devs + c, g] for c in range(col_devs)], axis=0
            )
            modes = jnp.dot(table_ref[...], cells, preferred_element_type=F32)
            for j, tile in enumerate(unpack_lanes(tiles_of(modes))):
                at = (r * groups + g) * PACK + j
                turn_ref[pl.ds(at, rows, stride=lats), :] = tile

    @pl.loop(0, slots)
    def _(s):
        own_ref[s] = turn_ref[pl.ds(pl.multiple_of(s * lats, 8), lats), :].astype(BF)
        other_ref[s] = turn_ref[
            pl.ds(pl.multiple_of((s + slots) * lats, 8), lats), :
        ].astype(BF)


def lon_back_kernel(col_devs, row_group, own_ref, other_ref, table_ref, out_ref):
    groups = out_ref.shape[1]
    cols = out_ref.shape[2]
    for r in range(row_group):
        for g in range(groups):
            tiles = []
            for j in range(0, PACK, 2):
                pair = []
                for k in range(2):
                    at = (r * groups + g) * PACK + j + k
                    pair.append(jnp.concatenate([own_ref[at], other_ref[at]], axis=0))
                cells = jnp.dot(
                    table_ref[...], jnp.concatenate(pair, axis=1), preferred_element_type=F32
                )
                tiles += tiles_of(cells)
            packed = jnp.concatenate(pack_lanes(tiles), axis=1).astype(BF)
            for c in range(col_devs):
                out_ref[r * col_devs + c, g] = packed[c * cols : (c + 1) * cols]


def gelu_parts(v):
    squash = jnp.tanh(gelu_root * (v + gelu_cube * (v * v * v)))
    return squash


def gelu(v):
    return 0.5 * v * (1.0 + gelu_parts(v))


def gelu_slope(v, squash):
    inner = gelu_root * (1.0 + 3.0 * gelu_cube * (v * v))
    return 0.5 * (1.0 + squash) + 0.5 * v * (1.0 - squash * squash) * inner


def latitudes(own_ref, other_ref, slot, half_slots):
    return jnp.concatenate(
        [own_ref[slot], other_ref[slot], own_ref[slot + half_slots], other_ref[slot + half_slots]],
        axis=0,
    )


def turn_out(turn_ref, value, slot, lats, rows, half_slots):
    for part in range(2):
        for dest in range(2):
            piece = value[(2 * part + dest) * lats : (2 * part + dest + 1) * lats]
            start = dest * lats * rows + part * half_slots + slot
            turn_ref[pl.ds(start, lats, stride=rows), :] = piece


def drain(turn_ref, own_ref, other_ref):
    lats, rows = own_ref.shape[0], own_ref.shape[1]

    @pl.loop(0, lats)
    def _(at):
        own_ref[at] = turn_ref[pl.ds(pl.multiple_of(at * rows, 8), rows), :].astype(BF)
        other_ref[at] = turn_ref[
            pl.ds(pl.multiple_of((at + lats) * rows, 8), rows), :
        ].astype(BF)


def mix_kernel(
    own_ref, other_ref, lat_ref, back_ref, wa_ref, ba_ref, wb_ref, bb_ref,
    own_out, other_out, modes_out, turn_ref,
):
    half_slots = own_ref.shape[0] // 2
    lats = own_ref.shape[1]

    @pl.loop(0, half_slots // 2)
    def _(step):
        slot = 2 * step
        cells = jnp.concatenate(
            [latitudes(own_ref, other_ref, slot + k, half_slots) for k in range(2)], axis=1
        )
        full = jnp.dot(lat_ref[...], cells, preferred_element_type=F32).astype(BF)
        real, imag = full[:LAT], full[LAT:]
        modes = jnp.concatenate(
            [
                jnp.concatenate([real[:, :LANES], imag[:, :LANES]], axis=1),
                jnp.concatenate([real[:, LANES:], imag[:, LANES:]], axis=1),
            ],
            axis=0,
        )
        modes_out[step] = modes
        pre_a = jnp.dot(modes, wa_ref[...], preferred_element_type=F32) + ba_ref[...]
        hidden = gelu(pre_a).astype(BF)
        pre_b = jnp.dot(hidden, wb_ref[...], preferred_element_type=F32) + bb_ref[...]
        shrunk = (pre_b - shrink_level * jnp.tanh(pre_b * (1.0 / shrink_soft))).astype(BF)
        mixed = jnp.concatenate(
            [
                jnp.concatenate([shrunk[:LAT, :LANES], shrunk[LAT:, :LANES]], axis=1),
                jnp.concatenate([shrunk[:LAT, LANES:], shrunk[LAT:, LANES:]], axis=1),
            ],
            axis=0,
        )
        back = jnp.dot(back_ref[...], mixed, preferred_element_type=F32)
        for k in range(2):
            turn_out(
                turn_ref, back[:, k * LANES : (k + 1) * LANES], slot + k, lats,
                2 * half_slots, half_slots,
            )

    drain(turn_ref, own_out, other_out)


def mix_back_kernel(
    own_ref, other_ref, modes_ref, lat_ref, back_ref, wa_ref, ba_ref, wb_ref, bb_ref,
    own_out, other_out, gwa_ref, gba_ref, gwb_ref, gbb_ref, turn_ref,
):
    half_slots = own_ref.shape[0] // 2
    lats = own_ref.shape[1]
    for ref in (gwa_ref, gba_ref, gwb_ref, gbb_ref):
        ref[...] = jnp.zeros_like(ref)
    outer = (((0,), (0,)), ((), ()))
    across = (((1,), (1,)), ((), ()))

    @pl.loop(0, half_slots // 2)
    def _(step):
        slot = 2 * step
        cells = jnp.concatenate(
            [latitudes(own_ref, other_ref, slot + k, half_slots) for k in range(2)], axis=1
        )
        full = jnp.dot(lat_ref[...], cells, preferred_element_type=F32)
        real, imag = full[:LAT], full[LAT:]
        grad = jnp.concatenate(
            [
                jnp.concatenate([real[:, :LANES], imag[:, :LANES]], axis=1),
                jnp.concatenate([real[:, LANES:], imag[:, LANES:]], axis=1),
            ],
            axis=0,
        )
        modes = modes_ref[step]
        pre_a = jnp.dot(modes, wa_ref[...], preferred_element_type=F32) + ba_ref[...]
        squash_a = gelu_parts(pre_a)
        hidden = (0.5 * pre_a * (1.0 + squash_a)).astype(BF)
        pre_b = jnp.dot(hidden, wb_ref[...], preferred_element_type=F32) + bb_ref[...]
        squash_b = jnp.tanh(pre_b * (1.0 / shrink_soft))
        factor = 1.0 - shrink_level / shrink_soft * (1.0 - squash_b * squash_b)
        grad_b = factor * grad
        gbb_ref[...] += jnp.sum(grad_b, axis=0, keepdims=True)
        grad_b = grad_b.astype(BF)
        grad_hidden = lax.dot_general(grad_b, wb_ref[...], across, preferred_element_type=F32)
        gwb_ref[...] += lax.dot_general(hidden, grad_b, outer, preferred_element_type=F32)
        grad_a = gelu_slope(pre_a, squash_a) * grad_hidden
        gba_ref[...] += jnp.sum(grad_a, axis=0, keepdims=True)
        grad_a = grad_a.astype(BF)
        grad_modes = lax.dot_general(
            grad_a, wa_ref[...], across, preferred_element_type=F32
        ).astype(BF)
        gwa_ref[...] += lax.dot_general(modes, grad_a, outer, preferred_element_type=F32)
        mixed = jnp.concatenate(
            [
                jnp.concatenate([grad_modes[:LAT, :LANES], grad_modes[LAT:, :LANES]], axis=1),
                jnp.concatenate([grad_modes[:LAT, LANES:], grad_modes[LAT:, LANES:]], axis=1),
            ],
            axis=0,
        )
        back = jnp.dot(back_ref[...], mixed, preferred_element_type=F32)
        for k in range(2):
            turn_out(
                turn_ref, back[:, k * LANES : (k + 1) * LANES], slot + k, lats,
                2 * half_slots, half_slots,
            )

    drain(turn_ref, own_out, other_out)


def per_device(
    inputs, valid_mask, cotangent, first_gain, first_shift, mix_weight_a, mix_bias_a,
    mix_weight_b, mix_bias_b, second_gain, second_shift, expand_weight, expand_bias,
    reduce_weight, reduce_bias,
):
    row_devs = lax.axis_size("rows")
    col_devs = lax.axis_size("cols")
    rows_here, cols_here, channels = inputs.shape
    block = channels // BLOCKS
    lon_size = cols_here * col_devs
    cols_pad = up_to(cols_here, 16)
    row_group = LAT // rows_here
    members = row_group * col_devs
    share = rows_here // CORES
    groups = share // PACK
    slots = (lon_size // 2 + 2) // 2
    slots_pad = up_to(slots, 16)
    lats = share * row_group
    half_rows = 2 * slots_pad
    all_rows = CORES * half_rows
    assert members == CORES * BLOCKS and block * PACK == 3 * LANES
    assert col_devs * cols_pad == all_rows and CORES * lats == LAT

    row_at, col_at = lax.axis_index("rows"), lax.axis_index("cols")
    core = col_at % CORES
    mine = (row_at % row_group) * (col_devs // CORES) + col_at // CORES

    def pick(table):
        return lax.dynamic_index_in_dim(jnp.asarray(table, BF), core, 0, keepdims=False)

    plain_np, weighted_np = lon_table(
        lon_size, col_devs, cols_here, cols_pad, slots, slots_pad
    )
    lat_np = lat_table(rows_here, row_group)
    lon_fwd, lon_wfwd = pick(plain_np), pick(weighted_np)
    lon_inv, lon_winv = (
        pick(np.swapaxes(plain_np, 1, 2)), pick(np.swapaxes(weighted_np, 1, 2))
    )
    lat_fwd, lat_inv = pick(lat_np), pick(np.swapaxes(lat_np, 1, 2))

    snap_groups = [
        [(s * row_group + r) * col_devs + c for r in range(row_group) for c in range(col_devs)]
        for s in range(row_devs // row_group)
    ]
    core_pairs = [
        (r * col_devs + c, r * col_devs + c ^ 1) for r in range(row_devs) for c in range(col_devs)
    ]

    def exchange(x):
        return lax.all_to_all(x, AXES, 0, 0, axis_index_groups=snap_groups, tiled=True)

    def swap(x):
        return lax.ppermute(x, AXES, core_pairs)

    def fold(x):
        return x.reshape((CORES, groups, PACK) + x.shape[1:])

    def row(v):
        return v.reshape(1, -1)

    mask = jnp.pad(
        valid_mask.astype(F32), ((0, 0), (0, cols_pad - cols_here))
    )[:, :, None]
    mask = fold(mask)
    x5, cot5 = fold(inputs), fold(cotangent)

    def lat_spec(cols, width):
        return pl.BlockSpec((CORES, 1, PACK, cols, width), lambda i: (0, i, 0, 0, 0))

    packed_spec = pl.BlockSpec(
        (BLOCKS, CORES, 1, cols_pad, 3 * LANES), lambda i: (0, 0, i, 0, 0)
    )
    row_spec = pl.BlockSpec((1, channels), lambda i: (0, 0))
    here_spec, pad_spec, mask_spec = (
        lat_spec(cols_here, channels), lat_spec(cols_pad, channels), lat_spec(cols_pad, 1)
    )
    packed_shape = (BLOCKS, CORES, groups, cols_pad, 3 * LANES)
    flat_shape = (members, groups, cols_pad, 3 * LANES)
    pad_shape = (CORES, groups, PACK, cols_pad, channels)
    here_shape = (CORES, groups, PACK, cols_here, channels)

    def shape(s, d):
        return jax.ShapeDtypeStruct(s, d)

    def lon_forward(cells, table):
        return pl.pallas_call(
            lambda *refs: lon_kernel(col_devs, row_group, *refs),
            out_shape=[shape((half_rows, lats, LANES), BF)] * 2,
            scratch_shapes=[pltpu.VMEM((all_rows * lats, LANES), F32)],
            compiler_params=params(),
            name="lon_forward",
        )(cells.reshape(flat_shape), table)

    def lon_backward(own, other, table):
        return pl.pallas_call(
            lambda *refs: lon_back_kernel(col_devs, row_group, *refs),
            out_shape=shape(flat_shape, BF),
            compiler_params=params(),
            name="lon_backward",
        )(own, other, table)

    def big_weight(w):
        w = lax.dynamic_index_in_dim(w, mine, 1, keepdims=False)
        gap = LANES - block
        w = jnp.pad(w, ((0, 0), (0, gap), (0, gap)))
        return jnp.concatenate(
            [jnp.concatenate([w[0], w[1]], 1), jnp.concatenate([-w[1], w[0]], 1)], 0
        )

    def big_bias(b):
        b = lax.dynamic_index_in_dim(b.reshape(2, BLOCKS, block), mine, 1, keepdims=False)
        return jnp.pad(b, ((0, 0), (0, LANES - block))).reshape(1, 2 * LANES)

    wa, wb = big_weight(mix_weight_a), big_weight(mix_weight_b)
    ba, bb = big_bias(mix_bias_a), big_bias(mix_bias_b)

    normed, send = pl.pallas_call(
        first_kernel,
        grid=(groups,),
        in_specs=[here_spec, mask_spec, row_spec, row_spec],
        out_specs=[pad_spec, packed_spec],
        out_shape=[shape(pad_shape, BF), shape(packed_shape, BF)],
        compiler_params=params(),
        name="first_norm",
    )(x5, mask, row(first_gain), row(first_shift))
    cells = exchange(send.reshape(flat_shape))

    own, other = lon_forward(cells, lon_fwd)
    other = swap(other)
    turn_scratch = [pltpu.VMEM((2 * lats * half_rows, LANES), F32)]
    lat_out = [shape((lats, half_rows, LANES), BF)] * 2
    own, other, modes = pl.pallas_call(
        mix_kernel,
        out_shape=lat_out + [shape((slots_pad // 2, 2 * LAT, 2 * LANES), BF)],
        scratch_shapes=turn_scratch,
        compiler_params=params(),
        name="mix",
    )(own, other, lat_fwd, lat_inv, wa, ba, wb, bb)
    other = swap(other)
    got = exchange(lon_backward(own, other, lon_winv))

    resid, tokens, cot_pad = pl.pallas_call(
        second_kernel,
        grid=(groups,),
        in_specs=[here_spec, pad_spec, mask_spec, here_spec, packed_spec, row_spec, row_spec],
        out_specs=[pad_spec, pad_spec, pad_spec],
        out_shape=[shape(pad_shape, F32), shape(pad_shape, BF), shape(pad_shape, BF)],
        compiler_params=params(),
        name="second_norm",
    )(x5, normed, mask, cot5, got.reshape(packed_shape), row(second_gain), row(second_shift))
    tokens2 = tokens.reshape(-1, channels)
    cot2 = cot_pad.reshape(-1, channels)
    pre_up = jnp.dot(tokens2, expand_weight, preferred_element_type=F32) + expand_bias
    squash = gelu_parts(pre_up)
    active = (0.5 * pre_up * (1.0 + squash)).astype(BF)
    branch = jnp.dot(active, reduce_weight, preferred_element_type=F32)
    outer = (((0,), (0,)), ((), ()))
    across = (((1,), (1,)), ((), ()))
    grad_reduce = lax.dot_general(active, cot2, outer, preferred_element_type=F32)
    grad_active = lax.dot_general(cot2, reduce_weight, across, preferred_element_type=F32)
    grad_pre = (gelu_slope(pre_up, squash) * grad_active).astype(BF)
    grad_expand = lax.dot_general(tokens2, grad_pre, outer, preferred_element_type=F32)
    grad_expand_bias = jnp.sum(grad_pre.astype(F32), axis=0)
    grad_tokens = lax.dot_general(grad_pre, expand_weight, across, preferred_element_type=F32)

    one_row = shape((1, channels), F32)
    outputs, grad_resid, send, g_gain2, g_shift2, g_rbias = pl.pallas_call(
        third_kernel,
        grid=(groups,),
        in_specs=[pad_spec, pad_spec, pad_spec, pad_spec, mask_spec, row_spec, row_spec],
        out_specs=[here_spec, pad_spec, packed_spec, row_spec, row_spec, row_spec],
        out_shape=[shape(here_shape, F32), shape(pad_shape, F32), shape(packed_shape, BF)]
        + [one_row] * 3,
        compiler_params=params(),
        name="second_back",
    )(
        resid, branch.reshape(pad_shape), grad_tokens.reshape(pad_shape), cot_pad, mask,
        row(second_gain), row(reduce_bias),
    )
    cells = exchange(send.reshape(flat_shape))

    own, other = lon_forward(cells, lon_wfwd)
    other = swap(other)
    square = shape((2 * LANES, 2 * LANES), F32)
    line = shape((1, 2 * LANES), F32)
    own, other, g_wa, g_ba, g_wb, g_bb = pl.pallas_call(
        mix_back_kernel,
        out_shape=lat_out + [square, line, square, line],
        scratch_shapes=turn_scratch,
        compiler_params=params(),
        name="mix_back",
    )(own, other, modes, lat_fwd, lat_inv, wa, ba, wb, bb)
    other = swap(other)
    got = exchange(lon_backward(own, other, lon_inv))

    grad_inputs, g_gain1, g_shift1 = pl.pallas_call(
        last_kernel,
        grid=(groups,),
        in_specs=[here_spec, pad_spec, mask_spec, packed_spec, row_spec],
        out_specs=[here_spec, row_spec, row_spec],
        out_shape=[shape(here_shape, F32)] + [one_row] * 2,
        compiler_params=params(),
        name="first_back",
    )(x5, grad_resid, mask, got.reshape(packed_shape), row(first_gain))

    def small_weight(g):
        rr, ri = g[:block, :block], g[:block, LANES : LANES + block]
        ir, ii = g[LANES : LANES + block, :block], g[LANES : LANES + block, LANES : LANES + block]
        pair = jnp.stack([rr + ii, ri - ir])[:, None]
        return lax.dynamic_update_slice(
            jnp.zeros((2, BLOCKS, block, block), F32), pair, (0, mine, 0, 0)
        )

    def small_bias(g):
        pair = g.reshape(2, 1, LANES)[:, :, :block]
        full = lax.dynamic_update_slice(jnp.zeros((2, BLOCKS, block), F32), pair, (0, mine, 0))
        return full.reshape(2, channels)

    big = lax.psum((grad_expand.astype(BF), grad_reduce.astype(BF)), AXES)
    g_expand, g_reduce = big[0].astype(F32), big[1].astype(F32)
    (g_gain1, g_shift1, g_wa, g_ba, g_wb, g_bb, g_gain2, g_shift2, g_ebias, g_rbias) = lax.psum(
        (
            g_gain1, g_shift1, small_weight(g_wa), small_bias(g_ba), small_weight(g_wb),
            small_bias(g_bb), g_gain2, g_shift2, grad_expand_bias, g_rbias,
        ),
        AXES,
    )

    def flat(v):
        return v.reshape(-1)

    return (
        outputs.reshape(inputs.shape), grad_inputs.reshape(inputs.shape),
        flat(g_gain1), flat(g_shift1), g_wa, g_ba, g_wb, g_bb, flat(g_gain2), flat(g_shift2),
        g_expand, g_ebias, g_reduce, flat(g_rbias),
    )


def solution(mesh):
    grid = P("rows", "cols", None)
    placed = (grid, P("rows", "cols"), grid) + (P(),) * 12
    return jax.shard_map(
        per_device,
        mesh=mesh,
        in_specs=placed,
        out_specs=(grid, grid) + (P(),) * 12,
        check_vma=False,
    )
```

time: 1410 us -> 603 us (0.43)
  blocking collectives: 472 us -> 41.7 us
  local copies, waits for them, and re-layouts: 379 us -> 43.2 us
  waiting for transfers between devices: 147 us -> 290 us
  other arithmetic: 154 us -> 14.2 us
  matrix products: 205 us -> 70.1 us
  Pallas kernels: 0 us -> 104 us
    all_to_all x9 -> x0, blocking collectives: 433 us -> none  [the longest x1 82.9 us: per_device(): lax.all_to_all(grad_chan_cells.reshape(chan_shape), 'rows', split_axis=0,...]
    psum x1 -> x2, waiting for transfers between devices: 4.08 us -> 228 us  [the longest x1 158 us: per_device(): big = lax.psum((grad_expand.astype(BF), grad_reduce.astype(BF)), AXES)]
    unnamed x227 -> x82, local copies, waits for them, and re-layouts: 173 us -> 30 us
    dot_general x102 -> x6, matrix products: 205 us -> 70.1 us  [the longest x1 16.4 us: per_device(): lax.dot_general(cot2, reduce_weight, across, preferred_element_type=F32)]
    pallas_call x0 -> x10, Pallas kernels: none -> 104 us  [the longest x1 26.1 us: per_device(): pl.pallas_call(mix_back_kernel, out_shape=lat_out + [square, line, square...]
    all_to_all x7 -> x4, waiting for transfers between devices: 143 us -> 59.1 us  [exchange(): lax.all_to_all(x, AXES, 0, 0, axis_index_groups=snap_groups, tiled=True)]
    all_to_all x16 -> x0, local copies, waits for them, and re-layouts: 74.8 us -> none  [the longest x1 9 us: per_device(): lax.all_to_all(grad_chan_cells.reshape(chan_shape), 'rows', split_axis=0,...]
    reduce_sum x10 -> x0, other arithmetic: 63.1 us -> none  [the longest x3 27.8 us: layer_norm(): return centred * lax.rsqrt(spread + norm_eps) * gain_in + shift_in]
  transfers between devices with their start and end apart: 8 -> 10, of which waited for: 8 -> 7; matrix products, arithmetic and copies ran while one was open for 17% -> 10% of each run, Pallas kernels for 0% -> 7%
where the time goes in v1:
time: 603 us; the launch traced here: 598 us
  waiting for transfers between devices  290 us (48%)
  Pallas kernels  104 us (17%)
  matrix products  70.1 us (12%)
  local copies, waits for them, and re-layouts  43.2 us (7%)
  blocking collectives  41.7 us (7%)
  starting transfers between devices  19.7 us (3%)
  between operations  14.8 us (2%)
  other arithmetic  14.2 us (2%)
    psum x1, waiting for transfers between devices, per_device(): big = lax.psum((grad_expand.astype(BF), grad_reduce.astype(BF)), AXES)  158 us
    psum x1, waiting for transfers between devices, per_device(): lax.psum((g_gain1, g_shift1, small_weight(g_wa), small_bias(g_ba), small_...  69.7 us
    all_to_all x4, waiting for transfers between devices, exchange(): lax.all_to_all(x, AXES, 0, 0, axis_index_groups=snap_groups, tiled=True)  59.1 us
    psum x1, blocking collectives, per_device(): lax.psum((g_gain1, g_shift1, small_weight(g_wa), small_bias(g_ba), small_...  41.7 us
    unnamed x82, local copies, waits for them, and re-layouts  30 us
    pallas_call x1, Pallas kernels, per_device(): pl.pallas_call(mix_back_kernel, out_shape=lat_out + [square, line, square...  26.1 us
    pallas_call x1, Pallas kernels, per_device(): pl.pallas_call(mix_kernel, out_shape=lat_out + [shape((slots_pad // 2, 2...  22.7 us
    all_to_all x4, starting transfers between devices, exchange(): lax.all_to_all(x, AXES, 0, 0, axis_index_groups=snap_groups, tiled=True)  18.5 us
  transfers between devices with their start and end apart: 10, of which 7 were waited for; matrix products, arithmetic and copies ran while one was open for 10% of the time, Pallas kernels for 7%

profile of v1, /device:TPU:0, one launch (start us, length us, event | category | flops | bytes accessed | tf_op | source)
XLA Modules:
  0.0 597.6 jit_solution(15166106835279309183)
XLA Ops:
  7.2 1.3 reshape.122.gain_ref
  8.4 1.3 reshape.123.shift_ref
  9.7 0.7 convert_element_type.32
  10.4 1.1 copy.44.mask_ref
  11.5 3.0 copy.43
  14.6 6.3 %first_norm.1 = (bf16[2,3,4,48,768]{4,3,2,1,0:T(8,128)(2,1)}, bf16[8,2,3,48,384]{4,3,2,1,0:T(8,128)(2,1)}) custom-call(bf16[2,3,4,45,768]{4,3,2,1,0:T(8,128)(2,1)} %bitcast.83, f32[2,3,4,48,1]{4,3,2,1,0:T(8,128)} %copy.44.mask_ref, f32[1,768]{1,0:T(1,128)} %reshape.122.gain_ref, f32[1,768]{1,0:T(1,128)} %reshape.123.shift_ref), custom_call_target="tpu_custom_call" | custom-call | tf_op jit(solution)/shard_map/first_norm/pallas_call | solution.py:539
  20.9 6.3 %all-to-all-start = ((bf16[16,3,48,384]{3,2,1,0:T(8,128)(2,1)}), bf16[16,3,48,384]{3,2,1,0:T(8,128)(2,1)S(1)}, u32[]{:S(2)}, u32[]{:S(2)}) async-start(bf16[16,3,48,384]{3,2,1,0:T(8,128)(2,1)} %bitcast.93), calls=%async_computation | async-start | bytes 3538944 | tf_op jit(solution)/shard_map/all_to_all | solution.py:472
  27.2 0.7 dynamic-slice_bitcast_fusion.5.refs_1_
  27.9 24.6 %all-to-all-done.refs_0_ = bf16[16,3,48,384]{3,2,1,0:T(8,128)(2,1)S(1)} async-done(((bf16[16,3,48,384]{3,2,1,0:T(8,128)(2,1)}), bf16[16,3,48,384]{3,2,1,0:T(8,128)(2,1)S(1)}, u32[]{:S(2)}, u32[]{:S(2)}) %all-to-all-start) | async-done | bytes 1769504 | tf_op jit(solution)/shard_map/all_to_all | solution.py:472
  52.5 1.2 copy-done.1
  53.7 5.7 lon_forward.2
  59.6 0.6 pad.22
  60.1 0.6 pad.20
  60.7 0.8 dynamic-slice_bitcast_fusion.6
  61.6 0.7 maximum_maximum_fusion.1.wb_ref
  62.3 0.7 maximum_maximum_fusion.wa_ref
  62.9 0.7 dynamic-slice_bitcast_fusion.3
  63.6 1.0 copy-done.10
  64.7 22.7 %mix.1 = (bf16[48,96,128]{2,1,0:T(8,128)(2,1)}, bf16[48,96,128]{2,1,0:T(8,128)(2,1)}, bf16[24,192,256]{2,1,0:T(8,128)(2,1)}) custom-call(bf16[96,48,128]{2,1,0:T(8,128)(2,1)} %get-tuple-element.43.own_ref, bf16[96,48,128]{2,1,0:T(8,128)(2,1)} %copy-done.10, bf16[192,192]{1,0:T(8,128)(2,1)} %get-tuple-element.121.lat_ref, ...), custom_call_target="tpu_custom_call" | custom-call | tf_op jit(solution)/shard_map/mix/pallas_call | solution.py:554
  87.4 0.5 collective-permute-start.1
  87.9 1.5 dynamic-slice_bitcast_fusion.2.refs_2_
  89.4 1.1 collective-permute-done.1.refs_1_
  90.6 1.0 copy-done.13
  91.6 3.7 lon_backward.2
  95.3 4.5 all-to-all-start.1
  99.8 0.6 reshape.131.gain_ref
  100.4 0.6 reshape.132.shift_ref
  100.9 0.6 reshape.137.bias_ref
  101.5 1.5 copy.45
  103.1 22.0 %all-to-all-done.1 = bf16[16,3,48,384]{3,2,1,0:T(8,128)(2,1)S(1)} async-done(((bf16[16,3,48,384]{3,2,1,0:T(8,128)(2,1)}), bf16[16,3,48,384]{3,2,1,0:T(8,128)(2,1)S(1)}, u32[]{:S(2)}, u32[]{:S(2)}) %all-to-all-start.1) | async-done | bytes 1769504 | tf_op jit(solution)/shard_map/all_to_all | solution.py:472
  125.1 1.2 copy-done.3
  126.3 8.8 %second_norm.1 = (f32[2,3,4,48,768]{4,3,2,1,0:T(8,128)}, bf16[2,3,4,48,768]{4,3,2,1,0:T(8,128)(2,1)}, bf16[2,3,4,48,768]{4,3,2,1,0:T(8,128)(2,1)}) custom-call(bf16[2,3,4,45,768]{4,3,2,1,0:T(8,128)(2,1)} %bitcast.84, bf16[2,3,4,48,768]{4,3,2,1,0:T(8,128)(2,1)} %get-tuple-element.41.normed_ref, f32[2,3,4,48,1]{4,3,2,1,0:T(8,128)} %copy.44.mask_ref, ...), custom_call_target="tpu_custom_call" | custom-call | tf_op jit(solution)/shard_map/second_norm/pallas_call | solution.py:564
  135.2 14.9 %multiply_convert_fusion = (bf16[1152,3072]{1,0:T(8,128)(2,1)}, f32[1152,3072]{1,0:T(8,128)}) fusion(f32[3072]{0:T(1024)S(1)} %copy-done.32, bf16[1152,768]{1,0:T(8,128)(2,1)} %bitcast.110, bf16[768,3072]{1,0:T(8,128)(2,1)} %param.32), kind=kOutput, calls=%fused_computation.12 | convolution fusion | flops 5471207424 | bytes 27734016 | tf_op jit(solution)/shard_map/dot_general | solution.py:575
  150.1 16.4 %convert_reduce_fusion = (f32[3072]{0:T(1024)S(1)}, bf16[1152,3072]{1,0:T(8,128)(2,1)}) fusion(bf16[1152,768]{1,0:T(8,128)(2,1)S(1)} %bitcast.94, bf16[3072,768]{1,0:T(8,128)(2,1)S(1)} %bitcast.109, f32[1152,3072]{1,0:T(8,128)} %get-tuple-element.117), kind=kOutput, calls=%fused_computation.11 | convolution fusion | flops 5506593792 | bytes 27734016 | tf_op jit(solution)/shard_map/dot_general | solution.py:582
  166.6 9.5 %fusion.18 = f32[1152,768]{1,0:T(8,128)} fusion(bf16[1152,3072]{1,0:T(8,128)(2,1)} %get-tuple-element.119, bf16[768,3072]{1,0:T(8,128)(2,1)S(1)} %bitcast.107), kind=kOutput, calls=%fused_computation.48 | convolution fusion | flops 5435817984 | bytes 15335424 | tf_op jit(solution)/shard_map/dot_general | solution.py:586
  176.1 7.5 %fusion.17 = f32[1152,768]{1,0:T(8,128)} fusion(bf16[1152,3072]{1,0:T(8,128)(2,1)S(1)} %copy-done.33, bf16[3072,768]{1,0:T(8,128)(2,1)S(1)} %bitcast.109), kind=kOutput, calls=%fused_computation.47 | convolution fusion | flops 5435817984 | bytes 15335424 | tf_op jit(solution)/shard_map/dot_general | solution.py:578
  183.6 11.9 %second_back.1 = (f32[2,3,4,45,768]{4,3,2,1,0:T(8,128)}, f32[2,3,4,48,768]{4,3,2,1,0:T(8,128)}, bf16[8,2,3,48,384]{4,3,2,1,0:T(8,128)(2,1)}, f32[1,768]{1,0:T(1,...) custom-call(f32[2,3,4,48,768]{4,3,2,1,0:T(8,128)} %get-tuple-element.47.resid_ref, f32[2,3,4,48,768]{4,3,2,1,0:T(8,128)} %bitcast.90, ...), custom_call_target="tpu_custom_call" | custom-call | tf_op jit(solution)/shard_map/second_back/pallas_call | solution.py:589
  195.5 3.9 all-to-all-start.2
  199.5 1.5 dynamic-slice_bitcast_fusion.1.refs_1_
  201.0 11.2 %convolution_convert_fusion = bf16[3072,768]{1,0:T(8,128)(2,1)} fusion(bf16[1152,3072]{1,0:T(8,128)(2,1)} %get-tuple-element.116, bf16[1152,768]{1,0:T(8,128)(2,1)S(1)} %bitcast.95), kind=kOutput, calls=%fused_computation.15 | convolution fusion | flops 5438177280 | bytes 13565952 | tf_op jit(solution)/shard_map/dot_general | solution.py:581
  212.3 12.5 %all-to-all-done.2.refs_0_ = bf16[16,3,48,384]{3,2,1,0:T(8,128)(2,1)S(1)} async-done(((bf16[16,3,48,384]{3,2,1,0:T(8,128)(2,1)}), bf16[16,3,48,384]{3,2,1,0:T(8,128)(2,1)S(1)}, u32[]{:S(2)}, u32[]{:S(2)}) %all-to-all-start.2) | async-done | bytes 1769504 | tf_op jit(solution)/shard_map/all_to_all | solution.py:472
  224.8 1.2 copy-done.2
  226.0 5.7 lon_forward.3
  231.7 10.5 %convolution_convert_fusion.1 = bf16[768,3072]{1,0:T(8,128)(2,1)} fusion(bf16[1152,768]{1,0:T(8,128)(2,1)} %bitcast.111, bf16[1152,3072]{1,0:T(8,128)(2,1)} %get-tuple-element.119), kind=kOutput, calls=%fused_computation.16 | convolution fusion | flops 5438177280 | bytes 13565952 | tf_op jit(solution)/shard_map/dot_general | solution.py:584
  242.2 1.0 copy-done.11
  243.2 26.1 %mix_back.1 = (bf16[48,96,128]{2,1,0:T(8,128)(2,1)}, bf16[48,96,128]{2,1,0:T(8,128)(2,1)}, f32[256,256]{1,0:T(8,128)}, f32[1,256]{1,0:T(1,128)}, f32[256,256]{1,0:T(8,128)}, /*index=5*/f32[1,256]{1,0:T(1,128)}) custom-call(bf16[96,48,128]{2,1,0:T(8,128)(2,1)} %get-tuple-element.53.own_ref, bf16[96,48,128]{2,1,0:T(8,128)(2,1)} %copy-done.11, ...), custom_call_target="tpu_custom_call" | custom-call | tf_op jit(solution)/shard_map/mix_back/pallas_call | solution.py:608
  269.4 0.6 collective-permute-start.3
  269.9 0.6 dynamic-slice_bitcast_fusion.refs_2_
  270.6 2.2 collective-permute-done.3.refs_1_
  272.8 1.0 copy-done.12
  273.8 3.7 lon_backward.3
  277.5 3.8 all-to-all-start.3
  281.7 0.7 copy-done.5
  282.7 5.7 copy.53
  288.9 158.0 %all-reduce.13.cloned.1.call-done = (bf16[768,3072]{1,0:T(8,128)(2,1)}, bf16[3072,768]{1,0:T(8,128)(2,1)}) async-done(((bf16[768,3072]{1,0:T(8,128)(2,1)}, bf16[3072,768]{1,0:T(8,128)(2,1)}), (bf16[768,3072]{1,0:T(8,128)(2,1)}, bf16[3072,768]{1,0:T(8,128)(2,1)})) %all-reduce.13.cloned.1.call-update) | async-done | bytes 9437200 | tf_op jit(solution)/shard_map/psum | solution.py:641
  446.9 7.5 %convert_element_type.36 = f32[768,3072]{1,0:T(8,128)} convert(bf16[768,3072]{1,0:T(8,128)(2,1)} %get-tuple-element.106) | non-fusion elementwise | flops 2359296 | bytes 14155776 | tf_op jit(solution)/shard_map/convert_element_type | solution.py:642
  454.5 4.5 convert_element_type.39
  458.9 1.2 copy-done
  460.1 9.1 %first_back.1 = (f32[2,3,4,45,768]{4,3,2,1,0:T(8,128)}, f32[1,768]{1,0:T(1,128)}, f32[1,768]{1,0:T(1,128)}) custom-call(bf16[2,3,4,45,768]{4,3,2,1,0:T(8,128)(2,1)} %bitcast.85, f32[2,3,4,48,768]{4,3,2,1,0:T(8,128)} %get-tuple-element.51.gresid_ref, f32[2,3,4,48,1]{4,3,2,1,0:T(8,128)} %copy.44.mask_ref, bf16[8,2,3,48,384]{4,3,2,1,0:T(8,128)(2,1)} %bitcast.86, ...), custom_call_target="tpu_custom_call" | custom-call | tf_op jit(solution)/shard_map/first_back/pallas_call | solution.py:618
  469.2 5.7 copy.54
  475.0 41.7 %all-reduce.5 = (f32[768]{0:T(1024)}, f32[768]{0:T(1024)}, f32[2,768]{1,0:T(2,128)}, f32[2,768]{1,0:T(2,128)}, f32[768]{0:T(1024)}, /*index=5*/f32[768]{0:T(1024)}, f32[3072]{0:T(1024)}, f32[768]{0:T(1024)}) all-reduce(f32[768]{0:T(1024)S(1)} %reduce, f32[768]{0:T(1024)S(1)} %reduce.1, ...), channel_id=1, replica_groups=mesh['rows'=8,'cols'=4] {'rows','cols'}, use_global_device_ids=true, to_apply=%region_0.1 | all-reduce | flops 9984 | bytes 79872 | tf_op jit(solution)/shard_map/psum | solution.py:643
  516.7 69.7 %all-reduce.11.cloned.1.call-done = (f32[2,8,96,96]{3,2,1,0:T(8,128)}, f32[2,8,96,96]{3,2,1,0:T(8,128)}) async-done(((f32[2,8,96,96]{3,2,1,0:T(8,128)}, f32[2,8,96,96]{3,2,1,0:T(8,128)}), (f32[2,8,96,96]{3,2,1,0:T(8,128)}, f32[2,8,96,96]{3,2,1,0:T(8,128)})) %all-reduce.11.cloned.1.call-update) | async-done | bytes 1179664 | tf_op jit(solution)/shard_map/psum | solution.py:643
  586.3 2.1 copy.66
  588.4 2.1 copy.67
  (103 shorter events, 1.5 us)
Async XLA Ops:
  11.5 15.7 %copy-start.17 = (bf16[2,192,192]{2,1,0:T(8,128)(2,1)S(1)}, bf16[2,192,192]{2,1,0:T(8,128)(2,1)}, u32[]{:S(2)}) copy-start(bf16[2,192,192]{2,1,0:T(8,128)(2,1)} %constant.101.clone) | copy-start | bytes 442372
  14.6 44.8 %copy-start.20 = (f32[2,768]{1,0:T(2,128)S(1)}, f32[2,768]{1,0:T(2,128)}, u32[]{:S(2)}) copy-start(f32[2,768]{1,0:T(2,128)} %param.27) | copy-start | bytes 18436
  14.6 44.9 %copy-start.21 = (f32[2,768]{1,0:T(2,128)S(1)}, f32[2,768]{1,0:T(2,128)}, u32[]{:S(2)}) copy-start(f32[2,768]{1,0:T(2,128)} %param.29) | copy-start | bytes 18436
  14.6 48.4 %copy-start.18 = (bf16[2,192,192]{2,1,0:T(8,128)(2,1)S(1)}, bf16[2,192,192]{2,1,0:T(8,128)(2,1)}, u32[]{:S(2)}) copy-start(bf16[2,192,192]{2,1,0:T(8,128)(2,1)} %constant.106.clone) | copy-start | bytes 442372
  14.6 48.4 %copy-start.19 = (bf16[2,192,192]{2,1,0:T(8,128)(2,1)S(1)}, bf16[2,192,192]{2,1,0:T(8,128)(2,1)}, u32[]{:S(2)}) copy-start(bf16[2,192,192]{2,1,0:T(8,128)(2,1)} %constant.105.clone) | copy-start | bytes 442372
  20.9 31.6 %all-to-all-start = ((bf16[16,3,48,384]{3,2,1,0:T(8,128)(2,1)}), bf16[16,3,48,384]{3,2,1,0:T(8,128)(2,1)S(1)}, u32[]{:S(2)}, u32[]{:S(2)}) async-start(bf16[16,3,48,384]{3,2,1,0:T(8,128)(2,1)} %bitcast.93), calls=%async_computation | async-start | bytes 3538944 | tf_op jit(solution)/shard_map/all_to_all | solution.py:472
  52.5 1.2 copy-start.1
  59.4 4.3 collective-permute-start
  63.6 1.0 copy-start.10
  64.6 35.1 %copy-start.22 = (f32[768]{0:T(1024)S(1)}, f32[768]{0:T(1024)}, u32[]{:S(2)}) copy-start(f32[768]{0:T(1024)} %param.30) | copy-start | bytes 9220
  64.6 35.7 %copy-start.23 = (f32[768]{0:T(1024)S(1)}, f32[768]{0:T(1024)}, u32[]{:S(2)}) copy-start(f32[768]{0:T(1024)} %param.31) | copy-start | bytes 9220
  64.6 36.3 %copy-start.24 = (f32[768]{0:T(1024)S(1)}, f32[768]{0:T(1024)}, u32[]{:S(2)}) copy-start(f32[768]{0:T(1024)} %param.35) | copy-start | bytes 9220
  64.7 36.9 %copy-start.9 = (bf16[24,45,768]{2,0,1:T(8,128)(2,1)S(1)}, bf16[24,45,768]{2,0,1:T(8,128)(2,1)}, u32[]{:S(2)}) copy-start(bf16[24,45,768]{2,0,1:T(8,128)(2,1)} %param.23) | copy-start | bytes 4976644
  87.4 3.2 collective-permute-start.1
  90.6 1.0 copy-start.13
  95.3 29.8 %all-to-all-start.1 = ((bf16[16,3,48,384]{3,2,1,0:T(8,128)(2,1)}), bf16[16,3,48,384]{3,2,1,0:T(8,128)(2,1)S(1)}, u32[]{:S(2)}, u32[]{:S(2)}) async-start(bf16[16,3,48,384]{3,2,1,0:T(8,128)(2,1)} %lon_backward.2), calls=%async_computation.1 | async-start | bytes 3538944 | tf_op jit(solution)/shard_map/all_to_all | solution.py:472
  101.5 33.6 %copy-start.32 = (f32[3072]{0:T(1024)S(1)}, f32[3072]{0:T(1024)}, u32[]{:S(2)}) copy-start(f32[3072]{0:T(1024)} %param.33) | copy-start | bytes 36868
  125.1 1.2 copy-start.3
  126.3 23.8 %slice-start.2 = ((s8[4718592]{0:T(1024)(128)(4,1)}), s8[524288]{0:T(1024)(128)(4,1)S(1)}, s32[]{:S(2)}) async-start(s8[4718592]{0:T(1024)(128)(4,1)} %bitcast.108), calls=%async_computation.8 | async-start | bytes 1048576
  135.1 15.0 %copy-start.7 = (bf16[2,3,4,48,768]{4,3,2,1,0:T(8,128)(2,1)S(1)}, bf16[2,3,4,48,768]{4,3,2,1,0:T(8,128)(2,1)}, u32[]{:S(2)}) copy-start(bf16[2,3,4,48,768]{4,3,2,1,0:T(8,128)(2,1)} %get-tuple-element.49.cot_ref) | copy-start | bytes 5308420
  135.2 14.9 %slice-start.3 = ((s8[4718592]{0:T(1024)(128)(4,1)}), s8[4194304]{0:T(1024)(128)(4,1)S(1)}, s32[]{:S(2)}) async-start(s8[4718592]{0:T(1024)(128)(4,1)} %bitcast.108), calls=%async_computation.9 | async-start | bytes 8388608
  135.2 31.4 %slice-start = ((s8[4718592]{0:T(1024)(128)(4,1)}), s8[4194304]{0:T(1024)(128)(4,1)S(1)}, s32[]{:S(2)}) async-start(s8[4718592]{0:T(1024)(128)(4,1)} %bitcast.106), calls=%async_computation.6 | async-start | bytes 8388608
  150.1 16.4 %slice-start.1 = ((s8[4718592]{0:T(1024)(128)(4,1)}), s8[524288]{0:T(1024)(128)(4,1)S(1)}, s32[]{:S(2)}) async-start(s8[4718592]{0:T(1024)(128)(4,1)} %bitcast.106), calls=%async_computation.7 | async-start | bytes 1048576
  166.6 9.6 %copy-start.33 = (bf16[1152,3072]{1,0:T(8,128)(2,1)S(1)}, bf16[1152,3072]{1,0:T(8,128)(2,1)}, u32[]{:S(2)}) copy-start(bf16[1152,3072]{1,0:T(8,128)(2,1)} %get-tuple-element.116) | copy-start | bytes 21233668
  183.6 17.4 %copy-start.8 = (bf16[2,3,4,48,768]{4,3,2,1,0:T(8,128)(2,1)S(1)}, bf16[2,3,4,48,768]{4,3,2,1,0:T(8,128)(2,1)}, u32[]{:S(2)}) copy-start(bf16[2,3,4,48,768]{4,3,2,1,0:T(8,128)(2,1)} %get-tuple-element.49.cot_ref) | copy-start | bytes 5308420
  195.5 29.3 %all-to-all-start.2 = ((bf16[16,3,48,384]{3,2,1,0:T(8,128)(2,1)}), bf16[16,3,48,384]{3,2,1,0:T(8,128)(2,1)S(1)}, u32[]{:S(2)}, u32[]{:S(2)}) async-start(bf16[16,3,48,384]{3,2,1,0:T(8,128)(2,1)} %bitcast.96), calls=%async_computation.2 | async-start | bytes 3538944 | tf_op jit(solution)/shard_map/all_to_all | solution.py:472
  199.4 247.5 %all-reduce.13.cloned.1.call-start = ((), (), s32[]{:S(2)}) async-start(), calls=%async_computation.5 | async-start | bytes 18874368 | tf_op jit(solution)/shard_map/psum | solution.py:641
  224.8 1.2 copy-start.2
  231.7 10.5 %collective-permute-start.2 = (bf16[96,48,128]{2,1,0:T(8,128)(2,1)}, bf16[96,48,128]{2,1,0:T(8,128)(2,1)S(1)}, u32[]{:S(2)}, u32[]{:S(2)}) collective-permute-start(bf16[96,48,128]{2,1,0:T(8,128)(2,1)} %get-tuple-element.54), channel_id=1, source_target_pairs={{0,1},{1,0},{2,3},{3,2},{4,5},{5,4},{6,7},{7,6},{8,9},{9,8},{10,11... | collective-permute-start | bytes 3538952 | tf_op jit(solution)/shard_map/ppermute | solution.py:475
  242.2 27.7 %copy-start.16 = (bf16[2,192,192]{2,1,0:T(8,128)(2,1)S(1)}, bf16[2,192,192]{2,1,0:T(8,128)(2,1)}, u32[]{:S(2)}) copy-start(bf16[2,192,192]{2,1,0:T(8,128)(2,1)} %constant.103.clone) | copy-start | bytes 442372
  242.2 1.0 copy-start.11
  269.3 12.0 %copy-start.15 = (f32[256,256]{1,0:T(8,128)S(1)}, f32[256,256]{1,0:T(8,128)}, u32[]{:S(2)}) copy-start(f32[256,256]{1,0:T(8,128)} %get-tuple-element.61) | copy-start | bytes 786436
  269.3 12.2 %copy-start.14 = (f32[256,256]{1,0:T(8,128)S(1)}, f32[256,256]{1,0:T(8,128)}, u32[]{:S(2)}) copy-start(f32[256,256]{1,0:T(8,128)} %get-tuple-element.63) | copy-start | bytes 786436
  269.4 3.4 collective-permute-start.3
  272.8 1.0 copy-start.12
  277.5 181.4 %all-to-all-start.3 = ((bf16[16,3,48,384]{3,2,1,0:T(8,128)(2,1)}), bf16[16,3,48,384]{3,2,1,0:T(8,128)(2,1)S(1)}, u32[]{:S(2)}, u32[]{:S(2)}) async-start(bf16[16,3,48,384]{3,2,1,0:T(8,128)(2,1)} %lon_backward.3), calls=%async_computation.3 | async-start | bytes 3538944 | tf_op jit(solution)/shard_map/all_to_all | solution.py:472
  281.3 305.0 %all-reduce.11.cloned.1.call-start = ((), (), s32[]{:S(2)}) async-start(), calls=%async_computation.4 | async-start | bytes 3145728 | tf_op jit(solution)/shard_map/psum | solution.py:643
  281.5 0.9 copy-start.5
  281.6 6.8 %copy-start.27 = (f32[1,768]{1,0:T(1,128)S(1)}, f32[1,768]{1,0:T(1,128)}, u32[]{:S(2)}) copy-start(f32[1,768]{1,0:T(1,128)} %get-tuple-element.65) | copy-start | bytes 9220
  281.6 6.8 %copy-start.26 = (f32[1,768]{1,0:T(1,128)S(1)}, f32[1,768]{1,0:T(1,128)}, u32[]{:S(2)}) copy-start(f32[1,768]{1,0:T(1,128)} %get-tuple-element.66) | copy-start | bytes 9220
  281.6 6.8 %copy-start.25 = (f32[1,768]{1,0:T(1,128)S(1)}, f32[1,768]{1,0:T(1,128)}, u32[]{:S(2)}) copy-start(f32[1,768]{1,0:T(1,128)} %get-tuple-element.67) | copy-start | bytes 9220
  281.6 6.9 %copy-start.31 = (f32[1,256]{1,0:T(1,128)S(1)}, f32[1,256]{1,0:T(1,128)}, u32[]{:S(2)}) copy-start(f32[1,256]{1,0:T(1,128)} %get-tuple-element.64) | copy-start | bytes 3076
  281.6 7.0 %copy-start.30 = (f32[1,256]{1,0:T(1,128)S(1)}, f32[1,256]{1,0:T(1,128)}, u32[]{:S(2)}) copy-start(f32[1,256]{1,0:T(1,128)} %get-tuple-element.62) | copy-start | bytes 3076
  281.7 0.9 copy-start.6
  446.9 7.5 %copy-start.4 = (bf16[3072,768]{1,0:T(8,128)(2,1)S(1)}, bf16[3072,768]{1,0:T(8,128)(2,1)}, u32[]{:S(2)}) copy-start(bf16[3072,768]{1,0:T(8,128)(2,1)} %get-tuple-element.107) | copy-start | bytes 14155780
  458.9 1.2 copy-start
  469.2 5.7 copy-start.29
  469.2 5.7 copy-start.28
Sparse Core Ops, SparseCore 0:
  242.3 204.5 all-reduce.12
  453.9 132.4 all-reduce.10

commit v2 on v1

--- a/solution.py
+++ b/solution.py
@@ -29,8 +29,38 @@
     return (value + step - 1) // step * step
 
 
-def params(limit=56):
-    return pltpu.CompilerParams(vmem_limit_bytes=limit * 1024 * 1024)
+def call(kernel, args, out_shape, us, after=(), in_specs=None, prefetch=(), vmem=12, **kw):
+    outs = out_shape if isinstance(out_shape, (list, tuple)) else [out_shape]
+    lead, n_in, n_after = len(prefetch), len(args), len(after)
+
+    def body(*refs):
+        kernel(*refs[: lead + n_in], *refs[lead + n_in + n_after :])
+
+    grid = kw.pop("grid", (1,))
+    whole = lambda x: pl.BlockSpec(x.shape, lambda *_, n=len(x.shape): (0,) * n)
+    specs = list(in_specs) if in_specs is not None else [whole(a) for a in args]
+    specs += [pl.BlockSpec(memory_space=pl.ANY)] * n_after
+    out_specs = kw.pop("out_specs", None) or [whole(o) for o in outs]
+    got = pl.pallas_call(
+        body,
+        grid_spec=pltpu.PrefetchScalarGridSpec(
+            num_scalar_prefetch=lead,
+            grid=grid,
+            in_specs=specs,
+            out_specs=out_specs,
+            scratch_shapes=kw.pop("scratch_shapes", ()),
+        ),
+        out_shape=outs,
+        compiler_params=pltpu.CompilerParams(vmem_limit_bytes=vmem * 1024 * 1024),
+        cost_estimate=pl.CostEstimate(
+            flops=0, bytes_accessed=int(us * 1e5), transcendentals=0
+        ),
+        **kw,
+    )(*prefetch, *args, *after)
+    return list(got) if isinstance(out_shape, (list, tuple)) else got[0]
+
+
+SPLIT = 3
 
 
 def lon_table(lon_size, col_devs, cols_here, cols_pad, slots, slots_pad):
@@ -51,7 +81,12 @@
             weights[half, slot] = 1.0 if edge else 2.0
     weighted = table * weights[:, None, :, None, None]
     rows = 2 * slots_pad
-    flat = [a.reshape(CORES, rows, col_devs * cols_pad) for a in (table, weighted)]
+    flat = [
+        a.reshape(CORES, 2, SPLIT, slots_pad // SPLIT, col_devs, cols_pad)
+        .swapaxes(1, 2)
+        .reshape(CORES, rows, col_devs * cols_pad)
+        for a in (table, weighted)
+    ]
     return [
         np.stack([np.concatenate([a[h], a[1 - h]], 0) for h in range(CORES)]) for a in flat
     ]
@@ -182,8 +217,8 @@
 
 
 def third_kernel(
-    resid_ref, branch_ref, gtok_ref, cot_ref, mask_ref, gain_ref, bias_ref,
-    out_ref, gresid_ref, send_ref, ggain_ref, gshift_ref, gbias_ref,
+    resid_ref, gtok_ref, cot_ref, mask_ref, gain_ref,
+    gresid_ref, send_ref, ggain_ref, gshift_ref, gbias_ref,
 ):
     @pl.when(pl.program_id(0) == 0)
     def _():
@@ -191,13 +226,10 @@
         gshift_ref[...] = jnp.zeros_like(gshift_ref)
         gbias_ref[...] = jnp.zeros_like(gbias_ref)
 
-    here = out_ref.shape[3]
     for half in range(CORES):
         lats = []
         for j in range(PACK):
-            resid = resid_ref[half, 0, j]
-            out_ref[half, 0, j] = (resid + branch_ref[half, 0, j] + bias_ref[...])[:here]
-            xhat, inv = stats(resid)
+            xhat, inv = stats(resid_ref[half, 0, j])
             gtok = gtok_ref[half, 0, j]
             cot = cot_ref[half, 0, j].astype(F32)
             ggain_ref[...] += jnp.sum(gtok * xhat, axis=0, keepdims=True)
@@ -229,6 +261,150 @@
             ggain_ref[...] += jnp.sum(grad * xhat, axis=0, keepdims=True)
             gshift_ref[...] += jnp.sum(grad, axis=0, keepdims=True)
             out_ref[half, 0, j] = (gres + norm_back(grad, xhat, inv, gain_ref[...]))[:here]
+
+
+OUTER = (((0,), (0,)), ((), ()))
+ACROSS = (((1,), (1,)), ((), ()))
+
+
+def chain_kernel(
+    tok_ref, cot_ref, up_ref, bias_ref, down_ref, act_ref, gpre_ref, gtok_ref, gbias_ref
+):
+    @pl.when(pl.program_id(0) == 0)
+    def _():
+        gtok_ref[...] = jnp.zeros_like(gtok_ref)
+
+    pre = jnp.dot(tok_ref[...], up_ref[...], preferred_element_type=F32) + bias_ref[...]
+    squash = gelu_parts(pre)
+    act_ref[...] = (0.5 * pre * (1.0 + squash)).astype(BF)
+    gact = lax.dot_general(cot_ref[...], down_ref[...], ACROSS, preferred_element_type=F32)
+    gpre = gelu_slope(pre, squash) * gact
+    gbias_ref[...] = jnp.sum(gpre, axis=0, keepdims=True)
+    gpre = gpre.astype(BF)
+    gpre_ref[...] = gpre
+    gtok_ref[...] += lax.dot_general(gpre, up_ref[...], ACROSS, preferred_element_type=F32)
+
+
+def split_store(value, tiles, sent_ref, kept_ref):
+    @pl.when(pl.program_id(0) < tiles)
+    def _():
+        sent_ref[...] = value
+
+    @pl.when(pl.program_id(0) >= tiles)
+    def _():
+        kept_ref[...] = value
+
+
+def weight_grad_kernel(core_ref, act_ref, cot_ref, sent_ref, kept_ref):
+    value = lax.dot_general(act_ref[...], cot_ref[...], OUTER, preferred_element_type=F32)
+    split_store(value.astype(BF), pl.num_programs(0) // 2, sent_ref, kept_ref)
+
+
+def branch_kernel(act_ref, down_ref, resid_ref, bias_ref, out_ref):
+    cols, here = resid_ref.shape[3], out_ref.shape[3]
+    rows = CORES * PACK * cols
+    act = act_ref[...].reshape(rows, act_ref.shape[-1])
+    branch = jnp.dot(act, down_ref[...], preferred_element_type=F32) + bias_ref[...]
+    for half in range(CORES):
+        for j in range(PACK):
+            at = (half * PACK + j) * cols
+            out_ref[half, 0, j] = (resid_ref[half, 0, j] + branch[at : at + cols])[:here]
+
+
+def plus(left, right):
+    return (left.astype(F32) + right.astype(F32)).astype(BF)
+
+
+def halve_first_kernel(bits_ref, *refs):
+    count = len(refs) // 6
+    for p in range(count):
+        a, b, c, d = refs[4 * p : 4 * p + 4]
+        low, high = plus(a[...], b[...]), plus(c[...], d[...])
+        first = bits_ref[p] == 0
+        refs[4 * count + 2 * p][...] = jnp.where(first, low, high)
+        refs[4 * count + 2 * p + 1][...] = jnp.where(first, high, low)
+
+
+def halve_kernel(bits_ref, *refs):
+    count = len(refs) // 6
+    for k in range(2 * count):
+        refs[4 * count + k][...] = plus(refs[2 * k][...], refs[2 * k + 1][...])
+
+
+def join_kernel(count, *refs):
+    for p in range(count):
+        n = refs[2 * p].shape[0]
+        value = plus(refs[2 * p][...], refs[2 * p + 1][...])
+        for out in refs[-2:]:
+            out[p * n : (p + 1) * n] = value
+
+
+def part_kernel(kept, got, *outs):
+    n, count = outs[0].shape[0], len(outs) // 2
+    for p in range(count):
+        rows = slice(p * n, (p + 1) * n)
+        value = plus(kept[rows], got[rows])
+        outs[p][...] = value
+        outs[count + p][...] = value
+
+
+def add_kernel(left, right, *outs):
+    value = left[...].astype(F32) + right[...].astype(F32)
+    for out in outs:
+        out[...] = value.astype(out.dtype)
+
+
+def tail_kernel(*refs):
+    for out in refs[-2:]:
+        at = 0
+        for ref in refs[:-2]:
+            out[:, at : at + ref.shape[1]] = ref[...]
+            at += ref.shape[1]
+
+
+def merge_kernel(count, single, bits_ref, *refs):
+    outs = refs[2 * count :]
+    for p in range(count):
+        own, got = refs[2 * p], refs[2 * p + 1]
+        n = own.shape[0]
+        for out in (outs[p::count] if not single else [o.at[p] for o in outs]):
+            out[pl.ds(pl.multiple_of(bits_ref[p] * n, 16), n), :] = own[...]
+            out[pl.ds(pl.multiple_of((1 - bits_ref[p]) * n, 16), n), :] = got[...]
+
+
+def widen_kernel(core_ref, reduce_ref, expand_ref, *refs):
+    reduce_out, expand_out = refs[-2:]
+    reduce_out[...] = reduce_ref[...].astype(F32)
+    expand_out[...] = expand_ref[...].astype(F32).T
+
+
+def collect_kernel(block, *refs):
+    n = (len(refs) - 1) // SPLIT
+    out = refs[-1]
+    out[...] = jnp.zeros_like(out)
+    for i in range(n // 2):
+        g = sum(refs[n * k + 2 * i][...] for k in range(SPLIT))
+        line = sum(refs[n * k + 2 * i + 1][...] for k in range(SPLIT))
+        top, low = g[:block], g[LANES : LANES + block]
+        at = 2 * i * block
+        out[at : at + block] = top[:, :LANES] + low[:, LANES:]
+        out[at + block : at + 2 * block] = top[:, LANES:] - low[:, :LANES]
+        base = n * block + 2 * i
+        out[base : base + 1] = line[:, :LANES]
+        out[base + 1 : base + 2] = line[:, LANES:]
+
+
+def spread_kernel(block, x_ref, wa_ref, wb_ref, ba_ref, bb_ref):
+    for i, (w, b) in enumerate(((wa_ref, ba_ref), (wb_ref, bb_ref))):
+        for part in range(2):
+            row = 4 * block + 2 * i + part
+            tiles = []
+            for q in range(BLOCKS):
+                at = (2 * i + part) * block
+                w[part, q] = x_ref[q, at : at + block, :block].astype(F32)
+                tail = x_ref[q, 4 * block :, :].astype(F32)
+                tiles.append(tail[2 * i + part : 2 * i + part + 1])
+            b[part : part + 1, :] = join_blocks(tiles)
 
 
 def lon_kernel(col_devs, row_group, x_ref, table_ref, own_ref, other_ref, turn_ref):
@@ -254,7 +430,8 @@
         ].astype(BF)
 
 
-def lon_back_kernel(col_devs, row_group, own_ref, other_ref, table_ref, out_ref):
+def lon_back_kernel(col_devs, row_group, pieces, table_ref, *refs):
+    out_ref = refs[pieces]
     groups = out_ref.shape[1]
     cols = out_ref.shape[2]
     for r in range(row_group):
@@ -264,7 +441,7 @@
                 pair = []
                 for k in range(2):
                     at = (r * groups + g) * PACK + j + k
-                    pair.append(jnp.concatenate([own_ref[at], other_ref[at]], axis=0))
+                    pair.append(jnp.concatenate([r_[at] for r_ in refs[:pieces]], axis=0))
                 cells = jnp.dot(
                     table_ref[...], jnp.concatenate(pair, axis=1), preferred_element_type=F32
                 )
@@ -288,18 +465,17 @@
     return 0.5 * (1.0 + squash) + 0.5 * v * (1.0 - squash * squash) * inner
 
 
-def latitudes(own_ref, other_ref, slot, half_slots):
+def latitudes(own_ref, other_ref, row, run):
     return jnp.concatenate(
-        [own_ref[slot], other_ref[slot], own_ref[slot + half_slots], other_ref[slot + half_slots]],
-        axis=0,
-    )
-
-
-def turn_out(turn_ref, value, slot, lats, rows, half_slots):
+        [own_ref[row], other_ref[row], own_ref[row + run], other_ref[row + run]], axis=0
+    )
+
+
+def turn_out(turn_ref, value, row, lats, rows, run):
     for part in range(2):
         for dest in range(2):
             piece = value[(2 * part + dest) * lats : (2 * part + dest + 1) * lats]
-            start = dest * lats * rows + part * half_slots + slot
+            start = dest * lats * rows + part * run + row
             turn_ref[pl.ds(start, lats, stride=rows), :] = piece
 
 
@@ -318,14 +494,15 @@
     own_ref, other_ref, lat_ref, back_ref, wa_ref, ba_ref, wb_ref, bb_ref,
     own_out, other_out, modes_out, turn_ref,
 ):
-    half_slots = own_ref.shape[0] // 2
-    lats = own_ref.shape[1]
-
-    @pl.loop(0, half_slots // 2)
+    lats, rows = own_ref.shape[1], own_ref.shape[0]
+    run = rows // 2 // SPLIT
+
+    @pl.loop(0, rows // 4)
     def _(step):
         slot = 2 * step
+        row = slot + slot // run * run
         cells = jnp.concatenate(
-            [latitudes(own_ref, other_ref, slot + k, half_slots) for k in range(2)], axis=1
+            [latitudes(own_ref, other_ref, row + k, run) for k in range(2)], axis=1
         )
         full = jnp.dot(lat_ref[...], cells, preferred_element_type=F32).astype(BF)
         real, imag = full[:LAT], full[LAT:]
@@ -350,10 +527,7 @@
         )
         back = jnp.dot(back_ref[...], mixed, preferred_element_type=F32)
         for k in range(2):
-            turn_out(
-                turn_ref, back[:, k * LANES : (k + 1) * LANES], slot + k, lats,
-                2 * half_slots, half_slots,
-            )
+            turn_out(turn_ref, back[:, k * LANES : (k + 1) * LANES], row + k, lats, rows, run)
 
     drain(turn_ref, own_out, other_out)
 
@@ -362,18 +536,16 @@
     own_ref, other_ref, modes_ref, lat_ref, back_ref, wa_ref, ba_ref, wb_ref, bb_ref,
     own_out, other_out, gwa_ref, gba_ref, gwb_ref, gbb_ref, turn_ref,
 ):
-    half_slots = own_ref.shape[0] // 2
-    lats = own_ref.shape[1]
+    lats, rows = own_ref.shape[1], own_ref.shape[0]
+    run = rows // 2
     for ref in (gwa_ref, gba_ref, gwb_ref, gbb_ref):
         ref[...] = jnp.zeros_like(ref)
-    outer = (((0,), (0,)), ((), ()))
-    across = (((1,), (1,)), ((), ()))
-
-    @pl.loop(0, half_slots // 2)
+
+    @pl.loop(0, run // 2)
     def _(step):
-        slot = 2 * step
+        row = 2 * step
         cells = jnp.concatenate(
-            [latitudes(own_ref, other_ref, slot + k, half_slots) for k in range(2)], axis=1
+            [latitudes(own_ref, other_ref, row + k, run) for k in range(2)], axis=1
         )
         full = jnp.dot(lat_ref[...], cells, preferred_element_type=F32)
         real, imag = full[:LAT], full[LAT:]
@@ -394,15 +566,15 @@
         grad_b = factor * grad
         gbb_ref[...] += jnp.sum(grad_b, axis=0, keepdims=True)
         grad_b = grad_b.astype(BF)
-        grad_hidden = lax.dot_general(grad_b, wb_ref[...], across, preferred_element_type=F32)
-        gwb_ref[...] += lax.dot_general(hidden, grad_b, outer, preferred_element_type=F32)
+        grad_hidden = lax.dot_general(grad_b, wb_ref[...], ACROSS, preferred_element_type=F32)
+        gwb_ref[...] += lax.dot_general(hidden, grad_b, OUTER, preferred_element_type=F32)
         grad_a = gelu_slope(pre_a, squash_a) * grad_hidden
         gba_ref[...] += jnp.sum(grad_a, axis=0, keepdims=True)
         grad_a = grad_a.astype(BF)
         grad_modes = lax.dot_general(
-            grad_a, wa_ref[...], across, preferred_element_type=F32
+            grad_a, wa_ref[...], ACROSS, preferred_element_type=F32
         ).astype(BF)
-        gwa_ref[...] += lax.dot_general(modes, grad_a, outer, preferred_element_type=F32)
+        gwa_ref[...] += lax.dot_general(modes, grad_a, OUTER, preferred_element_type=F32)
         mixed = jnp.concatenate(
             [
                 jnp.concatenate([grad_modes[:LAT, :LANES], grad_modes[LAT:, :LANES]], axis=1),
@@ -412,10 +584,7 @@
         )
         back = jnp.dot(back_ref[...], mixed, preferred_element_type=F32)
         for k in range(2):
-            turn_out(
-                turn_ref, back[:, k * LANES : (k + 1) * LANES], slot + k, lats,
-                2 * half_slots, half_slots,
-            )
+            turn_out(turn_ref, back[:, k * LANES : (k + 1) * LANES], row + k, lats, rows, run)
 
     drain(turn_ref, own_out, other_out)
 
@@ -504,22 +673,179 @@
     def shape(s, d):
         return jax.ShapeDtypeStruct(s, d)
 
-    def lon_forward(cells, table):
-        return pl.pallas_call(
+    index = row_at * col_devs + col_at
+    devices = row_devs * col_devs
+    all_bits = [2**k for k in range(16) if 2**k < devices]
+    cube, outer_bits = all_bits[1:4], all_bits[4:]
+    core_line = core.astype(jnp.int32).reshape(1)
+
+    def bit(mask_bit):
+        return (index // mask_bit) % 2
+
+    def partner(x, flip):
+        return lax.ppermute(x, AXES, [(d, d ^ flip) for d in range(devices)])
+
+
+    orders = [[cube[(p + k) % 3] for k in range(3)] for p in range(3)]
+
+    def bits(level):
+        return jnp.stack([bit(o[level]) for o in orders]).astype(jnp.int32)
+
+    def zipped(kept, got):
+        return [x for pair in zip(kept, got) for x in pair]
+
+    def merge(own, got, which, single, after):
+        n, (r, c) = len(own), own[0].shape
+        out = [shape((n, 2 * r, c), BF)] * 2 if single else [shape((2 * r, c), BF)] * (2 * n)
+        return call(
+            lambda *refs: merge_kernel(n, single, *refs), zipped(own, got), out, 2.0,
+            after=after, prefetch=[which], vmem=34 if single else 12, name="merge",
+        )
+
+    class Sum:
+        def __init__(self, kept, got):
+            self.kept, self.got, self.level = kept, got, 0
+
+        def send(self, arrays):
+            self.got = [partner(x, o[self.level]) for x, o in zip(arrays, orders)]
+
+        def halve(self, after=()):
+            first, n = self.level == 0, len(orders)
+            rows, wide = self.kept[0].shape
+            half = rows // n if first else rows // 2
+            tiles = 2 if first else 1
+            t = half // tiles
+            args, specs = [], []
+            if first:
+                for chunk in range(2 * n):
+                    grad, at = divmod(chunk, n)
+                    args += [self.kept[grad], self.got[grad]]
+                    specs += [pl.BlockSpec((t, wide), lambda i, b, at=at: (at * tiles + i, 0))] * 2
+            else:
+                for p in range(n):
+                    stay = lambda i, b, p=p: (b[p] * tiles + i, 0)
+                    leave = lambda i, b, p=p: ((1 - b[p]) * tiles + i, 0)
+                    args += [self.kept[p], self.got[p]] * 2
+                    specs += [pl.BlockSpec((t, wide), m) for m in (stay, stay, leave, leave)]
+            res = call(
+                halve_first_kernel if first else halve_kernel,
+                args, [shape((half, wide), BF)] * (2 * n), 3.0,
+                after=after, prefetch=[bits(self.level)], grid=(tiles,), in_specs=specs,
+                out_specs=[pl.BlockSpec((t, wide), lambda i, b: (i, 0))] * (2 * n), vmem=20 if first else 12, name="halve",
+            )
+            self.kept = res[0::2]
+            self.send(res[1::2])
+            self.level += 1
+            return self.kept[0]
+
+        def join(self, after=()):
+            n, (r, c) = len(orders), self.kept[0].shape
+            self.kept, sent = call(
+                lambda *refs: join_kernel(n, *refs), zipped(self.kept, self.got),
+                [shape((n * r, c), BF)] * 2, 1.5, after=after, name="join",
+            )
+            self.got = partner(sent, outer_bits[0])
+            for m in outer_bits[1:]:
+                self.kept, sent = add(self.kept, self.got, BF)
+                self.got = partner(sent, m)
+            return self.kept
+
+        def part(self, after=()):
+            n, (r, c) = len(orders), self.kept.shape
+            res = call(
+                part_kernel, [self.kept, self.got], [shape((r // n, c), BF)] * (2 * n), 1.5,
+                after=after, name="part",
+            )
+            self.kept = res[:n]
+            self.level = len(cube) - 1
+            self.send(res[n:])
+            return self.kept[0]
+
+        def double(self, after=()):
+            n, (r, c), single = len(orders), self.kept[0].shape, self.level == 0
+            res = merge(self.kept, self.got, bits(self.level), single, after)
+            self.level -= 1
+            if not single:
+                self.kept = res[:n]
+                self.send(res[n:])
+                return self.kept[0]
+            self.kept, sent = (x.reshape(2 * n * r, c) for x in res)
+            self.got = partner(sent, 1)
+            return self.kept
+
+        def widen(self):
+            (rows, c), t = self.kept.shape, 256
+            steps = rows // 2 // t
+            full = [shape((rows, c), F32), shape((c, rows), F32)]
+            done = []
+            for k, x in enumerate((self.kept, self.got)):
+                at = lambda i, h, k=k: jnp.where(h[0] == 0, k, 1 - k) * steps + i
+                done = call(
+                    widen_kernel, [x, x] + done, full, 5.0, prefetch=[core_line], grid=(steps,),
+                    in_specs=[
+                        pl.BlockSpec((t, c), lambda i, h: (i, 0)),
+                        pl.BlockSpec((t, c), lambda i, h: (steps + i, 0)),
+                    ] + [pl.BlockSpec(memory_space=pl.ANY)] * len(done),
+                    out_specs=[
+                        pl.BlockSpec((t, c), lambda i, h, at=at: (at(i, h), 0)),
+                        pl.BlockSpec((c, t), lambda i, h, at=at: (0, at(i, h))),
+                    ],
+                    input_output_aliases={3: 0, 4: 1} if done else {}, name="widen",
+                )
+            return done
+
+    def add(x, y, dtype, after=()):
+        return call(add_kernel, [x, y], [shape(x.shape, dtype)] * 2, 1.0, after=after, name="add")
+
+    class Modes:
+        def __init__(self, x):
+            self.flips = [1] + outer_bits
+            self.doubles = list(cube)
+            self.x, self.got = x, partner(x, 1)
+
+        def step(self, after=()):
+            if self.flips:
+                self.flips.pop(0)
+                left = self.flips or self.doubles
+                self.x, sent = add(self.x, self.got, BF, after)
+            else:
+                m = self.doubles.pop(0)
+                left = self.doubles
+                which = bit(m).astype(jnp.int32).reshape(1)
+                self.x, sent = merge([self.x], [self.got], which, False, after)
+            if left:
+                self.got = partner(sent, left[0])
+            return self.x
+
+    class Tail:
+        def __init__(self, x):
+            self.bits = list(all_bits)
+            self.x, self.got = x[0], partner(x[1], self.bits[0])
+
+        def step(self, after=()):
+            self.x, sent = add(self.x, self.got, F32, after)
+            self.bits.pop(0)
+            if self.bits:
+                self.got = partner(sent, self.bits[0])
+            return self.x
+
+
+    def lon_forward(cells, table, after=()):
+        return call(
             lambda *refs: lon_kernel(col_devs, row_group, *refs),
-            out_shape=[shape((half_rows, lats, LANES), BF)] * 2,
+            [cells.reshape(flat_shape), table],
+            [shape((half_rows, lats, LANES), BF)] * 2, 5.5, after=after,
             scratch_shapes=[pltpu.VMEM((all_rows * lats, LANES), F32)],
-            compiler_params=params(),
-            name="lon_forward",
-        )(cells.reshape(flat_shape), table)
-
-    def lon_backward(own, other, table):
-        return pl.pallas_call(
-            lambda *refs: lon_back_kernel(col_devs, row_group, *refs),
-            out_shape=shape(flat_shape, BF),
-            compiler_params=params(),
-            name="lon_backward",
-        )(own, other, table)
+            vmem=24, name="lon_forward",
+        )
+
+    def lon_backward(pieces, table, after=()):
+        return call(
+            lambda *refs: lon_back_kernel(
+                col_devs, row_group, len(pieces), refs[len(pieces)], *refs[: len(pieces)], refs[-1]
+            ),
+            [*pieces, table], shape(flat_shape, BF), 3.5, after=after, vmem=16, name="lon_backward",
+        )
 
     def big_weight(w):
         w = lax.dynamic_index_in_dim(w, mine, 1, keepdims=False)
@@ -536,117 +862,179 @@
     wa, wb = big_weight(mix_weight_a), big_weight(mix_weight_b)
     ba, bb = big_bias(mix_bias_a), big_bias(mix_bias_b)
 
-    normed, send = pl.pallas_call(
-        first_kernel,
-        grid=(groups,),
-        in_specs=[here_spec, mask_spec, row_spec, row_spec],
-        out_specs=[pad_spec, packed_spec],
-        out_shape=[shape(pad_shape, BF), shape(packed_shape, BF)],
-        compiler_params=params(),
-        name="first_norm",
-    )(x5, mask, row(first_gain), row(first_shift))
+    normed, send = call(
+        first_kernel, [x5, mask, row(first_gain), row(first_shift)],
+        [shape(pad_shape, BF), shape(packed_shape, BF)], 6.0,
+        grid=(groups,), in_specs=[here_spec, mask_spec, row_spec, row_spec],
+        out_specs=[pad_spec, packed_spec], vmem=16, name="first_norm",
+    )
     cells = exchange(send.reshape(flat_shape))
 
     own, other = lon_forward(cells, lon_fwd)
     other = swap(other)
-    turn_scratch = [pltpu.VMEM((2 * lats * half_rows, LANES), F32)]
-    lat_out = [shape((lats, half_rows, LANES), BF)] * 2
-    own, other, modes = pl.pallas_call(
-        mix_kernel,
-        out_shape=lat_out + [shape((slots_pad // 2, 2 * LAT, 2 * LANES), BF)],
-        scratch_shapes=turn_scratch,
-        compiler_params=params(),
-        name="mix",
-    )(own, other, lat_fwd, lat_inv, wa, ba, wb, bb)
+    own, other, modes = call(
+        mix_kernel, [own, other, lat_fwd, lat_inv, wa, ba, wb, bb],
+        [shape((lats, half_rows, LANES), BF)] * 2
+        + [shape((slots_pad // 2, 2 * LAT, 2 * LANES), BF)], 22.0,
+        scratch_shapes=[pltpu.VMEM((2 * lats * half_rows, LANES), F32)], vmem=32, name="mix",
+    )
     other = swap(other)
-    got = exchange(lon_backward(own, other, lon_winv))
-
-    resid, tokens, cot_pad = pl.pallas_call(
+    got = exchange(lon_backward([own, other], lon_winv))
+
+    resid, tokens, cot_pad = call(
         second_kernel,
+        [x5, normed, mask, cot5, got.reshape(packed_shape), row(second_gain), row(second_shift)],
+        [shape(pad_shape, F32), shape(pad_shape, BF), shape(pad_shape, BF)], 8.5,
         grid=(groups,),
         in_specs=[here_spec, pad_spec, mask_spec, here_spec, packed_spec, row_spec, row_spec],
-        out_specs=[pad_spec, pad_spec, pad_spec],
-        out_shape=[shape(pad_shape, F32), shape(pad_shape, BF), shape(pad_shape, BF)],
-        compiler_params=params(),
-        name="second_norm",
-    )(x5, normed, mask, cot5, got.reshape(packed_shape), row(second_gain), row(second_shift))
-    tokens2 = tokens.reshape(-1, channels)
-    cot2 = cot_pad.reshape(-1, channels)
-    pre_up = jnp.dot(tokens2, expand_weight, preferred_element_type=F32) + expand_bias
-    squash = gelu_parts(pre_up)
-    active = (0.5 * pre_up * (1.0 + squash)).astype(BF)
-    branch = jnp.dot(active, reduce_weight, preferred_element_type=F32)
-    outer = (((0,), (0,)), ((), ()))
-    across = (((1,), (1,)), ((), ()))
-    grad_reduce = lax.dot_general(active, cot2, outer, preferred_element_type=F32)
-    grad_active = lax.dot_general(cot2, reduce_weight, across, preferred_element_type=F32)
-    grad_pre = (gelu_slope(pre_up, squash) * grad_active).astype(BF)
-    grad_expand = lax.dot_general(tokens2, grad_pre, outer, preferred_element_type=F32)
-    grad_expand_bias = jnp.sum(grad_pre.astype(F32), axis=0)
-    grad_tokens = lax.dot_general(grad_pre, expand_weight, across, preferred_element_type=F32)
+        out_specs=[pad_spec, pad_spec, pad_spec], vmem=20, name="second_norm",
+    )
+    tokens2, cot2 = tokens.reshape(-1, channels), cot_pad.reshape(-1, channels)
+    count, hidden = tokens2.shape[0], expand_weight.shape[1]
+    tile = hidden // 6
+    all_tok = pl.BlockSpec((count, channels), lambda i: (0, 0))
+    by_col = lambda n: pl.BlockSpec((n, tile), lambda i: (0, i))
+    by_row = pl.BlockSpec((tile, channels), lambda i: (i, 0))
+    act, gpre, gtok, g_ebias = call(
+        chain_kernel,
+        [tokens2, cot2, expand_weight, row(expand_bias), reduce_weight],
+        [
+            shape((count, hidden), BF), shape((count, hidden), BF),
+            shape((count, channels), F32), shape((1, hidden), F32),
+        ],
+        25.0, grid=(6,),
+        in_specs=[all_tok, all_tok, by_col(channels), by_col(1), by_row],
+        out_specs=[by_col(count), by_col(count), all_tok, by_col(1)], vmem=46, name="mlp_chain",
+    )
+
+    halves = 3
+
+    def tile_of(i, c):
+        return jnp.where(i < halves, (1 - c[0]) * halves + i, c[0] * halves + i - halves)
+
+    def sent_at(i):
+        return jnp.minimum(i, halves - 1)
+
+    def kept_at(i):
+        return jnp.maximum(i - halves, 0)
+
+    all_tok_p = pl.BlockSpec((count, channels), lambda i, c: (0, 0))
+    hid_tile = pl.BlockSpec((count, tile), lambda i, c: (0, tile_of(i, c)))
+
+    def weight_grad(left, right, after, name):
+        return call(
+            weight_grad_kernel, [left, right], [shape((halves * tile, channels), BF)] * 2, 10.0,
+            after=after, prefetch=[core_line], grid=(6,), in_specs=[hid_tile, all_tok_p],
+            out_specs=[
+                pl.BlockSpec((tile, channels), lambda i, c: (sent_at(i), 0)),
+                pl.BlockSpec((tile, channels), lambda i, c: (kept_at(i), 0)),
+            ],
+            vmem=20, name=name,
+        )
+
+    sent_r, kept_r = weight_grad(act, cot2, [], "reduce_grad")
+    got_r = partner(sent_r, 1)
+    sent_e, kept_e = weight_grad(gpre, tokens2, [kept_r], "expand_grad")
+    sums = Sum([kept_r, kept_e], [got_r, partner(sent_e, 1)])
 
     one_row = shape((1, channels), F32)
-    outputs, grad_resid, send, g_gain2, g_shift2, g_rbias = pl.pallas_call(
+    grad_resid, send, g_gain2, g_shift2, g_rbias = call(
         third_kernel,
-        grid=(groups,),
-        in_specs=[pad_spec, pad_spec, pad_spec, pad_spec, mask_spec, row_spec, row_spec],
-        out_specs=[here_spec, pad_spec, packed_spec, row_spec, row_spec, row_spec],
-        out_shape=[shape(here_shape, F32), shape(pad_shape, F32), shape(packed_shape, BF)]
-        + [one_row] * 3,
-        compiler_params=params(),
-        name="second_back",
-    )(
-        resid, branch.reshape(pad_shape), grad_tokens.reshape(pad_shape), cot_pad, mask,
-        row(second_gain), row(reduce_bias),
+        [resid, gtok.reshape(pad_shape), cot_pad, mask, row(second_gain)],
+        [shape(pad_shape, F32), shape(packed_shape, BF)] + [one_row] * 3, 9.0, after=[kept_e],
+        grid=(groups,), in_specs=[pad_spec, pad_spec, pad_spec, mask_spec, row_spec],
+        out_specs=[pad_spec, packed_spec, row_spec, row_spec, row_spec], vmem=20, name="second_back",
     )
     cells = exchange(send.reshape(flat_shape))
 
-    own, other = lon_forward(cells, lon_wfwd)
+    token = sums.halve(after=[send])
+    own, other = lon_forward(cells, lon_wfwd, after=[token])
     other = swap(other)
+    token = sums.halve(after=[own])
     square = shape((2 * LANES, 2 * LANES), F32)
     line = shape((1, 2 * LANES), F32)
-    own, other, g_wa, g_ba, g_wb, g_bb = pl.pallas_call(
-        mix_back_kernel,
-        out_shape=lat_out + [square, line, square, line],
-        scratch_shapes=turn_scratch,
-        compiler_params=params(),
-        name="mix_back",
-    )(own, other, modes, lat_fwd, lat_inv, wa, ba, wb, bb)
-    other = swap(other)
-    got = exchange(lon_backward(own, other, lon_inv))
-
-    grad_inputs, g_gain1, g_shift1 = pl.pallas_call(
-        last_kernel,
-        grid=(groups,),
-        in_specs=[here_spec, pad_spec, mask_spec, packed_spec, row_spec],
-        out_specs=[here_spec, row_spec, row_spec],
-        out_shape=[shape(here_shape, F32)] + [one_row] * 2,
-        compiler_params=params(),
-        name="first_back",
-    )(x5, grad_resid, mask, got.reshape(packed_shape), row(first_gain))
-
-    def small_weight(g):
-        rr, ri = g[:block, :block], g[:block, LANES : LANES + block]
-        ir, ii = g[LANES : LANES + block, :block], g[LANES : LANES + block, LANES : LANES + block]
-        pair = jnp.stack([rr + ii, ri - ir])[:, None]
-        return lax.dynamic_update_slice(
-            jnp.zeros((2, BLOCKS, block, block), F32), pair, (0, mine, 0, 0)
-        )
-
-    def small_bias(g):
-        pair = g.reshape(2, 1, LANES)[:, :, :block]
-        full = lax.dynamic_update_slice(jnp.zeros((2, BLOCKS, block), F32), pair, (0, mine, 0))
-        return full.reshape(2, channels)
-
-    big = lax.psum((grad_expand.astype(BF), grad_reduce.astype(BF)), AXES)
-    g_expand, g_reduce = big[0].astype(F32), big[1].astype(F32)
-    (g_gain1, g_shift1, g_wa, g_ba, g_wb, g_bb, g_gain2, g_shift2, g_ebias, g_rbias) = lax.psum(
-        (
-            g_gain1, g_shift1, small_weight(g_wa), small_bias(g_ba), small_weight(g_wb),
-            small_bias(g_bb), g_gain2, g_shift2, grad_expand_bias, g_rbias,
-        ),
-        AXES,
-    )
+    run = half_rows // SPLIT
+    pieces, grads = [], []
+    for k in range(SPLIT):
+        here = pl.BlockSpec((run, lats, LANES), lambda i, k=k: (k, 0, 0))
+        steps = modes.shape[0] // SPLIT
+        const = lambda x: pl.BlockSpec(x.shape, lambda i: (0, 0))
+        o, t, *g = call(
+            mix_back_kernel, [own, other, modes, lat_fwd, lat_inv, wa, ba, wb, bb],
+            [shape((lats, run, LANES), BF)] * 2 + [square, line, square, line], 13.0,
+            after=[token],
+            in_specs=[
+                here, here, pl.BlockSpec((steps,) + modes.shape[1:], lambda i, k=k: (k, 0, 0)),
+            ] + [const(x) for x in (lat_fwd, lat_inv, wa, ba, wb, bb)],
+            scratch_shapes=[pltpu.VMEM((2 * lats * run, LANES), F32)], name="mix_back",
+        )
+        pieces.append((o, swap(t)))
+        grads.append(g)
+        if k < SPLIT - 1:
+            token = sums.halve(after=[o]) if k == 0 else sums.join(after=[o])
+    outputs = call(
+        branch_kernel,
+        [act.reshape(CORES, groups, PACK, cols_pad, hidden), reduce_weight, resid, row(reduce_bias)],
+        shape(here_shape, F32), 10.0, after=[o], grid=(groups,),
+        in_specs=[
+            lat_spec(cols_pad, hidden), pl.BlockSpec((hidden, channels), lambda i: (0, 0)),
+            pad_spec, row_spec,
+        ],
+        out_specs=[here_spec], vmem=26, name="branch",
+    )
+
+    modes_sum = Modes(
+        call(
+            lambda *refs: collect_kernel(block, *refs), sum(grads, []),
+            shape((up_to(4 * block + 4, 16), LANES), F32), 1.5, after=[outputs], name="collect",
+        )
+    )
+    token = sums.part(after=[modes_sum.x])
+    send = lon_backward(
+        [p[0] for p in pieces] + [p[1] for p in pieces], lon_inv, after=[token]
+    )
+    got = exchange(send)
+    token = modes_sum.step(after=[send])
+    token = sums.double(after=[token])
+    token = sums.double(after=[token])
+
+    grad_inputs, g_gain1, g_shift1 = call(
+        last_kernel, [x5, grad_resid, mask, got.reshape(packed_shape), row(first_gain)],
+        [shape(here_shape, F32)] + [one_row] * 2, 9.0, after=[token],
+        grid=(groups,), in_specs=[here_spec, pad_spec, mask_spec, packed_spec, row_spec],
+        out_specs=[here_spec, row_spec, row_spec], vmem=20, name="first_back",
+    )
+    tail_sum = Tail(
+        call(
+            tail_kernel, [g_gain1, g_shift1, g_gain2, g_shift2, g_rbias, g_ebias],
+            [shape((1, 5 * channels + hidden), F32)] * 2, 1.0, name="tail",
+        )
+    )
+    token = modes_sum.step(after=[tail_sum.x])
+    token = tail_sum.step(after=[token])
+    token = modes_sum.step(after=[token])
+    token = sums.double(after=[token])
+    token = tail_sum.step(after=[token])
+    token = modes_sum.step(after=[token])
+    token = tail_sum.step(after=[token])
+    token = modes_sum.step(after=[token])
+    while modes_sum.flips or modes_sum.doubles:
+        token = modes_sum.step(after=[token])
+    while tail_sum.bits:
+        token = tail_sum.step(after=[token])
+    g_reduce, g_expand = sums.widen()
+    spread = modes_sum.x.reshape(BLOCKS, -1, LANES)
+    weight_out, bias_out = shape(mix_weight_a.shape, F32), shape(mix_bias_a.shape, F32)
+    g_wa, g_wb, g_ba, g_bb = call(
+        lambda *refs: spread_kernel(block, *refs), [spread],
+        [weight_out, weight_out, bias_out, bias_out], 3.0, name="spread",
+    )
+
+    tail = tail_sum.x
+    g_gain1, g_shift1, g_gain2, g_shift2, g_rbias = (
+        tail[0, k * channels : (k + 1) * channels] for k in range(5)
+    )
+    g_ebias = tail[0, 5 * channels :]
 
     def flat(v):
         return v.reshape(-1)

time: 603 us -> 417 us (0.69)
  waiting for transfers between devices: 290 us -> 132 us
  matrix products: 70.1 us -> 0 us
  Pallas kernels: 104 us -> 153 us
  blocking collectives: 41.7 us -> 0 us
  starting transfers between devices: 19.7 us -> 59.7 us
  local copies, waits for them, and re-layouts: 43.2 us -> 63.6 us
  other arithmetic: 14.2 us -> 0.99 us
  between operations: 14.8 us -> 1.87 us
    psum x2 -> x0, waiting for transfers between devices: 228 us -> none  [the longest x1 158 us: per_device(): big = lax.psum((grad_expand.astype(BF), grad_reduce.astype(BF)), AXES)]
    ppermute x0 -> x32, waiting for transfers between devices: none -> 77.2 us  [partner(): return lax.ppermute(x, AXES, [(d, d ^ flip) for d in range(devices)])]
    dot_general x6 -> x0, matrix products: 70.1 us -> none  [the longest x1 16.4 us: per_device(): lax.dot_general(cot2, reduce_weight, across, preferred_element_type=F32)]
    pallas_call x10 -> x39, Pallas kernels: 104 us -> 153 us  [call(): pl.pallas_call(body, grid_spec=pltpu.PrefetchScalarGridSpec(num_scalar_pr...]
    psum x1 -> x0, blocking collectives: 41.7 us -> none  [per_device(): lax.psum((g_gain1, g_shift1, small_weight(g_wa), small_bias(g_ba), small_...]
    ppermute x0 -> x32, starting transfers between devices: none -> 38.1 us  [partner(): return lax.ppermute(x, AXES, [(d, d ^ flip) for d in range(devices)])]
    unnamed x82 -> x176, local copies, waits for them, and re-layouts: 30 us -> 59.6 us
    convert_element_type x2 -> x0, other arithmetic: 12 us -> none  [per_device(): g_expand, g_reduce = (big[0].astype(F32), big[1].astype(F32))]
  transfers between devices with their start and end apart: 10 -> 42, of which waited for: 7 -> 22; matrix products, arithmetic and copies ran while one was open for 10% -> 3% of each run, Pallas kernels for 7% -> 14%
where the time goes in v2:
time: 417 us; the launch traced here: 411 us
  Pallas kernels  153 us (37%)
  waiting for transfers between devices  132 us (32%)
  local copies, waits for them, and re-layouts  63.6 us (15%)
  starting transfers between devices  59.7 us (14%)
    pallas_call x39, Pallas kernels, call(): pl.pallas_call(body, grid_spec=pltpu.PrefetchScalarGridSpec(num_scalar_pr...  153 us
    ppermute x32, waiting for transfers between devices, partner(): return lax.ppermute(x, AXES, [(d, d ^ flip) for d in range(devices)])  77.2 us
    unnamed x176, local copies, waits for them, and re-layouts  59.6 us
    all_to_all x4, waiting for transfers between devices, exchange(): lax.all_to_all(x, AXES, 0, 0, axis_index_groups=snap_groups, tiled=True)  50 us
    ppermute x32, starting transfers between devices, partner(): return lax.ppermute(x, AXES, [(d, d ^ flip) for d in range(devices)])  38.1 us
    all_to_all x4, starting transfers between devices, exchange(): lax.all_to_all(x, AXES, 0, 0, axis_index_groups=snap_groups, tiled=True)  20.8 us
  transfers between devices with their start and end apart: 42, of which 22 were waited for; matrix products, arithmetic and copies ran while one was open for 3% of the time, Pallas kernels for 14%

profile of v2, /device:TPU:0, one launch (start us, length us, event | category | flops | bytes accessed | tf_op | source)
XLA Modules:
  0.0 410.9 jit_solution(277344374032038415)
XLA Ops:
  3.0 2.0 copy.41
  5.0 4.3 %first_norm.1 = (bf16[2,3,4,48,768]{4,3,2,1,0:T(8,128)(2,1)S(1)}, bf16[8,2,3,48,384]{4,3,2,1,0:T(8,128)(2,1)S(1)}) custom-call(bf16[2,3,4,45,768]{4,3,2,1,0:T(8,128)(2,1)S(1)} %bitcast.61, f32[2,3,4,48,1]{4,3,2,1,0:T(8,128)S(1)} %copy.42.refs_1_.refs_2_.refs_3_, f32[1,768]{1,0:T(1,128)S(1)} %reshape.112.refs_2_.refs_4_, f32[1,768]{1,0:T(1,128)S(1)} %reshape.113.refs_3_), custom_call_target="tpu_custom_call" | custom-call | bytes 600000 | tf_op jit(solution)/shard_map/first_norm/pallas_call | solution.py:44
  11.8 6.5 %all-to-all-start = ((bf16[16,3,48,384]{3,2,1,0:T(8,128)(2,1)}), bf16[16,3,48,384]{3,2,1,0:T(8,128)(2,1)}, u32[]{:S(2)}, u32[]{:S(2)}) async-start(bf16[16,3,48,384]{3,2,1,0:T(8,128)(2,1)} %bitcast.75), calls=%async_computation | async-start | bytes 3538944 | tf_op jit(solution)/shard_map/all_to_all | solution.py:641
  18.3 25.3 %all-to-all-done.refs_0_ = bf16[16,3,48,384]{3,2,1,0:T(8,128)(2,1)} async-done(((bf16[16,3,48,384]{3,2,1,0:T(8,128)(2,1)}), bf16[16,3,48,384]{3,2,1,0:T(8,128)(2,1)}, u32[]{:S(2)}, u32[]{:S(2)}) %all-to-all-start) | async-done | bytes 1769504 | tf_op jit(solution)/shard_map/all_to_all | solution.py:641
  43.6 5.3 %lon_forward.2 = (bf16[96,48,128]{2,1,0:T(8,128)(2,1)S(1)}, bf16[96,48,128]{2,1,0:T(8,128)(2,1)}) custom-call(bf16[16,3,48,384]{3,2,1,0:T(8,128)(2,1)} %all-to-all-done.refs_0_, bf16[192,192]{1,0:T(8,128)(2,1)S(1)} %dynamic-slice_bitcast_fusion.5.refs_1_), custom_call_target="tpu_custom_call" | custom-call | bytes 550000 | tf_op jit(solution)/shard_map/lon_forward/pallas_call | solution.py:44
  51.2 2.0 collective-permute-done.refs_1_
  54.4 20.1 %mix.1 = (bf16[48,96,128]{2,1,0:T(8,128)(2,1)S(1)}, bf16[48,96,128]{2,1,0:T(8,128)(2,1)S(1)}, bf16[24,192,256]{2,1,0:T(8,128)(2,1)S(1)}) custom-call(bf16[96,48,128]{2,1,0:T(8,128)(2,1)S(1)} %copy-done.40, bf16[96,48,128]{2,1,0:T(8,128)(2,1)} %collective-permute-done.refs_1_, bf16[192,192]{1,0:T(8,128)(2,1)S(1)} %get-tuple-element.280.refs_2_.refs_3_, ...), custom_call_target="tpu_custom_call" | custom-call | bytes 2200000 | tf_op jit(solution)/shard_map/mix/pallas_call | solution.py:44
  76.1 2.7 collective-permute-done.1.refs_1_
  80.9 5.0 %all-to-all-start.1 = ((bf16[16,3,48,384]{3,2,1,0:T(8,128)(2,1)}), bf16[16,3,48,384]{3,2,1,0:T(8,128)(2,1)}, u32[]{:S(2)}, u32[]{:S(2)}) async-start(bf16[16,3,48,384]{3,2,1,0:T(8,128)(2,1)} %copy-done.13), calls=%async_computation.1 | async-start | bytes 3538944 | tf_op jit(solution)/shard_map/all_to_all | solution.py:641
  86.0 3.0 copy.43
  88.9 22.3 %all-to-all-done.1 = bf16[16,3,48,384]{3,2,1,0:T(8,128)(2,1)} async-done(((bf16[16,3,48,384]{3,2,1,0:T(8,128)(2,1)}), bf16[16,3,48,384]{3,2,1,0:T(8,128)(2,1)}, u32[]{:S(2)}, u32[]{:S(2)}) %all-to-all-start.1) | async-done | bytes 1769504 | tf_op jit(solution)/shard_map/all_to_all | solution.py:641
  114.2 6.6 %second_norm.1 = (f32[2,3,4,48,768]{4,3,2,1,0:T(8,128)S(1)}, bf16[2,3,4,48,768]{4,3,2,1,0:T(8,128)(2,1)S(1)}, bf16[2,3,4,48,768]{4,3,2,1,0:T(8,128)(2,1)S(1)}) custom-call(bf16[2,3,4,45,768]{4,3,2,1,0:T(8,128)(2,1)S(1)} %bitcast.62, bf16[2,3,4,48,768]{4,3,2,1,0:T(8,128)(2,1)S(1)} %copy-done.38, f32[2,3,4,48,1]{4,3,2,1,0:T(8,128)S(1)} %copy.42.refs_1_.refs_2_.refs_3_, ...), custom_call_target="tpu_custom_call" | custom-call | bytes 850000 | tf_op jit(solution)/shard_map/second_norm/pallas_call | solution.py:44
  120.8 23.4 %mlp_chain.1 = (bf16[1152,3072]{1,0:T(8,128)(2,1)}, bf16[1152,3072]{1,0:T(8,128)(2,1)}, f32[1152,768]{1,0:T(8,128)S(1)}, f32[1,3072]{1,0:T(1,128)S(1)}) custom-call(bf16[1152,768]{1,0:T(8,128)(2,1)S(1)} %bitcast.70, bf16[1152,768]{1,0:T(8,128)(2,1)S(1)} %bitcast.66, bf16[768,3072]{1,0:T(8,128)(2,1)} %refs_2_.1, f32[1,3072]{1,0:T(1,128)S(1)} %bitcast.84, ...), custom_call_target="tpu_custom_call" | custom-call | bytes 2500000 | tf_op jit(solution)/shard_map/mlp_chain/pallas_call | solution.py:44
  144.2 1.9 copy-done.25
  146.1 3.0 copy-done.2
  149.1 8.4 %reduce_grad.1 = (bf16[1536,768]{1,0:T(8,128)(2,1)S(1)}, bf16[1536,768]{1,0:T(8,128)(2,1)S(1)}) custom-call(s32[1]{0:T(128)} %bitcast.24.refs_0_, bf16[1152,3072]{1,0:T(8,128)(2,1)S(1)} %copy-done.2, bf16[1152,768]{1,0:T(8,128)(2,1)S(1)} %bitcast.67), custom_call_target="tpu_custom_call" | custom-call | bytes 1000000 | tf_op jit(solution)/shard_map/reduce_grad/pallas_call | solution.py:44
  159.0 8.5 %expand_grad.1 = (bf16[1536,768]{1,0:T(8,128)(2,1)S(1)}, bf16[1536,768]{1,0:T(8,128)(2,1)S(1)}) custom-call(s32[1]{0:T(128)} %bitcast.24.refs_0_, bf16[1152,3072]{1,0:T(8,128)(2,1)S(1)} %copy-done.14, bf16[1152,768]{1,0:T(8,128)(2,1)S(1)} %bitcast.71, bf16[1536,768]{1,0:T(8,128)(2,1)S(1)} %get-tuple-element.140.refs_3_.refs_1_.refs_5_), custom_call_target="tpu_custom_call" | custom-call | bytes 1000000 | tf_op jit(solution)/shard_map/expand_grad/pallas_call | solution.py:44
  167.5 6.8 %second_back.1 = (f32[2,3,4,48,768]{4,3,2,1,0:T(8,128)S(1)}, bf16[8,2,3,48,384]{4,3,2,1,0:T(8,128)(2,1)S(1)}, f32[1,768]{1,0:T(1,128)S(1)}, f32[1,768]{1,0:T(1,128)S(1)}, f32[1,768]{1,0:T(1,128)S(1)}) custom-call(f32[2,3,4,48,768]{4,3,2,1,0:T(8,128)S(1)} %get-tuple-element.137.refs_0_.refs_2_, f32[2,3,4,48,768]{4,3,2,1,0:T(8,128)S(1)} %bitcast.72, ...), custom_call_target="tpu_custom_call" | custom-call | bytes 900000 | tf_op jit(solution)/shard_map/second_back/pallas_call | solution.py:44
  175.6 1.8 copy-done.23
  178.5 4.7 %all-to-all-start.2 = ((bf16[16,3,48,384]{3,2,1,0:T(8,128)(2,1)}), bf16[16,3,48,384]{3,2,1,0:T(8,128)(2,1)}, u32[]{:S(2)}, u32[]{:S(2)}) async-start(bf16[16,3,48,384]{3,2,1,0:T(8,128)(2,1)} %bitcast.69), calls=%async_computation.2 | async-start | bytes 3538944 | tf_op jit(solution)/shard_map/all_to_all | solution.py:641
  183.9 4.3 %collective-permute-done.3.refs_8_.refs_10_.refs_12_ = bf16[1536,768]{1,0:T(8,128)(2,1)} collective-permute-done((bf16[1536,768]{1,0:T(8,128)(2,1)}, bf16[1536,768]{1,0:T(8,128)(2,1)}, u32[]{:S(2)}, u32[]{:S(2)}) %collective-permute-start.3) | collective-permute-done | bytes 2359328 | tf_op jit(solution)/shard_map/ppermute | solution.py:686
  188.2 3.4 collective-permute-done.2.refs_2_.refs_4_.refs_6_
  191.6 1.7 copy-done.1
  194.7 4.3 %halve.3 = (bf16[512,768]{1,0:T(8,128)(2,1)S(1)}, bf16[512,768]{1,0:T(8,128)(2,1)}, bf16[512,768]{1,0:T(8,128)(2,1)S(1)}, bf16[512,768]{1,0:T(8,128)(2,1)}, bf16...) custom-call(s32[3]{0:T(128)S(1)} %pad_add_fusion.refs_0_, bf16[1536,768]{1,0:T(8,128)(2,1)S(1)} %copy-done.1, ...), custom_call_target="tpu_custom_call" | custom-call | bytes 300000 | tf_op jit(solution)/shard_map/halve/pallas_call | solution.py:44
  201.7 1.9 collective-permute-start.5
  203.6 1.5 collective-permute-start.6
  205.1 1.5 collective-permute-start.7
  206.6 2.4 all-to-all-done.2.refs_0_
  210.2 4.3 %lon_forward.3 = (bf16[96,48,128]{2,1,0:T(8,128)(2,1)S(1)}, bf16[96,48,128]{2,1,0:T(8,128)(2,1)S(1)}) custom-call(bf16[16,3,48,384]{3,2,1,0:T(8,128)(2,1)} %all-to-all-done.2.refs_0_, bf16[192,192]{1,0:T(8,128)(2,1)S(1)} %dynamic-slice_bitcast_fusion.1.refs_1_, bf16[512,768]{1,0:T(8,128)(2,1)S(1)} %copy-done.21), custom_call_target="tpu_custom_call" | custom-call | bytes 550000 | tf_op jit(solution)/shard_map/lon_forward/pallas_call | solution.py:44
  214.7 10.5 %collective-permute-done.5.refs_2_.refs_4_ = bf16[512,768]{1,0:T(8,128)(2,1)S(1)} collective-permute-done((bf16[512,768]{1,0:T(8,128)(2,1)}, bf16[512,768]{1,0:T(8,128)(2,1)S(1)}, u32[]{:S(2)}, u32[]{:S(2)}) %collective-permute-start.5) | collective-permute-done | bytes 786464 | tf_op jit(solution)/shard_map/ppermute | solution.py:686
  226.3 1.5 collective-permute-start.8
  228.1 2.0 collective-permute-start.10
  230.2 7.5 %mix_back.3 = (bf16[48,32,128]{2,1,0:T(8,128)(2,1)S(1)}, bf16[48,32,128]{2,1,0:T(8,128)(2,1)S(1)}, f32[256,256]{1,0:T(8,128)S(1)}, f32[1,256]{1,0:T(1,128)S(1)},...) custom-call(bf16[96,48,128]{2,1,0:T(8,128)(2,1)S(1)} %get-tuple-element.146.refs_13_.refs_0_, ...), custom_call_target="tpu_custom_call" | custom-call | bytes 1300000 | tf_op jit(solution)/shard_map/mix_back/pallas_call | solution.py:44
  239.4 1.8 collective-permute-start.11
  241.2 1.6 collective-permute-start.12
  243.2 7.5 %mix_back.4 = (bf16[48,32,128]{2,1,0:T(8,128)(2,1)S(1)}, bf16[48,32,128]{2,1,0:T(8,128)(2,1)S(1)}, f32[256,256]{1,0:T(8,128)S(1)}, f32[1,256]{1,0:T(1,128)S(1)},...) custom-call(bf16[96,48,128]{2,1,0:T(8,128)(2,1)S(1)} %get-tuple-element.146.refs_13_.refs_0_, ...), custom_call_target="tpu_custom_call" | custom-call | bytes 1300000 | tf_op jit(solution)/shard_map/mix_back/pallas_call | solution.py:44
  250.9 2.7 collective-permute-start.17
  254.0 7.5 %mix_back.5 = (bf16[48,32,128]{2,1,0:T(8,128)(2,1)S(1)}, bf16[48,32,128]{2,1,0:T(8,128)(2,1)S(1)}, f32[256,256]{1,0:T(8,128)S(1)}, f32[1,256]{1,0:T(1,128)S(1)},...) custom-call(bf16[96,48,128]{2,1,0:T(8,128)(2,1)S(1)} %get-tuple-element.146.refs_13_.refs_0_, ...), custom_call_target="tpu_custom_call" | custom-call | bytes 1300000 | tf_op jit(solution)/shard_map/mix_back/pallas_call | solution.py:44
  261.8 7.0 %branch.1.refs_12_ = f32[2,3,4,45,768]{4,3,2,1,0:T(8,128)S(1)} custom-call(bf16[2,3,4,48,3072]{4,3,2,1,0:T(8,128)(2,1)S(1)} %bitcast.60, bf16[3072,768]{1,0:T(8,128)(2,1)S(1)} %bitcast.65, f32[2,3,4,48,768]{4,3,2,1,0:T(8,128)S(1)} %copy-done.12, f32[1,768]{1,0:T(1,128)S(1)} %reshape.127.refs_3_, bf16[48,32,128]{2,1,0:T(8,128)(2,1)S(1)} %get-tuple-element.169.refs_4_.refs_2_), custom_call_target="tpu_custom_call" | custom-call | bytes 1000000 | tf_op jit(solution)/shard_map/branch/pallas_call | solution.py:44
  268.8 8.5 %collective-permute-done.17.refs_1_ = bf16[384,768]{1,0:T(8,128)(2,1)S(1)} collective-permute-done((bf16[384,768]{1,0:T(8,128)(2,1)S(1)}, bf16[384,768]{1,0:T(8,128)(2,1)S(1)}, u32[]{:S(2)}, u32[]{:S(2)}) %collective-permute-start.17) | collective-permute-done | bytes 589856 | tf_op jit(solution)/shard_map/ppermute | solution.py:686
  283.6 4.6 %all-to-all-start.3 = ((bf16[16,3,48,384]{3,2,1,0:T(8,128)(2,1)}), bf16[16,3,48,384]{3,2,1,0:T(8,128)(2,1)}, u32[]{:S(2)}, u32[]{:S(2)}) async-start(bf16[16,3,48,384]{3,2,1,0:T(8,128)(2,1)} %copy-done.7), calls=%async_computation.3 | async-start | bytes 3538944 | tf_op jit(solution)/shard_map/all_to_all | solution.py:641
  288.8 1.7 collective-permute-start.18
  292.0 1.5 collective-permute-start.20
  296.5 18.8 %collective-permute-done.18.refs_2_ = bf16[128,768]{1,0:T(8,128)(2,1)S(1)} collective-permute-done((bf16[128,768]{1,0:T(8,128)(2,1)}, bf16[128,768]{1,0:T(8,128)(2,1)S(1)}, u32[]{:S(2)}, u32[]{:S(2)}) %collective-permute-start.18) | collective-permute-done | bytes 196640 | tf_op jit(solution)/shard_map/ppermute | solution.py:686
  315.4 2.2 collective-permute-done.19.refs_4_
  323.5 2.0 collective-permute-start.24
  325.5 6.9 %collective-permute-done.22.refs_2_ = bf16[256,768]{1,0:T(8,128)(2,1)S(1)} collective-permute-done((bf16[256,768]{1,0:T(8,128)(2,1)S(1)}, bf16[256,768]{1,0:T(8,128)(2,1)S(1)}, u32[]{:S(2)}, u32[]{:S(2)}) %collective-permute-start.22) | collective-permute-done | bytes 393248 | tf_op jit(solution)/shard_map/ppermute | solution.py:686
  333.9 2.2 merge.7
  338.7 1.7 collective-permute-start.28
  346.2 2.0 copy-done.24
  349.4 8.1 %first_back.1 = (f32[2,3,4,45,768]{4,3,2,1,0:T(8,128)S(1)}, f32[1,768]{1,0:T(1,128)S(1)}, f32[1,768]{1,0:T(1,128)S(1)}) custom-call(bf16[2,3,4,45,768]{4,3,2,1,0:T(8,128)(2,1)S(1)} %bitcast.63, f32[2,3,4,48,768]{4,3,2,1,0:T(8,128)S(1)} %copy-done.24, f32[2,3,4,48,1]{4,3,2,1,0:T(8,128)S(1)} %copy-done.10, bf16[8,2,3,48,384]{4,3,2,1,0:T(8,128)(2,1)} %bitcast.32.refs_3_, ...), custom_call_target="tpu_custom_call" | custom-call | bytes 900000 | tf_op jit(solution)/shard_map/first_back/pallas_call | solution.py:44
  357.5 1.8 collective-permute-done.26.refs_1_
  362.1 2.9 collective-permute-done.31.refs_2_
  365.1 2.8 merge.9
  369.1 3.6 collective-permute-done.27.refs_1_
  372.7 2.7 collective-permute-done.33.refs_2_
  375.6 2.9 collective-permute-start.35
  379.9 2.5 collective-permute-done.32.refs_1_
  382.5 5.6 %collective-permute-done.35.refs_2_ = bf16[1600,128]{1,0:T(8,128)(2,1)S(1)} collective-permute-done((bf16[1600,128]{1,0:T(8,128)(2,1)S(1)}, bf16[1600,128]{1,0:T(8,128)(2,1)S(1)}, u32[]{:S(2)}, u32[]{:S(2)}) %collective-permute-start.35) | collective-permute-done | bytes 409632 | tf_op jit(solution)/shard_map/ppermute | solution.py:686
  389.2 2.3 collective-permute-start.36
  391.5 3.6 copy.47
  395.2 3.6 copy.48
  398.8 4.4 %widen.2 = (f32[3072,768]{1,0:T(8,128)}, f32[768,3072]{1,0:T(8,128)}) custom-call(s32[1]{0:T(128)} %bitcast.24.refs_0_, bf16[3072,768]{1,0:T(8,128)(2,1)S(1)} %bitcast.55, bf16[3072,768]{1,0:T(8,128)(2,1)S(1)} %bitcast.56), custom_call_target="tpu_custom_call" | custom-call | bytes 500000 | tf_op jit(solution)/shard_map/widen/pallas_call | solution.py:44
  406.3 4.4 %widen.3 = (f32[3072,768]{1,0:T(8,128)}, f32[768,3072]{1,0:T(8,128)}) custom-call(s32[1]{0:T(128)} %bitcast.24.refs_0_, bf16[3072,768]{1,0:T(8,128)(2,1)S(1)} %collective-permute-done.37.refs_1_.refs_2_, bf16[3072,768]{1,0:T(8,128)(2,1)S(1)} %collective-permute-done.37.refs_1_.refs_2_, ...), custom_call_target="tpu_custom_call", output_to_operand_aliasing={{0}: (3, {}), {1}: (4, {})} | custom-call | bytes 500000 | tf_op jit(solution)/shard_map/widen/pallas_call | solution.py:44
  (267 shorter events, 67.1 us)
Async XLA Ops:
  3.0 164.4 %copy-start.9 = (f32[2,3,4,48,1]{4,3,2,1,0:T(8,128)}, f32[2,3,4,48,1]{4,3,2,1,0:T(8,128)S(1)}, u32[]{:S(2)}) copy-start(f32[2,3,4,48,1]{4,3,2,1,0:T(8,128)S(1)} %copy.42.refs_1_.refs_2_.refs_3_) | copy-start | bytes 13828
  5.0 106.2 %copy-start.3 = (bf16[24,45,768]{2,1,0:T(8,128)(2,1)}, bf16[24,45,768]{2,1,0:T(8,128)(2,1)S(1)}, u32[]{:S(2)}) copy-start(bf16[24,45,768]{2,1,0:T(8,128)(2,1)S(1)} %copy.41) | copy-start | bytes 4976644
  11.8 38.2 %copy-start.77 = (f32[2,768]{1,0:T(2,128)S(1)}, f32[2,768]{1,0:T(2,128)}, u32[]{:S(2)}) copy-start(f32[2,768]{1,0:T(2,128)} %param.27) | copy-start | bytes 18436
  11.8 38.2 %copy-start.78 = (f32[2,768]{1,0:T(2,128)S(1)}, f32[2,768]{1,0:T(2,128)}, u32[]{:S(2)}) copy-start(f32[2,768]{1,0:T(2,128)} %param.29) | copy-start | bytes 18436
  11.8 31.8 %all-to-all-start = ((bf16[16,3,48,384]{3,2,1,0:T(8,128)(2,1)}), bf16[16,3,48,384]{3,2,1,0:T(8,128)(2,1)}, u32[]{:S(2)}, u32[]{:S(2)}) async-start(bf16[16,3,48,384]{3,2,1,0:T(8,128)(2,1)} %bitcast.75), calls=%async_computation | async-start | bytes 3538944 | tf_op jit(solution)/shard_map/all_to_all | solution.py:641
  18.3 32.8 %copy-start.75 = (bf16[2,192,192]{2,1,0:T(8,128)(2,1)S(1)}, bf16[2,192,192]{2,1,0:T(8,128)(2,1)}, u32[]{:S(2)}) copy-start(bf16[2,192,192]{2,1,0:T(8,128)(2,1)} %constant.201.clone) | copy-start | bytes 442372
  18.3 32.8 %copy-start.76 = (bf16[2,192,192]{2,1,0:T(8,128)(2,1)S(1)}, bf16[2,192,192]{2,1,0:T(8,128)(2,1)}, u32[]{:S(2)}) copy-start(bf16[2,192,192]{2,1,0:T(8,128)(2,1)} %constant.200.clone) | copy-start | bytes 442372
  49.9 26.2 %copy-start.73 = (bf16[2,192,192]{2,1,0:T(8,128)(2,1)S(1)}, bf16[2,192,192]{2,1,0:T(8,128)(2,1)}, u32[]{:S(2)}) copy-start(bf16[2,192,192]{2,1,0:T(8,128)(2,1)} %constant.199.clone) | copy-start | bytes 442372
  49.9 3.2 collective-permute-start
  76.0 2.8 collective-permute-start.1
  80.9 30.3 %all-to-all-start.1 = ((bf16[16,3,48,384]{3,2,1,0:T(8,128)(2,1)}), bf16[16,3,48,384]{3,2,1,0:T(8,128)(2,1)}, u32[]{:S(2)}, u32[]{:S(2)}) async-start(bf16[16,3,48,384]{3,2,1,0:T(8,128)(2,1)} %copy-done.13), calls=%async_computation.1 | async-start | bytes 3538944 | tf_op jit(solution)/shard_map/all_to_all | solution.py:641
  120.8 23.4 %copy-start.18 = (bf16[2,3,4,48,768]{4,3,2,1,0:T(8,128)(2,1)}, bf16[2,3,4,48,768]{4,3,2,1,0:T(8,128)(2,1)S(1)}, u32[]{:S(2)}) copy-start(bf16[2,3,4,48,768]{4,3,2,1,0:T(8,128)(2,1)S(1)} %get-tuple-element.134) | copy-start | bytes 5308420
  120.8 46.6 %copy-start.11 = (f32[2,3,4,48,768]{4,3,2,1,0:T(8,128)}, f32[2,3,4,48,768]{4,3,2,1,0:T(8,128)S(1)}, u32[]{:S(2)}) copy-start(f32[2,3,4,48,768]{4,3,2,1,0:T(8,128)S(1)} %get-tuple-element.137.refs_0_.refs_2_) | copy-start | bytes 10616836
  178.5 30.5 %all-to-all-start.2 = ((bf16[16,3,48,384]{3,2,1,0:T(8,128)(2,1)}), bf16[16,3,48,384]{3,2,1,0:T(8,128)(2,1)}, u32[]{:S(2)}, u32[]{:S(2)}) async-start(bf16[16,3,48,384]{3,2,1,0:T(8,128)(2,1)} %bitcast.69), calls=%async_computation.2 | async-start | bytes 3538944 | tf_op jit(solution)/shard_map/all_to_all | solution.py:641
  183.2 5.0 %collective-permute-start.3 = (bf16[1536,768]{1,0:T(8,128)(2,1)}, bf16[1536,768]{1,0:T(8,128)(2,1)}, u32[]{:S(2)}, u32[]{:S(2)}) collective-permute-start(bf16[1536,768]{1,0:T(8,128)(2,1)} %copy-done.67), channel_id=1, source_target_pairs={{0,1},{1,0},{2,3},{3,2},{4,5},{5,4},{6,7},{7,6},{8,9},{9,8},{10,11... | collective-permute-start | bytes 7077896 | tf_op jit(solution)/shard_map/ppermute | solution.py:686
  183.7 7.9 %collective-permute-start.2 = (bf16[1536,768]{1,0:T(8,128)(2,1)}, bf16[1536,768]{1,0:T(8,128)(2,1)}, u32[]{:S(2)}, u32[]{:S(2)}) collective-permute-start(bf16[1536,768]{1,0:T(8,128)(2,1)} %copy-done.66), channel_id=1, source_target_pairs={{0,1},{1,0},{2,3},{3,2},{4,5},{5,4},{6,7},{7,6},{8,9},{9,8},{10,11... | collective-permute-start | bytes 7077896 | tf_op jit(solution)/shard_map/ppermute | solution.py:686
  183.9 15.2 %copy-start.58 = (s32[3]{0:T(128)}, s32[3]{0:T(128)S(1)}, u32[]{:S(2)}) copy-start(s32[3]{0:T(128)S(1)} %pad_add_fusion.refs_0_) | copy-start | bytes 40
  201.7 23.5 %collective-permute-start.5 = (bf16[512,768]{1,0:T(8,128)(2,1)}, bf16[512,768]{1,0:T(8,128)(2,1)S(1)}, u32[]{:S(2)}, u32[]{:S(2)}) collective-permute-start(bf16[512,768]{1,0:T(8,128)(2,1)} %get-tuple-element.149), channel_id=1, source_target_pairs={{0,2},{1,3},{2,0},{3,1},{4,6},{5,7},{6,4},{7,5},{8,10},{9,11},{10,... | collective-permute-start | bytes 2359304 | tf_op jit(solution)/shard_map/ppermute | solution.py:686
  203.6 21.6 %collective-permute-start.6 = (bf16[512,768]{1,0:T(8,128)(2,1)}, bf16[512,768]{1,0:T(8,128)(2,1)S(1)}, u32[]{:S(2)}, u32[]{:S(2)}) collective-permute-start(bf16[512,768]{1,0:T(8,128)(2,1)} %get-tuple-element.151), channel_id=1, source_target_pairs={{0,4},{1,5},{2,6},{3,7},{4,0},{5,1},{6,2},{7,3},{8,12},{9,13},{10,... | collective-permute-start | bytes 2359304 | tf_op jit(solution)/shard_map/ppermute | solution.py:686
  205.1 20.1 %collective-permute-start.7 = (bf16[512,768]{1,0:T(8,128)(2,1)}, bf16[512,768]{1,0:T(8,128)(2,1)S(1)}, u32[]{:S(2)}, u32[]{:S(2)}) collective-permute-start(bf16[512,768]{1,0:T(8,128)(2,1)} %get-tuple-element.153), channel_id=1, source_target_pairs={{0,8},{1,9},{2,10},{3,11},{4,12},{5,13},{6,14},{7,15},{8,0},{9,1},... | collective-permute-start | bytes 2359304 | tf_op jit(solution)/shard_map/ppermute | solution.py:686
  210.2 15.0 %copy-start.22 = (bf16[512,768]{1,0:T(8,128)(2,1)S(1)}, bf16[512,768]{1,0:T(8,128)(2,1)}, u32[]{:S(2)}) copy-start(bf16[512,768]{1,0:T(8,128)(2,1)} %copy-done.20) | copy-start | bytes 2359300
  210.2 15.0 %copy-start.31 = (bf16[512,768]{1,0:T(8,128)(2,1)S(1)}, bf16[512,768]{1,0:T(8,128)(2,1)}, u32[]{:S(2)}) copy-start(bf16[512,768]{1,0:T(8,128)(2,1)} %copy-done.30) | copy-start | bytes 2359300
  210.2 15.0 %copy-start.33 = (bf16[512,768]{1,0:T(8,128)(2,1)S(1)}, bf16[512,768]{1,0:T(8,128)(2,1)}, u32[]{:S(2)}) copy-start(bf16[512,768]{1,0:T(8,128)(2,1)} %copy-done.32) | copy-start | bytes 2359300
  214.5 15.7 %collective-permute-start.4 = (bf16[96,48,128]{2,1,0:T(8,128)(2,1)S(1)}, bf16[96,48,128]{2,1,0:T(8,128)(2,1)S(1)}, u32[]{:S(2)}, u32[]{:S(2)}) collective-permute-start(bf16[96,48,128]{2,1,0:T(8,128)(2,1)S(1)} %get-tuple-element.147), channel_id=1, source_target_pairs={{0,1},{1,0},{2,3},{3,2},{4,5},{5,4},{6,7},{7,6},{8,9},{9,8},{10,11... | collective-permute-start | bytes 3538952 | tf_op jit(solution)/shard_map/ppermute | solution.py:644
  225.2 36.5 %slice-start.2 = ((s8[4718592]{0:T(1024)(128)(4,1)}), s8[4194304]{0:T(1024)(128)(4,1)S(1)}, s32[]{:S(2)}) async-start(s8[4718592]{0:T(1024)(128)(4,1)} %bitcast.64), calls=%async_computation.6 | async-start | bytes 8388608
  226.3 11.4 %collective-permute-start.8 = (bf16[256,768]{1,0:T(8,128)(2,1)S(1)}, bf16[256,768]{1,0:T(8,128)(2,1)S(1)}, u32[]{:S(2)}, u32[]{:S(2)}) collective-permute-start(bf16[256,768]{1,0:T(8,128)(2,1)S(1)} %get-tuple-element.155), channel_id=1, source_target_pairs={{0,4},{1,5},{2,6},{3,7},{4,0},{5,1},{6,2},{7,3},{8,12},{9,13},{10,... | collective-permute-start | bytes 1179656 | tf_op jit(solution)/shard_map/ppermute | solution.py:686
  227.8 10.8 %collective-permute-start.9 = (bf16[256,768]{1,0:T(8,128)(2,1)S(1)}, bf16[256,768]{1,0:T(8,128)(2,1)S(1)}, u32[]{:S(2)}, u32[]{:S(2)}) collective-permute-start(bf16[256,768]{1,0:T(8,128)(2,1)S(1)} %get-tuple-element.157), channel_id=1, source_target_pairs={{0,8},{1,9},{2,10},{3,11},{4,12},{5,13},{6,14},{7,15},{8,0},{9,1},... | collective-permute-start | bytes 1179656 | tf_op jit(solution)/shard_map/ppermute | solution.py:686
  228.1 10.5 %collective-permute-start.10 = (bf16[256,768]{1,0:T(8,128)(2,1)S(1)}, bf16[256,768]{1,0:T(8,128)(2,1)S(1)}, u32[]{:S(2)}, u32[]{:S(2)}) collective-permute-start(bf16[256,768]{1,0:T(8,128)(2,1)S(1)} %get-tuple-element.159), channel_id=1, source_target_pairs={{0,2},{1,3},{2,0},{3,1},{4,6},{5,7},{6,4},{7,5},{8,10},{9,11},{10,... | collective-permute-start | bytes 1179656 | tf_op jit(solution)/shard_map/ppermute | solution.py:686
  238.6 23.1 %slice-start.3 = ((s8[4718592]{0:T(1024)(128)(4,1)}), s8[524288]{0:T(1024)(128)(4,1)S(1)}, s32[]{:S(2)}) async-start(s8[4718592]{0:T(1024)(128)(4,1)} %bitcast.64), calls=%async_computation.7 | async-start | bytes 1048576
  239.4 11.2 %collective-permute-start.11 = (bf16[128,768]{1,0:T(8,128)(2,1)S(1)}, bf16[128,768]{1,0:T(8,128)(2,1)S(1)}, u32[]{:S(2)}, u32[]{:S(2)}) collective-permute-start(bf16[128,768]{1,0:T(8,128)(2,1)S(1)} %get-tuple-element.162), channel_id=1, source_target_pairs={{0,8},{1,9},{2,10},{3,11},{4,12},{5,13},{6,14},{7,15},{8,0},{9,1},... | collective-permute-start | bytes 589832 | tf_op jit(solution)/shard_map/ppermute | solution.py:686
  241.2 9.5 %collective-permute-start.12 = (bf16[128,768]{1,0:T(8,128)(2,1)S(1)}, bf16[128,768]{1,0:T(8,128)(2,1)S(1)}, u32[]{:S(2)}, u32[]{:S(2)}) collective-permute-start(bf16[128,768]{1,0:T(8,128)(2,1)S(1)} %get-tuple-element.164), channel_id=1, source_target_pairs={{0,2},{1,3},{2,0},{3,1},{4,6},{5,7},{6,4},{7,5},{8,10},{9,11},{10,... | collective-permute-start | bytes 589832 | tf_op jit(solution)/shard_map/ppermute | solution.py:686
  242.8 7.9 %collective-permute-start.13 = (bf16[128,768]{1,0:T(8,128)(2,1)S(1)}, bf16[128,768]{1,0:T(8,128)(2,1)S(1)}, u32[]{:S(2)}, u32[]{:S(2)}) collective-permute-start(bf16[128,768]{1,0:T(8,128)(2,1)S(1)} %get-tuple-element.166), channel_id=1, source_target_pairs={{0,4},{1,5},{2,6},{3,7},{4,0},{5,1},{6,2},{7,3},{8,12},{9,13},{10,... | collective-permute-start | bytes 589832 | tf_op jit(solution)/shard_map/ppermute | solution.py:686
  243.2 18.6 %slice-start = ((s8[7077888]{0:T(1024)(128)(4,1)}), s8[4194304]{0:T(1024)(128)(4,1)S(1)}, s32[]{:S(2)}) async-start(s8[7077888]{0:T(1024)(128)(4,1)} %bitcast.58), calls=%async_computation.4 | async-start | bytes 8388608
  250.9 26.5 %collective-permute-start.17 = (bf16[384,768]{1,0:T(8,128)(2,1)S(1)}, bf16[384,768]{1,0:T(8,128)(2,1)S(1)}, u32[]{:S(2)}, u32[]{:S(2)}) collective-permute-start(bf16[384,768]{1,0:T(8,128)(2,1)S(1)} %get-tuple-element.174), channel_id=1, source_target_pairs={{0,16},{1,17},{2,18},{3,19},{4,20},{5,21},{6,22},{7,23},{8,24},{9,... | collective-permute-start | bytes 1769480 | tf_op jit(solution)/shard_map/ppermute | solution.py:686
  253.5 27.4 %collective-permute-start.14 = (bf16[48,32,128]{2,1,0:T(8,128)(2,1)S(1)}, bf16[48,32,128]{2,1,0:T(8,128)(2,1)S(1)}, u32[]{:S(2)}, u32[]{:S(2)}) collective-permute-start(bf16[48,32,128]{2,1,0:T(8,128)(2,1)S(1)} %get-tuple-element.171), channel_id=1, source_target_pairs={{0,1},{1,0},{2,3},{3,2},{4,5},{5,4},{6,7},{7,6},{8,9},{9,8},{10,11... | collective-permute-start | bytes 1179656 | tf_op jit(solution)/shard_map/ppermute | solution.py:644
  253.5 27.4 %collective-permute-start.15 = (bf16[48,32,128]{2,1,0:T(8,128)(2,1)S(1)}, bf16[48,32,128]{2,1,0:T(8,128)(2,1)S(1)}, u32[]{:S(2)}, u32[]{:S(2)}) collective-permute-start(bf16[48,32,128]{2,1,0:T(8,128)(2,1)S(1)} %get-tuple-element.172), channel_id=1, source_target_pairs={{0,1},{1,0},{2,3},{3,2},{4,5},{5,4},{6,7},{7,6},{8,9},{9,8},{10,11... | collective-permute-start | bytes 1179656 | tf_op jit(solution)/shard_map/ppermute | solution.py:644
  261.6 19.3 %collective-permute-start.16 = (bf16[48,32,128]{2,1,0:T(8,128)(2,1)S(1)}, bf16[48,32,128]{2,1,0:T(8,128)(2,1)S(1)}, u32[]{:S(2)}, u32[]{:S(2)}) collective-permute-start(bf16[48,32,128]{2,1,0:T(8,128)(2,1)S(1)} %get-tuple-element.173), channel_id=1, source_target_pairs={{0,1},{1,0},{2,3},{3,2},{4,5},{5,4},{6,7},{7,6},{8,9},{9,8},{10,11... | collective-permute-start | bytes 1179656 | tf_op jit(solution)/shard_map/ppermute | solution.py:644
  283.6 60.0 %all-to-all-start.3 = ((bf16[16,3,48,384]{3,2,1,0:T(8,128)(2,1)}), bf16[16,3,48,384]{3,2,1,0:T(8,128)(2,1)}, u32[]{:S(2)}, u32[]{:S(2)}) async-start(bf16[16,3,48,384]{3,2,1,0:T(8,128)(2,1)} %copy-done.7), calls=%async_computation.3 | async-start | bytes 3538944 | tf_op jit(solution)/shard_map/all_to_all | solution.py:641
  288.3 45.6 %copy-start.55 = (s32[3]{0:T(128)S(1)}, s32[3]{0:T(128)}, u32[]{:S(2)}) copy-start(s32[3]{0:T(128)} %copy-done.54) | copy-start | bytes 40
  288.3 5.1 %collective-permute-start.21 = (f32[400,128]{1,0:T(8,128)}, f32[400,128]{1,0:T(8,128)S(1)}, u32[]{:S(2)}, u32[]{:S(2)}) collective-permute-start(f32[400,128]{1,0:T(8,128)} %copy-done.34), channel_id=1, source_target_pairs={{0,1},{1,0},{2,3},{3,2},{4,5},{5,4},{6,7},{7,6},{8,9},{9,8},{10,11... | collective-permute-start | bytes 614408 | tf_op jit(solution)/shard_map/ppermute | solution.py:686
  288.8 26.6 %collective-permute-start.18 = (bf16[128,768]{1,0:T(8,128)(2,1)}, bf16[128,768]{1,0:T(8,128)(2,1)S(1)}, u32[]{:S(2)}, u32[]{:S(2)}) collective-permute-start(bf16[128,768]{1,0:T(8,128)(2,1)} %copy-done.70), channel_id=1, source_target_pairs={{0,8},{1,9},{2,10},{3,11},{4,12},{5,13},{6,14},{7,15},{8,0},{9,1},... | collective-permute-start | bytes 589832 | tf_op jit(solution)/shard_map/ppermute | solution.py:686
  290.5 27.1 %collective-permute-start.19 = (bf16[128,768]{1,0:T(8,128)(2,1)}, bf16[128,768]{1,0:T(8,128)(2,1)S(1)}, u32[]{:S(2)}, u32[]{:S(2)}) collective-permute-start(bf16[128,768]{1,0:T(8,128)(2,1)} %copy-done.69), channel_id=1, source_target_pairs={{0,2},{1,3},{2,0},{3,1},{4,6},{5,7},{6,4},{7,5},{8,10},{9,11},{10,... | collective-permute-start | bytes 589832 | tf_op jit(solution)/shard_map/ppermute | solution.py:686
  292.0 25.6 %collective-permute-start.20 = (bf16[128,768]{1,0:T(8,128)(2,1)}, bf16[128,768]{1,0:T(8,128)(2,1)S(1)}, u32[]{:S(2)}, u32[]{:S(2)}) collective-permute-start(bf16[128,768]{1,0:T(8,128)(2,1)} %copy-done.68), channel_id=1, source_target_pairs={{0,4},{1,5},{2,6},{3,7},{4,0},{5,1},{6,2},{7,3},{8,12},{9,13},{10,... | collective-permute-start | bytes 589832 | tf_op jit(solution)/shard_map/ppermute | solution.py:686
  296.5 37.4 %copy-start.47 = (bf16[400,128]{1,0:T(8,128)(2,1)}, bf16[400,128]{1,0:T(8,128)(2,1)S(1)}, u32[]{:S(2)}) copy-start(bf16[400,128]{1,0:T(8,128)(2,1)S(1)} %get-tuple-element.193.refs_7_.refs_0_) | copy-start | bytes 307204
  321.7 10.7 %collective-permute-start.22 = (bf16[256,768]{1,0:T(8,128)(2,1)S(1)}, bf16[256,768]{1,0:T(8,128)(2,1)S(1)}, u32[]{:S(2)}, u32[]{:S(2)}) collective-permute-start(bf16[256,768]{1,0:T(8,128)(2,1)S(1)} %get-tuple-element.195), channel_id=1, source_target_pairs={{0,4},{1,5},{2,6},{3,7},{4,0},{5,1},{6,2},{7,3},{8,12},{9,13},{10,... | collective-permute-start | bytes 1179656 | tf_op jit(solution)/shard_map/ppermute | solution.py:686
  322.3 10.4 %collective-permute-start.23 = (bf16[256,768]{1,0:T(8,128)(2,1)S(1)}, bf16[256,768]{1,0:T(8,128)(2,1)S(1)}, u32[]{:S(2)}, u32[]{:S(2)}) collective-permute-start(bf16[256,768]{1,0:T(8,128)(2,1)S(1)} %get-tuple-element.197), channel_id=1, source_target_pairs={{0,8},{1,9},{2,10},{3,11},{4,12},{5,13},{6,14},{7,15},{8,0},{9,1},... | collective-permute-start | bytes 1179656 | tf_op jit(solution)/shard_map/ppermute | solution.py:686
  323.5 10.4 %collective-permute-start.24 = (bf16[256,768]{1,0:T(8,128)(2,1)S(1)}, bf16[256,768]{1,0:T(8,128)(2,1)S(1)}, u32[]{:S(2)}, u32[]{:S(2)}) collective-permute-start(bf16[256,768]{1,0:T(8,128)(2,1)S(1)} %get-tuple-element.199), channel_id=1, source_target_pairs={{0,2},{1,3},{2,0},{3,1},{4,6},{5,7},{6,4},{7,5},{8,10},{9,11},{10,... | collective-permute-start | bytes 1179656 | tf_op jit(solution)/shard_map/ppermute | solution.py:686
  338.7 26.3 %collective-permute-start.28 = (bf16[512,768]{1,0:T(8,128)(2,1)}, bf16[512,768]{1,0:T(8,128)(2,1)}, u32[]{:S(2)}, u32[]{:S(2)}) collective-permute-start(bf16[512,768]{1,0:T(8,128)(2,1)} %get-tuple-element.214), channel_id=1, source_target_pairs={{0,2},{1,3},{2,0},{3,1},{4,6},{5,7},{6,4},{7,5},{8,10},{9,11},{10,... | collective-permute-start | bytes 2359304 | tf_op jit(solution)/shard_map/ppermute | solution.py:686
  340.5 24.6 %collective-permute-start.29 = (bf16[512,768]{1,0:T(8,128)(2,1)}, bf16[512,768]{1,0:T(8,128)(2,1)}, u32[]{:S(2)}, u32[]{:S(2)}) collective-permute-start(bf16[512,768]{1,0:T(8,128)(2,1)} %get-tuple-element.216), channel_id=1, source_target_pairs={{0,4},{1,5},{2,6},{3,7},{4,0},{5,1},{6,2},{7,3},{8,12},{9,13},{10,... | collective-permute-start | bytes 2359304 | tf_op jit(solution)/shard_map/ppermute | solution.py:686
  340.8 24.2 %collective-permute-start.30 = (bf16[512,768]{1,0:T(8,128)(2,1)}, bf16[512,768]{1,0:T(8,128)(2,1)}, u32[]{:S(2)}, u32[]{:S(2)}) collective-permute-start(bf16[512,768]{1,0:T(8,128)(2,1)} %get-tuple-element.218), channel_id=1, source_target_pairs={{0,8},{1,9},{2,10},{3,11},{4,12},{5,13},{6,14},{7,15},{8,0},{9,1},... | collective-permute-start | bytes 2359304 | tf_op jit(solution)/shard_map/ppermute | solution.py:686
  342.3 17.1 %collective-permute-start.26 = (bf16[400,128]{1,0:T(8,128)(2,1)}, bf16[400,128]{1,0:T(8,128)(2,1)}, u32[]{:S(2)}, u32[]{:S(2)}) collective-permute-start(bf16[400,128]{1,0:T(8,128)(2,1)} %get-tuple-element.210), channel_id=1, source_target_pairs={{0,16},{1,17},{2,18},{3,19},{4,20},{5,21},{6,22},{7,23},{8,24},{9,... | collective-permute-start | bytes 307208 | tf_op jit(solution)/shard_map/ppermute | solution.py:686
  349.3 15.8 %copy-start.29 = (bf16[512,768]{1,0:T(8,128)(2,1)S(1)}, bf16[512,768]{1,0:T(8,128)(2,1)}, u32[]{:S(2)}) copy-start(bf16[512,768]{1,0:T(8,128)(2,1)} %copy-done.27) | copy-start | bytes 2359300
  349.3 15.7 %copy-start.44 = (bf16[512,768]{1,0:T(8,128)(2,1)S(1)}, bf16[512,768]{1,0:T(8,128)(2,1)}, u32[]{:S(2)}) copy-start(bf16[512,768]{1,0:T(8,128)(2,1)} %copy-done.43) | copy-start | bytes 2359300
  349.4 15.7 %copy-start.46 = (bf16[512,768]{1,0:T(8,128)(2,1)S(1)}, bf16[512,768]{1,0:T(8,128)(2,1)}, u32[]{:S(2)}) copy-start(bf16[512,768]{1,0:T(8,128)(2,1)} %copy-done.45) | copy-start | bytes 2359300
  349.4 15.7 %copy-start.59 = (s32[3]{0:T(128)S(1)}, s32[3]{0:T(128)}, u32[]{:S(2)}) copy-start(s32[3]{0:T(128)} %copy-done.58) | copy-start | bytes 40
  360.3 4.7 %collective-permute-start.31 = (bf16[400,128]{1,0:T(8,128)(2,1)S(1)}, bf16[400,128]{1,0:T(8,128)(2,1)S(1)}, u32[]{:S(2)}, u32[]{:S(2)}) collective-permute-start(bf16[400,128]{1,0:T(8,128)(2,1)S(1)} %get-tuple-element.219), channel_id=1, source_target_pairs={{0,2},{1,3},{2,0},{3,1},{4,6},{5,7},{6,4},{7,5},{8,10},{9,11},{10,... | collective-permute-start | bytes 307208 | tf_op jit(solution)/shard_map/ppermute | solution.py:686
  360.9 1.2 collective-permute-start.25
  367.9 38.4 %collective-permute-start.37 = (bf16[3072,768]{1,0:T(8,128)(2,1)S(1)}, bf16[3072,768]{1,0:T(8,128)(2,1)S(1)}, u32[]{:S(2)}, u32[]{:S(2)}) collective-permute-start(bf16[3072,768]{1,0:T(8,128)(2,1)S(1)} %bitcast.85), channel_id=1, source_target_pairs={{0,1},{1,0},{2,3},{3,2},{4,5},{5,4},{6,7},{7,6},{8,9},{9,8},{10,11... | collective-permute-start | bytes 14155784 | tf_op jit(solution)/shard_map/ppermute | solution.py:686
  368.0 7.5 %collective-permute-start.33 = (bf16[800,128]{1,0:T(8,128)(2,1)S(1)}, bf16[800,128]{1,0:T(8,128)(2,1)S(1)}, u32[]{:S(2)}, u32[]{:S(2)}) collective-permute-start(bf16[800,128]{1,0:T(8,128)(2,1)S(1)} %get-tuple-element.224), channel_id=1, source_target_pairs={{0,4},{1,5},{2,6},{3,7},{4,0},{5,1},{6,2},{7,3},{8,12},{9,13},{10,... | collective-permute-start | bytes 614408 | tf_op jit(solution)/shard_map/ppermute | solution.py:686
  368.8 3.9 collective-permute-start.27
  375.6 12.5 %collective-permute-start.35 = (bf16[1600,128]{1,0:T(8,128)(2,1)S(1)}, bf16[1600,128]{1,0:T(8,128)(2,1)S(1)}, u32[]{:S(2)}, u32[]{:S(2)}) collective-permute-start(bf16[1600,128]{1,0:T(8,128)(2,1)S(1)} %get-tuple-element.228), channel_id=1, source_target_pairs={{0,8},{1,9},{2,10},{3,11},{4,12},{5,13},{6,14},{7,15},{8,0},{9,1},... | collective-permute-start | bytes 1228808 | tf_op jit(solution)/shard_map/ppermute | solution.py:686
  378.5 3.9 collective-permute-start.32
  382.4 6.8 %collective-permute-start.34 = (f32[1,6912]{1,0:T(1,128)S(1)}, f32[1,6912]{1,0:T(1,128)S(1)}, u32[]{:S(2)}, u32[]{:S(2)}) collective-permute-start(f32[1,6912]{1,0:T(1,128)S(1)} %get-tuple-element.227), channel_id=1, source_target_pairs={{0,8},{1,9},{2,10},{3,11},{4,12},{5,13},{6,14},{7,15},{8,0},{9,1},... | collective-permute-start | bytes 82952 | tf_op jit(solution)/shard_map/ppermute | solution.py:686
  389.2 15.2 %collective-permute-start.36 = (f32[1,6912]{1,0:T(1,128)S(1)}, f32[1,6912]{1,0:T(1,128)S(1)}, u32[]{:S(2)}, u32[]{:S(2)}) collective-permute-start(f32[1,6912]{1,0:T(1,128)S(1)} %get-tuple-element.231), channel_id=1, source_target_pairs={{0,16},{1,17},{2,18},{3,19},{4,20},{5,21},{6,22},{7,23},{8,24},{9,... | collective-permute-start | bytes 82952 | tf_op jit(solution)/shard_map/ppermute | solution.py:686
  (64 other events, 230.3 us)

commit v3 on v2

--- a/solution.py
+++ b/solution.py
@@ -241,15 +241,19 @@
         store_packed(send_ref, half, lats)
 
 
+def store_lat(out_ref, half, j, rows_here, value):
+    at = half * (rows_here // CORES) + pl.program_id(0) * PACK + j
+    out_ref[:, at, :] = value[: out_ref.shape[0]]
+
+
 def last_kernel(
-    x_ref, gresid_ref, mask_ref, got_ref, gain_ref, out_ref, ggain_ref, gshift_ref
+    rows_here, x_ref, gresid_ref, mask_ref, got_ref, gain_ref, out_ref, ggain_ref, gshift_ref
 ):
     @pl.when(pl.program_id(0) == 0)
     def _():
         ggain_ref[...] = jnp.zeros_like(ggain_ref)
         gshift_ref[...] = jnp.zeros_like(gshift_ref)
 
-    here = out_ref.shape[3]
     rows = gresid_ref.shape[3]
     for half in range(CORES):
         got = load_packed(got_ref, half)
@@ -260,7 +264,9 @@
             grad = mask_ref[half, 0, j] * (gres + got[j])
             ggain_ref[...] += jnp.sum(grad * xhat, axis=0, keepdims=True)
             gshift_ref[...] += jnp.sum(grad, axis=0, keepdims=True)
-            out_ref[half, 0, j] = (gres + norm_back(grad, xhat, inv, gain_ref[...]))[:here]
+            store_lat(
+                out_ref, half, j, rows_here, gres + norm_back(grad, xhat, inv, gain_ref[...])
+            )
 
 
 OUTER = (((0,), (0,)), ((), ()))
@@ -285,30 +291,23 @@
     gtok_ref[...] += lax.dot_general(gpre, up_ref[...], ACROSS, preferred_element_type=F32)
 
 
-def split_store(value, tiles, sent_ref, kept_ref):
-    @pl.when(pl.program_id(0) < tiles)
-    def _():
-        sent_ref[...] = value
-
-    @pl.when(pl.program_id(0) >= tiles)
-    def _():
-        kept_ref[...] = value
-
-
-def weight_grad_kernel(core_ref, act_ref, cot_ref, sent_ref, kept_ref):
-    value = lax.dot_general(act_ref[...], cot_ref[...], OUTER, preferred_element_type=F32)
-    split_store(value.astype(BF), pl.num_programs(0) // 2, sent_ref, kept_ref)
-
-
-def branch_kernel(act_ref, down_ref, resid_ref, bias_ref, out_ref):
-    cols, here = resid_ref.shape[3], out_ref.shape[3]
+def weight_grad_kernel(core_ref, left_ref, right_ref, out_ref):
+    out_ref[...] = lax.dot_general(
+        left_ref[...], right_ref[...], OUTER, preferred_element_type=F32
+    ).astype(BF)
+
+
+def branch_kernel(rows_here, act_ref, down_ref, resid_ref, bias_ref, out_ref):
+    cols = resid_ref.shape[3]
     rows = CORES * PACK * cols
     act = act_ref[...].reshape(rows, act_ref.shape[-1])
     branch = jnp.dot(act, down_ref[...], preferred_element_type=F32) + bias_ref[...]
     for half in range(CORES):
         for j in range(PACK):
             at = (half * PACK + j) * cols
-            out_ref[half, 0, j] = (resid_ref[half, 0, j] + branch[at : at + cols])[:here]
+            store_lat(
+                out_ref, half, j, rows_here, resid_ref[half, 0, j] + branch[at : at + cols]
+            )
 
 
 def plus(left, right):
@@ -332,11 +331,20 @@
 
 
 def join_kernel(count, *refs):
+    stay, got = refs[count : count + 2]
     for p in range(count):
-        n = refs[2 * p].shape[0]
-        value = plus(refs[2 * p][...], refs[2 * p + 1][...])
+        n, m = refs[p].shape[0], stay.shape[0] // count
+        value = refs[p][...]
+        rows = slice(p * m, (p + 1) * m)
+        extra = (stay[rows] + got[rows]).astype(BF)
         for out in refs[-2:]:
-            out[p * n : (p + 1) * n] = value
+            out[p * (n + m) : p * (n + m) + n] = value
+            out[p * (n + m) + n : (p + 1) * (n + m)] = extra
+
+
+def settle_kernel(count, *refs):
+    for p in range(count):
+        refs[2 * count + p][...] = plus(refs[2 * p][...], refs[2 * p + 1][...])
 
 
 def part_kernel(kept, got, *outs):
@@ -373,38 +381,69 @@
 
 
 def widen_kernel(core_ref, reduce_ref, expand_ref, *refs):
-    reduce_out, expand_out = refs[-2:]
-    reduce_out[...] = reduce_ref[...].astype(F32)
-    expand_out[...] = expand_ref[...].astype(F32).T
-
-
-def collect_kernel(block, *refs):
-    n = (len(refs) - 1) // SPLIT
-    out = refs[-1]
-    out[...] = jnp.zeros_like(out)
-    for i in range(n // 2):
-        g = sum(refs[n * k + 2 * i][...] for k in range(SPLIT))
-        line = sum(refs[n * k + 2 * i + 1][...] for k in range(SPLIT))
+    reduce_out, expand_out, extra_r, extra_e = refs[-4:]
+    n = reduce_out.shape[0] // 2
+    for k in range(2):
+        at = k * (n + EXTRA)
+        reduce_out[k * n : (k + 1) * n] = reduce_ref[at : at + n].astype(F32)
+        expand_out[:, k * n : (k + 1) * n] = expand_ref[at : at + n].astype(F32).T
+        extra_r[k] = reduce_ref[at + n : at + n + EXTRA]
+        extra_e[k] = expand_ref[at + n : at + n + EXTRA]
+
+
+EXTRA = 16
+
+
+def collect_kernel(block, core_ref, grad_ref, *refs):
+    wide = 2 * LANES
+    halves, lines = [], []
+    for i in range(2):
+        g = grad_ref[i * wide : (i + 1) * wide]
+        at = 2 * wide + 8 * i
+        line = jnp.sum(grad_ref[at : at + 8], axis=0, keepdims=True)
         top, low = g[:block], g[LANES : LANES + block]
-        at = 2 * i * block
-        out[at : at + block] = top[:, :LANES] + low[:, LANES:]
-        out[at + block : at + 2 * block] = top[:, LANES:] - low[:, :LANES]
-        base = n * block + 2 * i
-        out[base : base + 1] = line[:, :LANES]
-        out[base + 1 : base + 2] = line[:, LANES:]
-
-
-def spread_kernel(block, x_ref, wa_ref, wb_ref, ba_ref, bb_ref):
-    for i, (w, b) in enumerate(((wa_ref, ba_ref), (wb_ref, bb_ref))):
-        for part in range(2):
-            row = 4 * block + 2 * i + part
-            tiles = []
-            for q in range(BLOCKS):
-                at = (2 * i + part) * block
-                w[part, q] = x_ref[q, at : at + block, :block].astype(F32)
-                tail = x_ref[q, 4 * block :, :].astype(F32)
-                tiles.append(tail[2 * i + part : 2 * i + part + 1])
-            b[part : part + 1, :] = join_blocks(tiles)
+        halves.append([top[:, :LANES] + low[:, LANES:], top[:, LANES:] - low[:, :LANES]])
+        lines += [line[:, :LANES], line[:, LANES:]]
+    rows = lax.broadcasted_iota(jnp.int32, (EXTRA, LANES), 0)
+    bias = sum(jnp.where(rows == k, line, 0.0) for k, line in enumerate(lines))
+    first = core_ref[0] == 0
+    for k, out in enumerate(refs[-2:]):
+        own = first if k == 0 else jnp.logical_not(first)
+        out[...] = jnp.zeros_like(out)
+        for p in range(2):
+            value = jnp.where(own, halves[0][p], halves[1][p])
+            for t in range(block // EXTRA):
+                at = slice(t * LANES, (t + 1) * LANES)
+                out[p * EXTRA : (p + 1) * EXTRA, at] = value[t * EXTRA : (t + 1) * EXTRA]
+        out[2 * EXTRA : 3 * EXTRA, :LANES] = jnp.where(own, bias, 0.0)
+
+
+def spread_kernel(block, core_ref, *refs):
+    own, got = refs[:2], refs[2:4]
+    wa_ref, wb_ref, ba_ref, bb_ref = refs[4:]
+    first = core_ref[0] == 0
+    per = own[0].shape[0]
+    biases = [[] for _ in range(4)]
+    for q in range(BLOCKS):
+        for half in range(CORES):
+            for p in range(3):
+                if half == 1 and p == 2:
+                    continue
+                k = sum(((q >> ((p + j) % 3)) & 1) << (2 - j) for j in range(3))
+                at = p * BLOCKS + k
+                mine, other = (r[at // per][at % per].astype(F32) for r in (own, got))
+                value = jnp.where(first, mine, other) if half == 0 else jnp.where(first, other, mine)
+                if p == 2:
+                    for i in range(4):
+                        biases[i].append(value[i : i + 1, :LANES])
+                    continue
+                out = wb_ref if half else wa_ref
+                for t in range(block // EXTRA):
+                    out[p, q, t * EXTRA : (t + 1) * EXTRA, :] = value[
+                        :, t * LANES : t * LANES + block
+                    ]
+    for i in range(4):
+        (bb_ref if i > 1 else ba_ref)[i % 2 : i % 2 + 1, :] = join_blocks(biases[i])
 
 
 def lon_kernel(col_devs, row_group, x_ref, table_ref, own_ref, other_ref, turn_ref):
@@ -532,14 +571,21 @@
     drain(turn_ref, own_out, other_out)
 
 
+def row_sums(value):
+    return jnp.sum(value.reshape(-1, 8, value.shape[1]), axis=0)
+
+
 def mix_back_kernel(
     own_ref, other_ref, modes_ref, lat_ref, back_ref, wa_ref, ba_ref, wb_ref, bb_ref,
-    own_out, other_out, gwa_ref, gba_ref, gwb_ref, gbb_ref, turn_ref,
+    *refs,
 ):
+    own_out, other_out, grad_ref, turn_ref = refs[-4:]
     lats, rows = own_ref.shape[1], own_ref.shape[0]
     run = rows // 2
-    for ref in (gwa_ref, gba_ref, gwb_ref, gbb_ref):
-        ref[...] = jnp.zeros_like(ref)
+    grad_ref[...] = refs[0][...] if len(refs) > 4 else jnp.zeros_like(grad_ref)
+    wide = wa_ref.shape[0]
+    gwa_ref, gwb_ref = grad_ref.at[:wide], grad_ref.at[wide : 2 * wide]
+    gba_ref, gbb_ref = grad_ref.at[2 * wide : 2 * wide + 8], grad_ref.at[2 * wide + 8 :]
 
     @pl.loop(0, run // 2)
     def _(step):
@@ -564,12 +610,12 @@
         squash_b = jnp.tanh(pre_b * (1.0 / shrink_soft))
         factor = 1.0 - shrink_level / shrink_soft * (1.0 - squash_b * squash_b)
         grad_b = factor * grad
-        gbb_ref[...] += jnp.sum(grad_b, axis=0, keepdims=True)
+        gbb_ref[...] += row_sums(grad_b)
         grad_b = grad_b.astype(BF)
         grad_hidden = lax.dot_general(grad_b, wb_ref[...], ACROSS, preferred_element_type=F32)
         gwb_ref[...] += lax.dot_general(hidden, grad_b, OUTER, preferred_element_type=F32)
         grad_a = gelu_slope(pre_a, squash_a) * grad_hidden
-        gba_ref[...] += jnp.sum(grad_a, axis=0, keepdims=True)
+        gba_ref[...] += row_sums(grad_a)
         grad_a = grad_a.astype(BF)
         grad_modes = lax.dot_general(
             grad_a, wa_ref[...], ACROSS, preferred_element_type=F32
@@ -738,11 +784,19 @@
             self.level += 1
             return self.kept[0]
 
-        def join(self, after=()):
+        def settle(self, after=()):
+            n = len(orders)
+            self.kept = call(
+                lambda *refs: settle_kernel(n, *refs), zipped(self.kept, self.got),
+                [shape(x.shape, BF) for x in self.kept], 1.0, after=after, name="settle",
+            )
+            return self.kept[0]
+
+        def join(self, stay, got, after=()):
             n, (r, c) = len(orders), self.kept[0].shape
             self.kept, sent = call(
-                lambda *refs: join_kernel(n, *refs), zipped(self.kept, self.got),
-                [shape((n * r, c), BF)] * 2, 1.5, after=after, name="join",
+                lambda *refs: join_kernel(n, *refs), self.kept + [stay, got],
+                [shape((n * (r + EXTRA), c), BF)] * 2, 1.5, after=after, name="join",
             )
             self.got = partner(sent, outer_bits[0])
             for m in outer_bits[1:]:
@@ -773,49 +827,32 @@
             self.got = partner(sent, 1)
             return self.kept
 
-        def widen(self):
-            (rows, c), t = self.kept.shape, 256
-            steps = rows // 2 // t
-            full = [shape((rows, c), F32), shape((c, rows), F32)]
-            done = []
-            for k, x in enumerate((self.kept, self.got)):
-                at = lambda i, h, k=k: jnp.where(h[0] == 0, k, 1 - k) * steps + i
-                done = call(
-                    widen_kernel, [x, x] + done, full, 5.0, prefetch=[core_line], grid=(steps,),
-                    in_specs=[
-                        pl.BlockSpec((t, c), lambda i, h: (i, 0)),
-                        pl.BlockSpec((t, c), lambda i, h: (steps + i, 0)),
-                    ] + [pl.BlockSpec(memory_space=pl.ANY)] * len(done),
-                    out_specs=[
-                        pl.BlockSpec((t, c), lambda i, h, at=at: (at(i, h), 0)),
-                        pl.BlockSpec((c, t), lambda i, h, at=at: (0, at(i, h))),
-                    ],
-                    input_output_aliases={3: 0, 4: 1} if done else {}, name="widen",
-                )
-            return done
+        def widen(self, done, after=()):
+            rows, c = self.kept.shape
+            chunk = rows // (len(orders) * BLOCKS)
+            t = 2 * (chunk - EXTRA)
+            steps = rows // chunk // 4
+            full_rows = CORES * steps * t
+            x = self.got if done else self.kept
+            full = [shape((full_rows, c), F32), shape((c, full_rows), F32)]
+            extra = [shape((2 * steps, EXTRA, c), BF)] * 2
+            at = lambda i, h: (1 - h[0] if done else h[0]) * steps + i
+            return call(
+                widen_kernel, [x, x] + done[:2], full + extra, 5.0, after=after,
+                prefetch=[core_line], grid=(steps,),
+                in_specs=[
+                    pl.BlockSpec((2 * chunk, c), lambda i, h: (i, 0)),
+                    pl.BlockSpec((2 * chunk, c), lambda i, h: (steps + i, 0)),
+                ] + [pl.BlockSpec(memory_space=pl.ANY)] * len(done[:2]),
+                out_specs=[
+                    pl.BlockSpec((t, c), lambda i, h: (at(i, h), 0)),
+                    pl.BlockSpec((c, t), lambda i, h: (0, at(i, h))),
+                ] + [pl.BlockSpec((2, EXTRA, c), lambda i, h: (i, 0, 0))] * 2,
+                input_output_aliases={3: 0, 4: 1} if done else {}, name="widen",
+            )
 
     def add(x, y, dtype, after=()):
         return call(add_kernel, [x, y], [shape(x.shape, dtype)] * 2, 1.0, after=after, name="add")
-
-    class Modes:
-        def __init__(self, x):
-            self.flips = [1] + outer_bits
-            self.doubles = list(cube)
-            self.x, self.got = x, partner(x, 1)
-
-        def step(self, after=()):
-            if self.flips:
-                self.flips.pop(0)
-                left = self.flips or self.doubles
-                self.x, sent = add(self.x, self.got, BF, after)
-            else:
-                m = self.doubles.pop(0)
-                left = self.doubles
-                which = bit(m).astype(jnp.int32).reshape(1)
-                self.x, sent = merge([self.x], [self.got], which, False, after)
-            if left:
-                self.got = partner(sent, left[0])
-            return self.x
 
     class Tail:
         def __init__(self, x):
@@ -829,6 +866,12 @@
                 self.got = partner(sent, self.bits[0])
             return self.x
 
+
+    turned_shape = shape((cols_here, rows_here, channels), F32)
+    turned_spec = pl.BlockSpec(turned_shape.shape, lambda i: (0, 0, 0))
+
+    def turn_back(x):
+        return x.swapaxes(0, 1)
 
     def lon_forward(cells, table, after=()):
         return call(
@@ -908,126 +951,110 @@
     )
 
     halves = 3
-
-    def tile_of(i, c):
-        return jnp.where(i < halves, (1 - c[0]) * halves + i, c[0] * halves + i - halves)
-
-    def sent_at(i):
-        return jnp.minimum(i, halves - 1)
-
-    def kept_at(i):
-        return jnp.maximum(i - halves, 0)
-
-    all_tok_p = pl.BlockSpec((count, channels), lambda i, c: (0, 0))
-    hid_tile = pl.BlockSpec((count, tile), lambda i, c: (0, tile_of(i, c)))
-
-    def weight_grad(left, right, after, name):
+    assert halves * CORES * tile == hidden
+
+    def weight_grad(left, right, own, after, name):
+        at = lambda i, c: (c[0] if own else 1 - c[0]) * halves + i
         return call(
-            weight_grad_kernel, [left, right], [shape((halves * tile, channels), BF)] * 2, 10.0,
-            after=after, prefetch=[core_line], grid=(6,), in_specs=[hid_tile, all_tok_p],
-            out_specs=[
-                pl.BlockSpec((tile, channels), lambda i, c: (sent_at(i), 0)),
-                pl.BlockSpec((tile, channels), lambda i, c: (kept_at(i), 0)),
+            weight_grad_kernel, [left, right], shape((halves * tile, channels), BF), 5.0,
+            after=after, prefetch=[core_line], grid=(halves,),
+            in_specs=[
+                pl.BlockSpec((count, tile), lambda i, c: (0, at(i, c))),
+                pl.BlockSpec((count, channels), lambda i, c: (0, 0)),
             ],
-            vmem=20, name=name,
-        )
-
-    sent_r, kept_r = weight_grad(act, cot2, [], "reduce_grad")
-    got_r = partner(sent_r, 1)
-    sent_e, kept_e = weight_grad(gpre, tokens2, [kept_r], "expand_grad")
-    sums = Sum([kept_r, kept_e], [got_r, partner(sent_e, 1)])
+            out_specs=[pl.BlockSpec((tile, channels), lambda i, c: (i, 0))], vmem=20, name=name,
+        )
 
     one_row = shape((1, channels), F32)
     grad_resid, send, g_gain2, g_shift2, g_rbias = call(
         third_kernel,
         [resid, gtok.reshape(pad_shape), cot_pad, mask, row(second_gain)],
-        [shape(pad_shape, F32), shape(packed_shape, BF)] + [one_row] * 3, 9.0, after=[kept_e],
+        [shape(pad_shape, F32), shape(packed_shape, BF)] + [one_row] * 3, 9.0,
         grid=(groups,), in_specs=[pad_spec, pad_spec, pad_spec, mask_spec, row_spec],
         out_specs=[pad_spec, packed_spec, row_spec, row_spec, row_spec], vmem=20, name="second_back",
     )
     cells = exchange(send.reshape(flat_shape))
 
-    token = sums.halve(after=[send])
-    own, other = lon_forward(cells, lon_wfwd, after=[token])
+    sent_r = weight_grad(act, cot2, False, [send], "reduce_grad")
+    sent_e = weight_grad(gpre, tokens2, False, [sent_r], "expand_grad")
+    kept_r = weight_grad(act, cot2, True, [sent_e], "reduce_grad")
+    kept_e = weight_grad(gpre, tokens2, True, [kept_r], "expand_grad")
+    sums = Sum([kept_r, kept_e], [partner(sent_r, 1), partner(sent_e, 1)])
+
+    own, other = lon_forward(cells, lon_wfwd, after=[kept_e])
     other = swap(other)
     token = sums.halve(after=[own])
-    square = shape((2 * LANES, 2 * LANES), F32)
-    line = shape((1, 2 * LANES), F32)
     run = half_rows // SPLIT
     pieces, grads = [], []
+    grad_shape = shape((4 * LANES + 16, 2 * LANES), F32)
     for k in range(SPLIT):
         here = pl.BlockSpec((run, lats, LANES), lambda i, k=k: (k, 0, 0))
         steps = modes.shape[0] // SPLIT
         const = lambda x: pl.BlockSpec(x.shape, lambda i: (0, 0))
-        o, t, *g = call(
-            mix_back_kernel, [own, other, modes, lat_fwd, lat_inv, wa, ba, wb, bb],
-            [shape((lats, run, LANES), BF)] * 2 + [square, line, square, line], 13.0,
+        o, t, g = call(
+            mix_back_kernel, [own, other, modes, lat_fwd, lat_inv, wa, ba, wb, bb] + grads,
+            [shape((lats, run, LANES), BF)] * 2 + [grad_shape], 13.0,
             after=[token],
             in_specs=[
                 here, here, pl.BlockSpec((steps,) + modes.shape[1:], lambda i, k=k: (k, 0, 0)),
-            ] + [const(x) for x in (lat_fwd, lat_inv, wa, ba, wb, bb)],
+            ] + [const(x) for x in (lat_fwd, lat_inv, wa, ba, wb, bb, *grads)],
             scratch_shapes=[pltpu.VMEM((2 * lats * run, LANES), F32)], name="mix_back",
         )
         pieces.append((o, swap(t)))
-        grads.append(g)
-        if k < SPLIT - 1:
-            token = sums.halve(after=[o]) if k == 0 else sums.join(after=[o])
+        grads = [g]
+        token = sums.halve(after=[o]) if k < SPLIT - 1 else o
+    token = sums.settle(after=[o])
+    send = lon_backward(
+        [p[0] for p in pieces] + [p[1] for p in pieces], lon_inv, after=[token]
+    )
+    got = exchange(send)
+    stay, leave = call(
+        lambda *refs: collect_kernel(block, *refs), grads,
+        [shape((3 * EXTRA, channels), F32)] * 2, 1.5, after=[send], prefetch=[core_line],
+        name="collect",
+    )
+    token = sums.join(stay, partner(leave, 1))
+
+    grad_inputs, g_gain1, g_shift1 = call(
+        lambda *refs: last_kernel(rows_here, *refs), [x5, grad_resid, mask, got.reshape(packed_shape), row(first_gain)],
+        [turned_shape] + [one_row] * 2, 9.0, after=[token],
+        grid=(groups,), in_specs=[here_spec, pad_spec, mask_spec, packed_spec, row_spec],
+        out_specs=[turned_spec, row_spec, row_spec], vmem=28, name="first_back",
+    )
+    tail_sum = Tail(
+        call(
+            tail_kernel, [g_gain1, g_shift1, g_gain2, g_shift2, g_rbias, g_ebias],
+            [shape((1, 5 * channels + hidden), F32)] * 2, 1.0, name="tail",
+        )
+    )
+    token = sums.part(after=[tail_sum.x])
+    token = tail_sum.step(after=[token])
+    token = sums.double(after=[token])
+    token = tail_sum.step(after=[token])
+    token = sums.double(after=[token])
     outputs = call(
-        branch_kernel,
+        lambda *refs: branch_kernel(rows_here, *refs),
         [act.reshape(CORES, groups, PACK, cols_pad, hidden), reduce_weight, resid, row(reduce_bias)],
-        shape(here_shape, F32), 10.0, after=[o], grid=(groups,),
+        turned_shape, 10.0, after=[token], grid=(groups,),
         in_specs=[
             lat_spec(cols_pad, hidden), pl.BlockSpec((hidden, channels), lambda i: (0, 0)),
             pad_spec, row_spec,
         ],
-        out_specs=[here_spec], vmem=26, name="branch",
-    )
-
-    modes_sum = Modes(
-        call(
-            lambda *refs: collect_kernel(block, *refs), sum(grads, []),
-            shape((up_to(4 * block + 4, 16), LANES), F32), 1.5, after=[outputs], name="collect",
-        )
-    )
-    token = sums.part(after=[modes_sum.x])
-    send = lon_backward(
-        [p[0] for p in pieces] + [p[1] for p in pieces], lon_inv, after=[token]
-    )
-    got = exchange(send)
-    token = modes_sum.step(after=[send])
-    token = sums.double(after=[token])
-    token = sums.double(after=[token])
-
-    grad_inputs, g_gain1, g_shift1 = call(
-        last_kernel, [x5, grad_resid, mask, got.reshape(packed_shape), row(first_gain)],
-        [shape(here_shape, F32)] + [one_row] * 2, 9.0, after=[token],
-        grid=(groups,), in_specs=[here_spec, pad_spec, mask_spec, packed_spec, row_spec],
-        out_specs=[here_spec, row_spec, row_spec], vmem=20, name="first_back",
-    )
-    tail_sum = Tail(
-        call(
-            tail_kernel, [g_gain1, g_shift1, g_gain2, g_shift2, g_rbias, g_ebias],
-            [shape((1, 5 * channels + hidden), F32)] * 2, 1.0, name="tail",
-        )
-    )
-    token = modes_sum.step(after=[tail_sum.x])
-    token = tail_sum.step(after=[token])
-    token = modes_sum.step(after=[token])
+        out_specs=[turned_spec], vmem=32, name="branch",
+    )
+
+    token = tail_sum.step(after=[outputs])
     token = sums.double(after=[token])
     token = tail_sum.step(after=[token])
-    token = modes_sum.step(after=[token])
-    token = tail_sum.step(after=[token])
-    token = modes_sum.step(after=[token])
-    while modes_sum.flips or modes_sum.doubles:
-        token = modes_sum.step(after=[token])
+    own_done = sums.widen([], after=[token])
+    token = own_done[0]
     while tail_sum.bits:
         token = tail_sum.step(after=[token])
-    g_reduce, g_expand = sums.widen()
-    spread = modes_sum.x.reshape(BLOCKS, -1, LANES)
+    g_reduce, g_expand, *got_extra = sums.widen(own_done, after=[token])
     weight_out, bias_out = shape(mix_weight_a.shape, F32), shape(mix_bias_a.shape, F32)
     g_wa, g_wb, g_ba, g_bb = call(
-        lambda *refs: spread_kernel(block, *refs), [spread],
-        [weight_out, weight_out, bias_out, bias_out], 3.0, name="spread",
+        lambda *refs: spread_kernel(block, *refs), own_done[2:] + got_extra,
+        [weight_out, weight_out, bias_out, bias_out], 3.0, prefetch=[core_line], name="spread",
     )
 
     tail = tail_sum.x
@@ -1040,7 +1067,7 @@
         return v.reshape(-1)
 
     return (
-        outputs.reshape(inputs.shape), grad_inputs.reshape(inputs.shape),
+        turn_back(outputs), turn_back(grad_inputs),
         flat(g_gain1), flat(g_shift1), g_wa, g_ba, g_wb, g_bb, flat(g_gain2), flat(g_shift2),
         g_expand, g_ebias, g_reduce, flat(g_rbias),
     )

time: 417 us -> 387 us (0.928)
  waiting for transfers between devices: 132 us -> 118 us
  starting transfers between devices: 59.7 us -> 45.8 us
  Pallas kernels: 153 us -> 160 us
  local copies, waits for them, and re-layouts: 63.6 us -> 59.2 us
    ppermute x32 -> x28, waiting for transfers between devices: 77.2 us -> 39.7 us  [partner(): return lax.ppermute(x, AXES, [(d, d ^ flip) for d in range(devices)])]
    all_to_all x4, waiting for transfers between devices: 50 us -> 75.8 us  [exchange(): lax.all_to_all(x, AXES, 0, 0, axis_index_groups=snap_groups, tiled=True)]
    ppermute x32 -> x28, starting transfers between devices: 38.1 us -> 25.1 us  [partner(): return lax.ppermute(x, AXES, [(d, d ^ flip) for d in range(devices)])]
    unnamed x176 -> x144, local copies, waits for them, and re-layouts: 59.6 us -> 49.3 us
    pallas_call x39 -> x37, Pallas kernels: 153 us -> 160 us  [call(): pl.pallas_call(body, grid_spec=pltpu.PrefetchScalarGridSpec(num_scalar_pr...]
  transfers between devices with their start and end apart: 42 -> 38, of which waited for: 22 -> 21; matrix products, arithmetic and copies ran while one was open for 3% -> 3% of each run, Pallas kernels for 14% -> 20%
where the time goes in v3:
time: 387 us; the launch traced here: 385 us
  Pallas kernels  160 us (41%)
  waiting for transfers between devices  118 us (30%)
  local copies, waits for them, and re-layouts  59.2 us (15%)
  starting transfers between devices  45.8 us (12%)
    pallas_call x37, Pallas kernels, call(): pl.pallas_call(body, grid_spec=pltpu.PrefetchScalarGridSpec(num_scalar_pr...  160 us
    all_to_all x4, waiting for transfers between devices, exchange(): lax.all_to_all(x, AXES, 0, 0, axis_index_groups=snap_groups, tiled=True)  75.8 us
    unnamed x144, local copies, waits for them, and re-layouts  49.3 us
    ppermute x28, waiting for transfers between devices, partner(): return lax.ppermute(x, AXES, [(d, d ^ flip) for d in range(devices)])  39.7 us
    ppermute x28, starting transfers between devices, partner(): return lax.ppermute(x, AXES, [(d, d ^ flip) for d in range(devices)])  25.1 us
    all_to_all x4, starting transfers between devices, exchange(): lax.all_to_all(x, AXES, 0, 0, axis_index_groups=snap_groups, tiled=True)  19.7 us
  transfers between devices with their start and end apart: 38, of which 21 were waited for; matrix products, arithmetic and copies ran while one was open for 3% of the time, Pallas kernels for 20%

profile of v3, /device:TPU:0, one launch (start us, length us, event | category | flops | bytes accessed | tf_op | source)
XLA Modules:
  0.0 385.1 jit_solution(16287111831516730502)
XLA Ops:
  3.0 2.0 copy.39
  5.0 4.4 %first_norm.1 = (bf16[2,3,4,48,768]{4,3,2,1,0:T(8,128)(2,1)S(1)}, bf16[8,2,3,48,384]{4,3,2,1,0:T(8,128)(2,1)S(1)}) custom-call(bf16[2,3,4,45,768]{4,3,2,1,0:T(8,128)(2,1)S(1)} %bitcast.61, f32[2,3,4,48,1]{4,3,2,1,0:T(8,128)S(1)} %copy.40.refs_1_.refs_2_.refs_3_, f32[1,768]{1,0:T(1,128)S(1)} %reshape.100.refs_2_.refs_4_, f32[1,768]{1,0:T(1,128)S(1)} %reshape.101.refs_3_), custom_call_target="tpu_custom_call" | custom-call | bytes 600000 | tf_op jit(solution)/shard_map/first_norm/pallas_call | solution.py:44
  11.8 6.3 %all-to-all-start = ((bf16[16,3,48,384]{3,2,1,0:T(8,128)(2,1)}), bf16[16,3,48,384]{3,2,1,0:T(8,128)(2,1)S(1)}, u32[]{:S(2)}, u32[]{:S(2)}) async-start(bf16[16,3,48,384]{3,2,1,0:T(8,128)(2,1)} %bitcast.74), calls=%async_computation | async-start | bytes 3538944 | tf_op jit(solution)/shard_map/all_to_all | solution.py:687
  18.1 1.5 dynamic-slice_bitcast_fusion.5.refs_1_
  19.7 23.7 %all-to-all-done.refs_0_ = bf16[16,3,48,384]{3,2,1,0:T(8,128)(2,1)S(1)} async-done(((bf16[16,3,48,384]{3,2,1,0:T(8,128)(2,1)}), bf16[16,3,48,384]{3,2,1,0:T(8,128)(2,1)S(1)}, u32[]{:S(2)}, u32[]{:S(2)}) %all-to-all-start) | async-done | bytes 1769504 | tf_op jit(solution)/shard_map/all_to_all | solution.py:687
  44.3 3.8 lon_forward.2
  52.3 20.1 %mix.1 = (bf16[48,96,128]{2,1,0:T(8,128)(2,1)S(1)}, bf16[48,96,128]{2,1,0:T(8,128)(2,1)S(1)}, bf16[24,192,256]{2,1,0:T(8,128)(2,1)S(1)}) custom-call(bf16[96,48,128]{2,1,0:T(8,128)(2,1)S(1)} %copy-done.41, bf16[96,48,128]{2,1,0:T(8,128)(2,1)} %collective-permute-done.refs_1_, bf16[192,192]{1,0:T(8,128)(2,1)S(1)} %get-tuple-element.226.refs_2_.refs_3_, ...), custom_call_target="tpu_custom_call" | custom-call | bytes 2200000 | tf_op jit(solution)/shard_map/mix/pallas_call | solution.py:44
  72.5 1.4 copy-done.10
  74.3 2.5 collective-permute-done.1.refs_1_
  76.7 2.1 lon_backward.2
  78.8 4.0 %all-to-all-start.1 = ((bf16[16,3,48,384]{3,2,1,0:T(8,128)(2,1)}), bf16[16,3,48,384]{3,2,1,0:T(8,128)(2,1)S(1)}, u32[]{:S(2)}, u32[]{:S(2)}) async-start(bf16[16,3,48,384]{3,2,1,0:T(8,128)(2,1)} %lon_backward.2), calls=%async_computation.1 | async-start | bytes 3538944 | tf_op jit(solution)/shard_map/all_to_all | solution.py:687
  83.5 1.3 reshape.110.refs_6_
  84.7 3.0 copy.41
  87.7 20.4 %all-to-all-done.1 = bf16[16,3,48,384]{3,2,1,0:T(8,128)(2,1)S(1)} async-done(((bf16[16,3,48,384]{3,2,1,0:T(8,128)(2,1)}), bf16[16,3,48,384]{3,2,1,0:T(8,128)(2,1)S(1)}, u32[]{:S(2)}, u32[]{:S(2)}) %all-to-all-start.1) | async-done | bytes 1769504 | tf_op jit(solution)/shard_map/all_to_all | solution.py:687
  110.3 1.5 copy-done.23
  111.8 1.5 copy-done.24
  113.3 1.5 copy-done.39
  115.5 5.8 %second_norm.1 = (f32[2,3,4,48,768]{4,3,2,1,0:T(8,128)S(1)}, bf16[2,3,4,48,768]{4,3,2,1,0:T(8,128)(2,1)S(1)}, bf16[2,3,4,48,768]{4,3,2,1,0:T(8,128)(2,1)S(1)}) custom-call(bf16[2,3,4,45,768]{4,3,2,1,0:T(8,128)(2,1)S(1)} %bitcast.62, bf16[2,3,4,48,768]{4,3,2,1,0:T(8,128)(2,1)S(1)} %copy-done.39, f32[2,3,4,48,1]{4,3,2,1,0:T(8,128)S(1)} %copy-done.16, ...), custom_call_target="tpu_custom_call" | custom-call | bytes 850000 | tf_op jit(solution)/shard_map/second_norm/pallas_call | solution.py:44
  121.3 23.5 %mlp_chain.1 = (bf16[1152,3072]{1,0:T(8,128)(2,1)}, bf16[1152,3072]{1,0:T(8,128)(2,1)}, f32[1152,768]{1,0:T(8,128)S(1)}, f32[1,3072]{1,0:T(1,128)S(1)}) custom-call(bf16[1152,768]{1,0:T(8,128)(2,1)S(1)} %bitcast.67, bf16[1152,768]{1,0:T(8,128)(2,1)S(1)} %bitcast.64, bf16[768,3072]{1,0:T(8,128)(2,1)} %refs_2_.1, f32[1,3072]{1,0:T(1,128)S(1)} %bitcast.83, ...), custom_call_target="tpu_custom_call" | custom-call | bytes 2500000 | tf_op jit(solution)/shard_map/mlp_chain/pallas_call | solution.py:44
  145.5 7.5 %second_back.1 = (f32[2,3,4,48,768]{4,3,2,1,0:T(8,128)S(1)}, bf16[8,2,3,48,384]{4,3,2,1,0:T(8,128)(2,1)}, f32[1,768]{1,0:T(1,128)S(1)}, f32[1,768]{1,0:T(1,128)S(1)}, f32[1,768]{1,0:T(1,128)S(1)}) custom-call(f32[2,3,4,48,768]{4,3,2,1,0:T(8,128)S(1)} %get-tuple-element.124.refs_0_.refs_2_, f32[2,3,4,48,768]{4,3,2,1,0:T(8,128)S(1)} %bitcast.73, ...), custom_call_target="tpu_custom_call" | custom-call | bytes 900000 | tf_op jit(solution)/shard_map/second_back/pallas_call | solution.py:44
  153.0 1.8 copy-done.25
  156.5 4.6 %all-to-all-start.2 = ((bf16[16,3,48,384]{3,2,1,0:T(8,128)(2,1)}), bf16[16,3,48,384]{3,2,1,0:T(8,128)(2,1)}, u32[]{:S(2)}, u32[]{:S(2)}) async-start(bf16[16,3,48,384]{3,2,1,0:T(8,128)(2,1)} %bitcast.28), calls=%async_computation.2 | async-start | bytes 3538944 | tf_op jit(solution)/shard_map/all_to_all | solution.py:687
  161.1 3.0 copy-done
  164.2 4.9 %reduce_grad.2.refs_3_ = bf16[1536,768]{1,0:T(8,128)(2,1)} custom-call(s32[1]{0:T(128)} %bitcast.26.refs_0_, bf16[1152,3072]{1,0:T(8,128)(2,1)S(1)} %copy-done, bf16[1152,768]{1,0:T(8,128)(2,1)S(1)} %bitcast.65, bf16[8,2,3,48,384]{4,3,2,1,0:T(8,128)(2,1)} %get-tuple-element.127.refs_3_), custom_call_target="tpu_custom_call" | custom-call | bytes 500000 | tf_op jit(solution)/shard_map/reduce_grad/pallas_call | solution.py:44
  169.1 4.9 %expand_grad.2.refs_3_ = bf16[1536,768]{1,0:T(8,128)(2,1)} custom-call(s32[1]{0:T(128)} %bitcast.26.refs_0_, bf16[1152,3072]{1,0:T(8,128)(2,1)S(1)} %copy-done.5, bf16[1152,768]{1,0:T(8,128)(2,1)S(1)} %bitcast.68, bf16[1536,768]{1,0:T(8,128)(2,1)} %reduce_grad.2.refs_3_), custom_call_target="tpu_custom_call" | custom-call | bytes 500000 | tf_op jit(solution)/shard_map/expand_grad/pallas_call | solution.py:44
  175.1 4.0 %reduce_grad.3.refs_3_.refs_1_.refs_5_ = bf16[1536,768]{1,0:T(8,128)(2,1)S(1)} custom-call(s32[1]{0:T(128)} %bitcast.26.refs_0_, bf16[1152,3072]{1,0:T(8,128)(2,1)S(1)} %bitcast.54, bf16[1152,768]{1,0:T(8,128)(2,1)S(1)} %bitcast.66, bf16[1536,768]{1,0:T(8,128)(2,1)} %expand_grad.2.refs_3_), custom_call_target="tpu_custom_call" | custom-call | bytes 500000 | tf_op jit(solution)/shard_map/reduce_grad/pallas_call | solution.py:44
  179.1 4.0 %expand_grad.3.refs_2_.refs_7_.refs_9_.refs_11_ = bf16[1536,768]{1,0:T(8,128)(2,1)S(1)} custom-call(s32[1]{0:T(128)} %bitcast.26.refs_0_, bf16[1152,3072]{1,0:T(8,128)(2,1)S(1)} %copy-done.5, bf16[1152,768]{1,0:T(8,128)(2,1)S(1)} %bitcast.69, bf16[1536,768]{1,0:T(8,128)(2,1)S(1)} %reduce_grad.3.refs_3_.refs_1_.refs_5_), custom_call_target="tpu_custom_call" | custom-call | bytes 500000 | tf_op jit(solution)/shard_map/expand_grad/pallas_call | solution.py:44
  183.2 1.4 copy-done.1
  184.6 1.6 all-to-all-done.2.refs_0_
  186.2 1.7 copy-done.2
  188.7 5.3 %lon_forward.3 = (bf16[96,48,128]{2,1,0:T(8,128)(2,1)S(1)}, bf16[96,48,128]{2,1,0:T(8,128)(2,1)}) custom-call(bf16[16,3,48,384]{3,2,1,0:T(8,128)(2,1)} %all-to-all-done.2.refs_0_, bf16[192,192]{1,0:T(8,128)(2,1)S(1)} %copy-done.47, bf16[1536,768]{1,0:T(8,128)(2,1)S(1)} %copy-done.2), custom_call_target="tpu_custom_call" | custom-call | bytes 550000 | tf_op jit(solution)/shard_map/lon_forward/pallas_call | solution.py:44
  194.1 1.7 copy-done.3
  195.8 3.9 %halve.3 = (bf16[512,768]{1,0:T(8,128)(2,1)S(1)}, bf16[512,768]{1,0:T(8,128)(2,1)S(1)}, bf16[512,768]{1,0:T(8,128)(2,1)S(1)}, bf16[512,768]{1,0:T(8,128)(2,1)S(1...) custom-call(s32[3]{0:T(128)S(1)} %pad_add_fusion.2.refs_0_, ...), custom_call_target="tpu_custom_call" | custom-call | bytes 300000 | tf_op jit(solution)/shard_map/halve/pallas_call | solution.py:44
  199.9 2.7 collective-permute-start.5
  203.6 8.5 %mix_back.3 = (bf16[48,32,128]{2,1,0:T(8,128)(2,1)S(1)}, bf16[48,32,128]{2,1,0:T(8,128)(2,1)S(1)}, f32[528,256]{1,0:T(8,128)S(1)}) custom-call(bf16[96,48,128]{2,1,0:T(8,128)(2,1)S(1)} %get-tuple-element.128.refs_13_.refs_0_, bf16[96,48,128]{2,1,0:T(8,128)(2,1)} %collective-permute-done.7.refs_1_, bf16[24,192,256]{2,1,0:T(8,128)(2,1)S(1)} %copy-done.11, ...), custom_call_target="tpu_custom_call" | custom-call | bytes 1300000 | tf_op jit(solution)/shard_map/mix_back/pallas_call | solution.py:44
  212.2 7.6 %collective-permute-done.4.refs_2_.refs_4_ = bf16[512,768]{1,0:T(8,128)(2,1)S(1)} collective-permute-done((bf16[512,768]{1,0:T(8,128)(2,1)S(1)}, bf16[512,768]{1,0:T(8,128)(2,1)S(1)}, u32[]{:S(2)}, u32[]{:S(2)}) %collective-permute-start.4) | collective-permute-done | bytes 786464 | tf_op jit(solution)/shard_map/ppermute | solution.py:732
  220.2 1.5 collective-permute-done.6.refs_10_.refs_12_
  224.9 8.5 %mix_back.4 = (bf16[48,32,128]{2,1,0:T(8,128)(2,1)S(1)}, bf16[48,32,128]{2,1,0:T(8,128)(2,1)S(1)}, f32[528,256]{1,0:T(8,128)S(1)}) custom-call(bf16[96,48,128]{2,1,0:T(8,128)(2,1)S(1)} %get-tuple-element.128.refs_13_.refs_0_, bf16[96,48,128]{2,1,0:T(8,128)(2,1)} %collective-permute-done.7.refs_1_, bf16[24,192,256]{2,1,0:T(8,128)(2,1)S(1)} %copy-done.11, ...), custom_call_target="tpu_custom_call" | custom-call | bytes 1300000 | tf_op jit(solution)/shard_map/mix_back/pallas_call | solution.py:44
  236.4 8.6 %mix_back.5 = (bf16[48,32,128]{2,1,0:T(8,128)(2,1)S(1)}, bf16[48,32,128]{2,1,0:T(8,128)(2,1)S(1)}, f32[528,256]{1,0:T(8,128)S(1)}) custom-call(bf16[96,48,128]{2,1,0:T(8,128)(2,1)S(1)} %get-tuple-element.128.refs_13_.refs_0_, bf16[96,48,128]{2,1,0:T(8,128)(2,1)} %collective-permute-done.7.refs_1_, bf16[24,192,256]{2,1,0:T(8,128)(2,1)S(1)} %copy-done.11, ...), custom_call_target="tpu_custom_call" | custom-call | bytes 1300000 | tf_op jit(solution)/shard_map/mix_back/pallas_call | solution.py:44
  246.1 1.6 collective-permute-start.13
  247.7 4.7 %collective-permute-done.12.refs_3_ = bf16[128,768]{1,0:T(8,128)(2,1)S(1)} collective-permute-done((bf16[128,768]{1,0:T(8,128)(2,1)S(1)}, bf16[128,768]{1,0:T(8,128)(2,1)S(1)}, u32[]{:S(2)}, u32[]{:S(2)}) %collective-permute-start.12) | collective-permute-done | bytes 196640 | tf_op jit(solution)/shard_map/ppermute | solution.py:732
  254.6 2.1 lon_backward.3.refs_2_
  257.3 4.8 %all-to-all-start.3 = ((bf16[16,3,48,384]{3,2,1,0:T(8,128)(2,1)}), bf16[16,3,48,384]{3,2,1,0:T(8,128)(2,1)}, u32[]{:S(2)}, u32[]{:S(2)}) async-start(bf16[16,3,48,384]{3,2,1,0:T(8,128)(2,1)} %lon_backward.3.refs_2_), calls=%async_computation.3 | async-start | bytes 3538944 | tf_op jit(solution)/shard_map/all_to_all | solution.py:687
  263.4 1.4 collective-permute-done.17.refs_4_
  268.3 2.6 collective-permute-start.18
  270.9 30.1 %all-to-all-done.3 = bf16[16,3,48,384]{3,2,1,0:T(8,128)(2,1)} async-done(((bf16[16,3,48,384]{3,2,1,0:T(8,128)(2,1)}), bf16[16,3,48,384]{3,2,1,0:T(8,128)(2,1)}, u32[]{:S(2)}, u32[]{:S(2)}) %all-to-all-start.3) | async-done | bytes 1769504 | tf_op jit(solution)/shard_map/all_to_all | solution.py:687
  301.0 1.5 copy-done.7
  302.5 2.0 copy-done.26
  305.6 10.5 %first_back.1 = (f32[45,24,768]{2,1,0:T(8,128)}, f32[1,768]{1,0:T(1,128)S(1)}, f32[1,768]{1,0:T(1,128)S(1)}) custom-call(bf16[2,3,4,45,768]{4,3,2,1,0:T(8,128)(2,1)S(1)} %bitcast.63, f32[2,3,4,48,768]{4,3,2,1,0:T(8,128)S(1)} %copy-done.26, f32[2,3,4,48,1]{4,3,2,1,0:T(8,128)S(1)} %copy-done.18, bf16[8,2,3,48,384]{4,3,2,1,0:T(8,128)(2,1)} %bitcast.31.refs_3_, ...), custom_call_target="tpu_custom_call" | custom-call | bytes 900000 | tf_op jit(solution)/shard_map/first_back/pallas_call | solution.py:44
  318.0 1.9 collective-permute-start.21
  321.1 3.4 collective-permute-done.19.refs_2_
  326.2 1.8 collective-permute-start.23
  328.0 1.7 collective-permute-start.24
  330.0 1.7 collective-permute-start.26
  331.7 8.9 %collective-permute-done.26.refs_1_ = f32[1,6912]{1,0:T(1,128)S(1)} collective-permute-done((f32[1,6912]{1,0:T(1,128)S(1)}, f32[1,6912]{1,0:T(1,128)S(1)}, u32[]{:S(2)}, u32[]{:S(2)}) %collective-permute-start.26) | collective-permute-done | bytes 27680 | tf_op jit(solution)/shard_map/ppermute | solution.py:732
  343.4 1.7 collective-permute-start.27
  345.1 2.3 copy-done.12
  347.4 9.4 %branch.1.refs_2_ = f32[45,24,768]{2,1,0:T(8,128)} custom-call(bf16[2,3,4,48,3072]{4,3,2,1,0:T(8,128)(2,1)S(1)} %bitcast.57, bf16[3072,768]{1,0:T(8,128)(2,1)S(1)} %copy-done.12, f32[2,3,4,48,768]{4,3,2,1,0:T(8,128)S(1)} %copy-done.20, f32[1,768]{1,0:T(1,128)S(1)} %reshape.115.refs_3_, bf16[576,768]{1,0:T(8,128)(2,1)S(1)} %get-tuple-element.189.refs_4_.refs_1_), custom_call_target="tpu_custom_call" | custom-call | bytes 1000000 | tf_op jit(solution)/shard_map/branch/pallas_call | solution.py:44
  356.8 5.0 %collective-permute-done.27.refs_1_ = f32[1,6912]{1,0:T(1,128)S(1)} collective-permute-done((f32[1,6912]{1,0:T(1,128)S(1)}, f32[1,6912]{1,0:T(1,128)S(1)}, u32[]{:S(2)}, u32[]{:S(2)}) %collective-permute-start.27) | collective-permute-done | bytes 27680 | tf_op jit(solution)/shard_map/ppermute | solution.py:732
  361.8 1.9 copy-done.21
  366.2 2.8 collective-permute-done.28.refs_1_
  369.1 4.5 %widen.2 = (f32[3072,768]{1,0:T(8,128)}, f32[768,3072]{1,0:T(8,128)}, bf16[12,16,768]{2,1,0:T(8,128)(2,1)S(1)}, bf16[12,16,768]{2,1,0:T(8,128)(2,1)S(1)}) custom-call(s32[1]{0:T(128)} %bitcast.26.refs_0_, bf16[3456,768]{1,0:T(8,128)(2,1)S(1)} %bitcast.59, bf16[3456,768]{1,0:T(8,128)(2,1)S(1)} %bitcast.60, f32[1,6912]{1,0:T(1,128)S(1)} %get-tuple-element.200.refs_3_.refs_0_), custom_call_target="tpu_custom_call" | custom-call | bytes 500000 | tf_op jit(solution)/shard_map/widen/pallas_call | solution.py:44
  373.9 3.7 copy-done.4
  379.4 4.4 %widen.3 = (f32[3072,768]{1,0:T(8,128)}, f32[768,3072]{1,0:T(8,128)}, bf16[12,16,768]{2,1,0:T(8,128)(2,1)S(1)}, bf16[12,16,768]{2,1,0:T(8,128)(2,1)S(1)}) custom-call(s32[1]{0:T(128)} %bitcast.26.refs_0_, bf16[3456,768]{1,0:T(8,128)(2,1)S(1)} %collective-permute-done.33.refs_1_.refs_2_, ...), custom_call_target="tpu_custom_call", output_to_operand_aliasing={{0}: (3, {}), {1}: (4, {})} | custom-call | bytes 500000 | tf_op jit(solution)/shard_map/widen/pallas_call | solution.py:44
  (225 shorter events, 49.7 us)
Async XLA Ops:
  5.0 104.3 %copy-start.6 = (bf16[24,45,768]{2,1,0:T(8,128)(2,1)}, bf16[24,45,768]{2,1,0:T(8,128)(2,1)S(1)}, u32[]{:S(2)}) copy-start(bf16[24,45,768]{2,1,0:T(8,128)(2,1)S(1)} %copy.39) | copy-start | bytes 4976644
  11.8 31.6 %all-to-all-start = ((bf16[16,3,48,384]{3,2,1,0:T(8,128)(2,1)}), bf16[16,3,48,384]{3,2,1,0:T(8,128)(2,1)S(1)}, u32[]{:S(2)}, u32[]{:S(2)}) async-start(bf16[16,3,48,384]{3,2,1,0:T(8,128)(2,1)} %bitcast.74), calls=%async_computation | async-start | bytes 3538944 | tf_op jit(solution)/shard_map/all_to_all | solution.py:687
  18.1 31.0 %copy-start.65 = (f32[2,768]{1,0:T(2,128)S(1)}, f32[2,768]{1,0:T(2,128)}, u32[]{:S(2)}) copy-start(f32[2,768]{1,0:T(2,128)} %param.27) | copy-start | bytes 18436
  49.1 3.2 collective-permute-start
  51.0 23.2 %copy-start.27 = (bf16[256,256]{1,0:T(8,128)(2,1)}, bf16[256,256]{1,0:T(8,128)(2,1)S(1)}, u32[]{:S(2)}) copy-start(bf16[256,256]{1,0:T(8,128)(2,1)S(1)} %maximum_maximum_fusion.1.refs_6_.refs_7_) | copy-start | bytes 393220
  51.0 23.2 %copy-start.64 = (bf16[2,192,192]{2,1,0:T(8,128)(2,1)S(1)}, bf16[2,192,192]{2,1,0:T(8,128)(2,1)}, u32[]{:S(2)}) copy-start(bf16[2,192,192]{2,1,0:T(8,128)(2,1)} %constant.187.clone) | copy-start | bytes 442372
  51.1 25.6 %copy-start.29 = (bf16[256,256]{1,0:T(8,128)(2,1)}, bf16[256,256]{1,0:T(8,128)(2,1)S(1)}, u32[]{:S(2)}) copy-start(bf16[256,256]{1,0:T(8,128)(2,1)S(1)} %maximum_maximum_fusion.refs_4_.refs_5_) | copy-start | bytes 393220
  52.2 24.5 %copy-start.33 = (bf16[192,192]{1,0:T(8,128)(2,1)}, bf16[192,192]{1,0:T(8,128)(2,1)S(1)}, u32[]{:S(2)}) copy-start(bf16[192,192]{1,0:T(8,128)(2,1)S(1)} %get-tuple-element.225.refs_3_.refs_4_) | copy-start | bytes 221188
  52.2 24.5 %copy-start.35 = (bf16[192,192]{1,0:T(8,128)(2,1)}, bf16[192,192]{1,0:T(8,128)(2,1)S(1)}, u32[]{:S(2)}) copy-start(bf16[192,192]{1,0:T(8,128)(2,1)S(1)} %get-tuple-element.226.refs_2_.refs_3_) | copy-start | bytes 221188
  73.8 2.9 collective-permute-start.1
  78.8 29.3 %all-to-all-start.1 = ((bf16[16,3,48,384]{3,2,1,0:T(8,128)(2,1)}), bf16[16,3,48,384]{3,2,1,0:T(8,128)(2,1)S(1)}, u32[]{:S(2)}, u32[]{:S(2)}) async-start(bf16[16,3,48,384]{3,2,1,0:T(8,128)(2,1)} %lon_backward.2), calls=%async_computation.1 | async-start | bytes 3538944 | tf_op jit(solution)/shard_map/all_to_all | solution.py:687
  121.3 23.6 %copy-start.13 = (bf16[2,3,4,48,768]{4,3,2,1,0:T(8,128)(2,1)}, bf16[2,3,4,48,768]{4,3,2,1,0:T(8,128)(2,1)S(1)}, u32[]{:S(2)}) copy-start(bf16[2,3,4,48,768]{4,3,2,1,0:T(8,128)(2,1)S(1)} %get-tuple-element.121) | copy-start | bytes 5308420
  121.3 24.2 %copy-start.19 = (f32[2,3,4,48,768]{4,3,2,1,0:T(8,128)}, f32[2,3,4,48,768]{4,3,2,1,0:T(8,128)S(1)}, u32[]{:S(2)}) copy-start(f32[2,3,4,48,768]{4,3,2,1,0:T(8,128)S(1)} %get-tuple-element.124.refs_0_.refs_2_) | copy-start | bytes 10616836
  121.3 39.8 %copy-start.8 = (bf16[2,3,4,48,768]{4,3,2,1,0:T(8,128)(2,1)}, bf16[2,3,4,48,768]{4,3,2,1,0:T(8,128)(2,1)S(1)}, u32[]{:S(2)}) copy-start(bf16[2,3,4,48,768]{4,3,2,1,0:T(8,128)(2,1)S(1)} %get-tuple-element.122.refs_2_) | copy-start | bytes 5308420
  121.3 24.1 %copy-start.17 = (f32[2,3,4,48,1]{4,3,2,1,0:T(8,128)S(1)}, f32[2,3,4,48,1]{4,3,2,1,0:T(8,128)}, u32[]{:S(2)}) copy-start(f32[2,3,4,48,1]{4,3,2,1,0:T(8,128)} %copy-done.15) | copy-start | bytes 13828
  156.5 29.7 %all-to-all-start.2 = ((bf16[16,3,48,384]{3,2,1,0:T(8,128)(2,1)}), bf16[16,3,48,384]{3,2,1,0:T(8,128)(2,1)}, u32[]{:S(2)}, u32[]{:S(2)}) async-start(bf16[16,3,48,384]{3,2,1,0:T(8,128)(2,1)} %bitcast.28), calls=%async_computation.2 | async-start | bytes 3538944 | tf_op jit(solution)/shard_map/all_to_all | solution.py:687
  174.0 20.1 %collective-permute-start.3 = (bf16[1536,768]{1,0:T(8,128)(2,1)}, bf16[1536,768]{1,0:T(8,128)(2,1)}, u32[]{:S(2)}, u32[]{:S(2)}) collective-permute-start(bf16[1536,768]{1,0:T(8,128)(2,1)} %expand_grad.2.refs_3_), channel_id=1, source_target_pairs={{0,1},{1,0},{2,3},{3,2},{4,5},{5,4},{6,7},{7,6},{8,9},{9,8},{10,11... | collective-permute-start | bytes 7077896 | tf_op jit(solution)/shard_map/ppermute | solution.py:732
  174.0 20.1 %collective-permute-start.2 = (bf16[1536,768]{1,0:T(8,128)(2,1)}, bf16[1536,768]{1,0:T(8,128)(2,1)}, u32[]{:S(2)}, u32[]{:S(2)}) collective-permute-start(bf16[1536,768]{1,0:T(8,128)(2,1)} %reduce_grad.2.refs_3_), channel_id=1, source_target_pairs={{0,1},{1,0},{2,3},{3,2},{4,5},{5,4},{6,7},{7,6},{8,9},{9,8},{10,11... | collective-permute-start | bytes 7077896 | tf_op jit(solution)/shard_map/ppermute | solution.py:732
  194.0 9.6 %collective-permute-start.7 = (bf16[96,48,128]{2,1,0:T(8,128)(2,1)}, bf16[96,48,128]{2,1,0:T(8,128)(2,1)}, u32[]{:S(2)}, u32[]{:S(2)}) collective-permute-start(bf16[96,48,128]{2,1,0:T(8,128)(2,1)} %get-tuple-element.135), channel_id=1, source_target_pairs={{0,1},{1,0},{2,3},{3,2},{4,5},{5,4},{6,7},{7,6},{8,9},{9,8},{10,11... | collective-permute-start | bytes 3538952 | tf_op jit(solution)/shard_map/ppermute | solution.py:690
  195.8 7.8 %copy-start.28 = (bf16[256,256]{1,0:T(8,128)(2,1)S(1)}, bf16[256,256]{1,0:T(8,128)(2,1)}, u32[]{:S(2)}) copy-start(bf16[256,256]{1,0:T(8,128)(2,1)} %copy-done.27) | copy-start | bytes 393220
  195.8 7.8 %copy-start.30 = (bf16[256,256]{1,0:T(8,128)(2,1)S(1)}, bf16[256,256]{1,0:T(8,128)(2,1)}, u32[]{:S(2)}) copy-start(bf16[256,256]{1,0:T(8,128)(2,1)} %copy-done.29) | copy-start | bytes 393220
  195.8 7.8 %copy-start.34 = (bf16[192,192]{1,0:T(8,128)(2,1)S(1)}, bf16[192,192]{1,0:T(8,128)(2,1)}, u32[]{:S(2)}) copy-start(bf16[192,192]{1,0:T(8,128)(2,1)} %copy-done.33) | copy-start | bytes 221188
  195.8 7.8 %copy-start.36 = (bf16[192,192]{1,0:T(8,128)(2,1)S(1)}, bf16[192,192]{1,0:T(8,128)(2,1)}, u32[]{:S(2)}) copy-start(bf16[192,192]{1,0:T(8,128)(2,1)} %copy-done.35) | copy-start | bytes 221188
  199.7 20.0 %collective-permute-start.4 = (bf16[512,768]{1,0:T(8,128)(2,1)S(1)}, bf16[512,768]{1,0:T(8,128)(2,1)S(1)}, u32[]{:S(2)}, u32[]{:S(2)}) collective-permute-start(bf16[512,768]{1,0:T(8,128)(2,1)S(1)} %get-tuple-element.130), channel_id=1, source_target_pairs={{0,2},{1,3},{2,0},{3,1},{4,6},{5,7},{6,4},{7,5},{8,10},{9,11},{10,... | collective-permute-start | bytes 2359304 | tf_op jit(solution)/shard_map/ppermute | solution.py:732
  199.9 20.3 %collective-permute-start.5 = (bf16[512,768]{1,0:T(8,128)(2,1)S(1)}, bf16[512,768]{1,0:T(8,128)(2,1)S(1)}, u32[]{:S(2)}, u32[]{:S(2)}) collective-permute-start(bf16[512,768]{1,0:T(8,128)(2,1)S(1)} %get-tuple-element.132), channel_id=1, source_target_pairs={{0,4},{1,5},{2,6},{3,7},{4,0},{5,1},{6,2},{7,3},{8,12},{9,13},{10,... | collective-permute-start | bytes 2359304 | tf_op jit(solution)/shard_map/ppermute | solution.py:732
  202.6 19.1 %collective-permute-start.6 = (bf16[512,768]{1,0:T(8,128)(2,1)S(1)}, bf16[512,768]{1,0:T(8,128)(2,1)S(1)}, u32[]{:S(2)}, u32[]{:S(2)}) collective-permute-start(bf16[512,768]{1,0:T(8,128)(2,1)S(1)} %get-tuple-element.134), channel_id=1, source_target_pairs={{0,8},{1,9},{2,10},{3,11},{4,12},{5,13},{6,14},{7,15},{8,0},{9,1},... | collective-permute-start | bytes 2359304 | tf_op jit(solution)/shard_map/ppermute | solution.py:732
  222.8 10.6 %collective-permute-start.8 = (bf16[256,768]{1,0:T(8,128)(2,1)S(1)}, bf16[256,768]{1,0:T(8,128)(2,1)S(1)}, u32[]{:S(2)}, u32[]{:S(2)}) collective-permute-start(bf16[256,768]{1,0:T(8,128)(2,1)S(1)} %get-tuple-element.139), channel_id=1, source_target_pairs={{0,4},{1,5},{2,6},{3,7},{4,0},{5,1},{6,2},{7,3},{8,12},{9,13},{10,... | collective-permute-start | bytes 1179656 | tf_op jit(solution)/shard_map/ppermute | solution.py:732
  223.1 10.3 %collective-permute-start.9 = (bf16[256,768]{1,0:T(8,128)(2,1)S(1)}, bf16[256,768]{1,0:T(8,128)(2,1)S(1)}, u32[]{:S(2)}, u32[]{:S(2)}) collective-permute-start(bf16[256,768]{1,0:T(8,128)(2,1)S(1)} %get-tuple-element.141), channel_id=1, source_target_pairs={{0,8},{1,9},{2,10},{3,11},{4,12},{5,13},{6,14},{7,15},{8,0},{9,1},... | collective-permute-start | bytes 1179656 | tf_op jit(solution)/shard_map/ppermute | solution.py:732
  224.4 9.9 %collective-permute-start.10 = (bf16[256,768]{1,0:T(8,128)(2,1)S(1)}, bf16[256,768]{1,0:T(8,128)(2,1)S(1)}, u32[]{:S(2)}, u32[]{:S(2)}) collective-permute-start(bf16[256,768]{1,0:T(8,128)(2,1)S(1)} %get-tuple-element.143), channel_id=1, source_target_pairs={{0,2},{1,3},{2,0},{3,1},{4,6},{5,7},{6,4},{7,5},{8,10},{9,11},{10,... | collective-permute-start | bytes 1179656 | tf_op jit(solution)/shard_map/ppermute | solution.py:732
  235.0 11.1 %collective-permute-start.11 = (bf16[128,768]{1,0:T(8,128)(2,1)S(1)}, bf16[128,768]{1,0:T(8,128)(2,1)S(1)}, u32[]{:S(2)}, u32[]{:S(2)}) collective-permute-start(bf16[128,768]{1,0:T(8,128)(2,1)S(1)} %get-tuple-element.147), channel_id=1, source_target_pairs={{0,8},{1,9},{2,10},{3,11},{4,12},{5,13},{6,14},{7,15},{8,0},{9,1},... | collective-permute-start | bytes 589832 | tf_op jit(solution)/shard_map/ppermute | solution.py:732
  235.9 18.6 %collective-permute-start.14 = (bf16[48,32,128]{2,1,0:T(8,128)(2,1)S(1)}, bf16[48,32,128]{2,1,0:T(8,128)(2,1)S(1)}, u32[]{:S(2)}, u32[]{:S(2)}) collective-permute-start(bf16[48,32,128]{2,1,0:T(8,128)(2,1)S(1)} %get-tuple-element.158), channel_id=1, source_target_pairs={{0,1},{1,0},{2,3},{3,2},{4,5},{5,4},{6,7},{7,6},{8,9},{9,8},{10,11... | collective-permute-start | bytes 1179656 | tf_op jit(solution)/shard_map/ppermute | solution.py:690
  235.9 18.6 %collective-permute-start.15 = (bf16[48,32,128]{2,1,0:T(8,128)(2,1)S(1)}, bf16[48,32,128]{2,1,0:T(8,128)(2,1)S(1)}, u32[]{:S(2)}, u32[]{:S(2)}) collective-permute-start(bf16[48,32,128]{2,1,0:T(8,128)(2,1)S(1)} %get-tuple-element.159), channel_id=1, source_target_pairs={{0,1},{1,0},{2,3},{3,2},{4,5},{5,4},{6,7},{7,6},{8,9},{9,8},{10,11... | collective-permute-start | bytes 1179656 | tf_op jit(solution)/shard_map/ppermute | solution.py:690
  236.4 11.2 %copy-start.62 = (bf16[2,192,192]{2,1,0:T(8,128)(2,1)S(1)}, bf16[2,192,192]{2,1,0:T(8,128)(2,1)}, u32[]{:S(2)}) copy-start(bf16[2,192,192]{2,1,0:T(8,128)(2,1)} %constant.186.clone) | copy-start | bytes 442372
  245.0 8.2 %copy-start.44 = (f32[528,256]{1,0:T(8,128)}, f32[528,256]{1,0:T(8,128)S(1)}, u32[]{:S(2)}) copy-start(f32[528,256]{1,0:T(8,128)S(1)} %get-tuple-element.157.refs_1_) | copy-start | bytes 1622020
  245.0 9.6 %collective-permute-start.16 = (bf16[48,32,128]{2,1,0:T(8,128)(2,1)S(1)}, bf16[48,32,128]{2,1,0:T(8,128)(2,1)S(1)}, u32[]{:S(2)}, u32[]{:S(2)}) collective-permute-start(bf16[48,32,128]{2,1,0:T(8,128)(2,1)S(1)} %get-tuple-element.160), channel_id=1, source_target_pairs={{0,1},{1,0},{2,3},{3,2},{4,5},{5,4},{6,7},{7,6},{8,9},{9,8},{10,11... | collective-permute-start | bytes 1179656 | tf_op jit(solution)/shard_map/ppermute | solution.py:690
  245.1 7.3 %collective-permute-start.12 = (bf16[128,768]{1,0:T(8,128)(2,1)S(1)}, bf16[128,768]{1,0:T(8,128)(2,1)S(1)}, u32[]{:S(2)}, u32[]{:S(2)}) collective-permute-start(bf16[128,768]{1,0:T(8,128)(2,1)S(1)} %get-tuple-element.149), channel_id=1, source_target_pairs={{0,2},{1,3},{2,0},{3,1},{4,6},{5,7},{6,4},{7,5},{8,10},{9,11},{10,... | collective-permute-start | bytes 589832 | tf_op jit(solution)/shard_map/ppermute | solution.py:732
  246.1 7.0 %collective-permute-start.13 = (bf16[128,768]{1,0:T(8,128)(2,1)S(1)}, bf16[128,768]{1,0:T(8,128)(2,1)S(1)}, u32[]{:S(2)}, u32[]{:S(2)}) collective-permute-start(bf16[128,768]{1,0:T(8,128)(2,1)S(1)} %get-tuple-element.151), channel_id=1, source_target_pairs={{0,4},{1,5},{2,6},{3,7},{4,0},{5,1},{6,2},{7,3},{8,12},{9,13},{10,... | collective-permute-start | bytes 589832 | tf_op jit(solution)/shard_map/ppermute | solution.py:732
  257.3 43.7 %copy-start.18 = (f32[2,3,4,48,1]{4,3,2,1,0:T(8,128)S(1)}, f32[2,3,4,48,1]{4,3,2,1,0:T(8,128)}, u32[]{:S(2)}) copy-start(f32[2,3,4,48,1]{4,3,2,1,0:T(8,128)} %copy-done.15) | copy-start | bytes 13828
  257.3 43.7 %all-to-all-start.3 = ((bf16[16,3,48,384]{3,2,1,0:T(8,128)(2,1)}), bf16[16,3,48,384]{3,2,1,0:T(8,128)(2,1)}, u32[]{:S(2)}, u32[]{:S(2)}) async-start(bf16[16,3,48,384]{3,2,1,0:T(8,128)(2,1)} %lon_backward.3.refs_2_), calls=%async_computation.3 | async-start | bytes 3538944 | tf_op jit(solution)/shard_map/all_to_all | solution.py:687
  263.2 81.8 %slice-start.2 = ((s8[7077888]{0:T(1024)(128)(4,1)}), s8[2883584]{0:T(1024)(128)(4,1)S(1)}, s32[]{:S(2)}) async-start(s8[7077888]{0:T(1024)(128)(4,1)} %bitcast.55), calls=%async_computation.6 | async-start | bytes 5767168
  263.3 1.4 collective-permute-start.17
  268.3 47.9 %collective-permute-start.18 = (bf16[432,768]{1,0:T(8,128)(2,1)}, bf16[432,768]{1,0:T(8,128)(2,1)}, u32[]{:S(2)}, u32[]{:S(2)}) collective-permute-start(bf16[432,768]{1,0:T(8,128)(2,1)} %get-tuple-element.164), channel_id=1, source_target_pairs={{0,16},{1,17},{2,18},{3,19},{4,20},{5,21},{6,22},{7,23},{8,24},{9,... | collective-permute-start | bytes 1990664 | tf_op jit(solution)/shard_map/ppermute | solution.py:732
  305.6 10.6 %copy-start.54 = (f32[1,3072]{1,0:T(1,128)S(1)}, f32[1,3072]{1,0:T(1,128)}, u32[]{:S(2)}) copy-start(f32[1,3072]{1,0:T(1,128)} %copy-done.53) | copy-start | bytes 36868
  305.6 10.6 %copy-start.57 = (f32[1,768]{1,0:T(1,128)S(1)}, f32[1,768]{1,0:T(1,128)}, u32[]{:S(2)}) copy-start(f32[1,768]{1,0:T(1,128)} %copy-done.56) | copy-start | bytes 9220
  305.6 10.6 %copy-start.59 = (f32[1,768]{1,0:T(1,128)S(1)}, f32[1,768]{1,0:T(1,128)}, u32[]{:S(2)}) copy-start(f32[1,768]{1,0:T(1,128)} %copy-done.58) | copy-start | bytes 9220
  305.6 10.6 %copy-start.61 = (f32[1,768]{1,0:T(1,128)S(1)}, f32[1,768]{1,0:T(1,128)}, u32[]{:S(2)}) copy-start(f32[1,768]{1,0:T(1,128)} %copy-done.60) | copy-start | bytes 9220
  305.6 39.4 %slice-start.3 = ((s8[7077888]{0:T(1024)(128)(4,1)}), s8[4194304]{0:T(1024)(128)(4,1)S(1)}, s32[]{:S(2)}) async-start(s8[7077888]{0:T(1024)(128)(4,1)} %bitcast.55), calls=%async_computation.7 | async-start | bytes 8388608
  317.5 7.0 %collective-permute-start.19 = (bf16[144,768]{1,0:T(8,128)(2,1)S(1)}, bf16[144,768]{1,0:T(8,128)(2,1)S(1)}, u32[]{:S(2)}, u32[]{:S(2)}) collective-permute-start(bf16[144,768]{1,0:T(8,128)(2,1)S(1)} %get-tuple-element.174), channel_id=1, source_target_pairs={{0,8},{1,9},{2,10},{3,11},{4,12},{5,13},{6,14},{7,15},{8,0},{9,1},... | collective-permute-start | bytes 663560 | tf_op jit(solution)/shard_map/ppermute | solution.py:732
  317.5 7.0 %collective-permute-start.20 = (bf16[144,768]{1,0:T(8,128)(2,1)S(1)}, bf16[144,768]{1,0:T(8,128)(2,1)S(1)}, u32[]{:S(2)}, u32[]{:S(2)}) collective-permute-start(bf16[144,768]{1,0:T(8,128)(2,1)S(1)} %get-tuple-element.176), channel_id=1, source_target_pairs={{0,2},{1,3},{2,0},{3,1},{4,6},{5,7},{6,4},{7,5},{8,10},{9,11},{10,... | collective-permute-start | bytes 663560 | tf_op jit(solution)/shard_map/ppermute | solution.py:732
  318.0 7.5 %collective-permute-start.21 = (bf16[144,768]{1,0:T(8,128)(2,1)S(1)}, bf16[144,768]{1,0:T(8,128)(2,1)S(1)}, u32[]{:S(2)}, u32[]{:S(2)}) collective-permute-start(bf16[144,768]{1,0:T(8,128)(2,1)S(1)} %get-tuple-element.178), channel_id=1, source_target_pairs={{0,4},{1,5},{2,6},{3,7},{4,0},{5,1},{6,2},{7,3},{8,12},{9,13},{10,... | collective-permute-start | bytes 663560 | tf_op jit(solution)/shard_map/ppermute | solution.py:732
  319.9 1.2 collective-permute-start.22
  325.5 19.6 %copy-start.20 = (f32[2,3,4,48,768]{4,3,2,1,0:T(8,128)S(1)}, f32[2,3,4,48,768]{4,3,2,1,0:T(8,128)}, u32[]{:S(2)}) copy-start(f32[2,3,4,48,768]{4,3,2,1,0:T(8,128)} %copy-done.19) | copy-start | bytes 10616836
  326.2 18.8 %copy-start.66 = (f32[768]{0:T(1024)S(1)}, f32[768]{0:T(1024)}, u32[]{:S(2)}) copy-start(f32[768]{0:T(1024)} %param.35) | copy-start | bytes 9220
  326.2 14.4 %collective-permute-start.23 = (bf16[288,768]{1,0:T(8,128)(2,1)S(1)}, bf16[288,768]{1,0:T(8,128)(2,1)S(1)}, u32[]{:S(2)}, u32[]{:S(2)}) collective-permute-start(bf16[288,768]{1,0:T(8,128)(2,1)S(1)} %get-tuple-element.182), channel_id=1, source_target_pairs={{0,4},{1,5},{2,6},{3,7},{4,0},{5,1},{6,2},{7,3},{8,12},{9,13},{10,... | collective-permute-start | bytes 1327112 | tf_op jit(solution)/shard_map/ppermute | solution.py:732
  328.0 12.6 %collective-permute-start.24 = (bf16[288,768]{1,0:T(8,128)(2,1)S(1)}, bf16[288,768]{1,0:T(8,128)(2,1)S(1)}, u32[]{:S(2)}, u32[]{:S(2)}) collective-permute-start(bf16[288,768]{1,0:T(8,128)(2,1)S(1)} %get-tuple-element.184), channel_id=1, source_target_pairs={{0,8},{1,9},{2,10},{3,11},{4,12},{5,13},{6,14},{7,15},{8,0},{9,1},... | collective-permute-start | bytes 1327112 | tf_op jit(solution)/shard_map/ppermute | solution.py:732
  329.7 11.0 %collective-permute-start.25 = (bf16[288,768]{1,0:T(8,128)(2,1)S(1)}, bf16[288,768]{1,0:T(8,128)(2,1)S(1)}, u32[]{:S(2)}, u32[]{:S(2)}) collective-permute-start(bf16[288,768]{1,0:T(8,128)(2,1)S(1)} %get-tuple-element.186), channel_id=1, source_target_pairs={{0,2},{1,3},{2,0},{3,1},{4,6},{5,7},{6,4},{7,5},{8,10},{9,11},{10,... | collective-permute-start | bytes 1327112 | tf_op jit(solution)/shard_map/ppermute | solution.py:732
  330.0 10.7 %collective-permute-start.26 = (f32[1,6912]{1,0:T(1,128)S(1)}, f32[1,6912]{1,0:T(1,128)S(1)}, u32[]{:S(2)}, u32[]{:S(2)}) collective-permute-start(f32[1,6912]{1,0:T(1,128)S(1)} %get-tuple-element.187), channel_id=1, source_target_pairs={{0,2},{1,3},{2,0},{3,1},{4,6},{5,7},{6,4},{7,5},{8,10},{9,11},{10,... | collective-permute-start | bytes 82952 | tf_op jit(solution)/shard_map/ppermute | solution.py:732
  341.6 22.2 %collective-permute-start.29 = (bf16[576,768]{1,0:T(8,128)(2,1)S(1)}, bf16[576,768]{1,0:T(8,128)(2,1)S(1)}, u32[]{:S(2)}, u32[]{:S(2)}) collective-permute-start(bf16[576,768]{1,0:T(8,128)(2,1)S(1)} %get-tuple-element.194), channel_id=1, source_target_pairs={{0,2},{1,3},{2,0},{3,1},{4,6},{5,7},{6,4},{7,5},{8,10},{9,11},{10,... | collective-permute-start | bytes 2654216 | tf_op jit(solution)/shard_map/ppermute | solution.py:732
  342.3 21.5 %collective-permute-start.30 = (bf16[576,768]{1,0:T(8,128)(2,1)S(1)}, bf16[576,768]{1,0:T(8,128)(2,1)S(1)}, u32[]{:S(2)}, u32[]{:S(2)}) collective-permute-start(bf16[576,768]{1,0:T(8,128)(2,1)S(1)} %get-tuple-element.196), channel_id=1, source_target_pairs={{0,4},{1,5},{2,6},{3,7},{4,0},{5,1},{6,2},{7,3},{8,12},{9,13},{10,... | collective-permute-start | bytes 2654216 | tf_op jit(solution)/shard_map/ppermute | solution.py:732
  342.6 21.2 %collective-permute-start.31 = (bf16[576,768]{1,0:T(8,128)(2,1)S(1)}, bf16[576,768]{1,0:T(8,128)(2,1)S(1)}, u32[]{:S(2)}, u32[]{:S(2)}) collective-permute-start(bf16[576,768]{1,0:T(8,128)(2,1)S(1)} %get-tuple-element.198), channel_id=1, source_target_pairs={{0,8},{1,9},{2,10},{3,11},{4,12},{5,13},{6,14},{7,15},{8,0},{9,1},... | collective-permute-start | bytes 2654216 | tf_op jit(solution)/shard_map/ppermute | solution.py:732
  343.4 18.4 %collective-permute-start.27 = (f32[1,6912]{1,0:T(1,128)S(1)}, f32[1,6912]{1,0:T(1,128)S(1)}, u32[]{:S(2)}, u32[]{:S(2)}) collective-permute-start(f32[1,6912]{1,0:T(1,128)S(1)} %get-tuple-element.191), channel_id=1, source_target_pairs={{0,4},{1,5},{2,6},{3,7},{4,0},{5,1},{6,2},{7,3},{8,12},{9,13},{10,... | collective-permute-start | bytes 82952 | tf_op jit(solution)/shard_map/ppermute | solution.py:732
  365.0 14.4 %collective-permute-start.33 = (bf16[3456,768]{1,0:T(8,128)(2,1)S(1)}, bf16[3456,768]{1,0:T(8,128)(2,1)S(1)}, u32[]{:S(2)}, u32[]{:S(2)}) collective-permute-start(bf16[3456,768]{1,0:T(8,128)(2,1)S(1)} %bitcast.84), channel_id=1, source_target_pairs={{0,1},{1,0},{2,3},{3,2},{4,5},{5,4},{6,7},{7,6},{8,9},{9,8},{10,11... | collective-permute-start | bytes 15925256 | tf_op jit(solution)/shard_map/ppermute | solution.py:732
  365.1 3.9 %collective-permute-start.28 = (f32[1,6912]{1,0:T(1,128)S(1)}, f32[1,6912]{1,0:T(1,128)S(1)}, u32[]{:S(2)}, u32[]{:S(2)}) collective-permute-start(f32[1,6912]{1,0:T(1,128)S(1)} %get-tuple-element.193), channel_id=1, source_target_pairs={{0,8},{1,9},{2,10},{3,11},{4,12},{5,13},{6,14},{7,15},{8,0},{9,1},... | collective-permute-start | bytes 82952 | tf_op jit(solution)/shard_map/ppermute | solution.py:732
  369.0 4.8 %collective-permute-start.32 = (f32[1,6912]{1,0:T(1,128)S(1)}, f32[1,6912]{1,0:T(1,128)S(1)}, u32[]{:S(2)}, u32[]{:S(2)}) collective-permute-start(f32[1,6912]{1,0:T(1,128)S(1)} %get-tuple-element.201), channel_id=1, source_target_pairs={{0,16},{1,17},{2,18},{3,19},{4,20},{5,21},{6,22},{7,23},{8,24},{9,... | collective-permute-start | bytes 82952 | tf_op jit(solution)/shard_map/ppermute | solution.py:732
  (45 other events, 103.5 us)

commit v4 on v3

--- a/solution.py
+++ b/solution.py
@@ -60,7 +60,8 @@
     return list(got) if isinstance(out_shape, (list, tuple)) else got[0]
 
 
-SPLIT = 3
+SPLIT = 2
+UNROLL = 2
 
 
 def lon_table(lon_size, col_devs, cols_here, cols_pad, slots, slots_pad):
@@ -188,32 +189,40 @@
     return inv * (scaled - m1 - xhat * m2)
 
 
+def mask_column(mask_ref, lat, rows):
+    line = mask_ref[pl.ds(lat, 1), :].astype(F32)
+    shape = (rows, line.shape[1])
+    row, col = (lax.broadcasted_iota(jnp.int32, shape, k) for k in range(2))
+    return jnp.sum(jnp.where(row == col, line, 0.0), axis=1, keepdims=True)
+
+
 def first_kernel(x_ref, mask_ref, gain_ref, shift_ref, normed_ref, out_ref):
     rows = normed_ref.shape[3]
-    for half in range(CORES):
-        lats = []
-        for j in range(PACK):
-            x = pad_rows(x_ref[half, 0, j].astype(F32), rows)
-            xhat, _ = stats(x)
-            y = mask_ref[half, 0, j] * (xhat * gain_ref[...] + shift_ref[...])
-            normed_ref[half, 0, j] = y.astype(BF)
-            lats.append(y)
-        store_packed(out_ref, half, lats)
+    half, first = 0, pl.program_id(0) * PACK
+    lats = []
+    for j in range(PACK):
+        x = pad_rows(x_ref[half, 0, j].astype(F32), rows)
+        xhat, _ = stats(x)
+        y = mask_column(mask_ref, first + j, rows) * (xhat * gain_ref[...] + shift_ref[...])
+        normed_ref[half, 0, j] = y.astype(BF)
+        lats.append(y)
+    store_packed(out_ref, half, lats)
 
 
 def second_kernel(
     x_ref, normed_ref, mask_ref, cot_ref, got_ref, gain_ref, shift_ref, resid_ref, tok_ref, cot_out
 ):
     rows = normed_ref.shape[3]
-    for half in range(CORES):
-        spatial = load_packed(got_ref, half)
-        for j in range(PACK):
-            x = pad_rows(x_ref[half, 0, j].astype(F32), rows)
-            resid = x + normed_ref[half, 0, j].astype(F32) + mask_ref[half, 0, j] * spatial[j]
-            resid_ref[half, 0, j] = resid
-            xhat, _ = stats(resid)
-            tok_ref[half, 0, j] = (xhat * gain_ref[...] + shift_ref[...]).astype(BF)
-            cot_out[half, 0, j] = pad_rows(cot_ref[half, 0, j].astype(F32), rows).astype(BF)
+    half, first = 0, pl.program_id(0) * PACK
+    spatial = load_packed(got_ref, half)
+    for j in range(PACK):
+        x = pad_rows(x_ref[half, 0, j].astype(F32), rows)
+        resid = x + normed_ref[half, 0, j].astype(F32)
+        resid = resid + mask_column(mask_ref, first + j, rows) * spatial[j]
+        resid_ref[half, 0, j] = resid
+        xhat, _ = stats(resid)
+        tok_ref[half, 0, j] = (xhat * gain_ref[...] + shift_ref[...]).astype(BF)
+        cot_out[half, 0, j] = pad_rows(cot_ref[half, 0, j].astype(F32), rows).astype(BF)
 
 
 def third_kernel(
@@ -226,28 +235,27 @@
         gshift_ref[...] = jnp.zeros_like(gshift_ref)
         gbias_ref[...] = jnp.zeros_like(gbias_ref)
 
-    for half in range(CORES):
-        lats = []
-        for j in range(PACK):
-            xhat, inv = stats(resid_ref[half, 0, j])
-            gtok = gtok_ref[half, 0, j]
-            cot = cot_ref[half, 0, j].astype(F32)
-            ggain_ref[...] += jnp.sum(gtok * xhat, axis=0, keepdims=True)
-            gshift_ref[...] += jnp.sum(gtok, axis=0, keepdims=True)
-            gbias_ref[...] += jnp.sum(cot, axis=0, keepdims=True)
-            gres = cot + norm_back(gtok, xhat, inv, gain_ref[...])
-            gresid_ref[half, 0, j] = gres
-            lats.append(mask_ref[half, 0, j] * gres)
-        store_packed(send_ref, half, lats)
-
-
-def store_lat(out_ref, half, j, rows_here, value):
-    at = half * (rows_here // CORES) + pl.program_id(0) * PACK + j
-    out_ref[:, at, :] = value[: out_ref.shape[0]]
+    half, first = 0, pl.program_id(0) * PACK
+    lats = []
+    for j in range(PACK):
+        xhat, inv = stats(resid_ref[half, 0, j])
+        gtok = gtok_ref[half, 0, j]
+        cot = cot_ref[half, 0, j].astype(F32)
+        ggain_ref[...] += jnp.sum(gtok * xhat, axis=0, keepdims=True)
+        gshift_ref[...] += jnp.sum(gtok, axis=0, keepdims=True)
+        gbias_ref[...] += jnp.sum(cot, axis=0, keepdims=True)
+        gres = cot + norm_back(gtok, xhat, inv, gain_ref[...])
+        gresid_ref[half, 0, j] = gres
+        lats.append(mask_column(mask_ref, first + j, gres.shape[0]) * gres)
+    store_packed(send_ref, half, lats)
+
+
+def store_lat(out_ref, lat, value):
+    out_ref[:, lat, :] = value[: out_ref.shape[0]]
 
 
 def last_kernel(
-    rows_here, x_ref, gresid_ref, mask_ref, got_ref, gain_ref, out_ref, ggain_ref, gshift_ref
+    x_ref, gresid_ref, mask_ref, got_ref, gain_ref, out_ref, ggain_ref, gshift_ref
 ):
     @pl.when(pl.program_id(0) == 0)
     def _():
@@ -255,18 +263,16 @@
         gshift_ref[...] = jnp.zeros_like(gshift_ref)
 
     rows = gresid_ref.shape[3]
-    for half in range(CORES):
-        got = load_packed(got_ref, half)
-        for j in range(PACK):
-            x = pad_rows(x_ref[half, 0, j].astype(F32), rows)
-            xhat, inv = stats(x)
-            gres = gresid_ref[half, 0, j]
-            grad = mask_ref[half, 0, j] * (gres + got[j])
-            ggain_ref[...] += jnp.sum(grad * xhat, axis=0, keepdims=True)
-            gshift_ref[...] += jnp.sum(grad, axis=0, keepdims=True)
-            store_lat(
-                out_ref, half, j, rows_here, gres + norm_back(grad, xhat, inv, gain_ref[...])
-            )
+    half, first = 0, pl.program_id(0) * PACK
+    got = load_packed(got_ref, half)
+    for j in range(PACK):
+        x = pad_rows(x_ref[half, 0, j].astype(F32), rows)
+        xhat, inv = stats(x)
+        gres = gresid_ref[half, 0, j]
+        grad = mask_column(mask_ref, first + j, rows) * (gres + got[j])
+        ggain_ref[...] += jnp.sum(grad * xhat, axis=0, keepdims=True)
+        gshift_ref[...] += jnp.sum(grad, axis=0, keepdims=True)
+        store_lat(out_ref, first + j, gres + norm_back(grad, xhat, inv, gain_ref[...]))
 
 
 OUTER = (((0,), (0,)), ((), ()))
@@ -297,7 +303,7 @@
     ).astype(BF)
 
 
-def branch_kernel(rows_here, act_ref, down_ref, resid_ref, bias_ref, out_ref):
+def branch_kernel(act_ref, down_ref, resid_ref, bias_ref, out_ref):
     cols = resid_ref.shape[3]
     rows = CORES * PACK * cols
     act = act_ref[...].reshape(rows, act_ref.shape[-1])
@@ -305,9 +311,8 @@
     for half in range(CORES):
         for j in range(PACK):
             at = (half * PACK + j) * cols
-            store_lat(
-                out_ref, half, j, rows_here, resid_ref[half, 0, j] + branch[at : at + cols]
-            )
+            lat = (half * pl.num_programs(0) + pl.program_id(0)) * PACK + j
+            store_lat(out_ref, lat, resid_ref[half, 0, j] + branch[at : at + cols])
 
 
 def plus(left, right):
@@ -345,6 +350,10 @@
 def settle_kernel(count, *refs):
     for p in range(count):
         refs[2 * count + p][...] = plus(refs[2 * p][...], refs[2 * p + 1][...])
+
+
+def touch_kernel(out):
+    out[...] = jnp.zeros_like(out)
 
 
 def part_kernel(kept, got, *outs):
@@ -536,7 +545,7 @@
     lats, rows = own_ref.shape[1], own_ref.shape[0]
     run = rows // 2 // SPLIT
 
-    @pl.loop(0, rows // 4)
+    @pl.loop(0, rows // 4, unroll=UNROLL)
     def _(step):
         slot = 2 * step
         row = slot + slot // run * run
@@ -587,7 +596,7 @@
     gwa_ref, gwb_ref = grad_ref.at[:wide], grad_ref.at[wide : 2 * wide]
     gba_ref, gbb_ref = grad_ref.at[2 * wide : 2 * wide + 8], grad_ref.at[2 * wide + 8 :]
 
-    @pl.loop(0, run // 2)
+    @pl.loop(0, run // 2, unroll=UNROLL)
     def _(step):
         row = 2 * step
         cells = jnp.concatenate(
@@ -695,22 +704,23 @@
     def row(v):
         return v.reshape(1, -1)
 
-    mask = jnp.pad(
-        valid_mask.astype(F32), ((0, 0), (0, cols_pad - cols_here))
-    )[:, :, None]
-    mask = fold(mask)
     x5, cot5 = fold(inputs), fold(cotangent)
 
     def lat_spec(cols, width):
+        return pl.BlockSpec(
+            (1, 1, PACK, cols, width), lambda i: (i // groups, i % groups, 0, 0, 0)
+        )
+
+    def both_spec(cols, width):
         return pl.BlockSpec((CORES, 1, PACK, cols, width), lambda i: (0, i, 0, 0, 0))
 
     packed_spec = pl.BlockSpec(
-        (BLOCKS, CORES, 1, cols_pad, 3 * LANES), lambda i: (0, 0, i, 0, 0)
-    )
+        (BLOCKS, 1, 1, cols_pad, 3 * LANES), lambda i: (0, i // groups, i % groups, 0, 0)
+    )
+    lat_steps = CORES * groups
     row_spec = pl.BlockSpec((1, channels), lambda i: (0, 0))
-    here_spec, pad_spec, mask_spec = (
-        lat_spec(cols_here, channels), lat_spec(cols_pad, channels), lat_spec(cols_pad, 1)
-    )
+    here_spec, pad_spec = lat_spec(cols_here, channels), lat_spec(cols_pad, channels)
+    mask, mask_spec = valid_mask, pl.BlockSpec((rows_here, cols_here), lambda i: (0, 0))
     packed_shape = (BLOCKS, CORES, groups, cols_pad, 3 * LANES)
     flat_shape = (members, groups, cols_pad, 3 * LANES)
     pad_shape = (CORES, groups, PACK, cols_pad, channels)
@@ -908,7 +918,7 @@
     normed, send = call(
         first_kernel, [x5, mask, row(first_gain), row(first_shift)],
         [shape(pad_shape, BF), shape(packed_shape, BF)], 6.0,
-        grid=(groups,), in_specs=[here_spec, mask_spec, row_spec, row_spec],
+        grid=(lat_steps,), in_specs=[here_spec, mask_spec, row_spec, row_spec],
         out_specs=[pad_spec, packed_spec], vmem=16, name="first_norm",
     )
     cells = exchange(send.reshape(flat_shape))
@@ -928,9 +938,9 @@
         second_kernel,
         [x5, normed, mask, cot5, got.reshape(packed_shape), row(second_gain), row(second_shift)],
         [shape(pad_shape, F32), shape(pad_shape, BF), shape(pad_shape, BF)], 8.5,
-        grid=(groups,),
+        grid=(lat_steps,),
         in_specs=[here_spec, pad_spec, mask_spec, here_spec, packed_spec, row_spec, row_spec],
-        out_specs=[pad_spec, pad_spec, pad_spec], vmem=20, name="second_norm",
+        out_specs=[pad_spec, pad_spec, pad_spec], vmem=56, name="second_norm",
     )
     tokens2, cot2 = tokens.reshape(-1, channels), cot_pad.reshape(-1, channels)
     count, hidden = tokens2.shape[0], expand_weight.shape[1]
@@ -970,8 +980,8 @@
         third_kernel,
         [resid, gtok.reshape(pad_shape), cot_pad, mask, row(second_gain)],
         [shape(pad_shape, F32), shape(packed_shape, BF)] + [one_row] * 3, 9.0,
-        grid=(groups,), in_specs=[pad_spec, pad_spec, pad_spec, mask_spec, row_spec],
-        out_specs=[pad_spec, packed_spec, row_spec, row_spec, row_spec], vmem=20, name="second_back",
+        grid=(lat_steps,), in_specs=[pad_spec, pad_spec, pad_spec, mask_spec, row_spec],
+        out_specs=[pad_spec, packed_spec, row_spec, row_spec, row_spec], vmem=56, name="second_back",
     )
     cells = exchange(send.reshape(flat_shape))
 
@@ -1002,8 +1012,8 @@
         )
         pieces.append((o, swap(t)))
         grads = [g]
-        token = sums.halve(after=[o]) if k < SPLIT - 1 else o
-    token = sums.settle(after=[o])
+        token = sums.halve(after=[o])
+    token = sums.settle(after=[token])
     send = lon_backward(
         [p[0] for p in pieces] + [p[1] for p in pieces], lon_inv, after=[token]
     )
@@ -1015,11 +1025,17 @@
     )
     token = sums.join(stay, partner(leave, 1))
 
+    touched = call(
+        touch_kernel, [], shape((8, LANES), F32), 0.5, after=[got, token], name="touch"
+    )
+    token = sums.part(after=[touched])
+    token = sums.double(after=[token])
+
     grad_inputs, g_gain1, g_shift1 = call(
-        lambda *refs: last_kernel(rows_here, *refs), [x5, grad_resid, mask, got.reshape(packed_shape), row(first_gain)],
+        last_kernel, [x5, grad_resid, mask, got.reshape(packed_shape), row(first_gain)],
         [turned_shape] + [one_row] * 2, 9.0, after=[token],
-        grid=(groups,), in_specs=[here_spec, pad_spec, mask_spec, packed_spec, row_spec],
-        out_specs=[turned_spec, row_spec, row_spec], vmem=28, name="first_back",
+        grid=(lat_steps,), in_specs=[here_spec, pad_spec, mask_spec, packed_spec, row_spec],
+        out_specs=[turned_spec, row_spec, row_spec], vmem=56, name="first_back",
     )
     tail_sum = Tail(
         call(
@@ -1027,18 +1043,15 @@
             [shape((1, 5 * channels + hidden), F32)] * 2, 1.0, name="tail",
         )
     )
-    token = sums.part(after=[tail_sum.x])
+    token = sums.double(after=[tail_sum.x])
     token = tail_sum.step(after=[token])
-    token = sums.double(after=[token])
-    token = tail_sum.step(after=[token])
-    token = sums.double(after=[token])
     outputs = call(
-        lambda *refs: branch_kernel(rows_here, *refs),
+        branch_kernel,
         [act.reshape(CORES, groups, PACK, cols_pad, hidden), reduce_weight, resid, row(reduce_bias)],
         turned_shape, 10.0, after=[token], grid=(groups,),
         in_specs=[
-            lat_spec(cols_pad, hidden), pl.BlockSpec((hidden, channels), lambda i: (0, 0)),
-            pad_spec, row_spec,
+            both_spec(cols_pad, hidden), pl.BlockSpec((hidden, channels), lambda i: (0, 0)),
+            both_spec(cols_pad, channels), row_spec,
         ],
         out_specs=[turned_spec], vmem=32, name="branch",
     )
@@ -1047,10 +1060,11 @@
     token = sums.double(after=[token])
     token = tail_sum.step(after=[token])
     own_done = sums.widen([], after=[token])
-    token = own_done[0]
+    token = tail_sum.step(after=[own_done[0]])
+    g_reduce, g_expand, *got_extra = sums.widen(own_done, after=[token])
+    token = got_extra[0]
     while tail_sum.bits:
         token = tail_sum.step(after=[token])
-    g_reduce, g_expand, *got_extra = sums.widen(own_done, after=[token])
     weight_out, bias_out = shape(mix_weight_a.shape, F32), shape(mix_bias_a.shape, F32)
     g_wa, g_wb, g_ba, g_bb = call(
         lambda *refs: spread_kernel(block, *refs), own_done[2:] + got_extra,

time: 387 us -> 359 us (0.928)
  local copies, waits for them, and re-layouts: 59.2 us -> 44.9 us
  Pallas kernels: 160 us -> 151 us
  waiting for transfers between devices: 118 us -> 112 us
    ppermute x28, waiting for transfers between devices: 39.7 us -> 27.1 us  [partner(): return lax.ppermute(x, AXES, [(d, d ^ flip) for d in range(devices)])]
    unnamed x144 -> x130, local copies, waits for them, and re-layouts: 49.3 us -> 38.4 us
    pallas_call x37, Pallas kernels: 160 us -> 151 us  [call(): pl.pallas_call(body, grid_spec=pltpu.PrefetchScalarGridSpec(num_scalar_pr...]
    all_to_all x4, waiting for transfers between devices: 75.8 us -> 80.9 us  [exchange(): lax.all_to_all(x, AXES, 0, 0, axis_index_groups=snap_groups, tiled=True)]
  transfers between devices with their start and end apart: 38 -> 37, of which waited for: 21 -> 18; matrix products, arithmetic and copies ran while one was open for 3% -> 2% of each run, Pallas kernels for 20% -> 22%
where the time goes in v4:
time: 359 us; the launch traced here: 358 us
  Pallas kernels  151 us (42%)
  waiting for transfers between devices  112 us (31%)
  starting transfers between devices  47.4 us (13%)
  local copies, waits for them, and re-layouts  44.9 us (13%)
    pallas_call x37, Pallas kernels, call(): pl.pallas_call(body, grid_spec=pltpu.PrefetchScalarGridSpec(num_scalar_pr...  151 us
    all_to_all x4, waiting for transfers between devices, exchange(): lax.all_to_all(x, AXES, 0, 0, axis_index_groups=snap_groups, tiled=True)  80.9 us
    unnamed x130, local copies, waits for them, and re-layouts  38.4 us
    ppermute x28, starting transfers between devices, partner(): return lax.ppermute(x, AXES, [(d, d ^ flip) for d in range(devices)])  27.8 us
    ppermute x28, waiting for transfers between devices, partner(): return lax.ppermute(x, AXES, [(d, d ^ flip) for d in range(devices)])  27.1 us
    all_to_all x4, starting transfers between devices, exchange(): lax.all_to_all(x, AXES, 0, 0, axis_index_groups=snap_groups, tiled=True)  18.9 us
  transfers between devices with their start and end apart: 37, of which 18 were waited for; matrix products, arithmetic and copies ran while one was open for 2% of the time, Pallas kernels for 22%

profile of v4, /device:TPU:0, one launch (start us, length us, event | category | flops | bytes accessed | tf_op | source)
XLA Modules:
  0.0 358.0 jit_solution(15016123995500391163)
XLA Ops:
  2.0 1.8 copy.37
  3.8 3.3 first_norm.1
  9.5 6.3 %all-to-all-start = ((bf16[16,3,48,384]{3,2,1,0:T(8,128)(2,1)}), bf16[16,3,48,384]{3,2,1,0:T(8,128)(2,1)S(1)}, u32[]{:S(2)}, u32[]{:S(2)}) async-start(bf16[16,3,48,384]{3,2,1,0:T(8,128)(2,1)} %bitcast.77), calls=%async_computation | async-start | bytes 3538944 | tf_op jit(solution)/shard_map/all_to_all | solution.py:696
  16.9 24.3 %all-to-all-done.refs_0_ = bf16[16,3,48,384]{3,2,1,0:T(8,128)(2,1)S(1)} async-done(((bf16[16,3,48,384]{3,2,1,0:T(8,128)(2,1)}), bf16[16,3,48,384]{3,2,1,0:T(8,128)(2,1)S(1)}, u32[]{:S(2)}, u32[]{:S(2)}) %all-to-all-start) | async-done | bytes 1769504 | tf_op jit(solution)/shard_map/all_to_all | solution.py:696
  41.1 3.8 %lon_forward.2 = (bf16[96,48,128]{2,1,0:T(8,128)(2,1)S(1)}, bf16[96,48,128]{2,1,0:T(8,128)(2,1)}) custom-call(bf16[16,3,48,384]{3,2,1,0:T(8,128)(2,1)S(1)} %all-to-all-done.refs_0_, bf16[192,192]{1,0:T(8,128)(2,1)S(1)} %dynamic-slice_bitcast_fusion.5.refs_1_), custom_call_target="tpu_custom_call" | custom-call | bytes 550000 | tf_op jit(solution)/shard_map/lon_forward/pallas_call | solution.py:44
  46.2 1.8 collective-permute-done.refs_1_
  48.0 15.4 %mix.1 = (bf16[48,96,128]{2,1,0:T(8,128)(2,1)S(1)}, bf16[48,96,128]{2,1,0:T(8,128)(2,1)S(1)}, bf16[24,192,256]{2,1,0:T(8,128)(2,1)S(1)}) custom-call(bf16[96,48,128]{2,1,0:T(8,128)(2,1)S(1)} %get-tuple-element.114.refs_0_, bf16[96,48,128]{2,1,0:T(8,128)(2,1)S(1)} %collective-permute-done.refs_1_, bf16[192,192]{1,0:T(8,128)(2,1)S(1)} %get-tuple-element.220.refs_2_.refs_3_, ...), custom_call_target="tpu_custom_call" | custom-call | bytes 2200000 | tf_op jit(solution)/shard_map/mix/pallas_call | solution.py:44
  63.4 1.5 copy-done.15
  65.0 2.7 collective-permute-done.1.refs_1_
  67.7 2.1 lon_backward.2
  69.8 4.1 %all-to-all-start.1 = ((bf16[16,3,48,384]{3,2,1,0:T(8,128)(2,1)}), bf16[16,3,48,384]{3,2,1,0:T(8,128)(2,1)S(1)}, u32[]{:S(2)}, u32[]{:S(2)}) async-start(bf16[16,3,48,384]{3,2,1,0:T(8,128)(2,1)} %lon_backward.2), calls=%async_computation.1 | async-start | bytes 3538944 | tf_op jit(solution)/shard_map/all_to_all | solution.py:696
  75.1 1.5 copy.38
  76.6 22.6 %all-to-all-done.1 = bf16[16,3,48,384]{3,2,1,0:T(8,128)(2,1)S(1)} async-done(((bf16[16,3,48,384]{3,2,1,0:T(8,128)(2,1)}), bf16[16,3,48,384]{3,2,1,0:T(8,128)(2,1)S(1)}, u32[]{:S(2)}, u32[]{:S(2)}) %all-to-all-start.1) | async-done | bytes 1769504 | tf_op jit(solution)/shard_map/all_to_all | solution.py:696
  100.4 8.1 %second_norm.1 = (f32[2,3,4,48,768]{4,3,2,1,0:T(8,128)}, bf16[2,3,4,48,768]{4,3,2,1,0:T(8,128)(2,1)}, bf16[2,3,4,48,768]{4,3,2,1,0:T(8,128)(2,1)}) custom-call(bf16[2,3,4,45,768]{4,3,2,1,0:T(8,128)(2,1)} %bitcast.65, bf16[2,3,4,48,768]{4,3,2,1,0:T(8,128)(2,1)} %copy-done.24, s32[24,45]{1,0:T(8,128)} %refs_2_.5, bf16[2,3,4,45,768]{4,3,2,1,0:T(8,128)(2,1)} %bitcast.87, ...), custom_call_target="tpu_custom_call" | custom-call | bytes 850000 | tf_op jit(solution)/shard_map/second_norm/pallas_call | solution.py:44
  108.5 1.5 copy-done.6
  110.0 1.5 copy-done.11
  111.5 22.2 %mlp_chain.1 = (bf16[1152,3072]{1,0:T(8,128)(2,1)}, bf16[1152,3072]{1,0:T(8,128)(2,1)}, f32[1152,768]{1,0:T(8,128)S(1)}, f32[1,3072]{1,0:T(1,128)S(1)}) custom-call(bf16[1152,768]{1,0:T(8,128)(2,1)S(1)} %bitcast.71, bf16[1152,768]{1,0:T(8,128)(2,1)S(1)} %bitcast.67, bf16[768,3072]{1,0:T(8,128)(2,1)} %refs_2_.4, f32[1,3072]{1,0:T(1,128)S(1)} %bitcast.84, ...), custom_call_target="tpu_custom_call" | custom-call | bytes 2500000 | tf_op jit(solution)/shard_map/mlp_chain/pallas_call | solution.py:44
  133.6 1.8 copy-done.18
  136.0 8.8 %second_back.1 = (f32[2,3,4,48,768]{4,3,2,1,0:T(8,128)}, bf16[8,2,3,48,384]{4,3,2,1,0:T(8,128)(2,1)}, f32[1,768]{1,0:T(1,128)}, f32[1,768]{1,0:T(1,128)}, f32[1,768]{1,0:T(1,128)}) custom-call(f32[2,3,4,48,768]{4,3,2,1,0:T(8,128)} %get-tuple-element.121.refs_0_.refs_2_, f32[2,3,4,48,768]{4,3,2,1,0:T(8,128)} %bitcast.76, ...), custom_call_target="tpu_custom_call" | custom-call | bytes 900000 | tf_op jit(solution)/shard_map/second_back/pallas_call | solution.py:44
  144.8 4.6 %all-to-all-start.2 = ((bf16[16,3,48,384]{3,2,1,0:T(8,128)(2,1)}), bf16[16,3,48,384]{3,2,1,0:T(8,128)(2,1)}, u32[]{:S(2)}, u32[]{:S(2)}) async-start(bf16[16,3,48,384]{3,2,1,0:T(8,128)(2,1)} %bitcast.75), calls=%async_computation.2 | async-start | bytes 3538944 | tf_op jit(solution)/shard_map/all_to_all | solution.py:696
  149.4 3.0 copy-done
  152.5 1.5 copy-done.7
  153.9 1.5 copy-done.17
  155.4 4.9 %reduce_grad.2.refs_3_ = bf16[1536,768]{1,0:T(8,128)(2,1)} custom-call(s32[1]{0:T(128)} %bitcast.25.refs_0_, bf16[1152,3072]{1,0:T(8,128)(2,1)S(1)} %copy-done, bf16[1152,768]{1,0:T(8,128)(2,1)S(1)} %bitcast.68, bf16[8,2,3,48,384]{4,3,2,1,0:T(8,128)(2,1)S(1)} %copy-done.17), custom_call_target="tpu_custom_call" | custom-call | bytes 500000 | tf_op jit(solution)/shard_map/reduce_grad/pallas_call | solution.py:44
  160.3 4.9 %expand_grad.2.refs_3_ = bf16[1536,768]{1,0:T(8,128)(2,1)} custom-call(s32[1]{0:T(128)} %bitcast.25.refs_0_, bf16[1152,3072]{1,0:T(8,128)(2,1)S(1)} %bitcast.61, bf16[1152,768]{1,0:T(8,128)(2,1)S(1)} %bitcast.72, bf16[1536,768]{1,0:T(8,128)(2,1)} %reduce_grad.2.refs_3_), custom_call_target="tpu_custom_call" | custom-call | bytes 500000 | tf_op jit(solution)/shard_map/expand_grad/pallas_call | solution.py:44
  166.4 4.0 %reduce_grad.3.refs_3_.refs_1_.refs_5_ = bf16[1536,768]{1,0:T(8,128)(2,1)S(1)} custom-call(s32[1]{0:T(128)} %bitcast.25.refs_0_, bf16[1152,3072]{1,0:T(8,128)(2,1)S(1)} %bitcast.53, bf16[1152,768]{1,0:T(8,128)(2,1)S(1)} %bitcast.69, bf16[1536,768]{1,0:T(8,128)(2,1)} %expand_grad.2.refs_3_), custom_call_target="tpu_custom_call" | custom-call | bytes 500000 | tf_op jit(solution)/shard_map/reduce_grad/pallas_call | solution.py:44
  170.5 4.0 %expand_grad.3.refs_2_.refs_7_.refs_9_.refs_11_ = bf16[1536,768]{1,0:T(8,128)(2,1)S(1)} custom-call(s32[1]{0:T(128)} %bitcast.25.refs_0_, bf16[1152,3072]{1,0:T(8,128)(2,1)S(1)} %bitcast.63, bf16[1152,768]{1,0:T(8,128)(2,1)S(1)} %bitcast.73, bf16[1536,768]{1,0:T(8,128)(2,1)S(1)} %reduce_grad.3.refs_3_.refs_1_.refs_5_), custom_call_target="tpu_custom_call" | custom-call | bytes 500000 | tf_op jit(solution)/shard_map/expand_grad/pallas_call | solution.py:44
  174.5 1.4 copy-done.1
  175.9 1.7 copy-done.2
  178.4 5.3 %lon_forward.3 = (bf16[96,48,128]{2,1,0:T(8,128)(2,1)S(1)}, bf16[96,48,128]{2,1,0:T(8,128)(2,1)}) custom-call(bf16[16,3,48,384]{3,2,1,0:T(8,128)(2,1)} %all-to-all-done.2.refs_0_, bf16[192,192]{1,0:T(8,128)(2,1)S(1)} %copy-done.33, bf16[1536,768]{1,0:T(8,128)(2,1)S(1)} %copy-done.2), custom_call_target="tpu_custom_call" | custom-call | bytes 550000 | tf_op jit(solution)/shard_map/lon_forward/pallas_call | solution.py:44
  183.9 1.7 copy-done.3
  185.6 3.9 %halve.3 = (bf16[512,768]{1,0:T(8,128)(2,1)S(1)}, bf16[512,768]{1,0:T(8,128)(2,1)S(1)}, bf16[512,768]{1,0:T(8,128)(2,1)S(1)}, bf16[512,768]{1,0:T(8,128)(2,1)S(1...) custom-call(s32[3]{0:T(128)S(1)} %pad_add_fusion.refs_0_, ...), custom_call_target="tpu_custom_call" | custom-call | bytes 300000 | tf_op jit(solution)/shard_map/halve/pallas_call | solution.py:44
  189.5 1.8 collective-permute-start.5
  191.3 1.5 collective-permute-start.6
  192.8 1.5 collective-permute-start.7
  194.4 10.3 %mix_back.2 = (bf16[48,48,128]{2,1,0:T(8,128)(2,1)S(1)}, bf16[48,48,128]{2,1,0:T(8,128)(2,1)S(1)}, f32[528,256]{1,0:T(8,128)S(1)}) custom-call(bf16[96,48,128]{2,1,0:T(8,128)(2,1)S(1)} %get-tuple-element.126.refs_13_.refs_0_, bf16[96,48,128]{2,1,0:T(8,128)(2,1)} %collective-permute-done.2.refs_1_, bf16[24,192,256]{2,1,0:T(8,128)(2,1)S(1)} %copy-done.16, ...), custom_call_target="tpu_custom_call" | custom-call | bytes 1300000 | tf_op jit(solution)/shard_map/mix_back/pallas_call | solution.py:44
  204.7 4.8 %collective-permute-done.5.refs_2_.refs_4_ = bf16[512,768]{1,0:T(8,128)(2,1)S(1)} collective-permute-done((bf16[512,768]{1,0:T(8,128)(2,1)S(1)}, bf16[512,768]{1,0:T(8,128)(2,1)S(1)}, u32[]{:S(2)}, u32[]{:S(2)}) %collective-permute-start.5) | collective-permute-done | bytes 786464 | tf_op jit(solution)/shard_map/ppermute | solution.py:742
  209.5 1.3 collective-permute-done.6.refs_6_.refs_8_
  213.7 1.5 collective-permute-start.11
  215.7 10.3 %mix_back.3 = (bf16[48,48,128]{2,1,0:T(8,128)(2,1)S(1)}, bf16[48,48,128]{2,1,0:T(8,128)(2,1)S(1)}, f32[528,256]{1,0:T(8,128)S(1)}) custom-call(bf16[96,48,128]{2,1,0:T(8,128)(2,1)S(1)} %get-tuple-element.126.refs_13_.refs_0_, bf16[96,48,128]{2,1,0:T(8,128)(2,1)} %collective-permute-done.2.refs_1_, bf16[24,192,256]{2,1,0:T(8,128)(2,1)S(1)} %copy-done.16, ...), custom_call_target="tpu_custom_call" | custom-call | bytes 1300000 | tf_op jit(solution)/shard_map/mix_back/pallas_call | solution.py:44
  228.0 1.6 collective-permute-start.14
  229.6 1.5 collective-permute-start.15
  231.1 3.4 collective-permute-done.13.refs_1_
  236.1 2.0 lon_backward.3.refs_2_
  238.1 3.9 %all-to-all-start.3 = ((bf16[16,3,48,384]{3,2,1,0:T(8,128)(2,1)}), bf16[16,3,48,384]{3,2,1,0:T(8,128)(2,1)S(1)}, u32[]{:S(2)}, u32[]{:S(2)}) async-start(bf16[16,3,48,384]{3,2,1,0:T(8,128)(2,1)} %lon_backward.3.refs_2_), calls=%async_computation.3 | async-start | bytes 3538944 | tf_op jit(solution)/shard_map/all_to_all | solution.py:696
  244.5 2.6 collective-permute-start.17
  247.1 34.1 %all-to-all-done.3.refs_0_ = bf16[16,3,48,384]{3,2,1,0:T(8,128)(2,1)S(1)} async-done(((bf16[16,3,48,384]{3,2,1,0:T(8,128)(2,1)}), bf16[16,3,48,384]{3,2,1,0:T(8,128)(2,1)S(1)}, u32[]{:S(2)}, u32[]{:S(2)}) %all-to-all-start.3) | async-done | bytes 1769504 | tf_op jit(solution)/shard_map/all_to_all | solution.py:696
  282.3 3.3 collective-permute-start.19
  285.6 3.7 %collective-permute-done.18.refs_2_ = bf16[144,768]{1,0:T(8,128)(2,1)S(1)} collective-permute-done((bf16[144,768]{1,0:T(8,128)(2,1)S(1)}, bf16[144,768]{1,0:T(8,128)(2,1)S(1)}, u32[]{:S(2)}, u32[]{:S(2)}) %collective-permute-start.18) | collective-permute-done | bytes 221216 | tf_op jit(solution)/shard_map/ppermute | solution.py:742
  290.5 1.5 collective-permute-done.20.refs_6_
  292.0 1.8 merge.3
  296.9 9.6 %first_back.1 = (f32[45,24,768]{2,1,0:T(8,128)}, f32[1,768]{1,0:T(1,128)}, f32[1,768]{1,0:T(1,128)}) custom-call(bf16[2,3,4,45,768]{4,3,2,1,0:T(8,128)(2,1)} %bitcast.66, f32[2,3,4,48,768]{4,3,2,1,0:T(8,128)} %get-tuple-element.123.refs_1_, s32[24,45]{1,0:T(8,128)} %refs_2_.5, bf16[8,2,3,48,384]{4,3,2,1,0:T(8,128)(2,1)} %bitcast.70, f32[1,768]{1,0:T(1,128)} %copy-done.35, ...), custom_call_target="tpu_custom_call" | custom-call | bytes 900000 | tf_op jit(solution)/shard_map/first_back/pallas_call | solution.py:44
  309.0 2.4 merge.4
  311.4 1.8 collective-permute-start.27
  314.4 1.7 collective-permute-start.29
  317.6 2.3 copy-done.9
  320.0 9.4 %branch.1.refs_2_ = f32[45,24,768]{2,1,0:T(8,128)} custom-call(bf16[2,3,4,48,3072]{4,3,2,1,0:T(8,128)(2,1)S(1)} %bitcast.56, bf16[3072,768]{1,0:T(8,128)(2,1)S(1)} %copy-done.9, f32[2,3,4,48,768]{4,3,2,1,0:T(8,128)S(1)} %copy-done.13, f32[1,768]{1,0:T(1,128)S(1)} %reshape.115.refs_3_, f32[1,6912]{1,0:T(1,128)S(1)} %get-tuple-element.181.refs_4_.refs_0_), custom_call_target="tpu_custom_call" | custom-call | bytes 1000000 | tf_op jit(solution)/shard_map/branch/pallas_call | solution.py:44
  329.3 2.9 collective-permute-done.25.refs_1_
  332.2 1.9 copy-done.14
  336.0 3.4 collective-permute-done.26.refs_1_
  340.1 4.4 %widen.2 = (f32[3072,768]{1,0:T(8,128)}, f32[768,3072]{1,0:T(8,128)}, bf16[12,16,768]{2,1,0:T(8,128)(2,1)S(1)}, bf16[12,16,768]{2,1,0:T(8,128)(2,1)S(1)}) custom-call(s32[1]{0:T(128)} %bitcast.25.refs_0_, bf16[3456,768]{1,0:T(8,128)(2,1)S(1)} %bitcast.58, bf16[3456,768]{1,0:T(8,128)(2,1)S(1)} %bitcast.59, f32[1,6912]{1,0:T(1,128)S(1)} %get-tuple-element.192.refs_3_.refs_0_), custom_call_target="tpu_custom_call" | custom-call | bytes 500000 | tf_op jit(solution)/shard_map/widen/pallas_call | solution.py:44
  344.5 3.7 %copy-done.4 = f32[3072,768]{1,0:T(8,128)S(1)} copy-done((f32[3072,768]{1,0:T(8,128)S(1)}, f32[3072,768]{1,0:T(8,128)}, u32[]{:S(2)}) %copy-start.4) | copy-done | bytes 9437208
  348.2 2.3 collective-permute-start.31
  350.5 4.4 %widen.3 = (f32[3072,768]{1,0:T(8,128)}, f32[768,3072]{1,0:T(8,128)}, bf16[12,16,768]{2,1,0:T(8,128)(2,1)S(1)}, bf16[12,16,768]{2,1,0:T(8,128)(2,1)S(1)}) custom-call(s32[1]{0:T(128)} %bitcast.25.refs_0_, bf16[3456,768]{1,0:T(8,128)(2,1)S(1)} %collective-permute-done.32.refs_1_.refs_2_, ...), custom_call_target="tpu_custom_call", output_to_operand_aliasing={{0}: (3, {}), {1}: (4, {})} | custom-call | bytes 500000 | tf_op jit(solution)/shard_map/widen/pallas_call | solution.py:44
  (208 shorter events, 37.1 us)
Async XLA Ops:
  9.5 31.6 %all-to-all-start = ((bf16[16,3,48,384]{3,2,1,0:T(8,128)(2,1)}), bf16[16,3,48,384]{3,2,1,0:T(8,128)(2,1)S(1)}, u32[]{:S(2)}, u32[]{:S(2)}) async-start(bf16[16,3,48,384]{3,2,1,0:T(8,128)(2,1)} %bitcast.77), calls=%async_computation | async-start | bytes 3538944 | tf_op jit(solution)/shard_map/all_to_all | solution.py:696
  15.8 29.1 %copy-start.51 = (f32[2,768]{1,0:T(2,128)S(1)}, f32[2,768]{1,0:T(2,128)}, u32[]{:S(2)}) copy-start(f32[2,768]{1,0:T(2,128)} %param.27) | copy-start | bytes 18436
  15.8 29.2 %copy-start.52 = (f32[2,768]{1,0:T(2,128)S(1)}, f32[2,768]{1,0:T(2,128)}, u32[]{:S(2)}) copy-start(f32[2,768]{1,0:T(2,128)} %param.29) | copy-start | bytes 18436
  15.9 30.3 %copy-start.49 = (bf16[2,192,192]{2,1,0:T(8,128)(2,1)S(1)}, bf16[2,192,192]{2,1,0:T(8,128)(2,1)}, u32[]{:S(2)}) copy-start(bf16[2,192,192]{2,1,0:T(8,128)(2,1)} %constant.189.clone) | copy-start | bytes 442372
  15.9 30.3 %copy-start.50 = (bf16[2,192,192]{2,1,0:T(8,128)(2,1)S(1)}, bf16[2,192,192]{2,1,0:T(8,128)(2,1)}, u32[]{:S(2)}) copy-start(bf16[2,192,192]{2,1,0:T(8,128)(2,1)} %constant.188.clone) | copy-start | bytes 442372
  44.9 3.1 collective-permute-start
  46.1 18.9 %copy-start.19 = (bf16[256,256]{1,0:T(8,128)(2,1)}, bf16[256,256]{1,0:T(8,128)(2,1)S(1)}, u32[]{:S(2)}) copy-start(bf16[256,256]{1,0:T(8,128)(2,1)S(1)} %maximum_maximum_fusion.1.refs_6_.refs_7_) | copy-start | bytes 393220
  46.1 18.9 %copy-start.48 = (bf16[2,192,192]{2,1,0:T(8,128)(2,1)S(1)}, bf16[2,192,192]{2,1,0:T(8,128)(2,1)}, u32[]{:S(2)}) copy-start(bf16[2,192,192]{2,1,0:T(8,128)(2,1)} %constant.187.clone) | copy-start | bytes 442372
  46.2 21.6 %copy-start.21 = (bf16[256,256]{1,0:T(8,128)(2,1)}, bf16[256,256]{1,0:T(8,128)(2,1)S(1)}, u32[]{:S(2)}) copy-start(bf16[256,256]{1,0:T(8,128)(2,1)S(1)} %maximum_maximum_fusion.refs_4_.refs_5_) | copy-start | bytes 393220
  46.2 21.5 %copy-start.27 = (bf16[192,192]{1,0:T(8,128)(2,1)}, bf16[192,192]{1,0:T(8,128)(2,1)S(1)}, u32[]{:S(2)}) copy-start(bf16[192,192]{1,0:T(8,128)(2,1)S(1)} %get-tuple-element.219.refs_3_.refs_4_) | copy-start | bytes 221188
  46.2 21.5 %copy-start.29 = (bf16[192,192]{1,0:T(8,128)(2,1)}, bf16[192,192]{1,0:T(8,128)(2,1)S(1)}, u32[]{:S(2)}) copy-start(bf16[192,192]{1,0:T(8,128)(2,1)S(1)} %get-tuple-element.220.refs_2_.refs_3_) | copy-start | bytes 221188
  64.9 2.8 collective-permute-start.1
  69.8 29.4 %all-to-all-start.1 = ((bf16[16,3,48,384]{3,2,1,0:T(8,128)(2,1)}), bf16[16,3,48,384]{3,2,1,0:T(8,128)(2,1)S(1)}, u32[]{:S(2)}, u32[]{:S(2)}) async-start(bf16[16,3,48,384]{3,2,1,0:T(8,128)(2,1)} %lon_backward.2), calls=%async_computation.1 | async-start | bytes 3538944 | tf_op jit(solution)/shard_map/all_to_all | solution.py:696
  100.4 8.1 %copy-start.38 = (f32[3072]{0:T(1024)S(1)}, f32[3072]{0:T(1024)}, u32[]{:S(2)}) copy-start(f32[3072]{0:T(1024)} %param.33) | copy-start | bytes 36868
  136.0 24.3 %slice-start.4 = ((s8[7077888]{0:T(1024)(128)(4,1)}), s8[2883584]{0:T(1024)(128)(4,1)S(1)}, s32[]{:S(2)}) async-start(s8[7077888]{0:T(1024)(128)(4,1)} %bitcast.60), calls=%async_computation.8 | async-start | bytes 5767168
  144.8 31.1 %all-to-all-start.2 = ((bf16[16,3,48,384]{3,2,1,0:T(8,128)(2,1)}), bf16[16,3,48,384]{3,2,1,0:T(8,128)(2,1)}, u32[]{:S(2)}, u32[]{:S(2)}) async-start(bf16[16,3,48,384]{3,2,1,0:T(8,128)(2,1)} %bitcast.75), calls=%async_computation.2 | async-start | bytes 3538944 | tf_op jit(solution)/shard_map/all_to_all | solution.py:696
  160.3 6.1 %slice-start = ((s8[7077888]{0:T(1024)(128)(4,1)}), s8[4194304]{0:T(1024)(128)(4,1)S(1)}, s32[]{:S(2)}) async-start(s8[7077888]{0:T(1024)(128)(4,1)} %bitcast.52), calls=%async_computation.4 | async-start | bytes 8388608
  160.3 10.1 %slice-start.6 = ((s8[7077888]{0:T(1024)(128)(4,1)}), s8[4194304]{0:T(1024)(128)(4,1)S(1)}, s32[]{:S(2)}) async-start(s8[7077888]{0:T(1024)(128)(4,1)} %bitcast.62), calls=%async_computation.10 | async-start | bytes 8388608
  165.2 18.6 %collective-permute-start.4 = (bf16[1536,768]{1,0:T(8,128)(2,1)}, bf16[1536,768]{1,0:T(8,128)(2,1)}, u32[]{:S(2)}, u32[]{:S(2)}) collective-permute-start(bf16[1536,768]{1,0:T(8,128)(2,1)} %expand_grad.2.refs_3_), channel_id=1, source_target_pairs={{0,1},{1,0},{2,3},{3,2},{4,5},{5,4},{6,7},{7,6},{8,9},{9,8},{10,11... | collective-permute-start | bytes 7077896 | tf_op jit(solution)/shard_map/ppermute | solution.py:742
  165.3 18.6 %collective-permute-start.3 = (bf16[1536,768]{1,0:T(8,128)(2,1)}, bf16[1536,768]{1,0:T(8,128)(2,1)}, u32[]{:S(2)}, u32[]{:S(2)}) collective-permute-start(bf16[1536,768]{1,0:T(8,128)(2,1)} %reduce_grad.2.refs_3_), channel_id=1, source_target_pairs={{0,1},{1,0},{2,3},{3,2},{4,5},{5,4},{6,7},{7,6},{8,9},{9,8},{10,11... | collective-permute-start | bytes 7077896 | tf_op jit(solution)/shard_map/ppermute | solution.py:742
  183.8 10.6 %collective-permute-start.2 = (bf16[96,48,128]{2,1,0:T(8,128)(2,1)}, bf16[96,48,128]{2,1,0:T(8,128)(2,1)}, u32[]{:S(2)}, u32[]{:S(2)}) collective-permute-start(bf16[96,48,128]{2,1,0:T(8,128)(2,1)} %get-tuple-element.127), channel_id=1, source_target_pairs={{0,1},{1,0},{2,3},{3,2},{4,5},{5,4},{6,7},{7,6},{8,9},{9,8},{10,11... | collective-permute-start | bytes 3538952 | tf_op jit(solution)/shard_map/ppermute | solution.py:699
  185.6 8.8 %copy-start.16 = (bf16[24,192,256]{2,1,0:T(8,128)(2,1)S(1)}, bf16[24,192,256]{2,1,0:T(8,128)(2,1)}, u32[]{:S(2)}) copy-start(bf16[24,192,256]{2,1,0:T(8,128)(2,1)} %copy-done.15) | copy-start | bytes 7077892
  185.6 8.8 %copy-start.20 = (bf16[256,256]{1,0:T(8,128)(2,1)S(1)}, bf16[256,256]{1,0:T(8,128)(2,1)}, u32[]{:S(2)}) copy-start(bf16[256,256]{1,0:T(8,128)(2,1)} %copy-done.19) | copy-start | bytes 393220
  185.6 8.8 %copy-start.22 = (bf16[256,256]{1,0:T(8,128)(2,1)S(1)}, bf16[256,256]{1,0:T(8,128)(2,1)}, u32[]{:S(2)}) copy-start(bf16[256,256]{1,0:T(8,128)(2,1)} %copy-done.21) | copy-start | bytes 393220
  185.6 8.8 %copy-start.28 = (bf16[192,192]{1,0:T(8,128)(2,1)S(1)}, bf16[192,192]{1,0:T(8,128)(2,1)}, u32[]{:S(2)}) copy-start(bf16[192,192]{1,0:T(8,128)(2,1)} %copy-done.27) | copy-start | bytes 221188
  185.6 8.8 %copy-start.30 = (bf16[192,192]{1,0:T(8,128)(2,1)S(1)}, bf16[192,192]{1,0:T(8,128)(2,1)}, u32[]{:S(2)}) copy-start(bf16[192,192]{1,0:T(8,128)(2,1)} %copy-done.29) | copy-start | bytes 221188
  189.5 20.0 %collective-permute-start.5 = (bf16[512,768]{1,0:T(8,128)(2,1)S(1)}, bf16[512,768]{1,0:T(8,128)(2,1)S(1)}, u32[]{:S(2)}, u32[]{:S(2)}) collective-permute-start(bf16[512,768]{1,0:T(8,128)(2,1)S(1)} %get-tuple-element.132), channel_id=1, source_target_pairs={{0,2},{1,3},{2,0},{3,1},{4,6},{5,7},{6,4},{7,5},{8,10},{9,11},{10,... | collective-permute-start | bytes 2359304 | tf_op jit(solution)/shard_map/ppermute | solution.py:742
  191.3 19.5 %collective-permute-start.6 = (bf16[512,768]{1,0:T(8,128)(2,1)S(1)}, bf16[512,768]{1,0:T(8,128)(2,1)S(1)}, u32[]{:S(2)}, u32[]{:S(2)}) collective-permute-start(bf16[512,768]{1,0:T(8,128)(2,1)S(1)} %get-tuple-element.134), channel_id=1, source_target_pairs={{0,4},{1,5},{2,6},{3,7},{4,0},{5,1},{6,2},{7,3},{8,12},{9,13},{10,... | collective-permute-start | bytes 2359304 | tf_op jit(solution)/shard_map/ppermute | solution.py:742
  192.8 19.2 %collective-permute-start.7 = (bf16[512,768]{1,0:T(8,128)(2,1)S(1)}, bf16[512,768]{1,0:T(8,128)(2,1)S(1)}, u32[]{:S(2)}, u32[]{:S(2)}) collective-permute-start(bf16[512,768]{1,0:T(8,128)(2,1)S(1)} %get-tuple-element.136), channel_id=1, source_target_pairs={{0,8},{1,9},{2,10},{3,11},{4,12},{5,13},{6,14},{7,15},{8,0},{9,1},... | collective-permute-start | bytes 2359304 | tf_op jit(solution)/shard_map/ppermute | solution.py:742
  213.1 13.6 %collective-permute-start.10 = (bf16[256,768]{1,0:T(8,128)(2,1)S(1)}, bf16[256,768]{1,0:T(8,128)(2,1)S(1)}, u32[]{:S(2)}, u32[]{:S(2)}) collective-permute-start(bf16[256,768]{1,0:T(8,128)(2,1)S(1)} %get-tuple-element.141), channel_id=1, source_target_pairs={{0,4},{1,5},{2,6},{3,7},{4,0},{5,1},{6,2},{7,3},{8,12},{9,13},{10,... | collective-permute-start | bytes 1179656 | tf_op jit(solution)/shard_map/ppermute | solution.py:742
  213.7 13.0 %collective-permute-start.11 = (bf16[256,768]{1,0:T(8,128)(2,1)S(1)}, bf16[256,768]{1,0:T(8,128)(2,1)S(1)}, u32[]{:S(2)}, u32[]{:S(2)}) collective-permute-start(bf16[256,768]{1,0:T(8,128)(2,1)S(1)} %get-tuple-element.143), channel_id=1, source_target_pairs={{0,8},{1,9},{2,10},{3,11},{4,12},{5,13},{6,14},{7,15},{8,0},{9,1},... | collective-permute-start | bytes 1179656 | tf_op jit(solution)/shard_map/ppermute | solution.py:742
  215.2 11.5 %collective-permute-start.12 = (bf16[256,768]{1,0:T(8,128)(2,1)S(1)}, bf16[256,768]{1,0:T(8,128)(2,1)S(1)}, u32[]{:S(2)}, u32[]{:S(2)}) collective-permute-start(bf16[256,768]{1,0:T(8,128)(2,1)S(1)} %get-tuple-element.145), channel_id=1, source_target_pairs={{0,2},{1,3},{2,0},{3,1},{4,6},{5,7},{6,4},{7,5},{8,10},{9,11},{10,... | collective-permute-start | bytes 1179656 | tf_op jit(solution)/shard_map/ppermute | solution.py:742
  226.0 10.0 %collective-permute-start.9 = (bf16[48,48,128]{2,1,0:T(8,128)(2,1)S(1)}, bf16[48,48,128]{2,1,0:T(8,128)(2,1)S(1)}, u32[]{:S(2)}, u32[]{:S(2)}) collective-permute-start(bf16[48,48,128]{2,1,0:T(8,128)(2,1)S(1)} %get-tuple-element.140), channel_id=1, source_target_pairs={{0,1},{1,0},{2,3},{3,2},{4,5},{5,4},{6,7},{7,6},{8,9},{9,8},{10,11... | collective-permute-start | bytes 1769480 | tf_op jit(solution)/shard_map/ppermute | solution.py:699
  226.1 10.0 %collective-permute-start.8 = (bf16[48,48,128]{2,1,0:T(8,128)(2,1)S(1)}, bf16[48,48,128]{2,1,0:T(8,128)(2,1)S(1)}, u32[]{:S(2)}, u32[]{:S(2)}) collective-permute-start(bf16[48,48,128]{2,1,0:T(8,128)(2,1)S(1)} %get-tuple-element.139), channel_id=1, source_target_pairs={{0,1},{1,0},{2,3},{3,2},{4,5},{5,4},{6,7},{7,6},{8,9},{9,8},{10,11... | collective-permute-start | bytes 1769480 | tf_op jit(solution)/shard_map/ppermute | solution.py:699
  227.5 7.0 %collective-permute-start.13 = (bf16[128,768]{1,0:T(8,128)(2,1)S(1)}, bf16[128,768]{1,0:T(8,128)(2,1)S(1)}, u32[]{:S(2)}, u32[]{:S(2)}) collective-permute-start(bf16[128,768]{1,0:T(8,128)(2,1)S(1)} %get-tuple-element.147), channel_id=1, source_target_pairs={{0,8},{1,9},{2,10},{3,11},{4,12},{5,13},{6,14},{7,15},{8,0},{9,1},... | collective-permute-start | bytes 589832 | tf_op jit(solution)/shard_map/ppermute | solution.py:742
  228.0 6.6 %collective-permute-start.14 = (bf16[128,768]{1,0:T(8,128)(2,1)S(1)}, bf16[128,768]{1,0:T(8,128)(2,1)S(1)}, u32[]{:S(2)}, u32[]{:S(2)}) collective-permute-start(bf16[128,768]{1,0:T(8,128)(2,1)S(1)} %get-tuple-element.149), channel_id=1, source_target_pairs={{0,2},{1,3},{2,0},{3,1},{4,6},{5,7},{6,4},{7,5},{8,10},{9,11},{10,... | collective-permute-start | bytes 589832 | tf_op jit(solution)/shard_map/ppermute | solution.py:742
  229.6 6.3 %collective-permute-start.15 = (bf16[128,768]{1,0:T(8,128)(2,1)S(1)}, bf16[128,768]{1,0:T(8,128)(2,1)S(1)}, u32[]{:S(2)}, u32[]{:S(2)}) collective-permute-start(bf16[128,768]{1,0:T(8,128)(2,1)S(1)} %get-tuple-element.151), channel_id=1, source_target_pairs={{0,4},{1,5},{2,6},{3,7},{4,0},{5,1},{6,2},{7,3},{8,12},{9,13},{10,... | collective-permute-start | bytes 589832 | tf_op jit(solution)/shard_map/ppermute | solution.py:742
  238.1 43.0 %all-to-all-start.3 = ((bf16[16,3,48,384]{3,2,1,0:T(8,128)(2,1)}), bf16[16,3,48,384]{3,2,1,0:T(8,128)(2,1)S(1)}, u32[]{:S(2)}, u32[]{:S(2)}) async-start(bf16[16,3,48,384]{3,2,1,0:T(8,128)(2,1)} %lon_backward.3.refs_2_), calls=%async_computation.3 | async-start | bytes 3538944 | tf_op jit(solution)/shard_map/all_to_all | solution.py:696
  242.1 1.4 collective-permute-start.16
  244.5 36.6 %collective-permute-start.17 = (bf16[432,768]{1,0:T(8,128)(2,1)}, bf16[432,768]{1,0:T(8,128)(2,1)S(1)}, u32[]{:S(2)}, u32[]{:S(2)}) collective-permute-start(bf16[432,768]{1,0:T(8,128)(2,1)} %get-tuple-element.159), channel_id=1, source_target_pairs={{0,16},{1,17},{2,18},{3,19},{4,20},{5,21},{6,22},{7,23},{8,24},{9,... | collective-permute-start | bytes 1990664 | tf_op jit(solution)/shard_map/ppermute | solution.py:742
  281.1 36.5 %slice-start.2 = ((s8[7077888]{0:T(1024)(128)(4,1)}), s8[4194304]{0:T(1024)(128)(4,1)S(1)}, s32[]{:S(2)}) async-start(s8[7077888]{0:T(1024)(128)(4,1)} %bitcast.54), calls=%async_computation.6 | async-start | bytes 8388608
  282.3 7.0 %collective-permute-start.18 = (bf16[144,768]{1,0:T(8,128)(2,1)S(1)}, bf16[144,768]{1,0:T(8,128)(2,1)S(1)}, u32[]{:S(2)}, u32[]{:S(2)}) collective-permute-start(bf16[144,768]{1,0:T(8,128)(2,1)S(1)} %get-tuple-element.161), channel_id=1, source_target_pairs={{0,8},{1,9},{2,10},{3,11},{4,12},{5,13},{6,14},{7,15},{8,0},{9,1},... | collective-permute-start | bytes 663560 | tf_op jit(solution)/shard_map/ppermute | solution.py:742
  282.3 8.2 %collective-permute-start.19 = (bf16[144,768]{1,0:T(8,128)(2,1)S(1)}, bf16[144,768]{1,0:T(8,128)(2,1)S(1)}, u32[]{:S(2)}, u32[]{:S(2)}) collective-permute-start(bf16[144,768]{1,0:T(8,128)(2,1)S(1)} %get-tuple-element.163), channel_id=1, source_target_pairs={{0,2},{1,3},{2,0},{3,1},{4,6},{5,7},{6,4},{7,5},{8,10},{9,11},{10,... | collective-permute-start | bytes 663560 | tf_op jit(solution)/shard_map/ppermute | solution.py:742
  285.6 6.4 %collective-permute-start.20 = (bf16[144,768]{1,0:T(8,128)(2,1)S(1)}, bf16[144,768]{1,0:T(8,128)(2,1)S(1)}, u32[]{:S(2)}, u32[]{:S(2)}) collective-permute-start(bf16[144,768]{1,0:T(8,128)(2,1)S(1)} %get-tuple-element.165), channel_id=1, source_target_pairs={{0,4},{1,5},{2,6},{3,7},{4,0},{5,1},{6,2},{7,3},{8,12},{9,13},{10,... | collective-permute-start | bytes 663560 | tf_op jit(solution)/shard_map/ppermute | solution.py:742
  295.3 12.6 %collective-permute-start.22 = (bf16[288,768]{1,0:T(8,128)(2,1)}, bf16[288,768]{1,0:T(8,128)(2,1)}, u32[]{:S(2)}, u32[]{:S(2)}) collective-permute-start(bf16[288,768]{1,0:T(8,128)(2,1)} %get-tuple-element.175), channel_id=1, source_target_pairs={{0,4},{1,5},{2,6},{3,7},{4,0},{5,1},{6,2},{7,3},{8,12},{9,13},{10,... | collective-permute-start | bytes 1327112 | tf_op jit(solution)/shard_map/ppermute | solution.py:742
  295.6 12.4 %collective-permute-start.23 = (bf16[288,768]{1,0:T(8,128)(2,1)}, bf16[288,768]{1,0:T(8,128)(2,1)}, u32[]{:S(2)}, u32[]{:S(2)}) collective-permute-start(bf16[288,768]{1,0:T(8,128)(2,1)} %get-tuple-element.177), channel_id=1, source_target_pairs={{0,8},{1,9},{2,10},{3,11},{4,12},{5,13},{6,14},{7,15},{8,0},{9,1},... | collective-permute-start | bytes 1327112 | tf_op jit(solution)/shard_map/ppermute | solution.py:742
  296.6 11.4 %collective-permute-start.24 = (bf16[288,768]{1,0:T(8,128)(2,1)}, bf16[288,768]{1,0:T(8,128)(2,1)}, u32[]{:S(2)}, u32[]{:S(2)}) collective-permute-start(bf16[288,768]{1,0:T(8,128)(2,1)} %get-tuple-element.179), channel_id=1, source_target_pairs={{0,2},{1,3},{2,0},{3,1},{4,6},{5,7},{6,4},{7,5},{8,10},{9,11},{10,... | collective-permute-start | bytes 1327112 | tf_op jit(solution)/shard_map/ppermute | solution.py:742
  296.9 9.7 %copy-start.37 = (f32[1,3072]{1,0:T(1,128)S(1)}, f32[1,3072]{1,0:T(1,128)}, u32[]{:S(2)}) copy-start(f32[1,3072]{1,0:T(1,128)} %copy-done.36) | copy-start | bytes 36868
  296.9 9.7 %copy-start.39 = (f32[1,768]{1,0:T(1,128)S(1)}, f32[1,768]{1,0:T(1,128)}, u32[]{:S(2)}) copy-start(f32[1,768]{1,0:T(1,128)} %get-tuple-element.169.refs_2_) | copy-start | bytes 9220
  296.9 9.7 %copy-start.40 = (f32[1,768]{1,0:T(1,128)S(1)}, f32[1,768]{1,0:T(1,128)}, u32[]{:S(2)}) copy-start(f32[1,768]{1,0:T(1,128)} %get-tuple-element.170.refs_3_) | copy-start | bytes 9220
  296.9 9.7 %copy-start.41 = (f32[1,768]{1,0:T(1,128)S(1)}, f32[1,768]{1,0:T(1,128)}, u32[]{:S(2)}) copy-start(f32[1,768]{1,0:T(1,128)} %get-tuple-element.171.refs_4_) | copy-start | bytes 9220
  296.9 11.1 %copy-start.26 = (bf16[288,768]{1,0:T(8,128)(2,1)S(1)}, bf16[288,768]{1,0:T(8,128)(2,1)}, u32[]{:S(2)}) copy-start(bf16[288,768]{1,0:T(8,128)(2,1)} %copy-done.25) | copy-start | bytes 1327108
  296.9 20.7 %slice-start.3 = ((s8[7077888]{0:T(1024)(128)(4,1)}), s8[2883584]{0:T(1024)(128)(4,1)S(1)}, s32[]{:S(2)}) async-start(s8[7077888]{0:T(1024)(128)(4,1)} %bitcast.54), calls=%async_computation.7 | async-start | bytes 5767168
  309.0 8.6 %copy-start.55 = (f32[768]{0:T(1024)S(1)}, f32[768]{0:T(1024)}, u32[]{:S(2)}) copy-start(f32[768]{0:T(1024)} %param.35) | copy-start | bytes 9220
  309.0 8.6 %copy-start.13 = (f32[2,3,4,48,768]{4,3,2,1,0:T(8,128)S(1)}, f32[2,3,4,48,768]{4,3,2,1,0:T(8,128)}, u32[]{:S(2)}) copy-start(f32[2,3,4,48,768]{4,3,2,1,0:T(8,128)} %get-tuple-element.121.refs_0_.refs_2_) | copy-start | bytes 10616836
  311.4 22.7 %collective-permute-start.27 = (bf16[576,768]{1,0:T(8,128)(2,1)S(1)}, bf16[576,768]{1,0:T(8,128)(2,1)S(1)}, u32[]{:S(2)}, u32[]{:S(2)}) collective-permute-start(bf16[576,768]{1,0:T(8,128)(2,1)S(1)} %get-tuple-element.186), channel_id=1, source_target_pairs={{0,2},{1,3},{2,0},{3,1},{4,6},{5,7},{6,4},{7,5},{8,10},{9,11},{10,... | collective-permute-start | bytes 2654216 | tf_op jit(solution)/shard_map/ppermute | solution.py:742
  313.3 20.9 %collective-permute-start.28 = (bf16[576,768]{1,0:T(8,128)(2,1)S(1)}, bf16[576,768]{1,0:T(8,128)(2,1)S(1)}, u32[]{:S(2)}, u32[]{:S(2)}) collective-permute-start(bf16[576,768]{1,0:T(8,128)(2,1)S(1)} %get-tuple-element.188), channel_id=1, source_target_pairs={{0,4},{1,5},{2,6},{3,7},{4,0},{5,1},{6,2},{7,3},{8,12},{9,13},{10,... | collective-permute-start | bytes 2654216 | tf_op jit(solution)/shard_map/ppermute | solution.py:742
  314.4 19.8 %collective-permute-start.29 = (bf16[576,768]{1,0:T(8,128)(2,1)S(1)}, bf16[576,768]{1,0:T(8,128)(2,1)S(1)}, u32[]{:S(2)}, u32[]{:S(2)}) collective-permute-start(bf16[576,768]{1,0:T(8,128)(2,1)S(1)} %get-tuple-element.190), channel_id=1, source_target_pairs={{0,8},{1,9},{2,10},{3,11},{4,12},{5,13},{6,14},{7,15},{8,0},{9,1},... | collective-permute-start | bytes 2654216 | tf_op jit(solution)/shard_map/ppermute | solution.py:742
  316.0 1.2 collective-permute-start.21
  317.2 14.9 %collective-permute-start.25 = (f32[1,6912]{1,0:T(1,128)S(1)}, f32[1,6912]{1,0:T(1,128)S(1)}, u32[]{:S(2)}, u32[]{:S(2)}) collective-permute-start(f32[1,6912]{1,0:T(1,128)S(1)} %get-tuple-element.183), channel_id=1, source_target_pairs={{0,2},{1,3},{2,0},{3,1},{4,6},{5,7},{6,4},{7,5},{8,10},{9,11},{10,... | collective-permute-start | bytes 82952 | tf_op jit(solution)/shard_map/ppermute | solution.py:742
  335.4 15.1 %collective-permute-start.32 = (bf16[3456,768]{1,0:T(8,128)(2,1)S(1)}, bf16[3456,768]{1,0:T(8,128)(2,1)S(1)}, u32[]{:S(2)}, u32[]{:S(2)}) collective-permute-start(bf16[3456,768]{1,0:T(8,128)(2,1)S(1)} %bitcast.85), channel_id=1, source_target_pairs={{0,1},{1,0},{2,3},{3,2},{4,5},{5,4},{6,7},{7,6},{8,9},{9,8},{10,11... | collective-permute-start | bytes 15925256 | tf_op jit(solution)/shard_map/ppermute | solution.py:742
  335.5 3.9 %collective-permute-start.26 = (f32[1,6912]{1,0:T(1,128)S(1)}, f32[1,6912]{1,0:T(1,128)S(1)}, u32[]{:S(2)}, u32[]{:S(2)}) collective-permute-start(f32[1,6912]{1,0:T(1,128)S(1)} %get-tuple-element.185), channel_id=1, source_target_pairs={{0,4},{1,5},{2,6},{3,7},{4,0},{5,1},{6,2},{7,3},{8,12},{9,13},{10,... | collective-permute-start | bytes 82952 | tf_op jit(solution)/shard_map/ppermute | solution.py:742
  339.4 5.1 %collective-permute-start.30 = (f32[1,6912]{1,0:T(1,128)S(1)}, f32[1,6912]{1,0:T(1,128)S(1)}, u32[]{:S(2)}, u32[]{:S(2)}) collective-permute-start(f32[1,6912]{1,0:T(1,128)S(1)} %get-tuple-element.193), channel_id=1, source_target_pairs={{0,8},{1,9},{2,10},{3,11},{4,12},{5,13},{6,14},{7,15},{8,0},{9,1},... | collective-permute-start | bytes 82952 | tf_op jit(solution)/shard_map/ppermute | solution.py:742
  348.2 6.7 %collective-permute-start.31 = (f32[1,6912]{1,0:T(1,128)S(1)}, f32[1,6912]{1,0:T(1,128)S(1)}, u32[]{:S(2)}, u32[]{:S(2)}) collective-permute-start(f32[1,6912]{1,0:T(1,128)S(1)} %get-tuple-element.196), channel_id=1, source_target_pairs={{0,16},{1,17},{2,18},{3,19},{4,20},{5,21},{6,22},{7,23},{8,24},{9,... | collective-permute-start | bytes 82952 | tf_op jit(solution)/shard_map/ppermute | solution.py:742
  (37 other events, 100.9 us)

commit v5 on v4

--- a/solution.py
+++ b/solution.py
@@ -29,13 +29,15 @@
     return (value + step - 1) // step * step
 
 
-def call(kernel, args, out_shape, us, after=(), in_specs=None, prefetch=(), vmem=12, **kw):
+def call(kernel, args, out_shape, us, after=(), in_specs=None, prefetch=(), vmem=12, hbm=(), pin=False, **kw):
     outs = out_shape if isinstance(out_shape, (list, tuple)) else [out_shape]
     lead, n_in, n_after = len(prefetch), len(args), len(after)
 
     def body(*refs):
         kernel(*refs[: lead + n_in], *refs[lead + n_in + n_after :])
 
+    if pin:
+        args = [pltpu.with_memory_space_constraint(x, pltpu.HBM) for x in args]
     grid = kw.pop("grid", (1,))
     whole = lambda x: pl.BlockSpec(x.shape, lambda *_, n=len(x.shape): (0,) * n)
     specs = list(in_specs) if in_specs is not None else [whole(a) for a in args]
@@ -50,7 +52,7 @@
             out_specs=out_specs,
             scratch_shapes=kw.pop("scratch_shapes", ()),
         ),
-        out_shape=outs,
+        out_shape=[pltpu.HBM(o.shape, o.dtype) if k in hbm else o for k, o in enumerate(outs)],
         compiler_params=pltpu.CompilerParams(vmem_limit_bytes=vmem * 1024 * 1024),
         cost_estimate=pl.CostEstimate(
             flops=0, bytes_accessed=int(us * 1e5), transcendentals=0
@@ -61,7 +63,8 @@
 
 
 SPLIT = 2
-UNROLL = 2
+UNROLL = 1
+WIDE = 12
 
 
 def lon_table(lon_size, col_devs, cols_here, cols_pad, slots, slots_pad):
@@ -203,14 +206,20 @@
     for j in range(PACK):
         x = pad_rows(x_ref[half, 0, j].astype(F32), rows)
         xhat, _ = stats(x)
-        y = mask_column(mask_ref, first + j, rows) * (xhat * gain_ref[...] + shift_ref[...])
+        y = mask_column(mask_ref, first + j, rows) * (xhat * gain_ref[...][None] + shift_ref[...][None])
         normed_ref[half, 0, j] = y.astype(BF)
         lats.append(y)
     store_packed(out_ref, half, lats)
 
 
+def pad_kernel(x_ref, out_ref):
+    rows = out_ref.shape[3]
+    for j in range(PACK):
+        out_ref[0, 0, j] = pad_rows(x_ref[0, 0, j].astype(F32), rows).astype(BF)
+
+
 def second_kernel(
-    x_ref, normed_ref, mask_ref, cot_ref, got_ref, gain_ref, shift_ref, resid_ref, tok_ref, cot_out
+    x_ref, normed_ref, mask_ref, got_ref, gain_ref, shift_ref, resid_ref, tok_ref
 ):
     rows = normed_ref.shape[3]
     half, first = 0, pl.program_id(0) * PACK
@@ -222,7 +231,6 @@
         resid_ref[half, 0, j] = resid
         xhat, _ = stats(resid)
         tok_ref[half, 0, j] = (xhat * gain_ref[...] + shift_ref[...]).astype(BF)
-        cot_out[half, 0, j] = pad_rows(cot_ref[half, 0, j].astype(F32), rows).astype(BF)
 
 
 def third_kernel(
@@ -239,13 +247,13 @@
     lats = []
     for j in range(PACK):
         xhat, inv = stats(resid_ref[half, 0, j])
-        gtok = gtok_ref[half, 0, j]
+        gtok = gtok_ref[half, 0, j].astype(F32)
         cot = cot_ref[half, 0, j].astype(F32)
         ggain_ref[...] += jnp.sum(gtok * xhat, axis=0, keepdims=True)
         gshift_ref[...] += jnp.sum(gtok, axis=0, keepdims=True)
         gbias_ref[...] += jnp.sum(cot, axis=0, keepdims=True)
         gres = cot + norm_back(gtok, xhat, inv, gain_ref[...])
-        gresid_ref[half, 0, j] = gres
+        gresid_ref[half, 0, j] = gres.astype(gresid_ref.dtype)
         lats.append(mask_column(mask_ref, first + j, gres.shape[0]) * gres)
     store_packed(send_ref, half, lats)
 
@@ -268,7 +276,7 @@
     for j in range(PACK):
         x = pad_rows(x_ref[half, 0, j].astype(F32), rows)
         xhat, inv = stats(x)
-        gres = gresid_ref[half, 0, j]
+        gres = gresid_ref[half, 0, j].astype(F32)
         grad = mask_column(mask_ref, first + j, rows) * (gres + got[j])
         ggain_ref[...] += jnp.sum(grad * xhat, axis=0, keepdims=True)
         gshift_ref[...] += jnp.sum(grad, axis=0, keepdims=True)
@@ -280,30 +288,36 @@
 
 
 def chain_kernel(
-    tok_ref, cot_ref, up_ref, bias_ref, down_ref, act_ref, gpre_ref, gtok_ref, gbias_ref
+    tok_ref, cot_ref, up_ref, bias_ref, down_ref, act_ref, gpre_ref, gtok_ref, gbias_ref, sum_ref
 ):
     @pl.when(pl.program_id(0) == 0)
     def _():
-        gtok_ref[...] = jnp.zeros_like(gtok_ref)
+        sum_ref[...] = jnp.zeros_like(sum_ref)
 
     pre = jnp.dot(tok_ref[...], up_ref[...], preferred_element_type=F32) + bias_ref[...]
-    squash = gelu_parts(pre)
-    act_ref[...] = (0.5 * pre * (1.0 + squash)).astype(BF)
+    gate = gelu_gate(pre)
+    act_ref[...] = (pre * gate).astype(BF)
     gact = lax.dot_general(cot_ref[...], down_ref[...], ACROSS, preferred_element_type=F32)
-    gpre = gelu_slope(pre, squash) * gact
+    gpre = gelu_slope(pre, gate) * gact
     gbias_ref[...] = jnp.sum(gpre, axis=0, keepdims=True)
     gpre = gpre.astype(BF)
     gpre_ref[...] = gpre
-    gtok_ref[...] += lax.dot_general(gpre, up_ref[...], ACROSS, preferred_element_type=F32)
-
-
-def weight_grad_kernel(core_ref, left_ref, right_ref, out_ref):
+    sum_ref[...] += lax.dot_general(gpre, up_ref[...], ACROSS, preferred_element_type=F32)
+
+    @pl.when(pl.program_id(0) == pl.num_programs(0) - 1)
+    def _():
+        gtok_ref[...] = sum_ref[...].astype(gtok_ref.dtype)
+
+
+def weight_grad_kernel(core_ref, left_ref, right_ref, out_ref, token_ref):
+    token_ref[...] = jnp.zeros_like(token_ref)
     out_ref[...] = lax.dot_general(
         left_ref[...], right_ref[...], OUTER, preferred_element_type=F32
     ).astype(BF)
 
 
-def branch_kernel(act_ref, down_ref, resid_ref, bias_ref, out_ref):
+def branch_kernel(act_ref, down_ref, resid_ref, bias_ref, out_ref, token_ref):
+    token_ref[...] = jnp.zeros_like(token_ref)
     cols = resid_ref.shape[3]
     rows = CORES * PACK * cols
     act = act_ref[...].reshape(rows, act_ref.shape[-1])
@@ -470,7 +484,7 @@
                 at = (r * groups + g) * PACK + j
                 turn_ref[pl.ds(at, rows, stride=lats), :] = tile
 
-    @pl.loop(0, slots)
+    @pl.loop(0, slots, unroll=4)
     def _(s):
         own_ref[s] = turn_ref[pl.ds(pl.multiple_of(s * lats, 8), lats), :].astype(BF)
         other_ref[s] = turn_ref[
@@ -499,18 +513,30 @@
                 out_ref[r * col_devs + c, g] = packed[c * cols : (c + 1) * cols]
 
 
-def gelu_parts(v):
-    squash = jnp.tanh(gelu_root * (v + gelu_cube * (v * v * v)))
-    return squash
-
-
-def gelu(v):
-    return 0.5 * v * (1.0 + gelu_parts(v))
-
-
-def gelu_slope(v, squash):
-    inner = gelu_root * (1.0 + 3.0 * gelu_cube * (v * v))
-    return 0.5 * (1.0 + squash) + 0.5 * v * (1.0 - squash * squash) * inner
+def gelu_gate(v):
+    inner = v * (gelu_root * gelu_cube * (v * v) + gelu_root)
+    return 0.5 * jnp.tanh(inner) + 0.5
+
+
+def gelu_slope(v, gate):
+    inner = 6.0 * gelu_root * gelu_cube * (v * v) + 2.0 * gelu_root
+    return gate + (v * gate) * (1.0 - gate) * inner
+
+
+def slots_down(real, imag):
+    return [
+        jnp.concatenate([v[:, k * LANES : (k + 1) * LANES] for v in (real, imag)], axis=1)
+        for k in range(WIDE)
+    ]
+
+
+def slots_across(value):
+    rows = [value[k * LAT : (k + 1) * LAT] for k in range(WIDE)]
+    parts = [
+        jnp.concatenate([r[:, p * LANES : (p + 1) * LANES] for r in rows], axis=1)
+        for p in range(2)
+    ]
+    return jnp.concatenate(parts, axis=0)
 
 
 def latitudes(own_ref, other_ref, row, run):
@@ -530,7 +556,7 @@
 def drain(turn_ref, own_ref, other_ref):
     lats, rows = own_ref.shape[0], own_ref.shape[1]
 
-    @pl.loop(0, lats)
+    @pl.loop(0, lats, unroll=4)
     def _(at):
         own_ref[at] = turn_ref[pl.ds(pl.multiple_of(at * rows, 8), rows), :].astype(BF)
         other_ref[at] = turn_ref[
@@ -545,36 +571,24 @@
     lats, rows = own_ref.shape[1], own_ref.shape[0]
     run = rows // 2 // SPLIT
 
-    @pl.loop(0, rows // 4, unroll=UNROLL)
+    @pl.loop(0, rows // 2 // WIDE, unroll=UNROLL)
     def _(step):
-        slot = 2 * step
+        slot = WIDE * step
         row = slot + slot // run * run
         cells = jnp.concatenate(
-            [latitudes(own_ref, other_ref, row + k, run) for k in range(2)], axis=1
+            [latitudes(own_ref, other_ref, row + k, run) for k in range(WIDE)], axis=1
         )
         full = jnp.dot(lat_ref[...], cells, preferred_element_type=F32).astype(BF)
         real, imag = full[:LAT], full[LAT:]
-        modes = jnp.concatenate(
-            [
-                jnp.concatenate([real[:, :LANES], imag[:, :LANES]], axis=1),
-                jnp.concatenate([real[:, LANES:], imag[:, LANES:]], axis=1),
-            ],
-            axis=0,
-        )
+        modes = jnp.concatenate(slots_down(real, imag), axis=0)
         modes_out[step] = modes
         pre_a = jnp.dot(modes, wa_ref[...], preferred_element_type=F32) + ba_ref[...]
-        hidden = gelu(pre_a).astype(BF)
+        hidden = (pre_a * gelu_gate(pre_a)).astype(BF)
         pre_b = jnp.dot(hidden, wb_ref[...], preferred_element_type=F32) + bb_ref[...]
         shrunk = (pre_b - shrink_level * jnp.tanh(pre_b * (1.0 / shrink_soft))).astype(BF)
-        mixed = jnp.concatenate(
-            [
-                jnp.concatenate([shrunk[:LAT, :LANES], shrunk[LAT:, :LANES]], axis=1),
-                jnp.concatenate([shrunk[:LAT, LANES:], shrunk[LAT:, LANES:]], axis=1),
-            ],
-            axis=0,
-        )
+        mixed = slots_across(shrunk)
         back = jnp.dot(back_ref[...], mixed, preferred_element_type=F32)
-        for k in range(2):
+        for k in range(WIDE):
             turn_out(turn_ref, back[:, k * LANES : (k + 1) * LANES], row + k, lats, rows, run)
 
     drain(turn_ref, own_out, other_out)
@@ -596,49 +610,38 @@
     gwa_ref, gwb_ref = grad_ref.at[:wide], grad_ref.at[wide : 2 * wide]
     gba_ref, gbb_ref = grad_ref.at[2 * wide : 2 * wide + 8], grad_ref.at[2 * wide + 8 :]
 
-    @pl.loop(0, run // 2, unroll=UNROLL)
+    @pl.loop(0, run // WIDE, unroll=UNROLL)
     def _(step):
-        row = 2 * step
+        row = WIDE * step
         cells = jnp.concatenate(
-            [latitudes(own_ref, other_ref, row + k, run) for k in range(2)], axis=1
+            [latitudes(own_ref, other_ref, row + k, run) for k in range(WIDE)], axis=1
         )
         full = jnp.dot(lat_ref[...], cells, preferred_element_type=F32)
         real, imag = full[:LAT], full[LAT:]
-        grad = jnp.concatenate(
-            [
-                jnp.concatenate([real[:, :LANES], imag[:, :LANES]], axis=1),
-                jnp.concatenate([real[:, LANES:], imag[:, LANES:]], axis=1),
-            ],
-            axis=0,
-        )
+        grad = jnp.concatenate(slots_down(real, imag), axis=0)
         modes = modes_ref[step]
         pre_a = jnp.dot(modes, wa_ref[...], preferred_element_type=F32) + ba_ref[...]
-        squash_a = gelu_parts(pre_a)
-        hidden = (0.5 * pre_a * (1.0 + squash_a)).astype(BF)
+        gate_a = gelu_gate(pre_a)
+        hidden = (pre_a * gate_a).astype(BF)
         pre_b = jnp.dot(hidden, wb_ref[...], preferred_element_type=F32) + bb_ref[...]
         squash_b = jnp.tanh(pre_b * (1.0 / shrink_soft))
-        factor = 1.0 - shrink_level / shrink_soft * (1.0 - squash_b * squash_b)
+        level = shrink_level / shrink_soft
+        factor = level * (squash_b * squash_b) + (1.0 - level)
         grad_b = factor * grad
         gbb_ref[...] += row_sums(grad_b)
         grad_b = grad_b.astype(BF)
         grad_hidden = lax.dot_general(grad_b, wb_ref[...], ACROSS, preferred_element_type=F32)
         gwb_ref[...] += lax.dot_general(hidden, grad_b, OUTER, preferred_element_type=F32)
-        grad_a = gelu_slope(pre_a, squash_a) * grad_hidden
+        grad_a = gelu_slope(pre_a, gate_a) * grad_hidden
         gba_ref[...] += row_sums(grad_a)
         grad_a = grad_a.astype(BF)
         grad_modes = lax.dot_general(
             grad_a, wa_ref[...], ACROSS, preferred_element_type=F32
         ).astype(BF)
         gwa_ref[...] += lax.dot_general(modes, grad_a, OUTER, preferred_element_type=F32)
-        mixed = jnp.concatenate(
-            [
-                jnp.concatenate([grad_modes[:LAT, :LANES], grad_modes[LAT:, :LANES]], axis=1),
-                jnp.concatenate([grad_modes[:LAT, LANES:], grad_modes[LAT:, LANES:]], axis=1),
-            ],
-            axis=0,
-        )
+        mixed = slots_across(grad_modes)
         back = jnp.dot(back_ref[...], mixed, preferred_element_type=F32)
-        for k in range(2):
+        for k in range(WIDE):
             turn_out(turn_ref, back[:, k * LANES : (k + 1) * LANES], row + k, lats, rows, run)
 
     drain(turn_ref, own_out, other_out)
@@ -719,6 +722,7 @@
     )
     lat_steps = CORES * groups
     row_spec = pl.BlockSpec((1, channels), lambda i: (0, 0))
+    line_spec = pl.BlockSpec((channels,), lambda i: (0,))
     here_spec, pad_spec = lat_spec(cols_here, channels), lat_spec(cols_pad, channels)
     mask, mask_spec = valid_mask, pl.BlockSpec((rows_here, cols_here), lambda i: (0, 0))
     packed_shape = (BLOCKS, CORES, groups, cols_pad, 3 * LANES)
@@ -858,7 +862,7 @@
                     pl.BlockSpec((t, c), lambda i, h: (at(i, h), 0)),
                     pl.BlockSpec((c, t), lambda i, h: (0, at(i, h))),
                 ] + [pl.BlockSpec((2, EXTRA, c), lambda i, h: (i, 0, 0))] * 2,
-                input_output_aliases={3: 0, 4: 1} if done else {}, name="widen",
+                input_output_aliases={3: 0, 4: 1} if done else {}, hbm=(0, 1), name="widen",
             )
 
     def add(x, y, dtype, after=()):
@@ -916,9 +920,9 @@
     ba, bb = big_bias(mix_bias_a), big_bias(mix_bias_b)
 
     normed, send = call(
-        first_kernel, [x5, mask, row(first_gain), row(first_shift)],
-        [shape(pad_shape, BF), shape(packed_shape, BF)], 6.0,
-        grid=(lat_steps,), in_specs=[here_spec, mask_spec, row_spec, row_spec],
+        first_kernel, [x5, mask, first_gain, first_shift],
+        [shape(pad_shape, BF), shape(packed_shape, BF)], 6.0, hbm=(0, 1),
+        grid=(lat_steps,), in_specs=[here_spec, mask_spec, line_spec, line_spec],
         out_specs=[pad_spec, packed_spec], vmem=16, name="first_norm",
     )
     cells = exchange(send.reshape(flat_shape))
@@ -928,19 +932,25 @@
     own, other, modes = call(
         mix_kernel, [own, other, lat_fwd, lat_inv, wa, ba, wb, bb],
         [shape((lats, half_rows, LANES), BF)] * 2
-        + [shape((slots_pad // 2, 2 * LAT, 2 * LANES), BF)], 22.0,
-        scratch_shapes=[pltpu.VMEM((2 * lats * half_rows, LANES), F32)], vmem=32, name="mix",
+        + [shape((slots_pad // WIDE, WIDE * LAT, 2 * LANES), BF)], 22.0,
+        scratch_shapes=[pltpu.VMEM((2 * lats * half_rows, LANES), F32)], vmem=32, hbm=(2,), name="mix",
     )
     other = swap(other)
-    got = exchange(lon_backward([own, other], lon_winv))
-
-    resid, tokens, cot_pad = call(
+    lon_out = lon_backward([own, other], lon_winv)
+    got = exchange(lon_out)
+
+    cot_pad = call(
+        pad_kernel, [cot5], shape(pad_shape, BF), 2.0, after=[lon_out], grid=(lat_steps,),
+        in_specs=[here_spec], out_specs=[pad_spec], name="pad",
+    )
+
+    resid, tokens = call(
         second_kernel,
-        [x5, normed, mask, cot5, got.reshape(packed_shape), row(second_gain), row(second_shift)],
-        [shape(pad_shape, F32), shape(pad_shape, BF), shape(pad_shape, BF)], 8.5,
+        [x5, normed, mask, got.reshape(packed_shape), row(second_gain), row(second_shift)],
+        [shape(pad_shape, F32), shape(pad_shape, BF)], 8.5, after=[cot_pad],
         grid=(lat_steps,),
-        in_specs=[here_spec, pad_spec, mask_spec, here_spec, packed_spec, row_spec, row_spec],
-        out_specs=[pad_spec, pad_spec, pad_spec], vmem=56, name="second_norm",
+        in_specs=[here_spec, pad_spec, mask_spec, packed_spec, row_spec, row_spec],
+        out_specs=[pad_spec, pad_spec], vmem=56, name="second_norm",
     )
     tokens2, cot2 = tokens.reshape(-1, channels), cot_pad.reshape(-1, channels)
     count, hidden = tokens2.shape[0], expand_weight.shape[1]
@@ -953,11 +963,11 @@
         [tokens2, cot2, expand_weight, row(expand_bias), reduce_weight],
         [
             shape((count, hidden), BF), shape((count, hidden), BF),
-            shape((count, channels), F32), shape((1, hidden), F32),
+            shape((count, channels), BF), shape((1, hidden), F32),
         ],
         25.0, grid=(6,),
         in_specs=[all_tok, all_tok, by_col(channels), by_col(1), by_row],
-        out_specs=[by_col(count), by_col(count), all_tok, by_col(1)], vmem=46, name="mlp_chain",
+        out_specs=[by_col(count), by_col(count), all_tok, by_col(1)], scratch_shapes=[pltpu.VMEM((count, channels), F32)], vmem=46, hbm=(0, 1, 2), pin=True, name="mlp_chain",
     )
 
     halves = 3
@@ -966,32 +976,37 @@
     def weight_grad(left, right, own, after, name):
         at = lambda i, c: (c[0] if own else 1 - c[0]) * halves + i
         return call(
-            weight_grad_kernel, [left, right], shape((halves * tile, channels), BF), 5.0,
+            weight_grad_kernel, [left, right],
+            [shape((halves * tile, channels), BF), shape((8, LANES), F32)], 5.0,
             after=after, prefetch=[core_line], grid=(halves,),
             in_specs=[
                 pl.BlockSpec((count, tile), lambda i, c: (0, at(i, c))),
                 pl.BlockSpec((count, channels), lambda i, c: (0, 0)),
             ],
-            out_specs=[pl.BlockSpec((tile, channels), lambda i, c: (i, 0))], vmem=20, name=name,
+            out_specs=[
+                pl.BlockSpec((tile, channels), lambda i, c: (i, 0)),
+                pl.BlockSpec((8, LANES), lambda i, c: (0, 0)),
+            ],
+            vmem=20, name=name,
         )
 
     one_row = shape((1, channels), F32)
     grad_resid, send, g_gain2, g_shift2, g_rbias = call(
         third_kernel,
         [resid, gtok.reshape(pad_shape), cot_pad, mask, row(second_gain)],
-        [shape(pad_shape, F32), shape(packed_shape, BF)] + [one_row] * 3, 9.0,
+        [shape(pad_shape, BF), shape(packed_shape, BF)] + [one_row] * 3, 9.0,
         grid=(lat_steps,), in_specs=[pad_spec, pad_spec, pad_spec, mask_spec, row_spec],
         out_specs=[pad_spec, packed_spec, row_spec, row_spec, row_spec], vmem=56, name="second_back",
     )
     cells = exchange(send.reshape(flat_shape))
 
-    sent_r = weight_grad(act, cot2, False, [send], "reduce_grad")
-    sent_e = weight_grad(gpre, tokens2, False, [sent_r], "expand_grad")
-    kept_r = weight_grad(act, cot2, True, [sent_e], "reduce_grad")
-    kept_e = weight_grad(gpre, tokens2, True, [kept_r], "expand_grad")
+    sent_r, token = weight_grad(act, cot2, False, [g_gain2], "reduce_grad")
+    sent_e, token = weight_grad(gpre, tokens2, False, [token], "expand_grad")
+    kept_r, token = weight_grad(act, cot2, True, [token], "reduce_grad")
+    kept_e, token = weight_grad(gpre, tokens2, True, [token], "expand_grad")
     sums = Sum([kept_r, kept_e], [partner(sent_r, 1), partner(sent_e, 1)])
 
-    own, other = lon_forward(cells, lon_wfwd, after=[kept_e])
+    own, other = lon_forward(cells, lon_wfwd, after=[token])
     other = swap(other)
     token = sums.halve(after=[own])
     run = half_rows // SPLIT
@@ -1025,10 +1040,22 @@
     )
     token = sums.join(stay, partner(leave, 1))
 
+    outputs, token = call(
+        branch_kernel,
+        [act.reshape(CORES, groups, PACK, cols_pad, hidden), reduce_weight, resid, row(reduce_bias)],
+        [turned_shape, shape((8, LANES), F32)], 10.0, after=[token], grid=(groups,),
+        in_specs=[
+            both_spec(cols_pad, hidden), pl.BlockSpec((hidden, channels), lambda i: (0, 0)),
+            both_spec(cols_pad, channels), row_spec,
+        ],
+        out_specs=[turned_spec, pl.BlockSpec((8, LANES), lambda i: (0, 0))], vmem=32, name="branch",
+    )
+
     touched = call(
         touch_kernel, [], shape((8, LANES), F32), 0.5, after=[got, token], name="touch"
     )
     token = sums.part(after=[touched])
+    token = sums.double(after=[token])
     token = sums.double(after=[token])
 
     grad_inputs, g_gain1, g_shift1 = call(
@@ -1043,24 +1070,11 @@
             [shape((1, 5 * channels + hidden), F32)] * 2, 1.0, name="tail",
         )
     )
-    token = sums.double(after=[tail_sum.x])
-    token = tail_sum.step(after=[token])
-    outputs = call(
-        branch_kernel,
-        [act.reshape(CORES, groups, PACK, cols_pad, hidden), reduce_weight, resid, row(reduce_bias)],
-        turned_shape, 10.0, after=[token], grid=(groups,),
-        in_specs=[
-            both_spec(cols_pad, hidden), pl.BlockSpec((hidden, channels), lambda i: (0, 0)),
-            both_spec(cols_pad, channels), row_spec,
-        ],
-        out_specs=[turned_spec], vmem=32, name="branch",
-    )
-
-    token = tail_sum.step(after=[outputs])
+    token = tail_sum.step()
     token = sums.double(after=[token])
     token = tail_sum.step(after=[token])
     own_done = sums.widen([], after=[token])
-    token = tail_sum.step(after=[own_done[0]])
+    token = tail_sum.step(after=[own_done[2]])
     g_reduce, g_expand, *got_extra = sums.widen(own_done, after=[token])
     token = got_extra[0]
     while tail_sum.bits:

time: 359 us -> 331 us (0.922)
  Pallas kernels: 151 us -> 133 us
  local copies, waits for them, and re-layouts: 44.9 us -> 33.3 us
    pallas_call x37 -> x38, Pallas kernels: 151 us -> 133 us  [call(): pl.pallas_call(body, grid_spec=pltpu.PrefetchScalarGridSpec(num_scalar_pr...]
    ppermute x28, waiting for transfers between devices: 27.1 us -> 44.5 us  [partner(): return lax.ppermute(x, AXES, [(d, d ^ flip) for d in range(devices)])]
    all_to_all x4, waiting for transfers between devices: 80.9 us -> 63.8 us  [exchange(): lax.all_to_all(x, AXES, 0, 0, axis_index_groups=snap_groups, tiled=True)]
    unnamed x130 -> x114, local copies, waits for them, and re-layouts: 38.4 us -> 27.6 us
  transfers between devices with their start and end apart: 37 -> 37, of which waited for: 18 -> 27; matrix products, arithmetic and copies ran while one was open for 2% -> 2% of each run, Pallas kernels for 22% -> 21%
where the time goes in v5:
time: 331 us; the launch traced here: 330 us
  Pallas kernels  133 us (40%)
  waiting for transfers between devices  113 us (34%)
  starting transfers between devices  48.7 us (15%)
  local copies, waits for them, and re-layouts  33.3 us (10%)
    pallas_call x38, Pallas kernels, call(): pl.pallas_call(body, grid_spec=pltpu.PrefetchScalarGridSpec(num_scalar_pr...  133 us
    all_to_all x4, waiting for transfers between devices, exchange(): lax.all_to_all(x, AXES, 0, 0, axis_index_groups=snap_groups, tiled=True)  63.8 us
    ppermute x28, waiting for transfers between devices, partner(): return lax.ppermute(x, AXES, [(d, d ^ flip) for d in range(devices)])  44.5 us
    ppermute x28, starting transfers between devices, partner(): return lax.ppermute(x, AXES, [(d, d ^ flip) for d in range(devices)])  28.2 us
    unnamed x114, local copies, waits for them, and re-layouts  27.6 us
    all_to_all x4, starting transfers between devices, exchange(): lax.all_to_all(x, AXES, 0, 0, axis_index_groups=snap_groups, tiled=True)  19.7 us
  transfers between devices with their start and end apart: 37, of which 27 were waited for; matrix products, arithmetic and copies ran while one was open for 2% of the time, Pallas kernels for 21%

profile of v5, /device:TPU:0, one launch (start us, length us, event | category | flops | bytes accessed | tf_op | source)
XLA Modules:
  0.0 329.8 jit_solution(11679781583543387791)
XLA Ops:
  0.7 1.8 copy.37
  2.5 4.3 %first_norm.1 = (bf16[2,3,4,48,768]{4,3,2,1,0:T(8,128)(2,1)}, bf16[8,2,3,48,384]{4,3,2,1,0:T(8,128)(2,1)}) custom-call(bf16[2,3,4,45,768]{4,3,2,1,0:T(8,128)(2,1)S(1)} %bitcast.61, s32[24,45]{1,0:T(8,128)S(1)} %copy-done.26, f32[768]{0:T(1024)S(1)} %copy-done.27, f32[768]{0:T(1024)S(1)} %copy-done.35), custom_call_target="tpu_custom_call" | custom-call | bytes 600000 | tf_op jit(solution)/shard_map/first_norm/pallas_call | solution.py:46
  6.8 6.3 %all-to-all-start = ((bf16[16,3,48,384]{3,2,1,0:T(8,128)(2,1)}), bf16[16,3,48,384]{3,2,1,0:T(8,128)(2,1)S(1)}, u32[]{:S(2)}, u32[]{:S(2)}) async-start(bf16[16,3,48,384]{3,2,1,0:T(8,128)(2,1)} %bitcast.78), calls=%async_computation | async-start | bytes 3538944 | tf_op jit(solution)/shard_map/all_to_all | solution.py:699
  14.1 24.3 %all-to-all-done.refs_0_ = bf16[16,3,48,384]{3,2,1,0:T(8,128)(2,1)S(1)} async-done(((bf16[16,3,48,384]{3,2,1,0:T(8,128)(2,1)}), bf16[16,3,48,384]{3,2,1,0:T(8,128)(2,1)S(1)}, u32[]{:S(2)}, u32[]{:S(2)}) %all-to-all-start) | async-done | bytes 1769504 | tf_op jit(solution)/shard_map/all_to_all | solution.py:699
  38.4 3.5 %lon_forward.2 = (bf16[96,48,128]{2,1,0:T(8,128)(2,1)S(1)}, bf16[96,48,128]{2,1,0:T(8,128)(2,1)}) custom-call(bf16[16,3,48,384]{3,2,1,0:T(8,128)(2,1)S(1)} %all-to-all-done.refs_0_, bf16[192,192]{1,0:T(8,128)(2,1)S(1)} %dynamic-slice_bitcast_fusion.5.refs_1_), custom_call_target="tpu_custom_call" | custom-call | bytes 550000 | tf_op jit(solution)/shard_map/lon_forward/pallas_call | solution.py:46
  43.2 1.8 collective-permute-done.refs_1_
  45.0 8.5 %mix.1 = (bf16[48,96,128]{2,1,0:T(8,128)(2,1)S(1)}, bf16[48,96,128]{2,1,0:T(8,128)(2,1)S(1)}, bf16[4,1152,256]{2,1,0:T(8,128)(2,1)}) custom-call(bf16[96,48,128]{2,1,0:T(8,128)(2,1)S(1)} %get-tuple-element.123.refs_0_, bf16[96,48,128]{2,1,0:T(8,128)(2,1)S(1)} %collective-permute-done.refs_1_, bf16[192,192]{1,0:T(8,128)(2,1)S(1)} %get-tuple-element.238.refs_2_.refs_3_, ...), custom_call_target="tpu_custom_call" | custom-call | bytes 2200000 | tf_op jit(solution)/shard_map/mix/pallas_call | solution.py:46
  53.6 2.7 collective-permute-done.1.refs_1_
  56.3 2.1 lon_backward.2.refs_1_
  58.4 4.1 %all-to-all-start.1 = ((bf16[16,3,48,384]{3,2,1,0:T(8,128)(2,1)}), bf16[16,3,48,384]{3,2,1,0:T(8,128)(2,1)S(1)}, u32[]{:S(2)}, u32[]{:S(2)}) async-start(bf16[16,3,48,384]{3,2,1,0:T(8,128)(2,1)} %lon_backward.2.refs_1_), calls=%async_computation.1 | async-start | bytes 3538944 | tf_op jit(solution)/shard_map/all_to_all | solution.py:699
  64.3 1.2 copy-done.2
  65.5 22.2 %all-to-all-done.1 = bf16[16,3,48,384]{3,2,1,0:T(8,128)(2,1)S(1)} async-done(((bf16[16,3,48,384]{3,2,1,0:T(8,128)(2,1)}), bf16[16,3,48,384]{3,2,1,0:T(8,128)(2,1)S(1)}, u32[]{:S(2)}, u32[]{:S(2)}) %all-to-all-start.1) | async-done | bytes 1769504 | tf_op jit(solution)/shard_map/all_to_all | solution.py:699
  87.8 1.2 copy-done.42
  89.0 6.8 %second_norm.1 = (f32[2,3,4,48,768]{4,3,2,1,0:T(8,128)}, bf16[2,3,4,48,768]{4,3,2,1,0:T(8,128)(2,1)}) custom-call(bf16[2,3,4,45,768]{4,3,2,1,0:T(8,128)(2,1)} %bitcast.62, bf16[2,3,4,48,768]{4,3,2,1,0:T(8,128)(2,1)} %get-tuple-element.121.refs_1_, s32[24,45]{1,0:T(8,128)} %refs_2_.7, bf16[8,2,3,48,384]{4,3,2,1,0:T(8,128)(2,1)} %bitcast.76, ...), custom_call_target="tpu_custom_call" | custom-call | bytes 850000 | tf_op jit(solution)/shard_map/second_norm/pallas_call | solution.py:46
  95.8 24.1 %mlp_chain.1 = (bf16[1152,3072]{1,0:T(8,128)(2,1)}, bf16[1152,3072]{1,0:T(8,128)(2,1)}, bf16[1152,768]{1,0:T(8,128)(2,1)}, f32[1,3072]{1,0:T(1,128)S(1)}) custom-call(bf16[1152,768]{1,0:T(8,128)(2,1)} %bitcast.65, bf16[1152,768]{1,0:T(8,128)(2,1)} %bitcast.55, bf16[768,3072]{1,0:T(8,128)(2,1)} %refs_2_.6, f32[1,3072]{1,0:T(1,128)} %bitcast.81, ...), custom_call_target="tpu_custom_call" | custom-call | bytes 2500000 | tf_op jit(solution)/shard_map/mlp_chain/pallas_call | solution.py:46
  120.5 8.1 %second_back.1 = (bf16[2,3,4,48,768]{4,3,2,1,0:T(8,128)(2,1)}, bf16[8,2,3,48,384]{4,3,2,1,0:T(8,128)(2,1)}, f32[1,768]{1,0:T(1,128)}, f32[1,768]{1,0:T(1,128)}, f32[1,768]{1,0:T(1,128)}) custom-call(f32[2,3,4,48,768]{4,3,2,1,0:T(8,128)} %get-tuple-element.129.refs_0_.refs_2_, bf16[2,3,4,48,768]{4,3,2,1,0:T(8,128)(2,1)} %bitcast.79, ...), custom_call_target="tpu_custom_call" | custom-call | bytes 900000 | tf_op jit(solution)/shard_map/second_back/pallas_call | solution.py:46
  128.6 4.7 %all-to-all-start.2 = ((bf16[16,3,48,384]{3,2,1,0:T(8,128)(2,1)}), bf16[16,3,48,384]{3,2,1,0:T(8,128)(2,1)}, u32[]{:S(2)}, u32[]{:S(2)}) async-start(bf16[16,3,48,384]{3,2,1,0:T(8,128)(2,1)} %bitcast.77), calls=%async_computation.2 | async-start | bytes 3538944 | tf_op jit(solution)/shard_map/all_to_all | solution.py:699
  133.4 3.0 copy-done
  136.4 4.9 %reduce_grad.2 = (bf16[1536,768]{1,0:T(8,128)(2,1)}, f32[8,128]{1,0:T(8,128)S(1)}) custom-call(s32[1]{0:T(128)} %bitcast.25.refs_0_, bf16[1152,3072]{1,0:T(8,128)(2,1)S(1)} %copy-done, bf16[1152,768]{1,0:T(8,128)(2,1)S(1)} %bitcast.56, f32[1,768]{1,0:T(1,128)S(1)} %copy-done.28), custom_call_target="tpu_custom_call" | custom-call | bytes 500000 | tf_op jit(solution)/shard_map/reduce_grad/pallas_call | solution.py:46
  141.3 3.0 copy-done.4
  144.3 4.9 %expand_grad.2 = (bf16[1536,768]{1,0:T(8,128)(2,1)}, f32[8,128]{1,0:T(8,128)S(1)}) custom-call(s32[1]{0:T(128)} %bitcast.25.refs_0_, bf16[1152,3072]{1,0:T(8,128)(2,1)S(1)} %copy-done.4, bf16[1152,768]{1,0:T(8,128)(2,1)S(1)} %bitcast.66, f32[8,128]{1,0:T(8,128)S(1)} %get-tuple-element.133.refs_3_), custom_call_target="tpu_custom_call" | custom-call | bytes 500000 | tf_op jit(solution)/shard_map/expand_grad/pallas_call | solution.py:46
  150.4 4.0 %reduce_grad.3 = (bf16[1536,768]{1,0:T(8,128)(2,1)S(1)}, f32[8,128]{1,0:T(8,128)S(1)}) custom-call(s32[1]{0:T(128)} %bitcast.25.refs_0_, bf16[1152,3072]{1,0:T(8,128)(2,1)S(1)} %bitcast.53, bf16[1152,768]{1,0:T(8,128)(2,1)S(1)} %bitcast.57, f32[8,128]{1,0:T(8,128)S(1)} %get-tuple-element.134.refs_3_), custom_call_target="tpu_custom_call" | custom-call | bytes 500000 | tf_op jit(solution)/shard_map/reduce_grad/pallas_call | solution.py:46
  154.4 1.4 copy-done.6
  155.7 4.0 %expand_grad.3 = (bf16[1536,768]{1,0:T(8,128)(2,1)S(1)}, f32[8,128]{1,0:T(8,128)S(1)}) custom-call(s32[1]{0:T(128)} %bitcast.25.refs_0_, bf16[1152,3072]{1,0:T(8,128)(2,1)S(1)} %copy-done.4, bf16[1152,768]{1,0:T(8,128)(2,1)S(1)} %bitcast.67, f32[8,128]{1,0:T(8,128)S(1)} %get-tuple-element.137.refs_3_), custom_call_target="tpu_custom_call" | custom-call | bytes 500000 | tf_op jit(solution)/shard_map/expand_grad/pallas_call | solution.py:46
  159.7 1.4 copy-done.8
  163.3 5.0 %lon_forward.3 = (bf16[96,48,128]{2,1,0:T(8,128)(2,1)S(1)}, bf16[96,48,128]{2,1,0:T(8,128)(2,1)}) custom-call(bf16[16,3,48,384]{3,2,1,0:T(8,128)(2,1)} %all-to-all-done.2.refs_0_, bf16[192,192]{1,0:T(8,128)(2,1)S(1)} %copy-done.25, f32[8,128]{1,0:T(8,128)S(1)} %copy-done.37), custom_call_target="tpu_custom_call" | custom-call | bytes 550000 | tf_op jit(solution)/shard_map/lon_forward/pallas_call | solution.py:46
  168.5 1.7 copy-done.9
  170.2 3.9 %halve.3 = (bf16[512,768]{1,0:T(8,128)(2,1)S(1)}, bf16[512,768]{1,0:T(8,128)(2,1)S(1)}, bf16[512,768]{1,0:T(8,128)(2,1)S(1)}, bf16[512,768]{1,0:T(8,128)(2,1)S(1...) custom-call(s32[3]{0:T(128)S(1)} %pad_add_fusion.2.refs_0_, bf16[1536,768]{1,0:T(8,128)(2,1)S(1)} %copy-done.7, ...), custom_call_target="tpu_custom_call" | custom-call | bytes 300000 | tf_op jit(solution)/shard_map/halve/pallas_call | solution.py:46
  174.1 1.7 collective-permute-start.4
  175.9 1.5 collective-permute-start.5
  177.4 1.5 collective-permute-start.6
  179.0 5.7 %mix_back.2 = (bf16[48,48,128]{2,1,0:T(8,128)(2,1)S(1)}, bf16[48,48,128]{2,1,0:T(8,128)(2,1)S(1)}, f32[528,256]{1,0:T(8,128)S(1)}) custom-call(bf16[96,48,128]{2,1,0:T(8,128)(2,1)S(1)} %get-tuple-element.142.refs_13_.refs_0_, bf16[96,48,128]{2,1,0:T(8,128)(2,1)} %collective-permute-done.7.refs_1_, bf16[4,1152,256]{2,1,0:T(8,128)(2,1)S(1)} %copy-done.14, ...), custom_call_target="tpu_custom_call" | custom-call | bytes 1300000 | tf_op jit(solution)/shard_map/mix_back/pallas_call | solution.py:46
  184.7 9.4 %collective-permute-done.4.refs_2_.refs_4_ = bf16[512,768]{1,0:T(8,128)(2,1)S(1)} collective-permute-done((bf16[512,768]{1,0:T(8,128)(2,1)S(1)}, bf16[512,768]{1,0:T(8,128)(2,1)S(1)}, u32[]{:S(2)}, u32[]{:S(2)}) %collective-permute-start.4) | collective-permute-done | bytes 786464 | tf_op jit(solution)/shard_map/ppermute | solution.py:746
  194.1 1.3 collective-permute-done.5.refs_6_.refs_8_
  195.4 1.2 collective-permute-done.6.refs_10_.refs_12_
  198.3 1.5 collective-permute-start.9
  200.3 5.9 %mix_back.3 = (bf16[48,48,128]{2,1,0:T(8,128)(2,1)S(1)}, bf16[48,48,128]{2,1,0:T(8,128)(2,1)S(1)}, f32[528,256]{1,0:T(8,128)S(1)}) custom-call(bf16[96,48,128]{2,1,0:T(8,128)(2,1)S(1)} %get-tuple-element.142.refs_13_.refs_0_, bf16[96,48,128]{2,1,0:T(8,128)(2,1)} %collective-permute-done.7.refs_1_, bf16[4,1152,256]{2,1,0:T(8,128)(2,1)S(1)} %copy-done.14, ...), custom_call_target="tpu_custom_call" | custom-call | bytes 1300000 | tf_op jit(solution)/shard_map/mix_back/pallas_call | solution.py:46
  208.0 1.2 collective-permute-done.10.refs_10_.refs_12_
  211.2 1.4 collective-permute-start.13
  212.6 3.2 collective-permute-done.11.refs_1_
  217.1 2.1 lon_backward.3.refs_2_
  219.1 4.6 %all-to-all-start.3 = ((bf16[16,3,48,384]{3,2,1,0:T(8,128)(2,1)}), bf16[16,3,48,384]{3,2,1,0:T(8,128)(2,1)S(1)}, u32[]{:S(2)}, u32[]{:S(2)}) async-start(bf16[16,3,48,384]{3,2,1,0:T(8,128)(2,1)} %lon_backward.3.refs_2_), calls=%async_computation.3 | async-start | bytes 3538944 | tf_op jit(solution)/shard_map/all_to_all | solution.py:699
  226.2 2.6 collective-permute-start.17
  228.8 3.0 copy-done.1
  231.8 2.3 copy-done.10
  234.2 2.0 copy-done.13
  236.2 9.4 %branch.1 = (f32[45,24,768]{2,1,0:T(8,128)}, f32[8,128]{1,0:T(8,128)S(1)}) custom-call(bf16[2,3,4,48,3072]{4,3,2,1,0:T(8,128)(2,1)S(1)} %bitcast.54, bf16[3072,768]{1,0:T(8,128)(2,1)S(1)} %copy-done.10, f32[2,3,4,48,768]{4,3,2,1,0:T(8,128)S(1)} %copy-done.13, f32[1,768]{1,0:T(1,128)S(1)} %reshape.109.refs_3_, ...), custom_call_target="tpu_custom_call" | custom-call | bytes 1000000 | tf_op jit(solution)/shard_map/branch/pallas_call | solution.py:46
  245.5 17.3 %all-to-all-done.3.refs_0_ = bf16[16,3,48,384]{3,2,1,0:T(8,128)(2,1)S(1)} async-done(((bf16[16,3,48,384]{3,2,1,0:T(8,128)(2,1)}), bf16[16,3,48,384]{3,2,1,0:T(8,128)(2,1)S(1)}, u32[]{:S(2)}, u32[]{:S(2)}) %all-to-all-start.3) | async-done | bytes 1769504 | tf_op jit(solution)/shard_map/all_to_all | solution.py:699
  263.6 3.6 %collective-permute-start.19 = (bf16[144,768]{1,0:T(8,128)(2,1)S(1)}, bf16[144,768]{1,0:T(8,128)(2,1)S(1)}, u32[]{:S(2)}, u32[]{:S(2)}) collective-permute-start(bf16[144,768]{1,0:T(8,128)(2,1)S(1)} %get-tuple-element.182), channel_id=1, source_target_pairs={{0,2},{1,3},{2,0},{3,1},{4,6},{5,7},{6,4},{7,5},{8,10},{9,11},{10,... | collective-permute-start | bytes 663560 | tf_op jit(solution)/shard_map/ppermute | solution.py:746
  267.3 2.8 collective-permute-done.18.refs_2_
  270.0 2.2 collective-permute-done.19.refs_4_
  272.2 1.5 collective-permute-done.20.refs_6_
  276.0 8.8 %collective-permute-done.21.refs_2_ = bf16[288,768]{1,0:T(8,128)(2,1)S(1)} collective-permute-done((bf16[288,768]{1,0:T(8,128)(2,1)S(1)}, bf16[288,768]{1,0:T(8,128)(2,1)S(1)}, u32[]{:S(2)}, u32[]{:S(2)}) %collective-permute-start.21) | collective-permute-done | bytes 442400 | tf_op jit(solution)/shard_map/ppermute | solution.py:746
  287.7 1.6 collective-permute-start.27
  289.3 1.3 collective-permute-start.28
  291.2 9.3 %first_back.1 = (f32[45,24,768]{2,1,0:T(8,128)}, f32[1,768]{1,0:T(1,128)}, f32[1,768]{1,0:T(1,128)}) custom-call(bf16[2,3,4,45,768]{4,3,2,1,0:T(8,128)(2,1)} %bitcast.63, bf16[2,3,4,48,768]{4,3,2,1,0:T(8,128)(2,1)} %get-tuple-element.176.refs_1_, s32[24,45]{1,0:T(8,128)} %refs_2_.7, bf16[8,2,3,48,384]{4,3,2,1,0:T(8,128)(2,1)} %bitcast.64, ...), custom_call_target="tpu_custom_call" | custom-call | bytes 900000 | tf_op jit(solution)/shard_map/first_back/pallas_call | solution.py:46
  303.1 2.9 collective-permute-done.26.refs_2_
  306.1 1.5 collective-permute-done.28.refs_6_
  307.5 1.2 merge.5
  310.0 2.8 collective-permute-done.25.refs_1_
  313.1 4.4 %widen.2 = (f32[3072,768]{1,0:T(8,128)}, f32[768,3072]{1,0:T(8,128)}, bf16[12,16,768]{2,1,0:T(8,128)(2,1)S(1)}, bf16[12,16,768]{2,1,0:T(8,128)(2,1)S(1)}) custom-call(s32[1]{0:T(128)} %bitcast.25.refs_0_, bf16[3456,768]{1,0:T(8,128)(2,1)S(1)} %bitcast.59, bf16[3456,768]{1,0:T(8,128)(2,1)S(1)} %bitcast.60, f32[1,6912]{1,0:T(1,128)S(1)} %get-tuple-element.208.refs_3_.refs_0_), custom_call_target="tpu_custom_call" | custom-call | bytes 500000 | tf_op jit(solution)/shard_map/widen/pallas_call | solution.py:46
  318.6 4.4 %widen.3 = (f32[3072,768]{1,0:T(8,128)}, f32[768,3072]{1,0:T(8,128)}, bf16[12,16,768]{2,1,0:T(8,128)(2,1)S(1)}, bf16[12,16,768]{2,1,0:T(8,128)(2,1)S(1)}) custom-call(s32[1]{0:T(128)} %bitcast.25.refs_0_, bf16[3456,768]{1,0:T(8,128)(2,1)S(1)} %collective-permute-done.31.refs_1_.refs_2_, ...), custom_call_target="tpu_custom_call", output_to_operand_aliasing={{0}: (3, {}), {1}: (4, {})} | custom-call | bytes 500000 | tf_op jit(solution)/shard_map/widen/pallas_call | solution.py:46
  323.1 2.8 collective-permute-start.32
  325.9 1.2 spread.1
  (189 shorter events, 32.5 us)
Async XLA Ops:
  6.8 31.6 %all-to-all-start = ((bf16[16,3,48,384]{3,2,1,0:T(8,128)(2,1)}), bf16[16,3,48,384]{3,2,1,0:T(8,128)(2,1)S(1)}, u32[]{:S(2)}, u32[]{:S(2)}) async-start(bf16[16,3,48,384]{3,2,1,0:T(8,128)(2,1)} %bitcast.78), calls=%async_computation | async-start | bytes 3538944 | tf_op jit(solution)/shard_map/all_to_all | solution.py:699
  13.1 28.8 %copy-start.49 = (f32[2,768]{1,0:T(2,128)S(1)}, f32[2,768]{1,0:T(2,128)}, u32[]{:S(2)}) copy-start(f32[2,768]{1,0:T(2,128)} %param.27) | copy-start | bytes 18436
  13.1 28.9 %copy-start.50 = (f32[2,768]{1,0:T(2,128)S(1)}, f32[2,768]{1,0:T(2,128)}, u32[]{:S(2)}) copy-start(f32[2,768]{1,0:T(2,128)} %param.29) | copy-start | bytes 18436
  13.1 30.0 %copy-start.47 = (bf16[2,192,192]{2,1,0:T(8,128)(2,1)S(1)}, bf16[2,192,192]{2,1,0:T(8,128)(2,1)}, u32[]{:S(2)}) copy-start(bf16[2,192,192]{2,1,0:T(8,128)(2,1)} %constant.189.clone) | copy-start | bytes 442372
  13.1 30.0 %copy-start.48 = (bf16[2,192,192]{2,1,0:T(8,128)(2,1)S(1)}, bf16[2,192,192]{2,1,0:T(8,128)(2,1)}, u32[]{:S(2)}) copy-start(bf16[2,192,192]{2,1,0:T(8,128)(2,1)} %constant.188.clone) | copy-start | bytes 442372
  41.9 3.1 collective-permute-start
  43.0 10.6 %copy-start.17 = (bf16[256,256]{1,0:T(8,128)(2,1)}, bf16[256,256]{1,0:T(8,128)(2,1)S(1)}, u32[]{:S(2)}) copy-start(bf16[256,256]{1,0:T(8,128)(2,1)S(1)} %maximum_maximum_fusion.1.refs_6_.refs_7_) | copy-start | bytes 393220
  43.1 10.5 %copy-start.46 = (bf16[2,192,192]{2,1,0:T(8,128)(2,1)S(1)}, bf16[2,192,192]{2,1,0:T(8,128)(2,1)}, u32[]{:S(2)}) copy-start(bf16[2,192,192]{2,1,0:T(8,128)(2,1)} %constant.187.clone) | copy-start | bytes 442372
  43.1 13.2 %copy-start.19 = (bf16[256,256]{1,0:T(8,128)(2,1)}, bf16[256,256]{1,0:T(8,128)(2,1)S(1)}, u32[]{:S(2)}) copy-start(bf16[256,256]{1,0:T(8,128)(2,1)S(1)} %maximum_maximum_fusion.refs_4_.refs_5_) | copy-start | bytes 393220
  43.1 13.2 %copy-start.21 = (bf16[192,192]{1,0:T(8,128)(2,1)}, bf16[192,192]{1,0:T(8,128)(2,1)S(1)}, u32[]{:S(2)}) copy-start(bf16[192,192]{1,0:T(8,128)(2,1)S(1)} %get-tuple-element.237.refs_3_.refs_4_) | copy-start | bytes 221188
  43.2 13.1 %copy-start.23 = (bf16[192,192]{1,0:T(8,128)(2,1)}, bf16[192,192]{1,0:T(8,128)(2,1)S(1)}, u32[]{:S(2)}) copy-start(bf16[192,192]{1,0:T(8,128)(2,1)S(1)} %get-tuple-element.238.refs_2_.refs_3_) | copy-start | bytes 221188
  53.4 2.8 collective-permute-start.1
  58.4 29.4 %all-to-all-start.1 = ((bf16[16,3,48,384]{3,2,1,0:T(8,128)(2,1)}), bf16[16,3,48,384]{3,2,1,0:T(8,128)(2,1)S(1)}, u32[]{:S(2)}, u32[]{:S(2)}) async-start(bf16[16,3,48,384]{3,2,1,0:T(8,128)(2,1)} %lon_backward.2.refs_1_), calls=%async_computation.1 | async-start | bytes 3538944 | tf_op jit(solution)/shard_map/all_to_all | solution.py:699
  128.6 33.1 %all-to-all-start.2 = ((bf16[16,3,48,384]{3,2,1,0:T(8,128)(2,1)}), bf16[16,3,48,384]{3,2,1,0:T(8,128)(2,1)}, u32[]{:S(2)}, u32[]{:S(2)}) async-start(bf16[16,3,48,384]{3,2,1,0:T(8,128)(2,1)} %bitcast.77), calls=%async_computation.2 | async-start | bytes 3538944 | tf_op jit(solution)/shard_map/all_to_all | solution.py:699
  136.4 13.9 %slice-start = ((s8[7077888]{0:T(1024)(128)(4,1)}), s8[4194304]{0:T(1024)(128)(4,1)S(1)}, s32[]{:S(2)}) async-start(s8[7077888]{0:T(1024)(128)(4,1)} %bitcast.52), calls=%async_computation.4 | async-start | bytes 8388608
  144.3 5.4 %copy-start.45 = (bf16[2,192,192]{2,1,0:T(8,128)(2,1)S(1)}, bf16[2,192,192]{2,1,0:T(8,128)(2,1)}, u32[]{:S(2)}) copy-start(bf16[2,192,192]{2,1,0:T(8,128)(2,1)} %constant.185.clone) | copy-start | bytes 442372
  144.3 6.1 %slice-start.1 = ((s8[7077888]{0:T(1024)(128)(4,1)}), s8[2883584]{0:T(1024)(128)(4,1)S(1)}, s32[]{:S(2)}) async-start(s8[7077888]{0:T(1024)(128)(4,1)} %bitcast.52), calls=%async_computation.5 | async-start | bytes 5767168
  149.2 19.3 %collective-permute-start.3 = (bf16[1536,768]{1,0:T(8,128)(2,1)}, bf16[1536,768]{1,0:T(8,128)(2,1)}, u32[]{:S(2)}, u32[]{:S(2)}) collective-permute-start(bf16[1536,768]{1,0:T(8,128)(2,1)} %get-tuple-element.139), channel_id=1, source_target_pairs={{0,1},{1,0},{2,3},{3,2},{4,5},{5,4},{6,7},{7,6},{8,9},{9,8},{10,11... | collective-permute-start | bytes 7077896 | tf_op jit(solution)/shard_map/ppermute | solution.py:746
  149.2 19.2 %collective-permute-start.2 = (bf16[1536,768]{1,0:T(8,128)(2,1)}, bf16[1536,768]{1,0:T(8,128)(2,1)}, u32[]{:S(2)}, u32[]{:S(2)}) collective-permute-start(bf16[1536,768]{1,0:T(8,128)(2,1)} %get-tuple-element.136), channel_id=1, source_target_pairs={{0,1},{1,0},{2,3},{3,2},{4,5},{5,4},{6,7},{7,6},{8,9},{9,8},{10,11... | collective-permute-start | bytes 7077896 | tf_op jit(solution)/shard_map/ppermute | solution.py:746
  155.7 12.7 %copy-start.7 = (bf16[1536,768]{1,0:T(8,128)(2,1)S(1)}, bf16[1536,768]{1,0:T(8,128)(2,1)}, u32[]{:S(2)}) copy-start(bf16[1536,768]{1,0:T(8,128)(2,1)} %copy-done.6) | copy-start | bytes 7077892
  168.3 10.6 %collective-permute-start.7 = (bf16[96,48,128]{2,1,0:T(8,128)(2,1)}, bf16[96,48,128]{2,1,0:T(8,128)(2,1)}, u32[]{:S(2)}, u32[]{:S(2)}) collective-permute-start(bf16[96,48,128]{2,1,0:T(8,128)(2,1)} %get-tuple-element.149), channel_id=1, source_target_pairs={{0,1},{1,0},{2,3},{3,2},{4,5},{5,4},{6,7},{7,6},{8,9},{9,8},{10,11... | collective-permute-start | bytes 3538952 | tf_op jit(solution)/shard_map/ppermute | solution.py:702
  168.5 5.6 %copy-start.33 = (s32[3]{0:T(128)}, s32[3]{0:T(128)S(1)}, u32[]{:S(2)}) copy-start(s32[3]{0:T(128)S(1)} %pad_add_fusion.2.refs_0_) | copy-start | bytes 40
  170.2 8.8 %copy-start.14 = (bf16[4,1152,256]{2,1,0:T(8,128)(2,1)S(1)}, bf16[4,1152,256]{2,1,0:T(8,128)(2,1)}, u32[]{:S(2)}) copy-start(bf16[4,1152,256]{2,1,0:T(8,128)(2,1)} %get-tuple-element.150.refs_2_) | copy-start | bytes 7077892
  170.2 8.8 %copy-start.18 = (bf16[256,256]{1,0:T(8,128)(2,1)S(1)}, bf16[256,256]{1,0:T(8,128)(2,1)}, u32[]{:S(2)}) copy-start(bf16[256,256]{1,0:T(8,128)(2,1)} %copy-done.17) | copy-start | bytes 393220
  170.2 8.8 %copy-start.20 = (bf16[256,256]{1,0:T(8,128)(2,1)S(1)}, bf16[256,256]{1,0:T(8,128)(2,1)}, u32[]{:S(2)}) copy-start(bf16[256,256]{1,0:T(8,128)(2,1)} %copy-done.19) | copy-start | bytes 393220
  170.2 8.8 %copy-start.22 = (bf16[192,192]{1,0:T(8,128)(2,1)S(1)}, bf16[192,192]{1,0:T(8,128)(2,1)}, u32[]{:S(2)}) copy-start(bf16[192,192]{1,0:T(8,128)(2,1)} %copy-done.21) | copy-start | bytes 221188
  170.2 8.8 %copy-start.24 = (bf16[192,192]{1,0:T(8,128)(2,1)S(1)}, bf16[192,192]{1,0:T(8,128)(2,1)}, u32[]{:S(2)}) copy-start(bf16[192,192]{1,0:T(8,128)(2,1)} %copy-done.23) | copy-start | bytes 221188
  174.1 20.0 %collective-permute-start.4 = (bf16[512,768]{1,0:T(8,128)(2,1)S(1)}, bf16[512,768]{1,0:T(8,128)(2,1)S(1)}, u32[]{:S(2)}, u32[]{:S(2)}) collective-permute-start(bf16[512,768]{1,0:T(8,128)(2,1)S(1)} %get-tuple-element.144), channel_id=1, source_target_pairs={{0,2},{1,3},{2,0},{3,1},{4,6},{5,7},{6,4},{7,5},{8,10},{9,11},{10,... | collective-permute-start | bytes 2359304 | tf_op jit(solution)/shard_map/ppermute | solution.py:746
  175.9 19.5 %collective-permute-start.5 = (bf16[512,768]{1,0:T(8,128)(2,1)S(1)}, bf16[512,768]{1,0:T(8,128)(2,1)S(1)}, u32[]{:S(2)}, u32[]{:S(2)}) collective-permute-start(bf16[512,768]{1,0:T(8,128)(2,1)S(1)} %get-tuple-element.146), channel_id=1, source_target_pairs={{0,4},{1,5},{2,6},{3,7},{4,0},{5,1},{6,2},{7,3},{8,12},{9,13},{10,... | collective-permute-start | bytes 2359304 | tf_op jit(solution)/shard_map/ppermute | solution.py:746
  177.4 19.2 %collective-permute-start.6 = (bf16[512,768]{1,0:T(8,128)(2,1)S(1)}, bf16[512,768]{1,0:T(8,128)(2,1)S(1)}, u32[]{:S(2)}, u32[]{:S(2)}) collective-permute-start(bf16[512,768]{1,0:T(8,128)(2,1)S(1)} %get-tuple-element.148), channel_id=1, source_target_pairs={{0,8},{1,9},{2,10},{3,11},{4,12},{5,13},{6,14},{7,15},{8,0},{9,1},... | collective-permute-start | bytes 2359304 | tf_op jit(solution)/shard_map/ppermute | solution.py:746
  178.9 17.6 %copy-start.31 = (s32[3]{0:T(128)}, s32[3]{0:T(128)S(1)}, u32[]{:S(2)}) copy-start(s32[3]{0:T(128)S(1)} %pad_add_fusion.1.refs_0_) | copy-start | bytes 40
  197.7 10.0 %collective-permute-start.8 = (bf16[256,768]{1,0:T(8,128)(2,1)S(1)}, bf16[256,768]{1,0:T(8,128)(2,1)S(1)}, u32[]{:S(2)}, u32[]{:S(2)}) collective-permute-start(bf16[256,768]{1,0:T(8,128)(2,1)S(1)} %get-tuple-element.153), channel_id=1, source_target_pairs={{0,4},{1,5},{2,6},{3,7},{4,0},{5,1},{6,2},{7,3},{8,12},{9,13},{10,... | collective-permute-start | bytes 1179656 | tf_op jit(solution)/shard_map/ppermute | solution.py:746
  198.3 9.7 %collective-permute-start.9 = (bf16[256,768]{1,0:T(8,128)(2,1)S(1)}, bf16[256,768]{1,0:T(8,128)(2,1)S(1)}, u32[]{:S(2)}, u32[]{:S(2)}) collective-permute-start(bf16[256,768]{1,0:T(8,128)(2,1)S(1)} %get-tuple-element.155), channel_id=1, source_target_pairs={{0,8},{1,9},{2,10},{3,11},{4,12},{5,13},{6,14},{7,15},{8,0},{9,1},... | collective-permute-start | bytes 1179656 | tf_op jit(solution)/shard_map/ppermute | solution.py:746
  199.8 9.4 %collective-permute-start.10 = (bf16[256,768]{1,0:T(8,128)(2,1)S(1)}, bf16[256,768]{1,0:T(8,128)(2,1)S(1)}, u32[]{:S(2)}, u32[]{:S(2)}) collective-permute-start(bf16[256,768]{1,0:T(8,128)(2,1)S(1)} %get-tuple-element.157), channel_id=1, source_target_pairs={{0,2},{1,3},{2,0},{3,1},{4,6},{5,7},{6,4},{7,5},{8,10},{9,11},{10,... | collective-permute-start | bytes 1179656 | tf_op jit(solution)/shard_map/ppermute | solution.py:746
  206.3 10.8 %collective-permute-start.15 = (bf16[48,48,128]{2,1,0:T(8,128)(2,1)S(1)}, bf16[48,48,128]{2,1,0:T(8,128)(2,1)S(1)}, u32[]{:S(2)}, u32[]{:S(2)}) collective-permute-start(bf16[48,48,128]{2,1,0:T(8,128)(2,1)S(1)} %get-tuple-element.171), channel_id=1, source_target_pairs={{0,1},{1,0},{2,3},{3,2},{4,5},{5,4},{6,7},{7,6},{8,9},{9,8},{10,11... | collective-permute-start | bytes 1769480 | tf_op jit(solution)/shard_map/ppermute | solution.py:702
  206.3 10.7 %collective-permute-start.14 = (bf16[48,48,128]{2,1,0:T(8,128)(2,1)S(1)}, bf16[48,48,128]{2,1,0:T(8,128)(2,1)S(1)}, u32[]{:S(2)}, u32[]{:S(2)}) collective-permute-start(bf16[48,48,128]{2,1,0:T(8,128)(2,1)S(1)} %get-tuple-element.170), channel_id=1, source_target_pairs={{0,1},{1,0},{2,3},{3,2},{4,5},{5,4},{6,7},{7,6},{8,9},{9,8},{10,11... | collective-permute-start | bytes 1769480 | tf_op jit(solution)/shard_map/ppermute | solution.py:702
  210.1 5.7 %collective-permute-start.11 = (bf16[128,768]{1,0:T(8,128)(2,1)S(1)}, bf16[128,768]{1,0:T(8,128)(2,1)S(1)}, u32[]{:S(2)}, u32[]{:S(2)}) collective-permute-start(bf16[128,768]{1,0:T(8,128)(2,1)S(1)} %get-tuple-element.161), channel_id=1, source_target_pairs={{0,8},{1,9},{2,10},{3,11},{4,12},{5,13},{6,14},{7,15},{8,0},{9,1},... | collective-permute-start | bytes 589832 | tf_op jit(solution)/shard_map/ppermute | solution.py:746
  210.6 5.7 %collective-permute-start.12 = (bf16[128,768]{1,0:T(8,128)(2,1)S(1)}, bf16[128,768]{1,0:T(8,128)(2,1)S(1)}, u32[]{:S(2)}, u32[]{:S(2)}) collective-permute-start(bf16[128,768]{1,0:T(8,128)(2,1)S(1)} %get-tuple-element.163), channel_id=1, source_target_pairs={{0,2},{1,3},{2,0},{3,1},{4,6},{5,7},{6,4},{7,5},{8,10},{9,11},{10,... | collective-permute-start | bytes 589832 | tf_op jit(solution)/shard_map/ppermute | solution.py:746
  211.2 5.7 %collective-permute-start.13 = (bf16[128,768]{1,0:T(8,128)(2,1)S(1)}, bf16[128,768]{1,0:T(8,128)(2,1)S(1)}, u32[]{:S(2)}, u32[]{:S(2)}) collective-permute-start(bf16[128,768]{1,0:T(8,128)(2,1)S(1)} %get-tuple-element.165), channel_id=1, source_target_pairs={{0,4},{1,5},{2,6},{3,7},{4,0},{5,1},{6,2},{7,3},{8,12},{9,13},{10,... | collective-permute-start | bytes 589832 | tf_op jit(solution)/shard_map/ppermute | solution.py:746
  219.1 43.7 %all-to-all-start.3 = ((bf16[16,3,48,384]{3,2,1,0:T(8,128)(2,1)}), bf16[16,3,48,384]{3,2,1,0:T(8,128)(2,1)S(1)}, u32[]{:S(2)}, u32[]{:S(2)}) async-start(bf16[16,3,48,384]{3,2,1,0:T(8,128)(2,1)} %lon_backward.3.refs_2_), calls=%async_computation.3 | async-start | bytes 3538944 | tf_op jit(solution)/shard_map/all_to_all | solution.py:699
  223.8 1.5 collective-permute-start.16
  226.2 36.6 %collective-permute-start.17 = (bf16[432,768]{1,0:T(8,128)(2,1)}, bf16[432,768]{1,0:T(8,128)(2,1)S(1)}, u32[]{:S(2)}, u32[]{:S(2)}) collective-permute-start(bf16[432,768]{1,0:T(8,128)(2,1)} %get-tuple-element.177), channel_id=1, source_target_pairs={{0,16},{1,17},{2,18},{3,19},{4,20},{5,21},{6,22},{7,23},{8,24},{9,... | collective-permute-start | bytes 1990664 | tf_op jit(solution)/shard_map/ppermute | solution.py:746
  262.8 11.6 %copy-start.11 = (bf16[16,3,48,384]{3,2,1,0:T(8,128)(2,1)}, bf16[16,3,48,384]{3,2,1,0:T(8,128)(2,1)S(1)}, u32[]{:S(2)}) copy-start(bf16[16,3,48,384]{3,2,1,0:T(8,128)(2,1)S(1)} %all-to-all-done.3.refs_0_) | copy-start | bytes 5308420
  262.8 22.5 %copy-start.32 = (s32[3]{0:T(128)S(1)}, s32[3]{0:T(128)}, u32[]{:S(2)}) copy-start(s32[3]{0:T(128)} %copy-done.31) | copy-start | bytes 40
  263.0 7.0 %collective-permute-start.18 = (bf16[144,768]{1,0:T(8,128)(2,1)S(1)}, bf16[144,768]{1,0:T(8,128)(2,1)S(1)}, u32[]{:S(2)}, u32[]{:S(2)}) collective-permute-start(bf16[144,768]{1,0:T(8,128)(2,1)S(1)} %get-tuple-element.180), channel_id=1, source_target_pairs={{0,8},{1,9},{2,10},{3,11},{4,12},{5,13},{6,14},{7,15},{8,0},{9,1},... | collective-permute-start | bytes 663560 | tf_op jit(solution)/shard_map/ppermute | solution.py:746
  263.6 8.6 %collective-permute-start.19 = (bf16[144,768]{1,0:T(8,128)(2,1)S(1)}, bf16[144,768]{1,0:T(8,128)(2,1)S(1)}, u32[]{:S(2)}, u32[]{:S(2)}) collective-permute-start(bf16[144,768]{1,0:T(8,128)(2,1)S(1)} %get-tuple-element.182), channel_id=1, source_target_pairs={{0,2},{1,3},{2,0},{3,1},{4,6},{5,7},{6,4},{7,5},{8,10},{9,11},{10,... | collective-permute-start | bytes 663560 | tf_op jit(solution)/shard_map/ppermute | solution.py:746
  267.3 6.4 %collective-permute-start.20 = (bf16[144,768]{1,0:T(8,128)(2,1)S(1)}, bf16[144,768]{1,0:T(8,128)(2,1)S(1)}, u32[]{:S(2)}, u32[]{:S(2)}) collective-permute-start(bf16[144,768]{1,0:T(8,128)(2,1)S(1)} %get-tuple-element.184), channel_id=1, source_target_pairs={{0,4},{1,5},{2,6},{3,7},{4,0},{5,1},{6,2},{7,3},{8,12},{9,13},{10,... | collective-permute-start | bytes 663560 | tf_op jit(solution)/shard_map/ppermute | solution.py:746
  274.4 10.3 %collective-permute-start.21 = (bf16[288,768]{1,0:T(8,128)(2,1)S(1)}, bf16[288,768]{1,0:T(8,128)(2,1)S(1)}, u32[]{:S(2)}, u32[]{:S(2)}) collective-permute-start(bf16[288,768]{1,0:T(8,128)(2,1)S(1)} %get-tuple-element.186), channel_id=1, source_target_pairs={{0,4},{1,5},{2,6},{3,7},{4,0},{5,1},{6,2},{7,3},{8,12},{9,13},{10,... | collective-permute-start | bytes 1327112 | tf_op jit(solution)/shard_map/ppermute | solution.py:746
  274.8 10.2 %collective-permute-start.22 = (bf16[288,768]{1,0:T(8,128)(2,1)S(1)}, bf16[288,768]{1,0:T(8,128)(2,1)S(1)}, u32[]{:S(2)}, u32[]{:S(2)}) collective-permute-start(bf16[288,768]{1,0:T(8,128)(2,1)S(1)} %get-tuple-element.188), channel_id=1, source_target_pairs={{0,8},{1,9},{2,10},{3,11},{4,12},{5,13},{6,14},{7,15},{8,0},{9,1},... | collective-permute-start | bytes 1327112 | tf_op jit(solution)/shard_map/ppermute | solution.py:746
  275.1 10.3 %collective-permute-start.23 = (bf16[288,768]{1,0:T(8,128)(2,1)S(1)}, bf16[288,768]{1,0:T(8,128)(2,1)S(1)}, u32[]{:S(2)}, u32[]{:S(2)}) collective-permute-start(bf16[288,768]{1,0:T(8,128)(2,1)S(1)} %get-tuple-element.190), channel_id=1, source_target_pairs={{0,2},{1,3},{2,0},{3,1},{4,6},{5,7},{6,4},{7,5},{8,10},{9,11},{10,... | collective-permute-start | bytes 1327112 | tf_op jit(solution)/shard_map/ppermute | solution.py:746
  287.2 18.8 %collective-permute-start.26 = (bf16[576,768]{1,0:T(8,128)(2,1)S(1)}, bf16[576,768]{1,0:T(8,128)(2,1)S(1)}, u32[]{:S(2)}, u32[]{:S(2)}) collective-permute-start(bf16[576,768]{1,0:T(8,128)(2,1)S(1)} %get-tuple-element.202), channel_id=1, source_target_pairs={{0,2},{1,3},{2,0},{3,1},{4,6},{5,7},{6,4},{7,5},{8,10},{9,11},{10,... | collective-permute-start | bytes 2654216 | tf_op jit(solution)/shard_map/ppermute | solution.py:746
  287.7 18.4 %collective-permute-start.27 = (bf16[576,768]{1,0:T(8,128)(2,1)S(1)}, bf16[576,768]{1,0:T(8,128)(2,1)S(1)}, u32[]{:S(2)}, u32[]{:S(2)}) collective-permute-start(bf16[576,768]{1,0:T(8,128)(2,1)S(1)} %get-tuple-element.204), channel_id=1, source_target_pairs={{0,4},{1,5},{2,6},{3,7},{4,0},{5,1},{6,2},{7,3},{8,12},{9,13},{10,... | collective-permute-start | bytes 2654216 | tf_op jit(solution)/shard_map/ppermute | solution.py:746
  289.3 18.3 %collective-permute-start.28 = (bf16[576,768]{1,0:T(8,128)(2,1)S(1)}, bf16[576,768]{1,0:T(8,128)(2,1)S(1)}, u32[]{:S(2)}, u32[]{:S(2)}) collective-permute-start(bf16[576,768]{1,0:T(8,128)(2,1)S(1)} %get-tuple-element.206), channel_id=1, source_target_pairs={{0,8},{1,9},{2,10},{3,11},{4,12},{5,13},{6,14},{7,15},{8,0},{9,1},... | collective-permute-start | bytes 2654216 | tf_op jit(solution)/shard_map/ppermute | solution.py:746
  291.2 9.3 %copy-start.30 = (f32[1,3072]{1,0:T(1,128)S(1)}, f32[1,3072]{1,0:T(1,128)}, u32[]{:S(2)}) copy-start(f32[1,3072]{1,0:T(1,128)} %copy-done.29) | copy-start | bytes 36868
  291.2 9.4 %copy-start.38 = (f32[1,768]{1,0:T(1,128)S(1)}, f32[1,768]{1,0:T(1,128)}, u32[]{:S(2)}) copy-start(f32[1,768]{1,0:T(1,128)} %get-tuple-element.195.refs_3_) | copy-start | bytes 9220
  291.2 9.4 %copy-start.39 = (f32[1,768]{1,0:T(1,128)S(1)}, f32[1,768]{1,0:T(1,128)}, u32[]{:S(2)}) copy-start(f32[1,768]{1,0:T(1,128)} %get-tuple-element.196.refs_4_) | copy-start | bytes 9220
  291.2 16.4 %copy-start.16 = (bf16[576,768]{1,0:T(8,128)(2,1)S(1)}, bf16[576,768]{1,0:T(8,128)(2,1)}, u32[]{:S(2)}) copy-start(bf16[576,768]{1,0:T(8,128)(2,1)} %copy-done.15) | copy-start | bytes 2654212
  291.2 16.4 %copy-start.34 = (s32[3]{0:T(128)S(1)}, s32[3]{0:T(128)}, u32[]{:S(2)}) copy-start(s32[3]{0:T(128)} %copy-done.33) | copy-start | bytes 40
  301.9 1.2 collective-permute-start.24
  308.8 9.9 %collective-permute-start.31 = (bf16[3456,768]{1,0:T(8,128)(2,1)S(1)}, bf16[3456,768]{1,0:T(8,128)(2,1)S(1)}, u32[]{:S(2)}, u32[]{:S(2)}) collective-permute-start(bf16[3456,768]{1,0:T(8,128)(2,1)S(1)} %bitcast.75), channel_id=1, source_target_pairs={{0,1},{1,0},{2,3},{3,2},{4,5},{5,4},{6,7},{7,6},{8,9},{9,8},{10,11... | collective-permute-start | bytes 15925256 | tf_op jit(solution)/shard_map/ppermute | solution.py:746
  308.9 3.9 %collective-permute-start.25 = (f32[1,6912]{1,0:T(1,128)S(1)}, f32[1,6912]{1,0:T(1,128)S(1)}, u32[]{:S(2)}, u32[]{:S(2)}) collective-permute-start(f32[1,6912]{1,0:T(1,128)S(1)} %get-tuple-element.201), channel_id=1, source_target_pairs={{0,2},{1,3},{2,0},{3,1},{4,6},{5,7},{6,4},{7,5},{8,10},{9,11},{10,... | collective-permute-start | bytes 82952 | tf_op jit(solution)/shard_map/ppermute | solution.py:746
  312.8 4.8 %collective-permute-start.29 = (f32[1,6912]{1,0:T(1,128)S(1)}, f32[1,6912]{1,0:T(1,128)S(1)}, u32[]{:S(2)}, u32[]{:S(2)}) collective-permute-start(f32[1,6912]{1,0:T(1,128)S(1)} %get-tuple-element.209), channel_id=1, source_target_pairs={{0,4},{1,5},{2,6},{3,7},{4,0},{5,1},{6,2},{7,3},{8,12},{9,13},{10,... | collective-permute-start | bytes 82952 | tf_op jit(solution)/shard_map/ppermute | solution.py:746
  317.6 5.5 %collective-permute-start.30 = (f32[1,6912]{1,0:T(1,128)S(1)}, f32[1,6912]{1,0:T(1,128)S(1)}, u32[]{:S(2)}, u32[]{:S(2)}) collective-permute-start(f32[1,6912]{1,0:T(1,128)S(1)} %get-tuple-element.212), channel_id=1, source_target_pairs={{0,8},{1,9},{2,10},{3,11},{4,12},{5,13},{6,14},{7,15},{8,0},{9,1},... | collective-permute-start | bytes 82952 | tf_op jit(solution)/shard_map/ppermute | solution.py:746
  323.1 4.8 %collective-permute-start.32 = (f32[1,6912]{1,0:T(1,128)S(1)}, f32[1,6912]{1,0:T(1,128)S(1)}, u32[]{:S(2)}, u32[]{:S(2)}) collective-permute-start(f32[1,6912]{1,0:T(1,128)S(1)} %get-tuple-element.218), channel_id=1, source_target_pairs={{0,16},{1,17},{2,18},{3,19},{4,20},{5,21},{6,22},{7,23},{8,24},{9,... | collective-permute-start | bytes 82952 | tf_op jit(solution)/shard_map/ppermute | solution.py:746
  (29 other events, 72.1 us)

commit v6 on v5

--- a/solution.py
+++ b/solution.py
@@ -37,7 +37,11 @@
         kernel(*refs[: lead + n_in], *refs[lead + n_in + n_after :])
 
     if pin:
-        args = [pltpu.with_memory_space_constraint(x, pltpu.HBM) for x in args]
+        at = range(len(args)) if pin is True else pin
+        args = [
+            pltpu.with_memory_space_constraint(x, pltpu.HBM) if k in at else x
+            for k, x in enumerate(args)
+        ]
     grid = kw.pop("grid", (1,))
     whole = lambda x: pl.BlockSpec(x.shape, lambda *_, n=len(x.shape): (0,) * n)
     specs = list(in_specs) if in_specs is not None else [whole(a) for a in args]
@@ -62,7 +66,7 @@
     return list(got) if isinstance(out_shape, (list, tuple)) else got[0]
 
 
-SPLIT = 2
+SPLIT = 1
 UNROLL = 1
 WIDE = 12
 
@@ -950,7 +954,7 @@
         [shape(pad_shape, F32), shape(pad_shape, BF)], 8.5, after=[cot_pad],
         grid=(lat_steps,),
         in_specs=[here_spec, pad_spec, mask_spec, packed_spec, row_spec, row_spec],
-        out_specs=[pad_spec, pad_spec], vmem=56, name="second_norm",
+        out_specs=[pad_spec, pad_spec], vmem=40, pin=(0, 1), name="second_norm",
     )
     tokens2, cot2 = tokens.reshape(-1, channels), cot_pad.reshape(-1, channels)
     count, hidden = tokens2.shape[0], expand_weight.shape[1]
@@ -1023,11 +1027,12 @@
             in_specs=[
                 here, here, pl.BlockSpec((steps,) + modes.shape[1:], lambda i, k=k: (k, 0, 0)),
             ] + [const(x) for x in (lat_fwd, lat_inv, wa, ba, wb, bb, *grads)],
-            scratch_shapes=[pltpu.VMEM((2 * lats * run, LANES), F32)], name="mix_back",
+            scratch_shapes=[pltpu.VMEM((2 * lats * run, LANES), F32)], vmem=34, name="mix_back",
         )
         pieces.append((o, swap(t)))
         grads = [g]
         token = sums.halve(after=[o])
+    token = sums.halve(after=[token])
     token = sums.settle(after=[token])
     send = lon_backward(
         [p[0] for p in pieces] + [p[1] for p in pieces], lon_inv, after=[token]
@@ -1062,7 +1067,7 @@
         last_kernel, [x5, grad_resid, mask, got.reshape(packed_shape), row(first_gain)],
         [turned_shape] + [one_row] * 2, 9.0, after=[token],
         grid=(lat_steps,), in_specs=[here_spec, pad_spec, mask_spec, packed_spec, row_spec],
-        out_specs=[turned_spec, row_spec, row_spec], vmem=56, name="first_back",
+        out_specs=[turned_spec, row_spec, row_spec], vmem=36, pin=(0, 1), name="first_back",
     )
     tail_sum = Tail(
         call(

time: 331 us -> 331 us (level)
    pallas_call x38 -> x37, Pallas kernels: 133 us -> 133 us  [call(): pl.pallas_call(body, grid_spec=pltpu.PrefetchScalarGridSpec(num_scalar_pr...]
    unnamed x114 -> x112, local copies, waits for them, and re-layouts: 27.6 us -> 27.5 us
  transfers between devices with their start and end apart: 37 -> 36, of which waited for: 27 -> 27; matrix products, arithmetic and copies ran while one was open for 2% -> 2% of each run, Pallas kernels for 21% -> 21%
where the time goes in v6:
time: 331 us; the launch traced here: 330 us
  Pallas kernels  133 us (40%)
  waiting for transfers between devices  115 us (35%)
  starting transfers between devices  48.3 us (15%)
  local copies, waits for them, and re-layouts  32 us (10%)
    pallas_call x37, Pallas kernels, call(): pl.pallas_call(body, grid_spec=pltpu.PrefetchScalarGridSpec(num_scalar_pr...  133 us
    all_to_all x4, waiting for transfers between devices, exchange(): lax.all_to_all(x, AXES, 0, 0, axis_index_groups=snap_groups, tiled=True)  64.2 us
    ppermute x28, waiting for transfers between devices, partner(): return lax.ppermute(x, AXES, [(d, d ^ flip) for d in range(devices)])  46.5 us
    ppermute x28, starting transfers between devices, partner(): return lax.ppermute(x, AXES, [(d, d ^ flip) for d in range(devices)])  28.3 us
    unnamed x112, local copies, waits for them, and re-layouts  27.5 us
    all_to_all x4, starting transfers between devices, exchange(): lax.all_to_all(x, AXES, 0, 0, axis_index_groups=snap_groups, tiled=True)  19.7 us
  transfers between devices with their start and end apart: 36, of which 27 were waited for; matrix products, arithmetic and copies ran while one was open for 2% of the time, Pallas kernels for 21%

profile of v6, /device:TPU:0, one launch (start us, length us, event | category | flops | bytes accessed | tf_op | source)
XLA Modules:
  0.0 329.7 jit_solution(14985358211861496982)
XLA Ops:
  0.7 1.8 copy.37
  2.5 4.3 %first_norm.1 = (bf16[2,3,4,48,768]{4,3,2,1,0:T(8,128)(2,1)}, bf16[8,2,3,48,384]{4,3,2,1,0:T(8,128)(2,1)}) custom-call(bf16[2,3,4,45,768]{4,3,2,1,0:T(8,128)(2,1)S(1)} %bitcast.61, s32[24,45]{1,0:T(8,128)S(1)} %copy-done.25, f32[768]{0:T(1024)S(1)} %copy-done.28, f32[768]{0:T(1024)S(1)} %copy-done.38), custom_call_target="tpu_custom_call" | custom-call | bytes 600000 | tf_op jit(solution)/shard_map/first_norm/pallas_call | solution.py:50
  6.8 6.3 %all-to-all-start = ((bf16[16,3,48,384]{3,2,1,0:T(8,128)(2,1)}), bf16[16,3,48,384]{3,2,1,0:T(8,128)(2,1)S(1)}, u32[]{:S(2)}, u32[]{:S(2)}) async-start(bf16[16,3,48,384]{3,2,1,0:T(8,128)(2,1)} %bitcast.76), calls=%async_computation | async-start | bytes 3538944 | tf_op jit(solution)/shard_map/all_to_all | solution.py:703
  14.1 24.3 %all-to-all-done.refs_0_ = bf16[16,3,48,384]{3,2,1,0:T(8,128)(2,1)S(1)} async-done(((bf16[16,3,48,384]{3,2,1,0:T(8,128)(2,1)}), bf16[16,3,48,384]{3,2,1,0:T(8,128)(2,1)S(1)}, u32[]{:S(2)}, u32[]{:S(2)}) %all-to-all-start) | async-done | bytes 1769504 | tf_op jit(solution)/shard_map/all_to_all | solution.py:703
  38.4 3.5 %lon_forward.2 = (bf16[96,48,128]{2,1,0:T(8,128)(2,1)S(1)}, bf16[96,48,128]{2,1,0:T(8,128)(2,1)}) custom-call(bf16[16,3,48,384]{3,2,1,0:T(8,128)(2,1)S(1)} %all-to-all-done.refs_0_, bf16[192,192]{1,0:T(8,128)(2,1)S(1)} %dynamic-slice_bitcast_fusion.5.refs_1_), custom_call_target="tpu_custom_call" | custom-call | bytes 550000 | tf_op jit(solution)/shard_map/lon_forward/pallas_call | solution.py:50
  43.2 1.8 collective-permute-done.refs_1_
  44.9 8.5 %mix.1 = (bf16[48,96,128]{2,1,0:T(8,128)(2,1)S(1)}, bf16[48,96,128]{2,1,0:T(8,128)(2,1)S(1)}, bf16[4,1152,256]{2,1,0:T(8,128)(2,1)}) custom-call(bf16[96,48,128]{2,1,0:T(8,128)(2,1)S(1)} %get-tuple-element.120.refs_0_, bf16[96,48,128]{2,1,0:T(8,128)(2,1)S(1)} %collective-permute-done.refs_1_, bf16[192,192]{1,0:T(8,128)(2,1)S(1)} %get-tuple-element.232.refs_2_.refs_3_, ...), custom_call_target="tpu_custom_call" | custom-call | bytes 2200000 | tf_op jit(solution)/shard_map/mix/pallas_call | solution.py:50
  53.6 2.7 collective-permute-done.1.refs_1_
  56.3 2.1 lon_backward.2.refs_1_
  58.3 4.1 %all-to-all-start.1 = ((bf16[16,3,48,384]{3,2,1,0:T(8,128)(2,1)}), bf16[16,3,48,384]{3,2,1,0:T(8,128)(2,1)S(1)}, u32[]{:S(2)}, u32[]{:S(2)}) async-start(bf16[16,3,48,384]{3,2,1,0:T(8,128)(2,1)} %lon_backward.2.refs_1_), calls=%async_computation.1 | async-start | bytes 3538944 | tf_op jit(solution)/shard_map/all_to_all | solution.py:703
  63.1 1.8 copy.38
  65.2 22.6 %all-to-all-done.1 = bf16[16,3,48,384]{3,2,1,0:T(8,128)(2,1)S(1)} async-done(((bf16[16,3,48,384]{3,2,1,0:T(8,128)(2,1)}), bf16[16,3,48,384]{3,2,1,0:T(8,128)(2,1)S(1)}, u32[]{:S(2)}, u32[]{:S(2)}) %all-to-all-start.1) | async-done | bytes 1769504 | tf_op jit(solution)/shard_map/all_to_all | solution.py:703
  88.5 5.5 %second_norm.1 = (f32[2,3,4,48,768]{4,3,2,1,0:T(8,128)S(1)}, bf16[2,3,4,48,768]{4,3,2,1,0:T(8,128)(2,1)S(1)}) custom-call(bf16[2,3,4,45,768]{4,3,2,1,0:T(8,128)(2,1)} %bitcast.62, bf16[2,3,4,48,768]{4,3,2,1,0:T(8,128)(2,1)} %get-tuple-element.118.refs_1_, s32[24,45]{1,0:T(8,128)S(1)} %copy-done.25, bf16[8,2,3,48,384]{4,3,2,1,0:T(8,128)(2,1)S(1)} %bitcast.68, ...), custom_call_target="tpu_custom_call" | custom-call | bytes 850000 | tf_op jit(solution)/shard_map/second_norm/pallas_call | solution.py:50
  94.0 1.2 copy-done.11
  95.3 1.8 copy-done.13
  97.1 24.1 %mlp_chain.1 = (bf16[1152,3072]{1,0:T(8,128)(2,1)}, bf16[1152,3072]{1,0:T(8,128)(2,1)}, bf16[1152,768]{1,0:T(8,128)(2,1)}, f32[1,3072]{1,0:T(1,128)S(1)}) custom-call(bf16[1152,768]{1,0:T(8,128)(2,1)} %bitcast.65, bf16[1152,768]{1,0:T(8,128)(2,1)} %bitcast.55, bf16[768,3072]{1,0:T(8,128)(2,1)} %refs_2_.6, f32[1,3072]{1,0:T(1,128)} %bitcast.79, ...), custom_call_target="tpu_custom_call" | custom-call | bytes 2500000 | tf_op jit(solution)/shard_map/mlp_chain/pallas_call | solution.py:50
  121.2 8.2 %second_back.1 = (bf16[2,3,4,48,768]{4,3,2,1,0:T(8,128)(2,1)}, bf16[8,2,3,48,384]{4,3,2,1,0:T(8,128)(2,1)}, f32[1,768]{1,0:T(1,128)}, f32[1,768]{1,0:T(1,128)}, f32[1,768]{1,0:T(1,128)}) custom-call(f32[2,3,4,48,768]{4,3,2,1,0:T(8,128)} %copy-done.13, bf16[2,3,4,48,768]{4,3,2,1,0:T(8,128)(2,1)} %bitcast.77, bf16[2,3,4,48,768]{4,3,2,1,0:T(8,128)(2,1)} %copy-done.2, ...), custom_call_target="tpu_custom_call" | custom-call | bytes 900000 | tf_op jit(solution)/shard_map/second_back/pallas_call | solution.py:50
  129.3 4.7 %all-to-all-start.2 = ((bf16[16,3,48,384]{3,2,1,0:T(8,128)(2,1)}), bf16[16,3,48,384]{3,2,1,0:T(8,128)(2,1)}, u32[]{:S(2)}, u32[]{:S(2)}) async-start(bf16[16,3,48,384]{3,2,1,0:T(8,128)(2,1)} %bitcast.75), calls=%async_computation.2 | async-start | bytes 3538944 | tf_op jit(solution)/shard_map/all_to_all | solution.py:703
  134.1 3.0 copy-done
  137.1 4.9 %reduce_grad.2 = (bf16[1536,768]{1,0:T(8,128)(2,1)}, f32[8,128]{1,0:T(8,128)S(1)}) custom-call(s32[1]{0:T(128)} %bitcast.25.refs_0_, bf16[1152,3072]{1,0:T(8,128)(2,1)S(1)} %copy-done, bf16[1152,768]{1,0:T(8,128)(2,1)S(1)} %bitcast.56, f32[1,768]{1,0:T(1,128)S(1)} %copy-done.30), custom_call_target="tpu_custom_call" | custom-call | bytes 500000 | tf_op jit(solution)/shard_map/reduce_grad/pallas_call | solution.py:50
  142.0 3.0 copy-done.4
  145.0 4.9 %expand_grad.2 = (bf16[1536,768]{1,0:T(8,128)(2,1)}, f32[8,128]{1,0:T(8,128)S(1)}) custom-call(s32[1]{0:T(128)} %bitcast.25.refs_0_, bf16[1152,3072]{1,0:T(8,128)(2,1)S(1)} %copy-done.4, bf16[1152,768]{1,0:T(8,128)(2,1)S(1)} %bitcast.66, f32[8,128]{1,0:T(8,128)S(1)} %get-tuple-element.130.refs_3_), custom_call_target="tpu_custom_call" | custom-call | bytes 500000 | tf_op jit(solution)/shard_map/expand_grad/pallas_call | solution.py:50
  151.0 4.0 %reduce_grad.3 = (bf16[1536,768]{1,0:T(8,128)(2,1)S(1)}, f32[8,128]{1,0:T(8,128)S(1)}) custom-call(s32[1]{0:T(128)} %bitcast.25.refs_0_, bf16[1152,3072]{1,0:T(8,128)(2,1)S(1)} %bitcast.53, bf16[1152,768]{1,0:T(8,128)(2,1)S(1)} %bitcast.57, f32[8,128]{1,0:T(8,128)S(1)} %get-tuple-element.131.refs_3_), custom_call_target="tpu_custom_call" | custom-call | bytes 500000 | tf_op jit(solution)/shard_map/reduce_grad/pallas_call | solution.py:50
  155.0 1.4 copy-done.6
  156.4 4.0 %expand_grad.3 = (bf16[1536,768]{1,0:T(8,128)(2,1)S(1)}, f32[8,128]{1,0:T(8,128)S(1)}) custom-call(s32[1]{0:T(128)} %bitcast.25.refs_0_, bf16[1152,3072]{1,0:T(8,128)(2,1)S(1)} %copy-done.4, bf16[1152,768]{1,0:T(8,128)(2,1)S(1)} %bitcast.67, f32[8,128]{1,0:T(8,128)S(1)} %get-tuple-element.134.refs_3_), custom_call_target="tpu_custom_call" | custom-call | bytes 500000 | tf_op jit(solution)/shard_map/expand_grad/pallas_call | solution.py:50
  160.4 1.4 copy-done.8
  164.0 5.0 %lon_forward.3 = (bf16[96,48,128]{2,1,0:T(8,128)(2,1)S(1)}, bf16[96,48,128]{2,1,0:T(8,128)(2,1)}) custom-call(bf16[16,3,48,384]{3,2,1,0:T(8,128)(2,1)} %all-to-all-done.2.refs_0_, bf16[192,192]{1,0:T(8,128)(2,1)S(1)} %copy-done.24, f32[8,128]{1,0:T(8,128)S(1)} %copy-done.40), custom_call_target="tpu_custom_call" | custom-call | bytes 550000 | tf_op jit(solution)/shard_map/lon_forward/pallas_call | solution.py:50
  169.2 1.7 copy-done.9
  170.9 3.9 %halve.3 = (bf16[512,768]{1,0:T(8,128)(2,1)S(1)}, bf16[512,768]{1,0:T(8,128)(2,1)S(1)}, bf16[512,768]{1,0:T(8,128)(2,1)S(1)}, bf16[512,768]{1,0:T(8,128)(2,1)S(1...) custom-call(s32[3]{0:T(128)S(1)} %pad_add_fusion.2.refs_0_, bf16[1536,768]{1,0:T(8,128)(2,1)S(1)} %copy-done.7, ...), custom_call_target="tpu_custom_call" | custom-call | bytes 300000 | tf_op jit(solution)/shard_map/halve/pallas_call | solution.py:50
  174.8 1.7 collective-permute-start.4
  176.6 1.5 collective-permute-start.5
  178.1 1.5 collective-permute-start.6
  179.6 12.4 %mix_back.1 = (bf16[48,96,128]{2,1,0:T(8,128)(2,1)S(1)}, bf16[48,96,128]{2,1,0:T(8,128)(2,1)S(1)}, f32[528,256]{1,0:T(8,128)S(1)}) custom-call(bf16[96,48,128]{2,1,0:T(8,128)(2,1)S(1)} %get-tuple-element.139.refs_13_.refs_0_, bf16[96,48,128]{2,1,0:T(8,128)(2,1)} %collective-permute-done.7.refs_1_, bf16[4,1152,256]{2,1,0:T(8,128)(2,1)S(1)} %copy-done.15, ...), custom_call_target="tpu_custom_call" | custom-call | bytes 1300000 | tf_op jit(solution)/shard_map/mix_back/pallas_call | solution.py:50
  192.2 2.5 collective-permute-done.4.refs_2_.refs_4_
  194.8 1.3 collective-permute-done.5.refs_6_.refs_8_
  199.0 1.5 collective-permute-start.9
  201.1 7.2 %collective-permute-done.8.refs_2_.refs_4_ = bf16[256,768]{1,0:T(8,128)(2,1)S(1)} collective-permute-done((bf16[256,768]{1,0:T(8,128)(2,1)S(1)}, bf16[256,768]{1,0:T(8,128)(2,1)S(1)}, u32[]{:S(2)}, u32[]{:S(2)}) %collective-permute-start.8) | collective-permute-done | bytes 393248 | tf_op jit(solution)/shard_map/ppermute | solution.py:750
  208.7 1.2 collective-permute-done.10.refs_10_.refs_12_
  212.0 1.4 collective-permute-start.13
  213.4 3.2 collective-permute-done.11.refs_1_
  217.8 2.1 lon_backward.3.refs_2_
  219.9 4.6 %all-to-all-start.3 = ((bf16[16,3,48,384]{3,2,1,0:T(8,128)(2,1)}), bf16[16,3,48,384]{3,2,1,0:T(8,128)(2,1)S(1)}, u32[]{:S(2)}, u32[]{:S(2)}) async-start(bf16[16,3,48,384]{3,2,1,0:T(8,128)(2,1)} %lon_backward.3.refs_2_), calls=%async_computation.3 | async-start | bytes 3538944 | tf_op jit(solution)/shard_map/all_to_all | solution.py:703
  226.9 2.6 collective-permute-start.16
  229.6 3.0 copy-done.1
  232.6 2.3 copy-done.10
  234.9 2.0 copy-done.14
  236.9 9.4 %branch.1 = (f32[45,24,768]{2,1,0:T(8,128)}, f32[8,128]{1,0:T(8,128)S(1)}) custom-call(bf16[2,3,4,48,3072]{4,3,2,1,0:T(8,128)(2,1)S(1)} %bitcast.54, bf16[3072,768]{1,0:T(8,128)(2,1)S(1)} %copy-done.10, f32[2,3,4,48,768]{4,3,2,1,0:T(8,128)S(1)} %copy-done.14, f32[1,768]{1,0:T(1,128)S(1)} %reshape.109.refs_3_, ...), custom_call_target="tpu_custom_call" | custom-call | bytes 1000000 | tf_op jit(solution)/shard_map/branch/pallas_call | solution.py:50
  246.3 17.3 %all-to-all-done.3.refs_0_ = bf16[16,3,48,384]{3,2,1,0:T(8,128)(2,1)S(1)} async-done(((bf16[16,3,48,384]{3,2,1,0:T(8,128)(2,1)}), bf16[16,3,48,384]{3,2,1,0:T(8,128)(2,1)S(1)}, u32[]{:S(2)}, u32[]{:S(2)}) %all-to-all-start.3) | async-done | bytes 1769504 | tf_op jit(solution)/shard_map/all_to_all | solution.py:703
  264.4 3.6 %collective-permute-start.18 = (bf16[144,768]{1,0:T(8,128)(2,1)S(1)}, bf16[144,768]{1,0:T(8,128)(2,1)S(1)}, u32[]{:S(2)}, u32[]{:S(2)}) collective-permute-start(bf16[144,768]{1,0:T(8,128)(2,1)S(1)} %get-tuple-element.176), channel_id=1, source_target_pairs={{0,2},{1,3},{2,0},{3,1},{4,6},{5,7},{6,4},{7,5},{8,10},{9,11},{10,... | collective-permute-start | bytes 663560 | tf_op jit(solution)/shard_map/ppermute | solution.py:750
  268.0 2.8 collective-permute-done.17.refs_2_
  270.8 2.2 collective-permute-done.18.refs_4_
  272.9 1.5 collective-permute-done.19.refs_6_
  276.7 8.8 %collective-permute-done.20.refs_2_ = bf16[288,768]{1,0:T(8,128)(2,1)S(1)} collective-permute-done((bf16[288,768]{1,0:T(8,128)(2,1)S(1)}, bf16[288,768]{1,0:T(8,128)(2,1)S(1)}, u32[]{:S(2)}, u32[]{:S(2)}) %collective-permute-start.20) | collective-permute-done | bytes 442400 | tf_op jit(solution)/shard_map/ppermute | solution.py:750
  287.6 1.6 collective-permute-start.26
  289.2 1.3 collective-permute-start.27
  290.5 8.9 %first_back.1 = (f32[45,24,768]{2,1,0:T(8,128)}, f32[1,768]{1,0:T(1,128)S(1)}, f32[1,768]{1,0:T(1,128)S(1)}) custom-call(bf16[2,3,4,45,768]{4,3,2,1,0:T(8,128)(2,1)} %bitcast.63, bf16[2,3,4,48,768]{4,3,2,1,0:T(8,128)(2,1)} %get-tuple-element.170.refs_1_, s32[24,45]{1,0:T(8,128)S(1)} %copy-done.26, bf16[8,2,3,48,384]{4,3,2,1,0:T(8,128)(2,1)S(1)} %bitcast.64, ...), custom_call_target="tpu_custom_call" | custom-call | bytes 900000 | tf_op jit(solution)/shard_map/first_back/pallas_call | solution.py:50
  300.7 5.1 %collective-permute-done.25.refs_2_ = bf16[576,768]{1,0:T(8,128)(2,1)S(1)} collective-permute-done((bf16[576,768]{1,0:T(8,128)(2,1)S(1)}, bf16[576,768]{1,0:T(8,128)(2,1)S(1)}, u32[]{:S(2)}, u32[]{:S(2)}) %collective-permute-start.25) | collective-permute-done | bytes 884768 | tf_op jit(solution)/shard_map/ppermute | solution.py:750
  306.0 1.5 collective-permute-done.27.refs_6_
  307.4 1.2 merge.5
  309.9 2.8 collective-permute-done.24.refs_1_
  313.0 4.4 %widen.2 = (f32[3072,768]{1,0:T(8,128)}, f32[768,3072]{1,0:T(8,128)}, bf16[12,16,768]{2,1,0:T(8,128)(2,1)S(1)}, bf16[12,16,768]{2,1,0:T(8,128)(2,1)S(1)}) custom-call(s32[1]{0:T(128)} %bitcast.25.refs_0_, bf16[3456,768]{1,0:T(8,128)(2,1)S(1)} %bitcast.59, bf16[3456,768]{1,0:T(8,128)(2,1)S(1)} %bitcast.60, f32[1,6912]{1,0:T(1,128)S(1)} %get-tuple-element.202.refs_3_.refs_0_), custom_call_target="tpu_custom_call" | custom-call | bytes 500000 | tf_op jit(solution)/shard_map/widen/pallas_call | solution.py:50
  318.6 4.4 %widen.3 = (f32[3072,768]{1,0:T(8,128)}, f32[768,3072]{1,0:T(8,128)}, bf16[12,16,768]{2,1,0:T(8,128)(2,1)S(1)}, bf16[12,16,768]{2,1,0:T(8,128)(2,1)S(1)}) custom-call(s32[1]{0:T(128)} %bitcast.25.refs_0_, bf16[3456,768]{1,0:T(8,128)(2,1)S(1)} %collective-permute-done.30.refs_1_.refs_2_, ...), custom_call_target="tpu_custom_call", output_to_operand_aliasing={{0}: (3, {}), {1}: (4, {})} | custom-call | bytes 500000 | tf_op jit(solution)/shard_map/widen/pallas_call | solution.py:50
  323.0 2.8 collective-permute-start.31
  325.8 1.2 spread.1
  (184 shorter events, 29.2 us)
Async XLA Ops:
  6.8 31.6 %all-to-all-start = ((bf16[16,3,48,384]{3,2,1,0:T(8,128)(2,1)}), bf16[16,3,48,384]{3,2,1,0:T(8,128)(2,1)S(1)}, u32[]{:S(2)}, u32[]{:S(2)}) async-start(bf16[16,3,48,384]{3,2,1,0:T(8,128)(2,1)} %bitcast.76), calls=%async_computation | async-start | bytes 3538944 | tf_op jit(solution)/shard_map/all_to_all | solution.py:703
  13.1 28.8 %copy-start.48 = (f32[2,768]{1,0:T(2,128)S(1)}, f32[2,768]{1,0:T(2,128)}, u32[]{:S(2)}) copy-start(f32[2,768]{1,0:T(2,128)} %param.27) | copy-start | bytes 18436
  13.1 28.9 %copy-start.49 = (f32[2,768]{1,0:T(2,128)S(1)}, f32[2,768]{1,0:T(2,128)}, u32[]{:S(2)}) copy-start(f32[2,768]{1,0:T(2,128)} %param.29) | copy-start | bytes 18436
  13.1 30.0 %copy-start.46 = (bf16[2,192,192]{2,1,0:T(8,128)(2,1)S(1)}, bf16[2,192,192]{2,1,0:T(8,128)(2,1)}, u32[]{:S(2)}) copy-start(bf16[2,192,192]{2,1,0:T(8,128)(2,1)} %constant.189.clone) | copy-start | bytes 442372
  13.1 30.0 %copy-start.47 = (bf16[2,192,192]{2,1,0:T(8,128)(2,1)S(1)}, bf16[2,192,192]{2,1,0:T(8,128)(2,1)}, u32[]{:S(2)}) copy-start(bf16[2,192,192]{2,1,0:T(8,128)(2,1)} %constant.188.clone) | copy-start | bytes 442372
  41.9 3.1 collective-permute-start
  42.1 11.4 %copy-start.32 = (f32[2,128]{1,0:T(2,128)}, f32[2,128]{1,0:T(2,128)S(1)}, u32[]{:S(2)}) copy-start(f32[2,128]{1,0:T(2,128)S(1)} %pad.18) | copy-start | bytes 3076
  42.1 11.3 %copy-start.34 = (f32[2,128]{1,0:T(2,128)}, f32[2,128]{1,0:T(2,128)S(1)}, u32[]{:S(2)}) copy-start(f32[2,128]{1,0:T(2,128)S(1)} %pad.16) | copy-start | bytes 3076
  43.0 10.5 %copy-start.16 = (bf16[256,256]{1,0:T(8,128)(2,1)}, bf16[256,256]{1,0:T(8,128)(2,1)S(1)}, u32[]{:S(2)}) copy-start(bf16[256,256]{1,0:T(8,128)(2,1)S(1)} %maximum_maximum_fusion.1.refs_6_.refs_7_) | copy-start | bytes 393220
  43.1 10.5 %copy-start.45 = (bf16[2,192,192]{2,1,0:T(8,128)(2,1)S(1)}, bf16[2,192,192]{2,1,0:T(8,128)(2,1)}, u32[]{:S(2)}) copy-start(bf16[2,192,192]{2,1,0:T(8,128)(2,1)} %constant.187.clone) | copy-start | bytes 442372
  43.1 13.2 %copy-start.18 = (bf16[256,256]{1,0:T(8,128)(2,1)}, bf16[256,256]{1,0:T(8,128)(2,1)S(1)}, u32[]{:S(2)}) copy-start(bf16[256,256]{1,0:T(8,128)(2,1)S(1)} %maximum_maximum_fusion.refs_4_.refs_5_) | copy-start | bytes 393220
  43.2 13.1 %copy-start.20 = (bf16[192,192]{1,0:T(8,128)(2,1)}, bf16[192,192]{1,0:T(8,128)(2,1)S(1)}, u32[]{:S(2)}) copy-start(bf16[192,192]{1,0:T(8,128)(2,1)S(1)} %get-tuple-element.231.refs_3_.refs_4_) | copy-start | bytes 221188
  43.2 15.2 %copy-start.22 = (bf16[192,192]{1,0:T(8,128)(2,1)}, bf16[192,192]{1,0:T(8,128)(2,1)S(1)}, u32[]{:S(2)}) copy-start(bf16[192,192]{1,0:T(8,128)(2,1)S(1)} %get-tuple-element.232.refs_2_.refs_3_) | copy-start | bytes 221188
  53.4 2.8 collective-permute-start.1
  58.3 29.4 %all-to-all-start.1 = ((bf16[16,3,48,384]{3,2,1,0:T(8,128)(2,1)}), bf16[16,3,48,384]{3,2,1,0:T(8,128)(2,1)S(1)}, u32[]{:S(2)}, u32[]{:S(2)}) async-start(bf16[16,3,48,384]{3,2,1,0:T(8,128)(2,1)} %lon_backward.2.refs_1_), calls=%async_computation.1 | async-start | bytes 3538944 | tf_op jit(solution)/shard_map/all_to_all | solution.py:703
  62.5 25.3 %copy-start.27 = (f32[1,768]{1,0:T(1,128)}, f32[1,768]{1,0:T(1,128)S(1)}, u32[]{:S(2)}) copy-start(f32[1,768]{1,0:T(1,128)S(1)} %reshape.102.refs_4_) | copy-start | bytes 9220
  65.1 28.9 %copy-start.2 = (bf16[2,3,4,48,768]{4,3,2,1,0:T(8,128)(2,1)}, bf16[2,3,4,48,768]{4,3,2,1,0:T(8,128)(2,1)S(1)}, u32[]{:S(2)}) copy-start(bf16[2,3,4,48,768]{4,3,2,1,0:T(8,128)(2,1)S(1)} %pad.69.refs_6_.refs_2_) | copy-start | bytes 5308420
  129.3 33.1 %all-to-all-start.2 = ((bf16[16,3,48,384]{3,2,1,0:T(8,128)(2,1)}), bf16[16,3,48,384]{3,2,1,0:T(8,128)(2,1)}, u32[]{:S(2)}, u32[]{:S(2)}) async-start(bf16[16,3,48,384]{3,2,1,0:T(8,128)(2,1)} %bitcast.75), calls=%async_computation.2 | async-start | bytes 3538944 | tf_op jit(solution)/shard_map/all_to_all | solution.py:703
  137.1 13.9 %slice-start = ((s8[7077888]{0:T(1024)(128)(4,1)}), s8[4194304]{0:T(1024)(128)(4,1)S(1)}, s32[]{:S(2)}) async-start(s8[7077888]{0:T(1024)(128)(4,1)} %bitcast.52), calls=%async_computation.4 | async-start | bytes 8388608
  145.0 6.0 %slice-start.1 = ((s8[7077888]{0:T(1024)(128)(4,1)}), s8[2883584]{0:T(1024)(128)(4,1)S(1)}, s32[]{:S(2)}) async-start(s8[7077888]{0:T(1024)(128)(4,1)} %bitcast.52), calls=%async_computation.5 | async-start | bytes 5767168
  149.9 19.3 %collective-permute-start.3 = (bf16[1536,768]{1,0:T(8,128)(2,1)}, bf16[1536,768]{1,0:T(8,128)(2,1)}, u32[]{:S(2)}, u32[]{:S(2)}) collective-permute-start(bf16[1536,768]{1,0:T(8,128)(2,1)} %get-tuple-element.136), channel_id=1, source_target_pairs={{0,1},{1,0},{2,3},{3,2},{4,5},{5,4},{6,7},{7,6},{8,9},{9,8},{10,11... | collective-permute-start | bytes 7077896 | tf_op jit(solution)/shard_map/ppermute | solution.py:750
  149.9 19.2 %collective-permute-start.2 = (bf16[1536,768]{1,0:T(8,128)(2,1)}, bf16[1536,768]{1,0:T(8,128)(2,1)}, u32[]{:S(2)}, u32[]{:S(2)}) collective-permute-start(bf16[1536,768]{1,0:T(8,128)(2,1)} %get-tuple-element.133), channel_id=1, source_target_pairs={{0,1},{1,0},{2,3},{3,2},{4,5},{5,4},{6,7},{7,6},{8,9},{9,8},{10,11... | collective-permute-start | bytes 7077896 | tf_op jit(solution)/shard_map/ppermute | solution.py:750
  156.4 12.7 %copy-start.7 = (bf16[1536,768]{1,0:T(8,128)(2,1)S(1)}, bf16[1536,768]{1,0:T(8,128)(2,1)}, u32[]{:S(2)}) copy-start(bf16[1536,768]{1,0:T(8,128)(2,1)} %copy-done.6) | copy-start | bytes 7077892
  169.0 10.6 %collective-permute-start.7 = (bf16[96,48,128]{2,1,0:T(8,128)(2,1)}, bf16[96,48,128]{2,1,0:T(8,128)(2,1)}, u32[]{:S(2)}, u32[]{:S(2)}) collective-permute-start(bf16[96,48,128]{2,1,0:T(8,128)(2,1)} %get-tuple-element.146), channel_id=1, source_target_pairs={{0,1},{1,0},{2,3},{3,2},{4,5},{5,4},{6,7},{7,6},{8,9},{9,8},{10,11... | collective-permute-start | bytes 3538952 | tf_op jit(solution)/shard_map/ppermute | solution.py:706
  170.8 8.8 %copy-start.15 = (bf16[4,1152,256]{2,1,0:T(8,128)(2,1)S(1)}, bf16[4,1152,256]{2,1,0:T(8,128)(2,1)}, u32[]{:S(2)}) copy-start(bf16[4,1152,256]{2,1,0:T(8,128)(2,1)} %get-tuple-element.147.refs_2_) | copy-start | bytes 7077892
  170.8 8.8 %copy-start.17 = (bf16[256,256]{1,0:T(8,128)(2,1)S(1)}, bf16[256,256]{1,0:T(8,128)(2,1)}, u32[]{:S(2)}) copy-start(bf16[256,256]{1,0:T(8,128)(2,1)} %copy-done.16) | copy-start | bytes 393220
  170.8 8.8 %copy-start.19 = (bf16[256,256]{1,0:T(8,128)(2,1)S(1)}, bf16[256,256]{1,0:T(8,128)(2,1)}, u32[]{:S(2)}) copy-start(bf16[256,256]{1,0:T(8,128)(2,1)} %copy-done.18) | copy-start | bytes 393220
  170.8 8.8 %copy-start.21 = (bf16[192,192]{1,0:T(8,128)(2,1)S(1)}, bf16[192,192]{1,0:T(8,128)(2,1)}, u32[]{:S(2)}) copy-start(bf16[192,192]{1,0:T(8,128)(2,1)} %copy-done.20) | copy-start | bytes 221188
  170.8 8.8 %copy-start.23 = (bf16[192,192]{1,0:T(8,128)(2,1)S(1)}, bf16[192,192]{1,0:T(8,128)(2,1)}, u32[]{:S(2)}) copy-start(bf16[192,192]{1,0:T(8,128)(2,1)} %copy-done.22) | copy-start | bytes 221188
  170.9 8.8 %copy-start.33 = (f32[2,128]{1,0:T(2,128)S(1)}, f32[2,128]{1,0:T(2,128)}, u32[]{:S(2)}) copy-start(f32[2,128]{1,0:T(2,128)} %copy-done.32) | copy-start | bytes 3076
  170.9 8.8 %copy-start.35 = (f32[2,128]{1,0:T(2,128)S(1)}, f32[2,128]{1,0:T(2,128)}, u32[]{:S(2)}) copy-start(f32[2,128]{1,0:T(2,128)} %copy-done.34) | copy-start | bytes 3076
  174.8 20.0 %collective-permute-start.4 = (bf16[512,768]{1,0:T(8,128)(2,1)S(1)}, bf16[512,768]{1,0:T(8,128)(2,1)S(1)}, u32[]{:S(2)}, u32[]{:S(2)}) collective-permute-start(bf16[512,768]{1,0:T(8,128)(2,1)S(1)} %get-tuple-element.141), channel_id=1, source_target_pairs={{0,2},{1,3},{2,0},{3,1},{4,6},{5,7},{6,4},{7,5},{8,10},{9,11},{10,... | collective-permute-start | bytes 2359304 | tf_op jit(solution)/shard_map/ppermute | solution.py:750
  176.6 19.5 %collective-permute-start.5 = (bf16[512,768]{1,0:T(8,128)(2,1)S(1)}, bf16[512,768]{1,0:T(8,128)(2,1)S(1)}, u32[]{:S(2)}, u32[]{:S(2)}) collective-permute-start(bf16[512,768]{1,0:T(8,128)(2,1)S(1)} %get-tuple-element.143), channel_id=1, source_target_pairs={{0,4},{1,5},{2,6},{3,7},{4,0},{5,1},{6,2},{7,3},{8,12},{9,13},{10,... | collective-permute-start | bytes 2359304 | tf_op jit(solution)/shard_map/ppermute | solution.py:750
  178.1 19.2 %collective-permute-start.6 = (bf16[512,768]{1,0:T(8,128)(2,1)S(1)}, bf16[512,768]{1,0:T(8,128)(2,1)S(1)}, u32[]{:S(2)}, u32[]{:S(2)}) collective-permute-start(bf16[512,768]{1,0:T(8,128)(2,1)S(1)} %get-tuple-element.145), channel_id=1, source_target_pairs={{0,8},{1,9},{2,10},{3,11},{4,12},{5,13},{6,14},{7,15},{8,0},{9,1},... | collective-permute-start | bytes 2359304 | tf_op jit(solution)/shard_map/ppermute | solution.py:750
  192.1 25.7 %collective-permute-start.14 = (bf16[48,96,128]{2,1,0:T(8,128)(2,1)S(1)}, bf16[48,96,128]{2,1,0:T(8,128)(2,1)S(1)}, u32[]{:S(2)}, u32[]{:S(2)}) collective-permute-start(bf16[48,96,128]{2,1,0:T(8,128)(2,1)S(1)} %get-tuple-element.165), channel_id=1, source_target_pairs={{0,1},{1,0},{2,3},{3,2},{4,5},{5,4},{6,7},{7,6},{8,9},{9,8},{10,11... | collective-permute-start | bytes 3538952 | tf_op jit(solution)/shard_map/ppermute | solution.py:706
  198.4 10.0 %collective-permute-start.8 = (bf16[256,768]{1,0:T(8,128)(2,1)S(1)}, bf16[256,768]{1,0:T(8,128)(2,1)S(1)}, u32[]{:S(2)}, u32[]{:S(2)}) collective-permute-start(bf16[256,768]{1,0:T(8,128)(2,1)S(1)} %get-tuple-element.150), channel_id=1, source_target_pairs={{0,4},{1,5},{2,6},{3,7},{4,0},{5,1},{6,2},{7,3},{8,12},{9,13},{10,... | collective-permute-start | bytes 1179656 | tf_op jit(solution)/shard_map/ppermute | solution.py:750
  199.0 9.7 %collective-permute-start.9 = (bf16[256,768]{1,0:T(8,128)(2,1)S(1)}, bf16[256,768]{1,0:T(8,128)(2,1)S(1)}, u32[]{:S(2)}, u32[]{:S(2)}) collective-permute-start(bf16[256,768]{1,0:T(8,128)(2,1)S(1)} %get-tuple-element.152), channel_id=1, source_target_pairs={{0,8},{1,9},{2,10},{3,11},{4,12},{5,13},{6,14},{7,15},{8,0},{9,1},... | collective-permute-start | bytes 1179656 | tf_op jit(solution)/shard_map/ppermute | solution.py:750
  200.5 9.4 %collective-permute-start.10 = (bf16[256,768]{1,0:T(8,128)(2,1)S(1)}, bf16[256,768]{1,0:T(8,128)(2,1)S(1)}, u32[]{:S(2)}, u32[]{:S(2)}) collective-permute-start(bf16[256,768]{1,0:T(8,128)(2,1)S(1)} %get-tuple-element.154), channel_id=1, source_target_pairs={{0,2},{1,3},{2,0},{3,1},{4,6},{5,7},{6,4},{7,5},{8,10},{9,11},{10,... | collective-permute-start | bytes 1179656 | tf_op jit(solution)/shard_map/ppermute | solution.py:750
  210.8 5.7 %collective-permute-start.11 = (bf16[128,768]{1,0:T(8,128)(2,1)S(1)}, bf16[128,768]{1,0:T(8,128)(2,1)S(1)}, u32[]{:S(2)}, u32[]{:S(2)}) collective-permute-start(bf16[128,768]{1,0:T(8,128)(2,1)S(1)} %get-tuple-element.156), channel_id=1, source_target_pairs={{0,8},{1,9},{2,10},{3,11},{4,12},{5,13},{6,14},{7,15},{8,0},{9,1},... | collective-permute-start | bytes 589832 | tf_op jit(solution)/shard_map/ppermute | solution.py:750
  211.4 5.7 %collective-permute-start.12 = (bf16[128,768]{1,0:T(8,128)(2,1)S(1)}, bf16[128,768]{1,0:T(8,128)(2,1)S(1)}, u32[]{:S(2)}, u32[]{:S(2)}) collective-permute-start(bf16[128,768]{1,0:T(8,128)(2,1)S(1)} %get-tuple-element.158), channel_id=1, source_target_pairs={{0,2},{1,3},{2,0},{3,1},{4,6},{5,7},{6,4},{7,5},{8,10},{9,11},{10,... | collective-permute-start | bytes 589832 | tf_op jit(solution)/shard_map/ppermute | solution.py:750
  212.0 5.7 %collective-permute-start.13 = (bf16[128,768]{1,0:T(8,128)(2,1)S(1)}, bf16[128,768]{1,0:T(8,128)(2,1)S(1)}, u32[]{:S(2)}, u32[]{:S(2)}) collective-permute-start(bf16[128,768]{1,0:T(8,128)(2,1)S(1)} %get-tuple-element.160), channel_id=1, source_target_pairs={{0,4},{1,5},{2,6},{3,7},{4,0},{5,1},{6,2},{7,3},{8,12},{9,13},{10,... | collective-permute-start | bytes 589832 | tf_op jit(solution)/shard_map/ppermute | solution.py:750
  219.9 43.7 %all-to-all-start.3 = ((bf16[16,3,48,384]{3,2,1,0:T(8,128)(2,1)}), bf16[16,3,48,384]{3,2,1,0:T(8,128)(2,1)S(1)}, u32[]{:S(2)}, u32[]{:S(2)}) async-start(bf16[16,3,48,384]{3,2,1,0:T(8,128)(2,1)} %lon_backward.3.refs_2_), calls=%async_computation.3 | async-start | bytes 3538944 | tf_op jit(solution)/shard_map/all_to_all | solution.py:703
  224.5 1.5 collective-permute-start.15
  226.9 36.6 %collective-permute-start.16 = (bf16[432,768]{1,0:T(8,128)(2,1)}, bf16[432,768]{1,0:T(8,128)(2,1)S(1)}, u32[]{:S(2)}, u32[]{:S(2)}) collective-permute-start(bf16[432,768]{1,0:T(8,128)(2,1)} %get-tuple-element.171), channel_id=1, source_target_pairs={{0,16},{1,17},{2,18},{3,19},{4,20},{5,21},{6,22},{7,23},{8,24},{9,... | collective-permute-start | bytes 1990664 | tf_op jit(solution)/shard_map/ppermute | solution.py:750
  263.7 7.0 %collective-permute-start.17 = (bf16[144,768]{1,0:T(8,128)(2,1)S(1)}, bf16[144,768]{1,0:T(8,128)(2,1)S(1)}, u32[]{:S(2)}, u32[]{:S(2)}) collective-permute-start(bf16[144,768]{1,0:T(8,128)(2,1)S(1)} %get-tuple-element.174), channel_id=1, source_target_pairs={{0,8},{1,9},{2,10},{3,11},{4,12},{5,13},{6,14},{7,15},{8,0},{9,1},... | collective-permute-start | bytes 663560 | tf_op jit(solution)/shard_map/ppermute | solution.py:750
  264.4 8.6 %collective-permute-start.18 = (bf16[144,768]{1,0:T(8,128)(2,1)S(1)}, bf16[144,768]{1,0:T(8,128)(2,1)S(1)}, u32[]{:S(2)}, u32[]{:S(2)}) collective-permute-start(bf16[144,768]{1,0:T(8,128)(2,1)S(1)} %get-tuple-element.176), channel_id=1, source_target_pairs={{0,2},{1,3},{2,0},{3,1},{4,6},{5,7},{6,4},{7,5},{8,10},{9,11},{10,... | collective-permute-start | bytes 663560 | tf_op jit(solution)/shard_map/ppermute | solution.py:750
  268.0 6.4 %collective-permute-start.19 = (bf16[144,768]{1,0:T(8,128)(2,1)S(1)}, bf16[144,768]{1,0:T(8,128)(2,1)S(1)}, u32[]{:S(2)}, u32[]{:S(2)}) collective-permute-start(bf16[144,768]{1,0:T(8,128)(2,1)S(1)} %get-tuple-element.178), channel_id=1, source_target_pairs={{0,4},{1,5},{2,6},{3,7},{4,0},{5,1},{6,2},{7,3},{8,12},{9,13},{10,... | collective-permute-start | bytes 663560 | tf_op jit(solution)/shard_map/ppermute | solution.py:750
  275.1 15.3 %copy-start.29 = (f32[768]{0:T(1024)S(1)}, f32[768]{0:T(1024)}, u32[]{:S(2)}) copy-start(f32[768]{0:T(1024)} %refs_2_.4) | copy-start | bytes 9220
  275.1 15.3 %copy-start.26 = (s32[24,45]{1,0:T(8,128)S(1)}, s32[24,45]{1,0:T(8,128)}, u32[]{:S(2)}) copy-start(s32[24,45]{1,0:T(8,128)} %refs_2_.7) | copy-start | bytes 12964
  275.2 10.3 %collective-permute-start.20 = (bf16[288,768]{1,0:T(8,128)(2,1)S(1)}, bf16[288,768]{1,0:T(8,128)(2,1)S(1)}, u32[]{:S(2)}, u32[]{:S(2)}) collective-permute-start(bf16[288,768]{1,0:T(8,128)(2,1)S(1)} %get-tuple-element.180), channel_id=1, source_target_pairs={{0,4},{1,5},{2,6},{3,7},{4,0},{5,1},{6,2},{7,3},{8,12},{9,13},{10,... | collective-permute-start | bytes 1327112 | tf_op jit(solution)/shard_map/ppermute | solution.py:750
  275.5 10.2 %collective-permute-start.21 = (bf16[288,768]{1,0:T(8,128)(2,1)S(1)}, bf16[288,768]{1,0:T(8,128)(2,1)S(1)}, u32[]{:S(2)}, u32[]{:S(2)}) collective-permute-start(bf16[288,768]{1,0:T(8,128)(2,1)S(1)} %get-tuple-element.182), channel_id=1, source_target_pairs={{0,8},{1,9},{2,10},{3,11},{4,12},{5,13},{6,14},{7,15},{8,0},{9,1},... | collective-permute-start | bytes 1327112 | tf_op jit(solution)/shard_map/ppermute | solution.py:750
  275.9 10.3 %collective-permute-start.22 = (bf16[288,768]{1,0:T(8,128)(2,1)S(1)}, bf16[288,768]{1,0:T(8,128)(2,1)S(1)}, u32[]{:S(2)}, u32[]{:S(2)}) collective-permute-start(bf16[288,768]{1,0:T(8,128)(2,1)S(1)} %get-tuple-element.184), channel_id=1, source_target_pairs={{0,2},{1,3},{2,0},{3,1},{4,6},{5,7},{6,4},{7,5},{8,10},{9,11},{10,... | collective-permute-start | bytes 1327112 | tf_op jit(solution)/shard_map/ppermute | solution.py:750
  287.0 18.9 %collective-permute-start.25 = (bf16[576,768]{1,0:T(8,128)(2,1)S(1)}, bf16[576,768]{1,0:T(8,128)(2,1)S(1)}, u32[]{:S(2)}, u32[]{:S(2)}) collective-permute-start(bf16[576,768]{1,0:T(8,128)(2,1)S(1)} %get-tuple-element.196), channel_id=1, source_target_pairs={{0,2},{1,3},{2,0},{3,1},{4,6},{5,7},{6,4},{7,5},{8,10},{9,11},{10,... | collective-permute-start | bytes 2654216 | tf_op jit(solution)/shard_map/ppermute | solution.py:750
  287.6 18.4 %collective-permute-start.26 = (bf16[576,768]{1,0:T(8,128)(2,1)S(1)}, bf16[576,768]{1,0:T(8,128)(2,1)S(1)}, u32[]{:S(2)}, u32[]{:S(2)}) collective-permute-start(bf16[576,768]{1,0:T(8,128)(2,1)S(1)} %get-tuple-element.198), channel_id=1, source_target_pairs={{0,4},{1,5},{2,6},{3,7},{4,0},{5,1},{6,2},{7,3},{8,12},{9,13},{10,... | collective-permute-start | bytes 2654216 | tf_op jit(solution)/shard_map/ppermute | solution.py:750
  289.2 18.3 %collective-permute-start.27 = (bf16[576,768]{1,0:T(8,128)(2,1)S(1)}, bf16[576,768]{1,0:T(8,128)(2,1)S(1)}, u32[]{:S(2)}, u32[]{:S(2)}) collective-permute-start(bf16[576,768]{1,0:T(8,128)(2,1)S(1)} %get-tuple-element.200), channel_id=1, source_target_pairs={{0,8},{1,9},{2,10},{3,11},{4,12},{5,13},{6,14},{7,15},{8,0},{9,1},... | collective-permute-start | bytes 2654216 | tf_op jit(solution)/shard_map/ppermute | solution.py:750
  290.5 9.0 %copy-start.41 = (f32[1,768]{1,0:T(1,128)S(1)}, f32[1,768]{1,0:T(1,128)}, u32[]{:S(2)}) copy-start(f32[1,768]{1,0:T(1,128)} %get-tuple-element.189.refs_3_) | copy-start | bytes 9220
  290.5 9.0 %copy-start.42 = (f32[1,768]{1,0:T(1,128)S(1)}, f32[1,768]{1,0:T(1,128)}, u32[]{:S(2)}) copy-start(f32[1,768]{1,0:T(1,128)} %get-tuple-element.190.refs_4_) | copy-start | bytes 9220
  290.5 16.9 %copy-start.37 = (s32[3]{0:T(128)S(1)}, s32[3]{0:T(128)}, u32[]{:S(2)}) copy-start(s32[3]{0:T(128)} %copy-done.36) | copy-start | bytes 40
  299.5 1.3 collective-permute-start.23
  308.7 9.9 %collective-permute-start.30 = (bf16[3456,768]{1,0:T(8,128)(2,1)S(1)}, bf16[3456,768]{1,0:T(8,128)(2,1)S(1)}, u32[]{:S(2)}, u32[]{:S(2)}) collective-permute-start(bf16[3456,768]{1,0:T(8,128)(2,1)S(1)} %bitcast.74), channel_id=1, source_target_pairs={{0,1},{1,0},{2,3},{3,2},{4,5},{5,4},{6,7},{7,6},{8,9},{9,8},{10,11... | collective-permute-start | bytes 15925256 | tf_op jit(solution)/shard_map/ppermute | solution.py:750
  308.7 3.9 %collective-permute-start.24 = (f32[1,6912]{1,0:T(1,128)S(1)}, f32[1,6912]{1,0:T(1,128)S(1)}, u32[]{:S(2)}, u32[]{:S(2)}) collective-permute-start(f32[1,6912]{1,0:T(1,128)S(1)} %get-tuple-element.195), channel_id=1, source_target_pairs={{0,2},{1,3},{2,0},{3,1},{4,6},{5,7},{6,4},{7,5},{8,10},{9,11},{10,... | collective-permute-start | bytes 82952 | tf_op jit(solution)/shard_map/ppermute | solution.py:750
  312.7 4.8 %collective-permute-start.28 = (f32[1,6912]{1,0:T(1,128)S(1)}, f32[1,6912]{1,0:T(1,128)S(1)}, u32[]{:S(2)}, u32[]{:S(2)}) collective-permute-start(f32[1,6912]{1,0:T(1,128)S(1)} %get-tuple-element.203), channel_id=1, source_target_pairs={{0,4},{1,5},{2,6},{3,7},{4,0},{5,1},{6,2},{7,3},{8,12},{9,13},{10,... | collective-permute-start | bytes 82952 | tf_op jit(solution)/shard_map/ppermute | solution.py:750
  317.5 5.6 %collective-permute-start.29 = (f32[1,6912]{1,0:T(1,128)S(1)}, f32[1,6912]{1,0:T(1,128)S(1)}, u32[]{:S(2)}, u32[]{:S(2)}) collective-permute-start(f32[1,6912]{1,0:T(1,128)S(1)} %get-tuple-element.206), channel_id=1, source_target_pairs={{0,8},{1,9},{2,10},{3,11},{4,12},{5,13},{6,14},{7,15},{8,0},{9,1},... | collective-permute-start | bytes 82952 | tf_op jit(solution)/shard_map/ppermute | solution.py:750
  323.0 4.8 %collective-permute-start.31 = (f32[1,6912]{1,0:T(1,128)S(1)}, f32[1,6912]{1,0:T(1,128)S(1)}, u32[]{:S(2)}, u32[]{:S(2)}) collective-permute-start(f32[1,6912]{1,0:T(1,128)S(1)} %get-tuple-element.212), channel_id=1, source_target_pairs={{0,16},{1,17},{2,18},{3,19},{4,20},{5,21},{6,22},{7,23},{8,24},{9,... | collective-permute-start | bytes 82952 | tf_op jit(solution)/shard_map/ppermute | solution.py:750
  (27 other events, 75.7 us)

commit v7 on v6

--- a/solution.py
+++ b/solution.py
@@ -991,7 +991,7 @@
                 pl.BlockSpec((tile, channels), lambda i, c: (i, 0)),
                 pl.BlockSpec((8, LANES), lambda i, c: (0, 0)),
             ],
-            vmem=20, name=name,
+            vmem=20, hbm=(0,) if own else (), name=name,
         )
 
     one_row = shape((1, channels), F32)

time: 331 us -> 330 us (level)
    unnamed x112 -> x108, local copies, waits for them, and re-layouts: 27.5 us -> 24.7 us
  transfers between devices with their start and end apart: 36 -> 36, of which waited for: 27 -> 27; matrix products, arithmetic and copies ran while one was open for 2% -> 2% of each run, Pallas kernels for 21% -> 22%
where the time goes in v7:
time: 330 us; the launch traced here: 329 us
  Pallas kernels  134 us (41%)
  waiting for transfers between devices  115 us (35%)
  starting transfers between devices  48.3 us (15%)
  local copies, waits for them, and re-layouts  29.2 us (9%)
    pallas_call x37, Pallas kernels, call(): pl.pallas_call(body, grid_spec=pltpu.PrefetchScalarGridSpec(num_scalar_pr...  134 us
    all_to_all x4, waiting for transfers between devices, exchange(): lax.all_to_all(x, AXES, 0, 0, axis_index_groups=snap_groups, tiled=True)  64.2 us
    ppermute x28, waiting for transfers between devices, partner(): return lax.ppermute(x, AXES, [(d, d ^ flip) for d in range(devices)])  46.5 us
    ppermute x28, starting transfers between devices, partner(): return lax.ppermute(x, AXES, [(d, d ^ flip) for d in range(devices)])  28.3 us
    unnamed x108, local copies, waits for them, and re-layouts  24.7 us
    all_to_all x4, starting transfers between devices, exchange(): lax.all_to_all(x, AXES, 0, 0, axis_index_groups=snap_groups, tiled=True)  19.8 us
  transfers between devices with their start and end apart: 36, of which 27 were waited for; matrix products, arithmetic and copies ran while one was open for 2% of the time, Pallas kernels for 22%

profile of v7, /device:TPU:0, one launch (start us, length us, event | category | flops | bytes accessed | tf_op | source)
XLA Modules:
  0.0 328.6 jit_solution(10898910721696130364)
XLA Ops:
  0.7 1.8 copy.37
  2.5 4.3 %first_norm.1 = (bf16[2,3,4,48,768]{4,3,2,1,0:T(8,128)(2,1)}, bf16[8,2,3,48,384]{4,3,2,1,0:T(8,128)(2,1)}) custom-call(bf16[2,3,4,45,768]{4,3,2,1,0:T(8,128)(2,1)S(1)} %bitcast.61, s32[24,45]{1,0:T(8,128)S(1)} %copy-done.23, f32[768]{0:T(1024)S(1)} %copy-done.26, f32[768]{0:T(1024)S(1)} %copy-done.36), custom_call_target="tpu_custom_call" | custom-call | bytes 600000 | tf_op jit(solution)/shard_map/first_norm/pallas_call | solution.py:50
  6.8 6.3 %all-to-all-start = ((bf16[16,3,48,384]{3,2,1,0:T(8,128)(2,1)}), bf16[16,3,48,384]{3,2,1,0:T(8,128)(2,1)S(1)}, u32[]{:S(2)}, u32[]{:S(2)}) async-start(bf16[16,3,48,384]{3,2,1,0:T(8,128)(2,1)} %bitcast.76), calls=%async_computation | async-start | bytes 3538944 | tf_op jit(solution)/shard_map/all_to_all | solution.py:703
  14.1 24.3 %all-to-all-done.refs_0_ = bf16[16,3,48,384]{3,2,1,0:T(8,128)(2,1)S(1)} async-done(((bf16[16,3,48,384]{3,2,1,0:T(8,128)(2,1)}), bf16[16,3,48,384]{3,2,1,0:T(8,128)(2,1)S(1)}, u32[]{:S(2)}, u32[]{:S(2)}) %all-to-all-start) | async-done | bytes 1769504 | tf_op jit(solution)/shard_map/all_to_all | solution.py:703
  38.4 3.5 %lon_forward.2 = (bf16[96,48,128]{2,1,0:T(8,128)(2,1)S(1)}, bf16[96,48,128]{2,1,0:T(8,128)(2,1)}) custom-call(bf16[16,3,48,384]{3,2,1,0:T(8,128)(2,1)S(1)} %all-to-all-done.refs_0_, bf16[192,192]{1,0:T(8,128)(2,1)S(1)} %dynamic-slice_bitcast_fusion.5.refs_1_), custom_call_target="tpu_custom_call" | custom-call | bytes 550000 | tf_op jit(solution)/shard_map/lon_forward/pallas_call | solution.py:50
  43.2 1.8 collective-permute-done.refs_1_
  44.9 8.5 %mix.1 = (bf16[48,96,128]{2,1,0:T(8,128)(2,1)S(1)}, bf16[48,96,128]{2,1,0:T(8,128)(2,1)S(1)}, bf16[4,1152,256]{2,1,0:T(8,128)(2,1)}) custom-call(bf16[96,48,128]{2,1,0:T(8,128)(2,1)S(1)} %get-tuple-element.120.refs_0_, bf16[96,48,128]{2,1,0:T(8,128)(2,1)S(1)} %collective-permute-done.refs_1_, bf16[192,192]{1,0:T(8,128)(2,1)S(1)} %get-tuple-element.232.refs_2_.refs_3_, ...), custom_call_target="tpu_custom_call" | custom-call | bytes 2200000 | tf_op jit(solution)/shard_map/mix/pallas_call | solution.py:50
  53.6 2.7 collective-permute-done.1.refs_1_
  56.3 2.1 lon_backward.2.refs_1_
  58.3 4.1 %all-to-all-start.1 = ((bf16[16,3,48,384]{3,2,1,0:T(8,128)(2,1)}), bf16[16,3,48,384]{3,2,1,0:T(8,128)(2,1)S(1)}, u32[]{:S(2)}, u32[]{:S(2)}) async-start(bf16[16,3,48,384]{3,2,1,0:T(8,128)(2,1)} %lon_backward.2.refs_1_), calls=%async_computation.1 | async-start | bytes 3538944 | tf_op jit(solution)/shard_map/all_to_all | solution.py:703
  63.1 1.8 copy.38
  65.2 22.6 %all-to-all-done.1 = bf16[16,3,48,384]{3,2,1,0:T(8,128)(2,1)S(1)} async-done(((bf16[16,3,48,384]{3,2,1,0:T(8,128)(2,1)}), bf16[16,3,48,384]{3,2,1,0:T(8,128)(2,1)S(1)}, u32[]{:S(2)}, u32[]{:S(2)}) %all-to-all-start.1) | async-done | bytes 1769504 | tf_op jit(solution)/shard_map/all_to_all | solution.py:703
  88.5 5.5 %second_norm.1 = (f32[2,3,4,48,768]{4,3,2,1,0:T(8,128)S(1)}, bf16[2,3,4,48,768]{4,3,2,1,0:T(8,128)(2,1)S(1)}) custom-call(bf16[2,3,4,45,768]{4,3,2,1,0:T(8,128)(2,1)} %bitcast.62, bf16[2,3,4,48,768]{4,3,2,1,0:T(8,128)(2,1)} %get-tuple-element.118.refs_1_, s32[24,45]{1,0:T(8,128)S(1)} %copy-done.23, bf16[8,2,3,48,384]{4,3,2,1,0:T(8,128)(2,1)S(1)} %bitcast.68, ...), custom_call_target="tpu_custom_call" | custom-call | bytes 850000 | tf_op jit(solution)/shard_map/second_norm/pallas_call | solution.py:50
  94.0 1.2 copy-done.9
  95.3 1.8 copy-done.11
  97.1 24.1 %mlp_chain.1 = (bf16[1152,3072]{1,0:T(8,128)(2,1)}, bf16[1152,3072]{1,0:T(8,128)(2,1)}, bf16[1152,768]{1,0:T(8,128)(2,1)}, f32[1,3072]{1,0:T(1,128)S(1)}) custom-call(bf16[1152,768]{1,0:T(8,128)(2,1)} %bitcast.65, bf16[1152,768]{1,0:T(8,128)(2,1)} %bitcast.55, bf16[768,3072]{1,0:T(8,128)(2,1)} %refs_2_.6, f32[1,3072]{1,0:T(1,128)} %bitcast.79, ...), custom_call_target="tpu_custom_call" | custom-call | bytes 2500000 | tf_op jit(solution)/shard_map/mlp_chain/pallas_call | solution.py:50
  121.2 8.1 %second_back.1 = (bf16[2,3,4,48,768]{4,3,2,1,0:T(8,128)(2,1)}, bf16[8,2,3,48,384]{4,3,2,1,0:T(8,128)(2,1)}, f32[1,768]{1,0:T(1,128)}, f32[1,768]{1,0:T(1,128)}, f32[1,768]{1,0:T(1,128)}) custom-call(f32[2,3,4,48,768]{4,3,2,1,0:T(8,128)} %copy-done.11, bf16[2,3,4,48,768]{4,3,2,1,0:T(8,128)(2,1)} %bitcast.77, bf16[2,3,4,48,768]{4,3,2,1,0:T(8,128)(2,1)} %copy-done.2, ...), custom_call_target="tpu_custom_call" | custom-call | bytes 900000 | tf_op jit(solution)/shard_map/second_back/pallas_call | solution.py:50
  129.3 4.7 %all-to-all-start.2 = ((bf16[16,3,48,384]{3,2,1,0:T(8,128)(2,1)}), bf16[16,3,48,384]{3,2,1,0:T(8,128)(2,1)}, u32[]{:S(2)}, u32[]{:S(2)}) async-start(bf16[16,3,48,384]{3,2,1,0:T(8,128)(2,1)} %bitcast.75), calls=%async_computation.2 | async-start | bytes 3538944 | tf_op jit(solution)/shard_map/all_to_all | solution.py:703
  134.1 3.0 copy-done
  137.1 4.9 %reduce_grad.2 = (bf16[1536,768]{1,0:T(8,128)(2,1)}, f32[8,128]{1,0:T(8,128)S(1)}) custom-call(s32[1]{0:T(128)} %bitcast.25.refs_0_, bf16[1152,3072]{1,0:T(8,128)(2,1)S(1)} %copy-done, bf16[1152,768]{1,0:T(8,128)(2,1)S(1)} %bitcast.56, f32[1,768]{1,0:T(1,128)S(1)} %copy-done.28), custom_call_target="tpu_custom_call" | custom-call | bytes 500000 | tf_op jit(solution)/shard_map/reduce_grad/pallas_call | solution.py:50
  142.0 3.0 copy-done.4
  145.0 4.9 %expand_grad.2 = (bf16[1536,768]{1,0:T(8,128)(2,1)}, f32[8,128]{1,0:T(8,128)S(1)}) custom-call(s32[1]{0:T(128)} %bitcast.25.refs_0_, bf16[1152,3072]{1,0:T(8,128)(2,1)S(1)} %copy-done.4, bf16[1152,768]{1,0:T(8,128)(2,1)S(1)} %bitcast.66, f32[8,128]{1,0:T(8,128)S(1)} %get-tuple-element.130.refs_3_), custom_call_target="tpu_custom_call" | custom-call | bytes 500000 | tf_op jit(solution)/shard_map/expand_grad/pallas_call | solution.py:50
  151.0 4.9 %reduce_grad.3 = (bf16[1536,768]{1,0:T(8,128)(2,1)}, f32[8,128]{1,0:T(8,128)S(1)}) custom-call(s32[1]{0:T(128)} %bitcast.25.refs_0_, bf16[1152,3072]{1,0:T(8,128)(2,1)S(1)} %bitcast.53, bf16[1152,768]{1,0:T(8,128)(2,1)S(1)} %bitcast.57, f32[8,128]{1,0:T(8,128)S(1)} %get-tuple-element.131.refs_3_), custom_call_target="tpu_custom_call" | custom-call | bytes 500000 | tf_op jit(solution)/shard_map/reduce_grad/pallas_call | solution.py:50
  155.9 4.9 %expand_grad.3 = (bf16[1536,768]{1,0:T(8,128)(2,1)}, f32[8,128]{1,0:T(8,128)S(1)}) custom-call(s32[1]{0:T(128)} %bitcast.25.refs_0_, bf16[1152,3072]{1,0:T(8,128)(2,1)S(1)} %copy-done.4, bf16[1152,768]{1,0:T(8,128)(2,1)S(1)} %bitcast.67, f32[8,128]{1,0:T(8,128)S(1)} %get-tuple-element.134.refs_3_), custom_call_target="tpu_custom_call" | custom-call | bytes 500000 | tf_op jit(solution)/shard_map/expand_grad/pallas_call | solution.py:50
  162.9 5.0 %lon_forward.3 = (bf16[96,48,128]{2,1,0:T(8,128)(2,1)S(1)}, bf16[96,48,128]{2,1,0:T(8,128)(2,1)}) custom-call(bf16[16,3,48,384]{3,2,1,0:T(8,128)(2,1)} %all-to-all-done.2.refs_0_, bf16[192,192]{1,0:T(8,128)(2,1)S(1)} %copy-done.22, f32[8,128]{1,0:T(8,128)S(1)} %copy-done.38), custom_call_target="tpu_custom_call" | custom-call | bytes 550000 | tf_op jit(solution)/shard_map/lon_forward/pallas_call | solution.py:50
  168.1 1.7 copy-done.7
  169.8 3.9 %halve.3 = (bf16[512,768]{1,0:T(8,128)(2,1)S(1)}, bf16[512,768]{1,0:T(8,128)(2,1)S(1)}, bf16[512,768]{1,0:T(8,128)(2,1)S(1)}, bf16[512,768]{1,0:T(8,128)(2,1)S(1...) custom-call(s32[3]{0:T(128)S(1)} %pad_add_fusion.2.refs_0_, bf16[1536,768]{1,0:T(8,128)(2,1)S(1)} %copy-done.6, ...), custom_call_target="tpu_custom_call" | custom-call | bytes 300000 | tf_op jit(solution)/shard_map/halve/pallas_call | solution.py:50
  173.7 1.7 collective-permute-start.4
  175.5 1.5 collective-permute-start.5
  177.0 1.5 collective-permute-start.6
  178.5 12.4 %mix_back.1 = (bf16[48,96,128]{2,1,0:T(8,128)(2,1)S(1)}, bf16[48,96,128]{2,1,0:T(8,128)(2,1)S(1)}, f32[528,256]{1,0:T(8,128)S(1)}) custom-call(bf16[96,48,128]{2,1,0:T(8,128)(2,1)S(1)} %get-tuple-element.139.refs_13_.refs_0_, bf16[96,48,128]{2,1,0:T(8,128)(2,1)} %collective-permute-done.7.refs_1_, bf16[4,1152,256]{2,1,0:T(8,128)(2,1)S(1)} %copy-done.13, ...), custom_call_target="tpu_custom_call" | custom-call | bytes 1300000 | tf_op jit(solution)/shard_map/mix_back/pallas_call | solution.py:50
  191.1 2.5 collective-permute-done.4.refs_2_.refs_4_
  193.7 1.3 collective-permute-done.5.refs_6_.refs_8_
  195.0 1.2 collective-permute-done.6.refs_10_.refs_12_
  197.9 1.5 collective-permute-start.9
  200.0 7.2 %collective-permute-done.8.refs_2_.refs_4_ = bf16[256,768]{1,0:T(8,128)(2,1)S(1)} collective-permute-done((bf16[256,768]{1,0:T(8,128)(2,1)S(1)}, bf16[256,768]{1,0:T(8,128)(2,1)S(1)}, u32[]{:S(2)}, u32[]{:S(2)}) %collective-permute-start.8) | collective-permute-done | bytes 393248 | tf_op jit(solution)/shard_map/ppermute | solution.py:750
  207.6 1.2 collective-permute-done.10.refs_10_.refs_12_
  210.9 1.4 collective-permute-start.13
  212.3 3.2 collective-permute-done.11.refs_1_
  216.7 2.1 lon_backward.3.refs_2_
  218.8 4.6 %all-to-all-start.3 = ((bf16[16,3,48,384]{3,2,1,0:T(8,128)(2,1)}), bf16[16,3,48,384]{3,2,1,0:T(8,128)(2,1)S(1)}, u32[]{:S(2)}, u32[]{:S(2)}) async-start(bf16[16,3,48,384]{3,2,1,0:T(8,128)(2,1)} %lon_backward.3.refs_2_), calls=%async_computation.3 | async-start | bytes 3538944 | tf_op jit(solution)/shard_map/all_to_all | solution.py:703
  225.8 2.6 collective-permute-start.16
  228.4 3.0 copy-done.1
  231.5 2.3 copy-done.8
  233.8 2.0 copy-done.12
  235.8 9.4 %branch.1 = (f32[45,24,768]{2,1,0:T(8,128)}, f32[8,128]{1,0:T(8,128)S(1)}) custom-call(bf16[2,3,4,48,3072]{4,3,2,1,0:T(8,128)(2,1)S(1)} %bitcast.54, bf16[3072,768]{1,0:T(8,128)(2,1)S(1)} %copy-done.8, f32[2,3,4,48,768]{4,3,2,1,0:T(8,128)S(1)} %copy-done.12, f32[1,768]{1,0:T(1,128)S(1)} %reshape.109.refs_3_, ...), custom_call_target="tpu_custom_call" | custom-call | bytes 1000000 | tf_op jit(solution)/shard_map/branch/pallas_call | solution.py:50
  245.2 17.3 %all-to-all-done.3.refs_0_ = bf16[16,3,48,384]{3,2,1,0:T(8,128)(2,1)S(1)} async-done(((bf16[16,3,48,384]{3,2,1,0:T(8,128)(2,1)}), bf16[16,3,48,384]{3,2,1,0:T(8,128)(2,1)S(1)}, u32[]{:S(2)}, u32[]{:S(2)}) %all-to-all-start.3) | async-done | bytes 1769504 | tf_op jit(solution)/shard_map/all_to_all | solution.py:703
  263.3 3.6 %collective-permute-start.18 = (bf16[144,768]{1,0:T(8,128)(2,1)S(1)}, bf16[144,768]{1,0:T(8,128)(2,1)S(1)}, u32[]{:S(2)}, u32[]{:S(2)}) collective-permute-start(bf16[144,768]{1,0:T(8,128)(2,1)S(1)} %get-tuple-element.176), channel_id=1, source_target_pairs={{0,2},{1,3},{2,0},{3,1},{4,6},{5,7},{6,4},{7,5},{8,10},{9,11},{10,... | collective-permute-start | bytes 663560 | tf_op jit(solution)/shard_map/ppermute | solution.py:750
  266.9 2.8 collective-permute-done.17.refs_2_
  269.7 2.2 collective-permute-done.18.refs_4_
  271.8 1.5 collective-permute-done.19.refs_6_
  275.6 8.8 %collective-permute-done.20.refs_2_ = bf16[288,768]{1,0:T(8,128)(2,1)S(1)} collective-permute-done((bf16[288,768]{1,0:T(8,128)(2,1)S(1)}, bf16[288,768]{1,0:T(8,128)(2,1)S(1)}, u32[]{:S(2)}, u32[]{:S(2)}) %collective-permute-start.20) | collective-permute-done | bytes 442400 | tf_op jit(solution)/shard_map/ppermute | solution.py:750
  286.5 1.6 collective-permute-start.26
  288.1 1.3 collective-permute-start.27
  289.4 8.9 %first_back.1 = (f32[45,24,768]{2,1,0:T(8,128)}, f32[1,768]{1,0:T(1,128)S(1)}, f32[1,768]{1,0:T(1,128)S(1)}) custom-call(bf16[2,3,4,45,768]{4,3,2,1,0:T(8,128)(2,1)} %bitcast.63, bf16[2,3,4,48,768]{4,3,2,1,0:T(8,128)(2,1)} %get-tuple-element.170.refs_1_, s32[24,45]{1,0:T(8,128)S(1)} %copy-done.24, bf16[8,2,3,48,384]{4,3,2,1,0:T(8,128)(2,1)S(1)} %bitcast.64, ...), custom_call_target="tpu_custom_call" | custom-call | bytes 900000 | tf_op jit(solution)/shard_map/first_back/pallas_call | solution.py:50
  298.4 1.2 collective-permute-done.23.refs_1_
  299.6 5.1 %collective-permute-done.25.refs_2_ = bf16[576,768]{1,0:T(8,128)(2,1)S(1)} collective-permute-done((bf16[576,768]{1,0:T(8,128)(2,1)S(1)}, bf16[576,768]{1,0:T(8,128)(2,1)S(1)}, u32[]{:S(2)}, u32[]{:S(2)}) %collective-permute-start.25) | collective-permute-done | bytes 884768 | tf_op jit(solution)/shard_map/ppermute | solution.py:750
  304.9 1.5 collective-permute-done.27.refs_6_
  306.3 1.2 merge.5
  308.8 2.8 collective-permute-done.24.refs_1_
  311.9 4.4 %widen.2 = (f32[3072,768]{1,0:T(8,128)}, f32[768,3072]{1,0:T(8,128)}, bf16[12,16,768]{2,1,0:T(8,128)(2,1)S(1)}, bf16[12,16,768]{2,1,0:T(8,128)(2,1)S(1)}) custom-call(s32[1]{0:T(128)} %bitcast.25.refs_0_, bf16[3456,768]{1,0:T(8,128)(2,1)S(1)} %bitcast.59, bf16[3456,768]{1,0:T(8,128)(2,1)S(1)} %bitcast.60, f32[1,6912]{1,0:T(1,128)S(1)} %get-tuple-element.202.refs_3_.refs_0_), custom_call_target="tpu_custom_call" | custom-call | bytes 500000 | tf_op jit(solution)/shard_map/widen/pallas_call | solution.py:50
  317.5 4.4 %widen.3 = (f32[3072,768]{1,0:T(8,128)}, f32[768,3072]{1,0:T(8,128)}, bf16[12,16,768]{2,1,0:T(8,128)(2,1)S(1)}, bf16[12,16,768]{2,1,0:T(8,128)(2,1)S(1)}) custom-call(s32[1]{0:T(128)} %bitcast.25.refs_0_, bf16[3456,768]{1,0:T(8,128)(2,1)S(1)} %collective-permute-done.30.refs_1_.refs_2_, ...), custom_call_target="tpu_custom_call", output_to_operand_aliasing={{0}: (3, {}), {1}: (4, {})} | custom-call | bytes 500000 | tf_op jit(solution)/shard_map/widen/pallas_call | solution.py:50
  321.9 2.8 collective-permute-start.31
  324.7 1.2 spread.1
  (180 shorter events, 26.7 us)
Async XLA Ops:
  6.8 31.6 %all-to-all-start = ((bf16[16,3,48,384]{3,2,1,0:T(8,128)(2,1)}), bf16[16,3,48,384]{3,2,1,0:T(8,128)(2,1)S(1)}, u32[]{:S(2)}, u32[]{:S(2)}) async-start(bf16[16,3,48,384]{3,2,1,0:T(8,128)(2,1)} %bitcast.76), calls=%async_computation | async-start | bytes 3538944 | tf_op jit(solution)/shard_map/all_to_all | solution.py:703
  13.1 28.8 %copy-start.46 = (f32[2,768]{1,0:T(2,128)S(1)}, f32[2,768]{1,0:T(2,128)}, u32[]{:S(2)}) copy-start(f32[2,768]{1,0:T(2,128)} %param.27) | copy-start | bytes 18436
  13.1 28.9 %copy-start.47 = (f32[2,768]{1,0:T(2,128)S(1)}, f32[2,768]{1,0:T(2,128)}, u32[]{:S(2)}) copy-start(f32[2,768]{1,0:T(2,128)} %param.29) | copy-start | bytes 18436
  13.1 30.0 %copy-start.44 = (bf16[2,192,192]{2,1,0:T(8,128)(2,1)S(1)}, bf16[2,192,192]{2,1,0:T(8,128)(2,1)}, u32[]{:S(2)}) copy-start(bf16[2,192,192]{2,1,0:T(8,128)(2,1)} %constant.189.clone) | copy-start | bytes 442372
  13.1 30.0 %copy-start.45 = (bf16[2,192,192]{2,1,0:T(8,128)(2,1)S(1)}, bf16[2,192,192]{2,1,0:T(8,128)(2,1)}, u32[]{:S(2)}) copy-start(bf16[2,192,192]{2,1,0:T(8,128)(2,1)} %constant.188.clone) | copy-start | bytes 442372
  41.9 3.1 collective-permute-start
  42.1 11.4 %copy-start.30 = (f32[2,128]{1,0:T(2,128)}, f32[2,128]{1,0:T(2,128)S(1)}, u32[]{:S(2)}) copy-start(f32[2,128]{1,0:T(2,128)S(1)} %pad.18) | copy-start | bytes 3076
  42.1 11.3 %copy-start.32 = (f32[2,128]{1,0:T(2,128)}, f32[2,128]{1,0:T(2,128)S(1)}, u32[]{:S(2)}) copy-start(f32[2,128]{1,0:T(2,128)S(1)} %pad.16) | copy-start | bytes 3076
  43.0 10.5 %copy-start.14 = (bf16[256,256]{1,0:T(8,128)(2,1)}, bf16[256,256]{1,0:T(8,128)(2,1)S(1)}, u32[]{:S(2)}) copy-start(bf16[256,256]{1,0:T(8,128)(2,1)S(1)} %maximum_maximum_fusion.1.refs_6_.refs_7_) | copy-start | bytes 393220
  43.1 10.5 %copy-start.43 = (bf16[2,192,192]{2,1,0:T(8,128)(2,1)S(1)}, bf16[2,192,192]{2,1,0:T(8,128)(2,1)}, u32[]{:S(2)}) copy-start(bf16[2,192,192]{2,1,0:T(8,128)(2,1)} %constant.187.clone) | copy-start | bytes 442372
  43.1 13.2 %copy-start.16 = (bf16[256,256]{1,0:T(8,128)(2,1)}, bf16[256,256]{1,0:T(8,128)(2,1)S(1)}, u32[]{:S(2)}) copy-start(bf16[256,256]{1,0:T(8,128)(2,1)S(1)} %maximum_maximum_fusion.refs_4_.refs_5_) | copy-start | bytes 393220
  43.2 13.1 %copy-start.18 = (bf16[192,192]{1,0:T(8,128)(2,1)}, bf16[192,192]{1,0:T(8,128)(2,1)S(1)}, u32[]{:S(2)}) copy-start(bf16[192,192]{1,0:T(8,128)(2,1)S(1)} %get-tuple-element.231.refs_3_.refs_4_) | copy-start | bytes 221188
  43.2 15.2 %copy-start.20 = (bf16[192,192]{1,0:T(8,128)(2,1)}, bf16[192,192]{1,0:T(8,128)(2,1)S(1)}, u32[]{:S(2)}) copy-start(bf16[192,192]{1,0:T(8,128)(2,1)S(1)} %get-tuple-element.232.refs_2_.refs_3_) | copy-start | bytes 221188
  53.4 2.8 collective-permute-start.1
  58.3 29.4 %all-to-all-start.1 = ((bf16[16,3,48,384]{3,2,1,0:T(8,128)(2,1)}), bf16[16,3,48,384]{3,2,1,0:T(8,128)(2,1)S(1)}, u32[]{:S(2)}, u32[]{:S(2)}) async-start(bf16[16,3,48,384]{3,2,1,0:T(8,128)(2,1)} %lon_backward.2.refs_1_), calls=%async_computation.1 | async-start | bytes 3538944 | tf_op jit(solution)/shard_map/all_to_all | solution.py:703
  62.5 25.3 %copy-start.25 = (f32[1,768]{1,0:T(1,128)}, f32[1,768]{1,0:T(1,128)S(1)}, u32[]{:S(2)}) copy-start(f32[1,768]{1,0:T(1,128)S(1)} %reshape.102.refs_4_) | copy-start | bytes 9220
  65.1 28.9 %copy-start.2 = (bf16[2,3,4,48,768]{4,3,2,1,0:T(8,128)(2,1)}, bf16[2,3,4,48,768]{4,3,2,1,0:T(8,128)(2,1)S(1)}, u32[]{:S(2)}) copy-start(bf16[2,3,4,48,768]{4,3,2,1,0:T(8,128)(2,1)S(1)} %pad.69.refs_6_.refs_2_) | copy-start | bytes 5308420
  129.3 32.0 %all-to-all-start.2 = ((bf16[16,3,48,384]{3,2,1,0:T(8,128)(2,1)}), bf16[16,3,48,384]{3,2,1,0:T(8,128)(2,1)}, u32[]{:S(2)}, u32[]{:S(2)}) async-start(bf16[16,3,48,384]{3,2,1,0:T(8,128)(2,1)} %bitcast.75), calls=%async_computation.2 | async-start | bytes 3538944 | tf_op jit(solution)/shard_map/all_to_all | solution.py:703
  137.1 13.9 %slice-start = ((s8[7077888]{0:T(1024)(128)(4,1)}), s8[4194304]{0:T(1024)(128)(4,1)S(1)}, s32[]{:S(2)}) async-start(s8[7077888]{0:T(1024)(128)(4,1)} %bitcast.52), calls=%async_computation.4 | async-start | bytes 8388608
  145.0 6.0 %slice-start.1 = ((s8[7077888]{0:T(1024)(128)(4,1)}), s8[2883584]{0:T(1024)(128)(4,1)S(1)}, s32[]{:S(2)}) async-start(s8[7077888]{0:T(1024)(128)(4,1)} %bitcast.52), calls=%async_computation.5 | async-start | bytes 5767168
  149.8 18.2 %collective-permute-start.3 = (bf16[1536,768]{1,0:T(8,128)(2,1)}, bf16[1536,768]{1,0:T(8,128)(2,1)}, u32[]{:S(2)}, u32[]{:S(2)}) collective-permute-start(bf16[1536,768]{1,0:T(8,128)(2,1)} %get-tuple-element.136), channel_id=1, source_target_pairs={{0,1},{1,0},{2,3},{3,2},{4,5},{5,4},{6,7},{7,6},{8,9},{9,8},{10,11... | collective-permute-start | bytes 7077896 | tf_op jit(solution)/shard_map/ppermute | solution.py:750
  149.9 18.1 %collective-permute-start.2 = (bf16[1536,768]{1,0:T(8,128)(2,1)}, bf16[1536,768]{1,0:T(8,128)(2,1)}, u32[]{:S(2)}, u32[]{:S(2)}) collective-permute-start(bf16[1536,768]{1,0:T(8,128)(2,1)} %get-tuple-element.133), channel_id=1, source_target_pairs={{0,1},{1,0},{2,3},{3,2},{4,5},{5,4},{6,7},{7,6},{8,9},{9,8},{10,11... | collective-permute-start | bytes 7077896 | tf_op jit(solution)/shard_map/ppermute | solution.py:750
  155.9 12.2 %copy-start.6 = (bf16[1536,768]{1,0:T(8,128)(2,1)S(1)}, bf16[1536,768]{1,0:T(8,128)(2,1)}, u32[]{:S(2)}) copy-start(bf16[1536,768]{1,0:T(8,128)(2,1)} %get-tuple-element.132.refs_1_.refs_3_.refs_5_) | copy-start | bytes 7077892
  167.9 10.6 %collective-permute-start.7 = (bf16[96,48,128]{2,1,0:T(8,128)(2,1)}, bf16[96,48,128]{2,1,0:T(8,128)(2,1)}, u32[]{:S(2)}, u32[]{:S(2)}) collective-permute-start(bf16[96,48,128]{2,1,0:T(8,128)(2,1)} %get-tuple-element.146), channel_id=1, source_target_pairs={{0,1},{1,0},{2,3},{3,2},{4,5},{5,4},{6,7},{7,6},{8,9},{9,8},{10,11... | collective-permute-start | bytes 3538952 | tf_op jit(solution)/shard_map/ppermute | solution.py:706
  169.7 8.8 %copy-start.13 = (bf16[4,1152,256]{2,1,0:T(8,128)(2,1)S(1)}, bf16[4,1152,256]{2,1,0:T(8,128)(2,1)}, u32[]{:S(2)}) copy-start(bf16[4,1152,256]{2,1,0:T(8,128)(2,1)} %get-tuple-element.147.refs_2_) | copy-start | bytes 7077892
  169.7 8.8 %copy-start.15 = (bf16[256,256]{1,0:T(8,128)(2,1)S(1)}, bf16[256,256]{1,0:T(8,128)(2,1)}, u32[]{:S(2)}) copy-start(bf16[256,256]{1,0:T(8,128)(2,1)} %copy-done.14) | copy-start | bytes 393220
  169.7 8.8 %copy-start.17 = (bf16[256,256]{1,0:T(8,128)(2,1)S(1)}, bf16[256,256]{1,0:T(8,128)(2,1)}, u32[]{:S(2)}) copy-start(bf16[256,256]{1,0:T(8,128)(2,1)} %copy-done.16) | copy-start | bytes 393220
  169.7 8.8 %copy-start.19 = (bf16[192,192]{1,0:T(8,128)(2,1)S(1)}, bf16[192,192]{1,0:T(8,128)(2,1)}, u32[]{:S(2)}) copy-start(bf16[192,192]{1,0:T(8,128)(2,1)} %copy-done.18) | copy-start | bytes 221188
  169.7 8.8 %copy-start.21 = (bf16[192,192]{1,0:T(8,128)(2,1)S(1)}, bf16[192,192]{1,0:T(8,128)(2,1)}, u32[]{:S(2)}) copy-start(bf16[192,192]{1,0:T(8,128)(2,1)} %copy-done.20) | copy-start | bytes 221188
  169.8 8.8 %copy-start.31 = (f32[2,128]{1,0:T(2,128)S(1)}, f32[2,128]{1,0:T(2,128)}, u32[]{:S(2)}) copy-start(f32[2,128]{1,0:T(2,128)} %copy-done.30) | copy-start | bytes 3076
  169.8 8.8 %copy-start.33 = (f32[2,128]{1,0:T(2,128)S(1)}, f32[2,128]{1,0:T(2,128)}, u32[]{:S(2)}) copy-start(f32[2,128]{1,0:T(2,128)} %copy-done.32) | copy-start | bytes 3076
  173.7 20.0 %collective-permute-start.4 = (bf16[512,768]{1,0:T(8,128)(2,1)S(1)}, bf16[512,768]{1,0:T(8,128)(2,1)S(1)}, u32[]{:S(2)}, u32[]{:S(2)}) collective-permute-start(bf16[512,768]{1,0:T(8,128)(2,1)S(1)} %get-tuple-element.141), channel_id=1, source_target_pairs={{0,2},{1,3},{2,0},{3,1},{4,6},{5,7},{6,4},{7,5},{8,10},{9,11},{10,... | collective-permute-start | bytes 2359304 | tf_op jit(solution)/shard_map/ppermute | solution.py:750
  175.5 19.5 %collective-permute-start.5 = (bf16[512,768]{1,0:T(8,128)(2,1)S(1)}, bf16[512,768]{1,0:T(8,128)(2,1)S(1)}, u32[]{:S(2)}, u32[]{:S(2)}) collective-permute-start(bf16[512,768]{1,0:T(8,128)(2,1)S(1)} %get-tuple-element.143), channel_id=1, source_target_pairs={{0,4},{1,5},{2,6},{3,7},{4,0},{5,1},{6,2},{7,3},{8,12},{9,13},{10,... | collective-permute-start | bytes 2359304 | tf_op jit(solution)/shard_map/ppermute | solution.py:750
  177.0 19.2 %collective-permute-start.6 = (bf16[512,768]{1,0:T(8,128)(2,1)S(1)}, bf16[512,768]{1,0:T(8,128)(2,1)S(1)}, u32[]{:S(2)}, u32[]{:S(2)}) collective-permute-start(bf16[512,768]{1,0:T(8,128)(2,1)S(1)} %get-tuple-element.145), channel_id=1, source_target_pairs={{0,8},{1,9},{2,10},{3,11},{4,12},{5,13},{6,14},{7,15},{8,0},{9,1},... | collective-permute-start | bytes 2359304 | tf_op jit(solution)/shard_map/ppermute | solution.py:750
  191.0 25.7 %collective-permute-start.14 = (bf16[48,96,128]{2,1,0:T(8,128)(2,1)S(1)}, bf16[48,96,128]{2,1,0:T(8,128)(2,1)S(1)}, u32[]{:S(2)}, u32[]{:S(2)}) collective-permute-start(bf16[48,96,128]{2,1,0:T(8,128)(2,1)S(1)} %get-tuple-element.165), channel_id=1, source_target_pairs={{0,1},{1,0},{2,3},{3,2},{4,5},{5,4},{6,7},{7,6},{8,9},{9,8},{10,11... | collective-permute-start | bytes 3538952 | tf_op jit(solution)/shard_map/ppermute | solution.py:706
  197.3 10.0 %collective-permute-start.8 = (bf16[256,768]{1,0:T(8,128)(2,1)S(1)}, bf16[256,768]{1,0:T(8,128)(2,1)S(1)}, u32[]{:S(2)}, u32[]{:S(2)}) collective-permute-start(bf16[256,768]{1,0:T(8,128)(2,1)S(1)} %get-tuple-element.150), channel_id=1, source_target_pairs={{0,4},{1,5},{2,6},{3,7},{4,0},{5,1},{6,2},{7,3},{8,12},{9,13},{10,... | collective-permute-start | bytes 1179656 | tf_op jit(solution)/shard_map/ppermute | solution.py:750
  197.9 9.7 %collective-permute-start.9 = (bf16[256,768]{1,0:T(8,128)(2,1)S(1)}, bf16[256,768]{1,0:T(8,128)(2,1)S(1)}, u32[]{:S(2)}, u32[]{:S(2)}) collective-permute-start(bf16[256,768]{1,0:T(8,128)(2,1)S(1)} %get-tuple-element.152), channel_id=1, source_target_pairs={{0,8},{1,9},{2,10},{3,11},{4,12},{5,13},{6,14},{7,15},{8,0},{9,1},... | collective-permute-start | bytes 1179656 | tf_op jit(solution)/shard_map/ppermute | solution.py:750
  199.4 9.4 %collective-permute-start.10 = (bf16[256,768]{1,0:T(8,128)(2,1)S(1)}, bf16[256,768]{1,0:T(8,128)(2,1)S(1)}, u32[]{:S(2)}, u32[]{:S(2)}) collective-permute-start(bf16[256,768]{1,0:T(8,128)(2,1)S(1)} %get-tuple-element.154), channel_id=1, source_target_pairs={{0,2},{1,3},{2,0},{3,1},{4,6},{5,7},{6,4},{7,5},{8,10},{9,11},{10,... | collective-permute-start | bytes 1179656 | tf_op jit(solution)/shard_map/ppermute | solution.py:750
  209.7 5.7 %collective-permute-start.11 = (bf16[128,768]{1,0:T(8,128)(2,1)S(1)}, bf16[128,768]{1,0:T(8,128)(2,1)S(1)}, u32[]{:S(2)}, u32[]{:S(2)}) collective-permute-start(bf16[128,768]{1,0:T(8,128)(2,1)S(1)} %get-tuple-element.156), channel_id=1, source_target_pairs={{0,8},{1,9},{2,10},{3,11},{4,12},{5,13},{6,14},{7,15},{8,0},{9,1},... | collective-permute-start | bytes 589832 | tf_op jit(solution)/shard_map/ppermute | solution.py:750
  210.3 5.7 %collective-permute-start.12 = (bf16[128,768]{1,0:T(8,128)(2,1)S(1)}, bf16[128,768]{1,0:T(8,128)(2,1)S(1)}, u32[]{:S(2)}, u32[]{:S(2)}) collective-permute-start(bf16[128,768]{1,0:T(8,128)(2,1)S(1)} %get-tuple-element.158), channel_id=1, source_target_pairs={{0,2},{1,3},{2,0},{3,1},{4,6},{5,7},{6,4},{7,5},{8,10},{9,11},{10,... | collective-permute-start | bytes 589832 | tf_op jit(solution)/shard_map/ppermute | solution.py:750
  210.9 5.7 %collective-permute-start.13 = (bf16[128,768]{1,0:T(8,128)(2,1)S(1)}, bf16[128,768]{1,0:T(8,128)(2,1)S(1)}, u32[]{:S(2)}, u32[]{:S(2)}) collective-permute-start(bf16[128,768]{1,0:T(8,128)(2,1)S(1)} %get-tuple-element.160), channel_id=1, source_target_pairs={{0,4},{1,5},{2,6},{3,7},{4,0},{5,1},{6,2},{7,3},{8,12},{9,13},{10,... | collective-permute-start | bytes 589832 | tf_op jit(solution)/shard_map/ppermute | solution.py:750
  218.8 43.7 %all-to-all-start.3 = ((bf16[16,3,48,384]{3,2,1,0:T(8,128)(2,1)}), bf16[16,3,48,384]{3,2,1,0:T(8,128)(2,1)S(1)}, u32[]{:S(2)}, u32[]{:S(2)}) async-start(bf16[16,3,48,384]{3,2,1,0:T(8,128)(2,1)} %lon_backward.3.refs_2_), calls=%async_computation.3 | async-start | bytes 3538944 | tf_op jit(solution)/shard_map/all_to_all | solution.py:703
  223.4 1.5 collective-permute-start.15
  225.8 36.6 %collective-permute-start.16 = (bf16[432,768]{1,0:T(8,128)(2,1)}, bf16[432,768]{1,0:T(8,128)(2,1)S(1)}, u32[]{:S(2)}, u32[]{:S(2)}) collective-permute-start(bf16[432,768]{1,0:T(8,128)(2,1)} %get-tuple-element.171), channel_id=1, source_target_pairs={{0,16},{1,17},{2,18},{3,19},{4,20},{5,21},{6,22},{7,23},{8,24},{9,... | collective-permute-start | bytes 1990664 | tf_op jit(solution)/shard_map/ppermute | solution.py:750
  262.6 7.0 %collective-permute-start.17 = (bf16[144,768]{1,0:T(8,128)(2,1)S(1)}, bf16[144,768]{1,0:T(8,128)(2,1)S(1)}, u32[]{:S(2)}, u32[]{:S(2)}) collective-permute-start(bf16[144,768]{1,0:T(8,128)(2,1)S(1)} %get-tuple-element.174), channel_id=1, source_target_pairs={{0,8},{1,9},{2,10},{3,11},{4,12},{5,13},{6,14},{7,15},{8,0},{9,1},... | collective-permute-start | bytes 663560 | tf_op jit(solution)/shard_map/ppermute | solution.py:750
  263.3 8.6 %collective-permute-start.18 = (bf16[144,768]{1,0:T(8,128)(2,1)S(1)}, bf16[144,768]{1,0:T(8,128)(2,1)S(1)}, u32[]{:S(2)}, u32[]{:S(2)}) collective-permute-start(bf16[144,768]{1,0:T(8,128)(2,1)S(1)} %get-tuple-element.176), channel_id=1, source_target_pairs={{0,2},{1,3},{2,0},{3,1},{4,6},{5,7},{6,4},{7,5},{8,10},{9,11},{10,... | collective-permute-start | bytes 663560 | tf_op jit(solution)/shard_map/ppermute | solution.py:750
  266.9 6.4 %collective-permute-start.19 = (bf16[144,768]{1,0:T(8,128)(2,1)S(1)}, bf16[144,768]{1,0:T(8,128)(2,1)S(1)}, u32[]{:S(2)}, u32[]{:S(2)}) collective-permute-start(bf16[144,768]{1,0:T(8,128)(2,1)S(1)} %get-tuple-element.178), channel_id=1, source_target_pairs={{0,4},{1,5},{2,6},{3,7},{4,0},{5,1},{6,2},{7,3},{8,12},{9,13},{10,... | collective-permute-start | bytes 663560 | tf_op jit(solution)/shard_map/ppermute | solution.py:750
  274.0 15.3 %copy-start.27 = (f32[768]{0:T(1024)S(1)}, f32[768]{0:T(1024)}, u32[]{:S(2)}) copy-start(f32[768]{0:T(1024)} %refs_2_.4) | copy-start | bytes 9220
  274.0 15.3 %copy-start.24 = (s32[24,45]{1,0:T(8,128)S(1)}, s32[24,45]{1,0:T(8,128)}, u32[]{:S(2)}) copy-start(s32[24,45]{1,0:T(8,128)} %refs_2_.7) | copy-start | bytes 12964
  274.1 10.3 %collective-permute-start.20 = (bf16[288,768]{1,0:T(8,128)(2,1)S(1)}, bf16[288,768]{1,0:T(8,128)(2,1)S(1)}, u32[]{:S(2)}, u32[]{:S(2)}) collective-permute-start(bf16[288,768]{1,0:T(8,128)(2,1)S(1)} %get-tuple-element.180), channel_id=1, source_target_pairs={{0,4},{1,5},{2,6},{3,7},{4,0},{5,1},{6,2},{7,3},{8,12},{9,13},{10,... | collective-permute-start | bytes 1327112 | tf_op jit(solution)/shard_map/ppermute | solution.py:750
  274.4 10.2 %collective-permute-start.21 = (bf16[288,768]{1,0:T(8,128)(2,1)S(1)}, bf16[288,768]{1,0:T(8,128)(2,1)S(1)}, u32[]{:S(2)}, u32[]{:S(2)}) collective-permute-start(bf16[288,768]{1,0:T(8,128)(2,1)S(1)} %get-tuple-element.182), channel_id=1, source_target_pairs={{0,8},{1,9},{2,10},{3,11},{4,12},{5,13},{6,14},{7,15},{8,0},{9,1},... | collective-permute-start | bytes 1327112 | tf_op jit(solution)/shard_map/ppermute | solution.py:750
  274.8 10.3 %collective-permute-start.22 = (bf16[288,768]{1,0:T(8,128)(2,1)S(1)}, bf16[288,768]{1,0:T(8,128)(2,1)S(1)}, u32[]{:S(2)}, u32[]{:S(2)}) collective-permute-start(bf16[288,768]{1,0:T(8,128)(2,1)S(1)} %get-tuple-element.184), channel_id=1, source_target_pairs={{0,2},{1,3},{2,0},{3,1},{4,6},{5,7},{6,4},{7,5},{8,10},{9,11},{10,... | collective-permute-start | bytes 1327112 | tf_op jit(solution)/shard_map/ppermute | solution.py:750
  285.9 18.9 %collective-permute-start.25 = (bf16[576,768]{1,0:T(8,128)(2,1)S(1)}, bf16[576,768]{1,0:T(8,128)(2,1)S(1)}, u32[]{:S(2)}, u32[]{:S(2)}) collective-permute-start(bf16[576,768]{1,0:T(8,128)(2,1)S(1)} %get-tuple-element.196), channel_id=1, source_target_pairs={{0,2},{1,3},{2,0},{3,1},{4,6},{5,7},{6,4},{7,5},{8,10},{9,11},{10,... | collective-permute-start | bytes 2654216 | tf_op jit(solution)/shard_map/ppermute | solution.py:750
  286.5 18.4 %collective-permute-start.26 = (bf16[576,768]{1,0:T(8,128)(2,1)S(1)}, bf16[576,768]{1,0:T(8,128)(2,1)S(1)}, u32[]{:S(2)}, u32[]{:S(2)}) collective-permute-start(bf16[576,768]{1,0:T(8,128)(2,1)S(1)} %get-tuple-element.198), channel_id=1, source_target_pairs={{0,4},{1,5},{2,6},{3,7},{4,0},{5,1},{6,2},{7,3},{8,12},{9,13},{10,... | collective-permute-start | bytes 2654216 | tf_op jit(solution)/shard_map/ppermute | solution.py:750
  288.1 18.3 %collective-permute-start.27 = (bf16[576,768]{1,0:T(8,128)(2,1)S(1)}, bf16[576,768]{1,0:T(8,128)(2,1)S(1)}, u32[]{:S(2)}, u32[]{:S(2)}) collective-permute-start(bf16[576,768]{1,0:T(8,128)(2,1)S(1)} %get-tuple-element.200), channel_id=1, source_target_pairs={{0,8},{1,9},{2,10},{3,11},{4,12},{5,13},{6,14},{7,15},{8,0},{9,1},... | collective-permute-start | bytes 2654216 | tf_op jit(solution)/shard_map/ppermute | solution.py:750
  289.4 9.0 %copy-start.39 = (f32[1,768]{1,0:T(1,128)S(1)}, f32[1,768]{1,0:T(1,128)}, u32[]{:S(2)}) copy-start(f32[1,768]{1,0:T(1,128)} %get-tuple-element.189.refs_3_) | copy-start | bytes 9220
  289.4 9.0 %copy-start.40 = (f32[1,768]{1,0:T(1,128)S(1)}, f32[1,768]{1,0:T(1,128)}, u32[]{:S(2)}) copy-start(f32[1,768]{1,0:T(1,128)} %get-tuple-element.190.refs_4_) | copy-start | bytes 9220
  289.4 16.9 %copy-start.35 = (s32[3]{0:T(128)S(1)}, s32[3]{0:T(128)}, u32[]{:S(2)}) copy-start(s32[3]{0:T(128)} %copy-done.34) | copy-start | bytes 40
  298.4 1.3 collective-permute-start.23
  307.6 9.9 %collective-permute-start.30 = (bf16[3456,768]{1,0:T(8,128)(2,1)S(1)}, bf16[3456,768]{1,0:T(8,128)(2,1)S(1)}, u32[]{:S(2)}, u32[]{:S(2)}) collective-permute-start(bf16[3456,768]{1,0:T(8,128)(2,1)S(1)} %bitcast.74), channel_id=1, source_target_pairs={{0,1},{1,0},{2,3},{3,2},{4,5},{5,4},{6,7},{7,6},{8,9},{9,8},{10,11... | collective-permute-start | bytes 15925256 | tf_op jit(solution)/shard_map/ppermute | solution.py:750
  307.6 3.9 %collective-permute-start.24 = (f32[1,6912]{1,0:T(1,128)S(1)}, f32[1,6912]{1,0:T(1,128)S(1)}, u32[]{:S(2)}, u32[]{:S(2)}) collective-permute-start(f32[1,6912]{1,0:T(1,128)S(1)} %get-tuple-element.195), channel_id=1, source_target_pairs={{0,2},{1,3},{2,0},{3,1},{4,6},{5,7},{6,4},{7,5},{8,10},{9,11},{10,... | collective-permute-start | bytes 82952 | tf_op jit(solution)/shard_map/ppermute | solution.py:750
  311.6 4.8 %collective-permute-start.28 = (f32[1,6912]{1,0:T(1,128)S(1)}, f32[1,6912]{1,0:T(1,128)S(1)}, u32[]{:S(2)}, u32[]{:S(2)}) collective-permute-start(f32[1,6912]{1,0:T(1,128)S(1)} %get-tuple-element.203), channel_id=1, source_target_pairs={{0,4},{1,5},{2,6},{3,7},{4,0},{5,1},{6,2},{7,3},{8,12},{9,13},{10,... | collective-permute-start | bytes 82952 | tf_op jit(solution)/shard_map/ppermute | solution.py:750
  316.4 5.6 %collective-permute-start.29 = (f32[1,6912]{1,0:T(1,128)S(1)}, f32[1,6912]{1,0:T(1,128)S(1)}, u32[]{:S(2)}, u32[]{:S(2)}) collective-permute-start(f32[1,6912]{1,0:T(1,128)S(1)} %get-tuple-element.206), channel_id=1, source_target_pairs={{0,8},{1,9},{2,10},{3,11},{4,12},{5,13},{6,14},{7,15},{8,0},{9,1},... | collective-permute-start | bytes 82952 | tf_op jit(solution)/shard_map/ppermute | solution.py:750
  321.9 4.8 %collective-permute-start.31 = (f32[1,6912]{1,0:T(1,128)S(1)}, f32[1,6912]{1,0:T(1,128)S(1)}, u32[]{:S(2)}, u32[]{:S(2)}) collective-permute-start(f32[1,6912]{1,0:T(1,128)S(1)} %get-tuple-element.212), channel_id=1, source_target_pairs={{0,16},{1,17},{2,18},{3,19},{4,20},{5,21},{6,22},{7,23},{8,24},{9,... | collective-permute-start | bytes 82952 | tf_op jit(solution)/shard_map/ppermute | solution.py:750
  (25 other events, 72.9 us)
